TPU v7x, 32 devices: a whole 2x2x4 slice. The times are simulated.
32 devices in a mesh: plane: 8 (over y, x, core), depth: 4 (over z).
Axes of the slice: x: 2, y: 2, z: 4, core: 2. Of those that a mesh axis runs over, the one named last changes fastest.
Arguments:
- intensity: int32 [8, 768, 512], P(None, 'plane', 'depth'), may hold values from 0 to 255, as said below
- temp_start: float32 [192, 128], P(('plane', 'depth')), may hold values from 3.8 to 4.6
- cure_start: float32 [192, 128], P(('plane', 'depth')), may hold values from 0.02 to 0.3
- tool_levels: float32 [8], replicated, may hold values from 3.7 to 4.7
- plan: int32 [3, 2], replicated, may hold values from 0 to 7
Outputs:
- temp_final: float32 [192, 128], P(('plane', 'depth'))
- cure_final: float32 [192, 128], P(('plane', 'depth'))
- conduct: float32 [3, 192, 128], P(None, ('plane', 'depth'))
Inputs may be any that keep to these rules, and one draw needn't show every extreme that they name: `intensity`: grey levels of a woven laminate.
All inputs are finite; a program needn't handle non-finite values.
Results may differ from a plain program's by a relative error of at most 0.0003.
Values may be sent and summed in bfloat16 or wider, within the bound.
No kernel may reach another device: no remote copies, remote signals or barrier semaphores. Data moves between devices by JAX's collectives and lax.ppermute only.
A program may use at most 64 MiB of HBM per device.

v0:
```python
import jax
import jax.numpy as jnp
import numpy as np
from jax import lax
from jax.sharding import PartitionSpec as P

ROWS = 8
R1 = 6
R2 = 10
COARSE = 4
STEPS = 3
LEVELS = 8


sigma_grad = 2.0
sigma_tensor = 3.3
conduct_matrix = 0.3
conduct_fiber = 1.5
time_step = 0.25
heat_release = 0.4
rate_first = 0.15
rate_second = 0.6
energy_first = 30.0
energy_second = 25.0
reference_temp = 4.2
tensor_eps = 1e-06


def extended(x, sides, width):
    for axis, dim in sides:
        size, length = (lax.axis_size(axis), x.shape[dim])
        up = [(i, (i + 1) % size) for i in range(size - 1)]
        down = [(j, i) for i, j in up]
        last = lax.slice_in_dim(x, length - width, length, axis=dim)
        first = lax.slice_in_dim(x, 0, width, axis=dim)
        before = lax.ppermute(last, axis, up)
        after = lax.ppermute(first, axis, down)
        x = jnp.concatenate([before, x, after], axis=dim)
    return x


def smooth_taps(radius, sigma):
    offsets = np.arange(-radius, radius + 1) * 1.0
    weights = np.exp(-0.5 * offsets * offsets / (sigma * sigma))
    return weights / weights.sum()


def slope_taps(radius, sigma):
    offsets = np.arange(-radius, radius + 1) * 1.0
    weights = np.exp(-0.5 * offsets * offsets / (sigma * sigma))
    return offsets * weights / np.sum(offsets * offsets * weights)


def row_weights(count, radius, sigma):
    taps = smooth_taps(radius, sigma)
    result = np.zeros(count)
    for source in range(count):
        for target in range(count):
            offset = target - source
            result[source] += taps[offset + radius]
    return result


def valid_conv(values, taps, axis):
    span = len(taps)
    count = values.shape[axis] - span + 1
    total = float(taps[0]) * lax.slice_in_dim(values, 0, count, axis=axis)
    for offset in range(1, span):
        total = total + float(taps[offset]) * lax.slice_in_dim(
            values, offset, offset + count, axis=axis
        )
    return total


def same_conv(values, taps, axis):
    radius = (len(taps) - 1) // 2
    widths = [(0, 0)] * values.ndim
    widths[axis] = (radius, radius)
    return valid_conv(jnp.pad(values, widths), taps, axis)


def gradients(field):
    smooth_grad = smooth_taps(R1, sigma_grad)
    slope_grad = slope_taps(R1, sigma_grad)
    flat_z = valid_conv(field, smooth_grad, 2)
    slope_z = valid_conv(field, slope_grad, 2)
    along_x = valid_conv(same_conv(flat_z, smooth_grad, 0), slope_grad, 1)
    along_y = valid_conv(same_conv(flat_z, slope_grad, 0), smooth_grad, 1)
    along_z = valid_conv(same_conv(slope_z, smooth_grad, 0), smooth_grad, 1)
    return (along_y, along_x, along_z)


def reduced_products(field, inside):
    along_y, along_x, along_z = gradients(field)
    weights = jnp.asarray(row_weights(ROWS, R2, sigma_tensor), jnp.float32)[:, None, None]
    pairs = (
        (along_y, along_y),
        (along_x, along_x),
        (along_z, along_z),
        (along_y, along_x),
        (along_y, along_z),
        (along_x, along_z),
    )
    result = jnp.stack([jnp.sum(weights * first * second, axis=0) for first, second in pairs])
    return result * inside


def region_mask(first_x, first_z, count_x, count_z, total_x, total_z):
    position_x = first_x + jnp.arange(count_x, dtype=jnp.int32)[:, None]
    position_z = first_z + jnp.arange(count_z, dtype=jnp.int32)[None, :]
    inside = (position_x >= 0) & (position_x < total_x) & (position_z >= 0) & (position_z < total_z)
    return jnp.where(inside, 1.0, 0.0).astype(jnp.float32)


def smooth_tensor(products):
    taps = smooth_taps(R2, sigma_tensor)
    return valid_conv(valid_conv(products, taps, 1), taps, 2)


def coarse_sums(tensor):
    fields, count_x, count_z = tensor.shape
    return tensor.reshape(fields, count_x // COARSE, COARSE, count_z // COARSE, COARSE).sum(
        axis=(2, 4)
    )


def conductivity(sums):
    trace = sums[0] + sums[1] + sums[2]
    scale = (conduct_fiber - conduct_matrix) / (2.0 * trace + tensor_eps)
    return jnp.stack(
        [
            conduct_matrix + scale * (trace - sums[1]),
            -scale * sums[5],
            conduct_matrix + scale * (trace - sums[2]),
        ]
    )


def tool_value(levels, index):
    return jnp.sum(
        jnp.where(jnp.arange(LEVELS, dtype=jnp.int32) == index, levels, jnp.zeros_like(levels))
    )


def cure_rate(temp, cure):
    first = rate_first * jnp.exp(energy_first * (1.0 / reference_temp - 1.0 / temp))
    second = rate_second * jnp.exp(energy_second * (1.0 / reference_temp - 1.0 / temp))
    return (first + second * jnp.sqrt(cure)) * (1.0 - cure) ** 1.5


def advance(padded, conduct, cure, top, bottom):
    height = padded.shape[0]
    upper = jnp.broadcast_to(top, (height, 1)).astype(padded.dtype)
    lower = jnp.broadcast_to(bottom, (height, 1)).astype(padded.dtype)
    full = jnp.concatenate([upper, padded, lower], axis=1)
    centre = full[1:-1, 1:-1]
    second_x = full[2:, 1:-1] - 2.0 * centre + full[:-2, 1:-1]
    second_z = full[1:-1, 2:] - 2.0 * centre + full[1:-1, :-2]
    cross = 0.25 * (full[2:, 2:] - full[2:, :-2] - full[:-2, 2:] + full[:-2, :-2])
    spread = conduct[0] * second_x + 2.0 * conduct[1] * cross + conduct[2] * second_z
    rate = cure_rate(centre, cure)
    return (centre + time_step * (spread + heat_release * rate), cure + time_step * rate)


def reflect(values, ghosts, axis, first, last):
    count = values.shape[axis]
    mirror_left = jnp.flip(lax.slice_in_dim(values, ghosts, 2 * ghosts, axis=axis), axis)
    mirror_right = jnp.flip(
        lax.slice_in_dim(values, count - 2 * ghosts, count - ghosts, axis=axis), axis
    )
    middle = lax.slice_in_dim(values, ghosts, count - ghosts, axis=axis)
    left = jnp.where(first, mirror_left, lax.slice_in_dim(values, 0, ghosts, axis=axis))
    right = jnp.where(
        last, mirror_right, lax.slice_in_dim(values, count - ghosts, count, axis=axis)
    )
    return jnp.concatenate([left, middle, right], axis=axis)


def on_device(intensity, temp_start, cure_start, tool_levels, plan):
    width = intensity.shape[1]
    depth = intensity.shape[2]
    plane_index = lax.axis_index("plane")
    depth_index = lax.axis_index("depth")
    total_x = width * lax.axis_size("plane")
    total_z = depth * lax.axis_size("depth")
    voxels = intensity.astype(jnp.bfloat16)
    wider = extended(voxels, (("plane", 1), ("depth", 2)), R1 + R2)
    field = wider.astype(jnp.float32) / 255.0
    inside = region_mask(
        plane_index * width - R2,
        depth_index * depth - R2,
        width + 2 * R2,
        depth + 2 * R2,
        total_x,
        total_z,
    )
    products = reduced_products(field, inside)
    conduct_local = conductivity(coarse_sums(smooth_tensor(products)))
    columns = lax.all_to_all(conduct_local, "depth", split_axis=1, concat_axis=2, tiled=True)
    flat_index = plane_index * lax.axis_size("depth") + depth_index
    first = flat_index == 0
    last = flat_index == lax.axis_size("plane") * lax.axis_size("depth") - 1
    tools = [
        (tool_value(tool_levels, plan[index, 0]), tool_value(tool_levels, plan[index, 1]))
        for index in range(STEPS)
    ]
    temp, cure = (temp_start, cure_start)
    for index in range(STEPS):
        padded = extended(temp, ((("plane", "depth"), 0),), 1)
        padded = reflect(padded, 1, 0, first, last)
        temp, cure = advance(padded, columns, cure, tools[index][0], tools[index][1])
    return (temp, cure, columns)


def solution(mesh):
    return jax.shard_map(
        on_device,
        mesh=mesh,
        in_specs=(
            P(None, "plane", "depth"),
            P(("plane", "depth"), None),
            P(("plane", "depth"), None),
            P(),
            P(),
        ),
        out_specs=(
            P(("plane", "depth"), None),
            P(("plane", "depth"), None),
            P(None, ("plane", "depth"), None),
        ),
        check_vma=False,
    )
```

profile of v0, /device:TPU:4, one launch (start us, length us, event | category | flops | bytes accessed | tf_op | source)
XLA Modules:
  0.0 108.5 jit_solution(4822084390055057190)
XLA Ops:
  1.7 1.9 %collective-permute-start = (bf16[8,16,128]{2,1,0:T(8,128)(2,1)S(1)}, bf16[8,16,128]{2,1,0:T(8,128)(2,1)S(1)}, u32[]{:S(2)}, u32[]{:S(2)}) collective-permute-start(bf16[8,16,128]{2,1,0:T(8,128)(2,1)S(1)} %get-tuple-element.24), channel_id=1, source_target_pairs={{0,4},{4,8},{8,12},{12,16},{16,20},{20,24},{24,28},{1,5},{5,9},{9,... | collective-permute-start | bytes 98312 | tf_op jit(solution)/shard_map/ppermute | solution.py:36
  3.6 4.5 %collective-permute-start.1 = (bf16[8,16,128]{2,1,0:T(8,128)(2,1)S(1)}, bf16[8,16,128]{2,1,0:T(8,128)(2,1)S(1)}, u32[]{:S(2)}, u32[]{:S(2)}) collective-permute-start(bf16[8,16,128]{2,1,0:T(8,128)(2,1)S(1)} %get-tuple-element.25), channel_id=1, source_target_pairs={{4,0},{8,4},{12,8},{16,12},{20,16},{24,20},{28,24},{5,1},{9,5},{13... | collective-permute-start | bytes 98312 | tf_op jit(solution)/shard_map/ppermute | solution.py:37
  8.9 4.9 %collective-permute-start.4 = (f32[1,128]{1,0:T(1,128)S(1)}, f32[1,128]{1,0:T(1,128)S(1)}, u32[]{:S(2)}, u32[]{:S(2)}) collective-permute-start(f32[1,128]{1,0:T(1,128)S(1)} %get-tuple-element.48), channel_id=1, source_target_pairs={{1,0},{2,1},{3,2},{4,3},{5,4},{6,5},{7,6},{8,7},{9,8},{10,9},{11,1... | collective-permute-start | bytes 1544 | tf_op jit(solution)/shard_map/ppermute | solution.py:37
  13.9 1.9 %collective-permute-start.5 = (f32[1,128]{1,0:T(1,128)S(1)}, f32[1,128]{1,0:T(1,128)S(1)}, u32[]{:S(2)}, u32[]{:S(2)}) collective-permute-start(f32[1,128]{1,0:T(1,128)S(1)} %get-tuple-element.47), channel_id=1, source_target_pairs={{0,1},{1,2},{2,3},{3,4},{4,5},{5,6},{6,7},{7,8},{8,9},{9,10},{10,1... | collective-permute-start | bytes 1544 | tf_op jit(solution)/shard_map/ppermute | solution.py:36
  17.5 5.2 %fusion.153 = (f32[]{:T(128)}, f32[]{:T(128)}, f32[]{:T(128)}, f32[]{:T(128)}, f32[]{:T(128)}, /*index=5*/f32[]{:T(128)}) fusion(f32[8]{0:T(128)} %param.9, s32[]{:T(128)} %bitcast.13, s32[]{:T(128)} %bitcast.11, s32[]{:T(128)} %bitcast.10, s32[]{:T(128)} %bitcast.9, s32[]{:T(128)} %bitcast.8, s32[]{:T(128)} %bitcast.12), kind=kLoop, calls=%fused_computation.333 | loop fusion | flops 138 | bytes 80 | tf_op jit(solution)/shard_map/reduce_sum | solution.py:140
  23.6 2.5 %collective-permute-start.2 = (bf16[8,128,16]{2,1,0:T(8,128)(2,1)S(1)}, bf16[8,128,16]{2,1,0:T(8,128)(2,1)S(1)}, u32[]{:S(2)}, u32[]{:S(2)}) collective-permute-start(bf16[8,128,16]{2,1,0:T(8,128)(2,1)S(1)} %get-tuple-element.22), channel_id=1, source_target_pairs={{0,1},{1,2},{2,3},{4,5},{5,6},{6,7},{8,9},{9,10},{10,11},{12,13},{... | collective-permute-start | bytes 98312 | tf_op jit(solution)/shard_map/ppermute | solution.py:36
  28.1 3.4 %collective-permute-done.2 = bf16[8,128,16]{2,1,0:T(8,128)(2,1)S(1)} collective-permute-done((bf16[8,128,16]{2,1,0:T(8,128)(2,1)S(1)}, bf16[8,128,16]{2,1,0:T(8,128)(2,1)S(1)}, u32[]{:S(2)}, u32[]{:S(2)}) %collective-permute-start.2) | collective-permute-done | bytes 32800 | tf_op jit(solution)/shard_map/ppermute | solution.py:36
  31.5 4.1 %collective-permute-done.3 = bf16[8,128,16]{2,1,0:T(8,128)(2,1)S(1)} collective-permute-done((bf16[8,128,16]{2,1,0:T(8,128)(2,1)S(1)}, bf16[8,128,16]{2,1,0:T(8,128)(2,1)S(1)}, u32[]{:S(2)}, u32[]{:S(2)}) %collective-permute-start.3) | collective-permute-done | bytes 32800 | tf_op jit(solution)/shard_map/ppermute | solution.py:37
  36.0 3.3 %multiply_add_fusion.3 = f32[8,128,148]{2,1,0:T(8,128)S(1)} fusion(f32[8,128,160]{2,1,0:T(8,128)S(1)} %convert_multiply_fusion), kind=kLoop, calls=%fused_computation.57 | loop fusion | flops 3788800 | bytes 8486912 | tf_op jit(solution)/shard_map/add | solution.py:69
  39.3 3.3 %multiply_add_fusion = f32[8,128,148]{2,1,0:T(8,128)S(1)} fusion(f32[8,128,160]{2,1,0:T(8,128)S(1)} %convert_multiply_fusion), kind=kLoop, calls=%fused_computation.54 | loop fusion | flops 3788800 | bytes 8486912 | tf_op jit(solution)/shard_map/add | solution.py:69
  44.5 5.3 %fusion.28 = (f32[116,148]{1,0:T(8,128)S(1)}, f32[116,148]{1,0:T(8,128)S(1)}, f32[116,148]{1,0:T(8,128)S(1)}, f32[116,148]{1,0:T(8,128)S(1)}, f32[116,148]{1,0:T(8,128)S(1)}, /*index=5*/f32[116,148]{1,0:T(8,128)S(1)}) fusion(f32[8]{0:T(128)S(1)} %copy-done.2, f32[8,128,148]{2,1,0:T(8,128)S(1)} %fusion.12, f32[8,128,148]{2,1,0:T(8,128)S(1)} %get-tuple-element.20, ...), kind=kLoop, calls=%fused_computation.63 | loop fusion | flops 12257952 | bytes 21837728 | tf_op jit(solution)/shard_map/reduce_sum | solution.py:104
  51.5 1.6 %fusion.86 = f32[6,96,128]{2,1,0:T(8,128)S(1)} fusion(f32[6,96,148]{2,1,0:T(8,128)S(1)} %fusion.66), kind=kLoop, calls=%fused_computation.183 | loop fusion | flops 3022848 | bytes 6488064 | tf_op jit(solution)/shard_map/add | solution.py:69
  53.1 11.2 %reshape.82 = f32[6,24,4,32,4]{4,3,2,1,0:T(8,128)} reshape(f32[6,96,128]{2,1,0:T(8,128)S(1)} %fusion.86) | data formatting | bytes 589824 | tf_op jit(solution)/shard_map/reshape | solution.py:122
  64.3 4.5 %reduce_sum.123 = f32[6,24,32]{2,1,0:T(8,128)S(1)} reduce(f32[6,24,4,32,4]{4,3,2,1,0:T(8,128)} %reshape.82, f32[]{:T(128)} %constant.66.clone.1), dimensions={2,4}, to_apply=%region_6.7 | reduce | flops 69120 | bytes 313348 | tf_op jit(solution)/shard_map/reduce_sum | solution.py:122
  69.5 5.4 %all-to-all-start = ((f32[4,1,576]{2,1,0:T(1,128)}), f32[4,1,576]{2,1,0:T(1,128)S(1)}, u32[]{:S(2)}, u32[]{:S(2)}) async-start(f32[4,1,576]{2,1,0:T(1,128)} %reshape.83), calls=%async_computation | async-start | bytes 20480 | tf_op jit(solution)/shard_map/all_to_all | solution.py:199
  75.0 5.6 %all-to-all-done = f32[4,1,576]{2,1,0:T(1,128)S(1)} async-done(((f32[4,1,576]{2,1,0:T(1,128)}), f32[4,1,576]{2,1,0:T(1,128)S(1)}, u32[]{:S(2)}, u32[]{:S(2)}) %all-to-all-start) | async-done | bytes 9248 | tf_op jit(solution)/shard_map/all_to_all | solution.py:199
  83.5 2.1 %collective-permute-start.6 = (f32[1,128]{1,0:T(1,128)S(1)}, f32[1,128]{1,0:T(1,128)S(1)}, u32[]{:S(2)}, u32[]{:S(2)}) collective-permute-start(f32[1,128]{1,0:T(1,128)S(1)} %get-tuple-element.42), channel_id=1, source_target_pairs={{1,0},{2,1},{3,2},{4,3},{5,4},{6,5},{7,6},{8,7},{9,8},{10,9},{11,1... | collective-permute-start | bytes 1544 | tf_op jit(solution)/shard_map/ppermute | solution.py:37
  85.7 3.7 %collective-permute-start.7 = (f32[1,128]{1,0:T(1,128)S(1)}, f32[1,128]{1,0:T(1,128)S(1)}, u32[]{:S(2)}, u32[]{:S(2)}) collective-permute-start(f32[1,128]{1,0:T(1,128)S(1)} %get-tuple-element.41), channel_id=1, source_target_pairs={{0,1},{1,2},{2,3},{3,4},{4,5},{5,6},{6,7},{7,8},{8,9},{9,10},{10,1... | collective-permute-start | bytes 1544 | tf_op jit(solution)/shard_map/ppermute | solution.py:36
  89.4 4.7 %collective-permute-done.7 = f32[1,128]{1,0:T(1,128)S(1)} collective-permute-done((f32[1,128]{1,0:T(1,128)S(1)}, f32[1,128]{1,0:T(1,128)S(1)}, u32[]{:S(2)}, u32[]{:S(2)}) %collective-permute-start.7) | collective-permute-done | bytes 544 | tf_op jit(solution)/shard_map/ppermute | solution.py:36
  94.1 2.0 %multiply_add_fusion.6 = (f32[6,128]{1,0:T(8,128)}, f32[6,128]{1,0:T(8,128)S(1)}, f32[6,128]{1,0:T(8,128)S(1)}) fusion(f32[6,128]{1,0:T(8,128)S(1)} %fusion.116, f32[6,128]{1,0:T(8,128)S(1)} %copy-done.1, f32[6,128]{1,0:T(8,128)S(1)} %copy-done, f32[6,128]{1,0:T(8,128)S(1)} %squeeze.19, f32[6,128]{1,0:T(8,128)S(1)} %mul.892, ...), kind=kLoop, calls=%fused_computation.306 | loop fusion | flops 41472 | bytes 37896 | tf_op jit(solution)/shard_map/add | solution.py:162
  96.2 1.9 %collective-permute-start.8 = (f32[1,128]{1,0:T(1,128)S(1)}, f32[1,128]{1,0:T(1,128)S(1)}, u32[]{:S(2)}, u32[]{:S(2)}) collective-permute-start(f32[1,128]{1,0:T(1,128)S(1)} %get-tuple-element.36), channel_id=1, source_target_pairs={{1,0},{2,1},{3,2},{4,3},{5,4},{6,5},{7,6},{8,7},{9,8},{10,9},{11,1... | collective-permute-start | bytes 1544 | tf_op jit(solution)/shard_map/ppermute | solution.py:37
  98.1 3.9 %collective-permute-start.9 = (f32[1,128]{1,0:T(1,128)S(1)}, f32[1,128]{1,0:T(1,128)S(1)}, u32[]{:S(2)}, u32[]{:S(2)}) collective-permute-start(f32[1,128]{1,0:T(1,128)S(1)} %get-tuple-element.35), channel_id=1, source_target_pairs={{0,1},{1,2},{2,3},{3,4},{4,5},{5,6},{6,7},{7,8},{8,9},{9,10},{10,1... | collective-permute-start | bytes 1544 | tf_op jit(solution)/shard_map/ppermute | solution.py:36
  102.7 3.8 %collective-permute-done.9 = f32[1,128]{1,0:T(1,128)S(1)} collective-permute-done((f32[1,128]{1,0:T(1,128)S(1)}, f32[1,128]{1,0:T(1,128)S(1)}, u32[]{:S(2)}, u32[]{:S(2)}) %collective-permute-start.9) | collective-permute-done | bytes 544 | tf_op jit(solution)/shard_map/ppermute | solution.py:36
  106.6 1.9 %fusion.142 = f32[6,128]{1,0:T(8,128)} fusion(f32[6,128]{1,0:T(8,128)S(1)} %get-tuple-element.17, f32[6,128]{1,0:T(8,128)S(1)} %mul.892, f32[8,128]{1,0:T(8,128)S(1)} %pad_maximum_fusion.10, f32[]{:T(128)} %get-tuple-element.14, f32[6,128]{1,0:T(8,128)S(1)} %squeeze.19, f32[]{:T(128)} %get-tuple-element.9, f32[6,128]{1,0:T(8,128)S(1)} %squeeze.16, ...), kind=kLoop, calls=%fused_computation.293 | loop fusion | flops 21504 | bytes 28680 | tf_op jit(solution)/shard_map/add | solution.py:162
  (63 shorter events, 14.7 us)
Async XLA Ops:
  1.7 21.7 %collective-permute-start = (bf16[8,16,128]{2,1,0:T(8,128)(2,1)S(1)}, bf16[8,16,128]{2,1,0:T(8,128)(2,1)S(1)}, u32[]{:S(2)}, u32[]{:S(2)}) collective-permute-start(bf16[8,16,128]{2,1,0:T(8,128)(2,1)S(1)} %get-tuple-element.24), channel_id=1, source_target_pairs={{0,4},{4,8},{8,12},{12,16},{16,20},{20,24},{24,28},{1,5},{5,9},{9,... | collective-permute-start | bytes 98312 | tf_op jit(solution)/shard_map/ppermute | solution.py:36
  3.6 19.8 %collective-permute-start.1 = (bf16[8,16,128]{2,1,0:T(8,128)(2,1)S(1)}, bf16[8,16,128]{2,1,0:T(8,128)(2,1)S(1)}, u32[]{:S(2)}, u32[]{:S(2)}) collective-permute-start(bf16[8,16,128]{2,1,0:T(8,128)(2,1)S(1)} %get-tuple-element.25), channel_id=1, source_target_pairs={{4,0},{8,4},{12,8},{16,12},{20,16},{24,20},{28,24},{5,1},{9,5},{13... | collective-permute-start | bytes 98312 | tf_op jit(solution)/shard_map/ppermute | solution.py:37
  8.9 13.7 %collective-permute-start.4 = (f32[1,128]{1,0:T(1,128)S(1)}, f32[1,128]{1,0:T(1,128)S(1)}, u32[]{:S(2)}, u32[]{:S(2)}) collective-permute-start(f32[1,128]{1,0:T(1,128)S(1)} %get-tuple-element.48), channel_id=1, source_target_pairs={{1,0},{2,1},{3,2},{4,3},{5,4},{6,5},{7,6},{8,7},{9,8},{10,9},{11,1... | collective-permute-start | bytes 1544 | tf_op jit(solution)/shard_map/ppermute | solution.py:37
  13.9 8.8 %collective-permute-start.5 = (f32[1,128]{1,0:T(1,128)S(1)}, f32[1,128]{1,0:T(1,128)S(1)}, u32[]{:S(2)}, u32[]{:S(2)}) collective-permute-start(f32[1,128]{1,0:T(1,128)S(1)} %get-tuple-element.47), channel_id=1, source_target_pairs={{0,1},{1,2},{2,3},{3,4},{4,5},{5,6},{6,7},{7,8},{8,9},{9,10},{10,1... | collective-permute-start | bytes 1544 | tf_op jit(solution)/shard_map/ppermute | solution.py:36
  23.6 8.0 %collective-permute-start.2 = (bf16[8,128,16]{2,1,0:T(8,128)(2,1)S(1)}, bf16[8,128,16]{2,1,0:T(8,128)(2,1)S(1)}, u32[]{:S(2)}, u32[]{:S(2)}) collective-permute-start(bf16[8,128,16]{2,1,0:T(8,128)(2,1)S(1)} %get-tuple-element.22), channel_id=1, source_target_pairs={{0,1},{1,2},{2,3},{4,5},{5,6},{6,7},{8,9},{9,10},{10,11},{12,13},{... | collective-permute-start | bytes 98312 | tf_op jit(solution)/shard_map/ppermute | solution.py:36
  26.0 9.6 %collective-permute-start.3 = (bf16[8,128,16]{2,1,0:T(8,128)(2,1)S(1)}, bf16[8,128,16]{2,1,0:T(8,128)(2,1)S(1)}, u32[]{:S(2)}, u32[]{:S(2)}) collective-permute-start(bf16[8,128,16]{2,1,0:T(8,128)(2,1)S(1)} %get-tuple-element.23), channel_id=1, source_target_pairs={{1,0},{2,1},{3,2},{5,4},{6,5},{7,6},{9,8},{10,9},{11,10},{13,12},{... | collective-permute-start | bytes 98312 | tf_op jit(solution)/shard_map/ppermute | solution.py:37
  42.6 1.9 %copy-start.2 = (f32[8]{0:T(128)S(1)}, f32[8]{0:T(128)}, u32[]{:S(2)}) copy-start(f32[8]{0:T(128)} %constant.27.clone) | copy-start | bytes 100
  64.3 10.7 %copy-start = (f32[6,128]{1,0:T(8,128)S(1)}, f32[6,128]{1,0:T(8,128)}, u32[]{:S(2)}) copy-start(f32[6,128]{1,0:T(8,128)} %param.7) | copy-start | bytes 9220
  64.3 17.9 %copy-start.1 = (f32[6,128]{1,0:T(8,128)S(1)}, f32[6,128]{1,0:T(8,128)}, u32[]{:S(2)}) copy-start(f32[6,128]{1,0:T(8,128)} %param.8) | copy-start | bytes 9220
  69.5 11.0 %all-to-all-start = ((f32[4,1,576]{2,1,0:T(1,128)}), f32[4,1,576]{2,1,0:T(1,128)S(1)}, u32[]{:S(2)}, u32[]{:S(2)}) async-start(f32[4,1,576]{2,1,0:T(1,128)} %reshape.83), calls=%async_computation | async-start | bytes 20480 | tf_op jit(solution)/shard_map/all_to_all | solution.py:199
  83.5 5.9 %collective-permute-start.6 = (f32[1,128]{1,0:T(1,128)S(1)}, f32[1,128]{1,0:T(1,128)S(1)}, u32[]{:S(2)}, u32[]{:S(2)}) collective-permute-start(f32[1,128]{1,0:T(1,128)S(1)} %get-tuple-element.42), channel_id=1, source_target_pairs={{1,0},{2,1},{3,2},{4,3},{5,4},{6,5},{7,6},{8,7},{9,8},{10,9},{11,1... | collective-permute-start | bytes 1544 | tf_op jit(solution)/shard_map/ppermute | solution.py:37
  85.7 8.5 %collective-permute-start.7 = (f32[1,128]{1,0:T(1,128)S(1)}, f32[1,128]{1,0:T(1,128)S(1)}, u32[]{:S(2)}, u32[]{:S(2)}) collective-permute-start(f32[1,128]{1,0:T(1,128)S(1)} %get-tuple-element.41), channel_id=1, source_target_pairs={{0,1},{1,2},{2,3},{3,4},{4,5},{5,6},{6,7},{7,8},{8,9},{9,10},{10,1... | collective-permute-start | bytes 1544 | tf_op jit(solution)/shard_map/ppermute | solution.py:36
  96.2 6.6 %collective-permute-start.8 = (f32[1,128]{1,0:T(1,128)S(1)}, f32[1,128]{1,0:T(1,128)S(1)}, u32[]{:S(2)}, u32[]{:S(2)}) collective-permute-start(f32[1,128]{1,0:T(1,128)S(1)} %get-tuple-element.36), channel_id=1, source_target_pairs={{1,0},{2,1},{3,2},{4,3},{5,4},{6,5},{7,6},{8,7},{9,8},{10,9},{11,1... | collective-permute-start | bytes 1544 | tf_op jit(solution)/shard_map/ppermute | solution.py:37
  98.1 8.5 %collective-permute-start.9 = (f32[1,128]{1,0:T(1,128)S(1)}, f32[1,128]{1,0:T(1,128)S(1)}, u32[]{:S(2)}, u32[]{:S(2)}) collective-permute-start(f32[1,128]{1,0:T(1,128)S(1)} %get-tuple-element.35), channel_id=1, source_target_pairs={{0,1},{1,2},{2,3},{3,4},{4,5},{5,6},{6,7},{7,8},{8,9},{9,10},{10,1... | collective-permute-start | bytes 1544 | tf_op jit(solution)/shard_map/ppermute | solution.py:36
where the time goes:
time: 109 us; the launch traced here: 108 us
  other arithmetic  35.6 us (33%)
  starting transfers between devices  34.2 us (31%)
  waiting for transfers between devices  21.7 us (20%)
  local copies, waits for them, and re-layouts  16 us (15%)
    ppermute x5, starting transfers between devices, extended(): after = lax.ppermute(first, axis, down)  14.8 us
    ppermute x5, starting transfers between devices, extended(): before = lax.ppermute(last, axis, up)  14 us
    ppermute x5, waiting for transfers between devices, extended(): before = lax.ppermute(last, axis, up)  11.9 us
    add x6, other arithmetic, valid_conv(): total + float(taps[offset]) * lax.slice_in_dim(values, offset, offset + c...  11.5 us
    reshape x1, local copies, waits for them, and re-layouts, coarse_sums(): tensor.reshape(fields, count_x // COARSE, COARSE, count_z // COARSE, COARSE)  11.2 us
    all_to_all x1, waiting for transfers between devices, on_device(): lax.all_to_all(conduct_local, 'depth', split_axis=1, concat_axis=2, tiled...  5.58 us
    all_to_all x1, starting transfers between devices, on_device(): lax.all_to_all(conduct_local, 'depth', split_axis=1, concat_axis=2, tiled...  5.44 us
    reduce_sum x1, other arithmetic, reduced_products(): jnp.sum(weights * first * second, axis=0)  5.29 us
  transfers between devices with their start and end apart: 11, of which 5 were waited for; matrix products, arithmetic and copies ran while one was open for 8% of the time, Pallas kernels for 0%

commit v1 on v0

v1 whole, which is shorter than its diff:
```python
import functools

import jax
import jax.numpy as jnp
import ml_dtypes
import numpy as np
from jax import lax
from jax.experimental import pallas as pl
from jax.experimental.pallas import tpu as pltpu
from jax.sharding import PartitionSpec as P

ROWS = 8
R1 = 6
R2 = 10
COARSE = 4
STEPS = 3

sigma_grad = 2.0
sigma_tensor = 3.3
conduct_matrix = 0.3
conduct_fiber = 1.5
time_step = 0.25
heat_release = 0.4
rate_first = 0.15
rate_second = 0.6
energy_first = 30.0
energy_second = 25.0
reference_temp = 4.2
tensor_eps = 1e-06

EDGE = 32
RIM = R1 + R2
LANES = 128
HALO = 2
GHOST = 3
BEFORE = EDGE // 2 // COARSE


def smooth_taps(radius, sigma):
    offsets = np.arange(-radius, radius + 1) * 1.0
    weights = np.exp(-0.5 * offsets * offsets / (sigma * sigma))
    return weights / weights.sum()


def slope_taps(radius, sigma):
    offsets = np.arange(-radius, radius + 1) * 1.0
    weights = np.exp(-0.5 * offsets * offsets / (sigma * sigma))
    return offsets * weights / np.sum(offsets * offsets * weights)


def row_weights(count, radius, sigma):
    taps = smooth_taps(radius, sigma)
    result = np.zeros(count)
    for source in range(count):
        for target in range(count):
            offset = target - source
            if abs(offset) <= radius:
                result[source] += taps[offset + radius]
    return result


def halves(matrix):
    high = matrix.astype(np.float32).astype(ml_dtypes.bfloat16)
    low = (matrix - high.astype(np.float64)).astype(np.float32).astype(ml_dtypes.bfloat16)
    return high, low


def sizes(width, depth):
    columns = width // COARSE + 2 * HALO
    cells = depth // COARSE + BEFORE
    span_x = columns * COARSE + 2 * R2
    span_z = cells * COARSE + 2 * R2
    pad_x = -(-span_x // 16) * 16
    return columns, cells, span_x, span_z, pad_x


def x_bands(width, depth):
    columns, cells, span_x, span_z, pad_x = sizes(width, depth)
    bands = np.zeros((2, pad_x, width + 2 * EDGE))
    first = EDGE - HALO * COARSE - R2 - R1
    for kind, taps in enumerate((smooth_taps(R1, sigma_grad), slope_taps(R1, sigma_grad))):
        for out in range(span_x):
            bands[kind, out, out + first : out + first + 2 * R1 + 1] = taps
    return bands.reshape(2 * pad_x, -1)


def z_bands(width, depth):
    columns, cells, span_x, span_z, pad_x = sizes(width, depth)
    bands = np.zeros((2, depth + LANES, 2 * LANES))
    for kind, taps in enumerate((smooth_taps(R1, sigma_grad), slope_taps(R1, sigma_grad))):
        for out in range(span_z):
            for k in range(2 * R1 + 1):
                place = out + k - R1 - R2 - BEFORE * COARSE
                if 0 <= place < depth:
                    bands[kind, place, out] = taps[k]
                elif -EDGE <= place < 0:
                    bands[kind, depth + EDGE + place, out] = taps[k]
    return bands


def coarse_bands(count, padded_in, padded_out):
    taps = smooth_taps(R2, sigma_tensor)
    bands = np.zeros((padded_in, padded_out))
    for cell in range(count):
        for voxel in range(COARSE):
            start = cell * COARSE + voxel
            bands[start : start + 2 * R2 + 1, cell] += taps
    return bands


def three_parts(values):
    high = values.astype(jnp.bfloat16).astype(jnp.float32)
    rest = values - high
    middle = rest.astype(jnp.bfloat16).astype(jnp.float32)
    return high, middle, (rest - middle).astype(jnp.bfloat16).astype(jnp.float32)


def column_slot(temp_ref, cure_ref, first):
    pad = jnp.zeros((8 - 2 * GHOST, temp_ref.shape[1]), jnp.float32)
    rows = pl.ds(first, GHOST)
    both = jnp.concatenate([temp_ref[rows, :], cure_ref[rows, :], pad], axis=0)
    high, middle, low = three_parts(both)
    return jnp.concatenate([high, middle, low, jnp.zeros_like(high)], axis=0).astype(jnp.bfloat16)


def pack_kernel(intensity, temp, cure, up, to_left, to_right, up_left, up_right):
    rows, width, depth = intensity.shape
    lane = lax.broadcasted_iota(jnp.int32, (width, depth), 1)
    for pair in range(2):
        packed = jnp.zeros((width, depth), jnp.float32)
        for block in range(rows // 2):
            values = intensity[2 * block + pair].astype(jnp.float32)
            shift = (EDGE * block + EDGE) % depth
            moved = values if shift == 0 else pltpu.roll(values, shift, 1)
            inside = (lane >= EDGE * block) & (lane < EDGE * block + EDGE)
            packed = jnp.where(inside, moved, packed)
        packed = packed.astype(jnp.bfloat16)
        up[pair] = packed
        up_left[pair] = packed[:EDGE]
        up_right[pair] = packed[width - EDGE :]
    for row in range(rows):
        to_left[row] = intensity[row, :EDGE, :].astype(jnp.float32).astype(jnp.bfloat16)
        to_right[row] = intensity[row, width - EDGE :, :].astype(jnp.float32).astype(jnp.bfloat16)
    count = temp.shape[0]
    left, right = column_slot(temp, cure, 0), column_slot(temp, cure, count - GHOST)
    for slot in range(temp.shape[1] // LANES):
        to_left[rows + slot] = left[:, slot * LANES : (slot + 1) * LANES]
        to_right[rows + slot] = right[:, slot * LANES : (slot + 1) * LANES]


def joined_columns(ref, rows):
    slots = [ref[slot].astype(jnp.float32) for slot in range(rows, ref.shape[0])]
    parts = jnp.concatenate(slots, axis=1)
    return (parts[0:8] + parts[8:16]) + parts[16:24]


def tensor_kernel(
    intensity, temp, cure, below, from_left, from_right, below_left, below_right,
    xh, xl, zh, zl, sx, sz, out, window, across, filtered, grads, products,
):
    rows, width, depth = intensity.shape
    columns, cells, span_x, span_z, pad_x = sizes(width, depth)
    planes, depths = lax.axis_size("plane"), lax.axis_size("depth")
    plane, layer = lax.axis_index("plane"), lax.axis_index("depth")

    for row in range(rows):
        half = (row % 2) * depth
        window[row // 2, 0:EDGE, half : half + depth] = from_left[row]
        window[row // 2, EDGE : EDGE + width, half : half + depth] = (
            intensity[row].astype(jnp.float32).astype(jnp.bfloat16)
        )
        window[row // 2, EDGE + width :, half : half + depth] = from_right[row]
    for pair in range(2):
        half = pair * depth
        window[rows // 2, 0:EDGE, half : half + depth] = below_left[pair]
        window[rows // 2, EDGE : EDGE + width, half : half + depth] = below[pair]
        window[rows // 2, EDGE + width :, half : half + depth] = below_right[pair]

    for pair in range(rows // 2 + 1):
        values = window[pair]
        result = jnp.dot(xh[...], values, preferred_element_type=jnp.float32) + jnp.dot(
            xl[...], values, preferred_element_type=jnp.float32
        )
        across[2 * pair] = result[:, :depth]
        across[2 * pair + 1] = result[:, depth:]

    smooth, slope = smooth_taps(R1, sigma_grad), slope_taps(R1, sigma_grad)

    def along_rows(taps, values, row):
        total = None
        for source in range(rows):
            offset = source - row
            tap = float(taps[offset + R1]) if abs(offset) <= R1 else 0.0
            if tap != 0.0:
                term = tap * values[source]
                total = term if total is None else total + term
        return total

    def filter_rows(group, carry):
        start = pl.multiple_of(group * 16, 16)
        for tile in range(2):
            kinds = []
            for kind in range(2):
                place = pl.ds(kind * pad_x + start, 16)
                if tile == 0:
                    kinds.append([across[row, place, :] for row in range(rows)])
                else:
                    packed = [across[rows + pair, place, :] for pair in range(2)]
                    kinds.append(
                        [
                            packed[row % 2]
                            if row < 2
                            else pltpu.roll(packed[row % 2], depth - EDGE * (row // 2), 1)
                            for row in range(rows)
                        ]
                    )
            flat, steep = kinds
            lanes = pl.ds(tile * depth, depth)
            for row in range(rows):
                target = (row, pl.ds(start, 16), lanes)
                filtered[(0,) + target] = along_rows(slope, flat, row).astype(jnp.bfloat16)
                filtered[(1,) + target] = along_rows(smooth, steep, row).astype(jnp.bfloat16)
                filtered[(2,) + target] = along_rows(smooth, flat, row).astype(jnp.bfloat16)
        return carry

    lax.fori_loop(0, pad_x // 16, filter_rows, 0)

    for kind in range(3):
        band = 1 if kind == 2 else 0
        for row in range(rows):
            values = filtered[kind, row]
            grads[kind, row] = jnp.dot(
                values, zh[band], preferred_element_type=jnp.float32
            ) + jnp.dot(values, zl[band], preferred_element_type=jnp.float32)

    weights = row_weights(rows, R2, sigma_tensor) / (255.0 * 255.0)
    pairs = ((0, 0), (1, 1), (2, 2), (0, 1), (0, 2), (1, 2))

    def multiply(group, carry):
        start = pl.multiple_of(group * 16, 16)
        for tile in range(2):
            place = (pl.ds(start, 16), pl.ds(tile * LANES, LANES))
            x_at = plane * width - HALO * COARSE - R2 + start
            x_at = x_at + lax.broadcasted_iota(jnp.int32, (16, LANES), 0)
            z_at = layer * depth - BEFORE * COARSE - R2 + tile * LANES
            z_at = z_at + lax.broadcasted_iota(jnp.int32, (16, LANES), 1)
            inside = (x_at >= 0) & (x_at < planes * width) & (z_at >= 0) & (z_at < depths * depth)
            inside = jnp.where(inside, 1.0, 0.0)
            totals = [None] * 6
            for row in range(rows):
                three = [grads[(kind, row) + place] for kind in range(3)]
                weighted = [float(weights[row]) * value for value in three]
                for index, (first, second) in enumerate(pairs):
                    term = weighted[first] * three[second]
                    totals[index] = term if row == 0 else totals[index] + term
            for index in range(6):
                products[(index,) + place] = (totals[index] * inside).astype(jnp.bfloat16)
        return carry

    lax.fori_loop(0, pad_x // 16, multiply, 0)

    sums = []
    for index in range(6):
        if index in (3, 4):
            continue
        part = jnp.dot(products[index], sz[...], preferred_element_type=jnp.float32)
        sums.append(jnp.dot(sx[...], part.astype(jnp.bfloat16), preferred_element_type=jnp.float32))
    trace = sums[0] + sums[1] + sums[2]
    scale = (conduct_fiber - conduct_matrix) / (2.0 * trace + tensor_eps)
    xx = conduct_matrix + scale * (trace - sums[1])
    xz = -scale * sums[3]
    zz = conduct_matrix + scale * (trace - sums[2])
    lane = lax.broadcasted_iota(jnp.int32, xx.shape, 1)
    joined = jnp.where(
        lane < cells,
        xx,
        jnp.where(lane < 2 * cells, pltpu.roll(xz, cells, 1), pltpu.roll(zz, 2 * cells, 1)),
    )

    count = temp.shape[0]
    lanes = temp.shape[1]
    pad = jnp.zeros((8 - 2 * GHOST, lanes), jnp.float32)
    own_first = jnp.concatenate([temp[0:GHOST, :], cure[0:GHOST, :], pad], axis=0)
    own_last = jnp.concatenate([temp[count - GHOST :, :], cure[count - GHOST :, :], pad], axis=0)
    left, right = joined_columns(from_left, rows), joined_columns(from_right, rows)
    height = count + 2 * HALO
    for target in range(out.shape[0]):
        piece = jnp.where(layer == target - 1, own_last, 0.0)
        piece = jnp.where(layer == target + 1, own_first, piece)
        if target == 0:
            piece = jnp.where(layer == depths - 1, left, piece)
        if target == out.shape[0] - 1:
            piece = jnp.where(layer == 0, right, piece)
        out[target, 0:height, 0:LANES] = joined[count * target : count * target + height]
        if lanes > LANES:
            out[target, 0:height, LANES:] = jnp.zeros((height, lanes - LANES), jnp.float32)
        out[target, height : height + 2 * GHOST, :] = piece[0 : 2 * GHOST]
        spare = out.shape[1] - height - 2 * GHOST
        if spare:
            out[target, height + 2 * GHOST :, :] = jnp.zeros((spare, lanes), jnp.float32)


def cure_kernel(cells, chunks, temp_in, cure_in, levels, plan, temp_out, cure_out, conduct_out):
    count, lanes = temp_in.shape
    parts = chunks.shape[0]
    planes, depths = lax.axis_size("plane"), lax.axis_size("depth")
    plane, layer = lax.axis_index("plane"), lax.axis_index("depth")
    height = count + 2 * HALO
    own = cells - BEFORE
    lane = lax.broadcasted_iota(jnp.int32, (16, lanes), 1)
    row = lax.broadcasted_iota(jnp.int32, (16, lanes), 0)

    conduct = [jnp.zeros((16, lanes), jnp.float32) for _ in range(3)]
    for part in range(parts):
        chunk = chunks[part, 0:16, :]
        here = lane >= own * part - BEFORE
        for kind in range(3):
            shift = (own * part - BEFORE - kind * cells) % lanes
            moved = chunk if shift == 0 else pltpu.roll(chunk, shift, 1)
            conduct[kind] = jnp.where(here, moved, conduct[kind])
    for kind in range(3):
        conduct_out[kind] = conduct[kind][HALO : HALO + count]

    before = chunks[lax.rem(layer + parts - 1, parts)][height : height + 2 * GHOST]
    after = chunks[lax.rem(layer + 1, parts)][height : height + 2 * GHOST]
    spare = jnp.full((16 - count - 2 * GHOST, lanes), 0.5, jnp.float32)
    temp = jnp.concatenate([before[:GHOST], temp_in[...], after[:GHOST], 8.0 * spare], axis=0)
    cure = jnp.concatenate([before[GHOST:], cure_in[...], after[GHOST:], spare], axis=0)
    gap = GHOST - HALO
    xx, xz, zz = [pltpu.roll(part, gap, 0) for part in conduct]

    first = (plane == 0) & (layer == 0)
    last = (plane == planes - 1) & (layer == depths - 1)
    for step in range(STEPS):
        top, bottom = levels[plan[step, 0]], levels[plan[step, 1]]
        temp = jnp.where((row < GHOST) & first, temp[GHOST : GHOST + 1], temp)
        temp = jnp.where(
            (row >= GHOST + count) & last, temp[GHOST + count - 1 : GHOST + count], temp
        )
        cooler = jnp.where(lane == 0, top, pltpu.roll(temp, 1, 1))
        later = jnp.where(lane == lanes - 1, bottom, pltpu.roll(temp, lanes - 1, 1))
        slant = later - cooler
        second_x = pltpu.roll(temp, 15, 0) - 2.0 * temp + pltpu.roll(temp, 1, 0)
        second_z = later - 2.0 * temp + cooler
        cross = 0.25 * (pltpu.roll(slant, 15, 0) - pltpu.roll(slant, 1, 0))
        spread = xx * second_x + 2.0 * xz * cross + zz * second_z
        inverse = 1.0 / reference_temp - 1.0 / temp
        left = 1.0 - cure
        rate = rate_first * jnp.exp(energy_first * inverse) + rate_second * jnp.exp(
            energy_second * inverse
        ) * jnp.sqrt(cure)
        rate = rate * (left * jnp.sqrt(left))
        temp = temp + time_step * (spread + heat_release * rate)
        cure = cure + time_step * rate
    temp_out[...] = temp[GHOST : GHOST + count]
    cure_out[...] = cure[GHOST : GHOST + count]


def on_device(intensity, temp_start, cure_start, tool_levels, plan):
    rows, width, depth = intensity.shape
    count, lanes = temp_start.shape
    planes, depths = lax.axis_size("plane"), lax.axis_size("depth")
    columns, cells, span_x, span_z, pad_x = sizes(width, depth)
    bf16 = jnp.bfloat16
    slots = rows + lanes // LANES
    params = pltpu.CompilerParams(vmem_limit_bytes=48 * 1024 * 1024)

    up, to_left, to_right, up_left, up_right = pl.pallas_call(
        pack_kernel,
        name="pack",
        out_shape=(
            jax.ShapeDtypeStruct((2, width, depth), bf16),
            jax.ShapeDtypeStruct((slots, EDGE, depth), bf16),
            jax.ShapeDtypeStruct((slots, EDGE, depth), bf16),
            jax.ShapeDtypeStruct((2, EDGE, depth), bf16),
            jax.ShapeDtypeStruct((2, EDGE, depth), bf16),
        ),
        compiler_params=params,
    )(intensity, temp_start, cure_start)

    def shifted(values, by_plane, by_depth):
        pairs = []
        for p in range(planes):
            for d in range(depths):
                q, e = p + by_plane, d + by_depth
                if 0 <= q < planes and 0 <= e < depths:
                    pairs.append((p * depths + d, q * depths + e))
        return lax.ppermute(values, ("plane", "depth"), pairs)

    from_left = shifted(to_right, 1, 0)
    from_right = shifted(to_left, -1, 0)
    below = shifted(up, 0, 1)
    below_left = shifted(up_right, 1, 1)
    below_right = shifted(up_left, -1, 1)

    xh, xl = halves(x_bands(width, depth))
    zh, zl = halves(z_bands(width, depth))
    sx, _ = halves(coarse_bands(columns, pad_x, -(-columns // 16) * 16).T)
    sz, _ = halves(coarse_bands(cells, 2 * LANES, LANES))
    height = -(-(count + 2 * HALO + 2 * GHOST) // 8) * 8
    chunks = pl.pallas_call(
        tensor_kernel,
        name="tensor",
        out_shape=jax.ShapeDtypeStruct((depths, height, lanes), jnp.float32),
        scratch_shapes=[
            pltpu.VMEM((rows // 2 + 1, width + 2 * EDGE, 2 * depth), bf16),
            pltpu.VMEM((rows + 2, 2 * pad_x, depth), jnp.float32),
            pltpu.VMEM((3, rows, pad_x, 2 * LANES), bf16),
            pltpu.VMEM((3, rows, pad_x, 2 * LANES), jnp.float32),
            pltpu.VMEM((6, pad_x, 2 * LANES), bf16),
        ],
        compiler_params=params,
    )(
        intensity, temp_start, cure_start, below, from_left, from_right, below_left, below_right,
        *[jnp.asarray(part) for part in (xh, xl, zh, zl, sx, sz)],
    )

    chunks = lax.all_to_all(chunks, "depth", split_axis=0, concat_axis=0, tiled=True)

    vmem = pl.BlockSpec(memory_space=pltpu.VMEM)
    smem = pl.BlockSpec(memory_space=pltpu.SMEM)
    return pl.pallas_call(
        functools.partial(cure_kernel, cells),
        name="cure",
        out_shape=(
            jax.ShapeDtypeStruct((count, lanes), jnp.float32),
            jax.ShapeDtypeStruct((count, lanes), jnp.float32),
            jax.ShapeDtypeStruct((3, count, lanes), jnp.float32),
        ),
        in_specs=[vmem, vmem, vmem, smem, smem],
        out_specs=(vmem, vmem, vmem),
        compiler_params=params,
    )(chunks, temp_start, cure_start, tool_levels, plan)


def solution(mesh):
    return jax.shard_map(
        on_device,
        mesh=mesh,
        in_specs=(
            P(None, "plane", "depth"),
            P(("plane", "depth"), None),
            P(("plane", "depth"), None),
            P(),
            P(),
        ),
        out_specs=(
            P(("plane", "depth"), None),
            P(("plane", "depth"), None),
            P(None, ("plane", "depth"), None),
        ),
        check_vma=False,
    )
```

time: 109 us -> 43.2 us (0.40)
  other arithmetic: 35.6 us -> 0 us
  waiting for transfers between devices: 21.7 us -> 6.93 us
  starting transfers between devices: 34.2 us -> 22 us
  local copies, waits for them, and re-layouts: 16 us -> 5.89 us
  Pallas kernels: 0 us -> 7.06 us
    add x10 -> x0, other arithmetic: 16.8 us -> none  [the longest x6 11.5 us: valid_conv(): total + float(taps[offset]) * lax.slice_in_dim(values, offset, offset + c...]
    reduce_sum x3 -> x0, other arithmetic: 14.9 us -> none  [the longest x1 5.29 us: reduced_products(): jnp.sum(weights * first * second, axis=0)]
    ppermute x10 -> x5, waiting for transfers between devices: 16.1 us -> 1.43 us  [shifted(): return lax.ppermute(values, ('plane', 'depth'), pairs)]
    reshape x1 -> x0, local copies, waits for them, and re-layouts: 11.2 us -> none  [coarse_sums(): tensor.reshape(fields, count_x // COARSE, COARSE, count_z // COARSE, COARSE)]
    ppermute x10 -> x5, starting transfers between devices: 28.8 us -> 18.6 us  [shifted(): return lax.ppermute(values, ('plane', 'depth'), pairs)]
    pallas_call x0 -> x3, Pallas kernels: none -> 7.06 us  [the longest x1 5.52 us: on_device(): pl.pallas_call(tensor_kernel, name='tensor', out_shape=jax.ShapeDtypeStru...]
    unnamed x13 -> x27, local copies, waits for them, and re-layouts: 0.87 us -> 5.89 us
    slice x8 -> x0, local copies, waits for them, and re-layouts: 2.45 us -> none  [the longest x1 1.52 us: on_device(): plan[index, 1]]
  transfers between devices with their start and end apart: 11 -> 6, of which waited for: 5 -> 2; matrix products, arithmetic and copies ran while one was open for 8% -> 0% of each run, Pallas kernels for 0% -> 0%
where the time goes in v1:
time: 43.2 us; the launch traced here: 42.6 us
  starting transfers between devices  22 us (51%)
  Pallas kernels  7.06 us (16%)
  waiting for transfers between devices  6.93 us (16%)
  local copies, waits for them, and re-layouts  5.89 us (14%)
  between operations  0.76 us (2%)
    ppermute x5, starting transfers between devices, shifted(): return lax.ppermute(values, ('plane', 'depth'), pairs)  18.6 us
    unnamed x27, local copies, waits for them, and re-layouts  5.89 us
    pallas_call x1, Pallas kernels, on_device(): pl.pallas_call(tensor_kernel, name='tensor', out_shape=jax.ShapeDtypeStru...  5.52 us
    all_to_all x1, waiting for transfers between devices, on_device(): lax.all_to_all(chunks, 'depth', split_axis=0, concat_axis=0, tiled=True)  5.51 us
    all_to_all x1, starting transfers between devices, on_device(): lax.all_to_all(chunks, 'depth', split_axis=0, concat_axis=0, tiled=True)  3.39 us
    pallas_call x1, Pallas kernels, on_device(): pl.pallas_call(functools.partial(cure_kernel, cells), name='cure', out_sh...  1.44 us
    ppermute x5, waiting for transfers between devices, shifted(): return lax.ppermute(values, ('plane', 'depth'), pairs)  1.43 us
  transfers between devices with their start and end apart: 6, of which 2 were waited for; matrix products, arithmetic and copies ran while one was open for 0% of the time, Pallas kernels for 0%

profile of v1, /device:TPU:4, one launch (start us, length us, event | category | flops | bytes accessed | tf_op | source)
XLA Modules:
  0.0 42.6 jit_solution(7030817457926000020)
XLA Ops:
  0.6 1.0 %copy-done = s32[8,96,128]{2,1,0:T(8,128)S(1)} copy-done((s32[8,96,128]{2,1,0:T(8,128)S(1)}, s32[8,96,128]{2,1,0:T(8,128)}, u32[]{:S(2)}) %copy-start) | copy-done | bytes 393240
  1.6 0.7 %copy-done.6 = f32[6,128]{1,0:T(8,128)S(1)} copy-done((f32[6,128]{1,0:T(8,128)S(1)}, f32[6,128]{1,0:T(8,128)}, u32[]{:S(2)}) %copy-start.6) | copy-done | bytes 3096
  2.3 0.7 %copy-done.8 = f32[6,128]{1,0:T(8,128)S(1)} copy-done((f32[6,128]{1,0:T(8,128)S(1)}, f32[6,128]{1,0:T(8,128)}, u32[]{:S(2)}) %copy-start.8) | copy-done | bytes 3096
  3.0 0.1 pack.1
  3.1 2.1 %collective-permute-start.1 = (bf16[9,32,128]{2,1,0:T(8,128)(2,1)S(1)}, bf16[9,32,128]{2,1,0:T(8,128)(2,1)S(1)}, u32[]{:S(2)}, u32[]{:S(2)}) collective-permute-start(bf16[9,32,128]{2,1,0:T(8,128)(2,1)S(1)} %get-tuple-element.9), channel_id=1, source_target_pairs={{0,4},{1,5},{2,6},{3,7},{4,8},{5,9},{6,10},{7,11},{8,12},{9,13},{1... | collective-permute-start | bytes 221192 | tf_op jit(solution)/shard_map/ppermute | solution.py:388
  5.2 4.5 %collective-permute-start.2 = (bf16[9,32,128]{2,1,0:T(8,128)(2,1)S(1)}, bf16[9,32,128]{2,1,0:T(8,128)(2,1)S(1)}, u32[]{:S(2)}, u32[]{:S(2)}) collective-permute-start(bf16[9,32,128]{2,1,0:T(8,128)(2,1)S(1)} %get-tuple-element.10), channel_id=1, source_target_pairs={{4,0},{5,1},{6,2},{7,3},{8,4},{9,5},{10,6},{11,7},{12,8},{13,9},{1... | collective-permute-start | bytes 221192 | tf_op jit(solution)/shard_map/ppermute | solution.py:388
  9.7 3.5 %collective-permute-start = (bf16[2,96,128]{2,1,0:T(8,128)(2,1)S(1)}, bf16[2,96,128]{2,1,0:T(8,128)(2,1)S(1)}, u32[]{:S(2)}, u32[]{:S(2)}) collective-permute-start(bf16[2,96,128]{2,1,0:T(8,128)(2,1)S(1)} %get-tuple-element.8), channel_id=1, source_target_pairs={{0,1},{1,2},{2,3},{4,5},{5,6},{6,7},{8,9},{9,10},{10,11},{12,13},{... | collective-permute-start | bytes 147464 | tf_op jit(solution)/shard_map/ppermute | solution.py:388
  13.2 1.8 %collective-permute-start.3 = (bf16[2,32,128]{2,1,0:T(8,128)(2,1)S(1)}, bf16[2,32,128]{2,1,0:T(8,128)(2,1)S(1)}, u32[]{:S(2)}, u32[]{:S(2)}) collective-permute-start(bf16[2,32,128]{2,1,0:T(8,128)(2,1)S(1)} %get-tuple-element.11), channel_id=1, source_target_pairs={{0,5},{1,6},{2,7},{4,9},{5,10},{6,11},{8,13},{9,14},{10,15},{12,17... | collective-permute-start | bytes 49160 | tf_op jit(solution)/shard_map/ppermute | solution.py:388
  15.0 6.7 %collective-permute-start.4 = (bf16[2,32,128]{2,1,0:T(8,128)(2,1)S(1)}, bf16[2,32,128]{2,1,0:T(8,128)(2,1)S(1)}, u32[]{:S(2)}, u32[]{:S(2)}) collective-permute-start(bf16[2,32,128]{2,1,0:T(8,128)(2,1)S(1)} %get-tuple-element.12), channel_id=1, source_target_pairs={{4,1},{5,2},{6,3},{8,5},{9,6},{10,7},{12,9},{13,10},{14,11},{16,13... | collective-permute-start | bytes 49160 | tf_op jit(solution)/shard_map/ppermute | solution.py:388
  21.7 0.0 collective-permute-done.3.below_left
  21.7 1.4 %collective-permute-done.4.below_right = bf16[2,32,128]{2,1,0:T(8,128)(2,1)S(1)} collective-permute-done((bf16[2,32,128]{2,1,0:T(8,128)(2,1)S(1)}, bf16[2,32,128]{2,1,0:T(8,128)(2,1)S(1)}, u32[]{:S(2)}, u32[]{:S(2)}) %collective-permute-start.4) | collective-permute-done | bytes 16416 | tf_op jit(solution)/shard_map/ppermute | solution.py:388
  23.1 0.0 collective-permute-done.below
  23.1 0.0 collective-permute-done.1.from_left
  23.2 0.0 copy-start.2
  23.2 0.9 %copy-done.2 = bf16[2,256,256]{2,1,0:T(8,128)(2,1)S(1)} copy-done((bf16[2,256,256]{2,1,0:T(8,128)(2,1)S(1)}, bf16[2,256,256]{2,1,0:T(8,128)(2,1)}, u32[]{:S(2)}) %copy-start.2) | copy-done | bytes 262168
  24.1 0.9 %copy-done.4 = bf16[288,160]{1,0:T(8,128)(2,1)S(1)} copy-done((bf16[288,160]{1,0:T(8,128)(2,1)S(1)}, bf16[288,160]{1,0:T(8,128)(2,1)}, u32[]{:S(2)}) %copy-start.4) | copy-done | bytes 92184
  25.0 0.8 %copy-done.5 = bf16[256,128]{1,0:T(8,128)(2,1)S(1)} copy-done((bf16[256,128]{1,0:T(8,128)(2,1)S(1)}, bf16[256,128]{1,0:T(8,128)(2,1)}, u32[]{:S(2)}) %copy-start.5) | copy-done | bytes 65560
  25.9 0.7 %copy-done.10 = bf16[32,144]{1,0:T(8,128)(2,1)S(1)} copy-done((bf16[32,144]{1,0:T(8,128)(2,1)S(1)}, bf16[32,144]{1,0:T(8,128)(2,1)}, u32[]{:S(2)}) %copy-start.10) | copy-done | bytes 9240
  26.6 5.5 %tensor.1 = f32[4,16,128]{2,1,0:T(8,128)} custom-call(s32[8,96,128]{2,1,0:T(8,128)S(1)} %copy-done, f32[6,128]{1,0:T(8,128)S(1)} %copy-done.6, f32[6,128]{1,0:T(8,128)S(1)} %copy-done.8, bf16[2,96,128]{2,1,0:T(8,128)(2,1)S(1)} %collective-permute-done.below, bf16[9,32,128]{2,1,0:T(8,128)(2,1)S(1)} %collective-permute-done.1.from_left, ...), custom_call_target="tpu_custom_call" | custom-call | tf_op jit(solution)/shard_map/tensor/pallas_call | solution.py:401
  32.1 3.4 %all-to-all-start = ((f32[4,16,128]{2,1,0:T(8,128)}), f32[4,16,128]{2,1,0:T(8,128)S(1)}, u32[]{:S(2)}, u32[]{:S(2)}) async-start(f32[4,16,128]{2,1,0:T(8,128)} %tensor.1), calls=%async_computation | async-start | bytes 65536 | tf_op jit(solution)/shard_map/all_to_all | solution.py:418
  35.5 0.0 copy-start.11
  35.6 0.1 copy.14.plan
  35.6 5.5 %all-to-all-done.chunks = f32[4,16,128]{2,1,0:T(8,128)S(1)} async-done(((f32[4,16,128]{2,1,0:T(8,128)}), f32[4,16,128]{2,1,0:T(8,128)S(1)}, u32[]{:S(2)}, u32[]{:S(2)}) %all-to-all-start) | async-done | bytes 32800 | tf_op jit(solution)/shard_map/all_to_all | solution.py:418
  41.2 1.4 %cure.5 = (f32[6,128]{1,0:T(8,128)}, f32[6,128]{1,0:T(8,128)}, f32[3,6,128]{2,1,0:T(8,128)}) custom-call(f32[4,16,128]{2,1,0:T(8,128)S(1)} %all-to-all-done.chunks, f32[6,128]{1,0:T(8,128)S(1)} %copy-done.7, f32[6,128]{1,0:T(8,128)S(1)} %copy-done.9, f32[8]{0:T(128)S(1)} %copy-done.11, s32[3,2]{1,0:T(4,128)S(1)} %copy.14.plan), custom_call_target="tpu_custom_call" | custom-call | tf_op jit(solution)/shard_map/cure/pallas_call | solution.py:422
  (18 shorter events, 0.0 us)
Async XLA Ops:
  0.6 1.0 %copy-start = (s32[8,96,128]{2,1,0:T(8,128)S(1)}, s32[8,96,128]{2,1,0:T(8,128)}, u32[]{:S(2)}) copy-start(s32[8,96,128]{2,1,0:T(8,128)} %intensity.3) | copy-start | bytes 1179652
  1.6 0.7 %copy-start.6 = (f32[6,128]{1,0:T(8,128)S(1)}, f32[6,128]{1,0:T(8,128)}, u32[]{:S(2)}) copy-start(f32[6,128]{1,0:T(8,128)} %temp_in.1) | copy-start | bytes 9220
  2.3 0.7 %copy-start.8 = (f32[6,128]{1,0:T(8,128)S(1)}, f32[6,128]{1,0:T(8,128)}, u32[]{:S(2)}) copy-start(f32[6,128]{1,0:T(8,128)} %cure_in.1) | copy-start | bytes 9220
  3.0 20.2 %copy-start.1 = (bf16[2,256,256]{2,1,0:T(8,128)(2,1)S(1)}, bf16[2,256,256]{2,1,0:T(8,128)(2,1)}, u32[]{:S(2)}) copy-start(bf16[2,256,256]{2,1,0:T(8,128)(2,1)} %constant.14.clone.zh) | copy-start | bytes 786436
  3.0 20.2 %copy-start.3 = (bf16[288,160]{1,0:T(8,128)(2,1)S(1)}, bf16[288,160]{1,0:T(8,128)(2,1)}, u32[]{:S(2)}) copy-start(bf16[288,160]{1,0:T(8,128)(2,1)} %constant.12.clone.xh) | copy-start | bytes 276484
  3.1 20.0 %collective-permute-start.1 = (bf16[9,32,128]{2,1,0:T(8,128)(2,1)S(1)}, bf16[9,32,128]{2,1,0:T(8,128)(2,1)S(1)}, u32[]{:S(2)}, u32[]{:S(2)}) collective-permute-start(bf16[9,32,128]{2,1,0:T(8,128)(2,1)S(1)} %get-tuple-element.9), channel_id=1, source_target_pairs={{0,4},{1,5},{2,6},{3,7},{4,8},{5,9},{6,10},{7,11},{8,12},{9,13},{1... | collective-permute-start | bytes 221192 | tf_op jit(solution)/shard_map/ppermute | solution.py:388
  5.2 18.0 %collective-permute-start.2 = (bf16[9,32,128]{2,1,0:T(8,128)(2,1)S(1)}, bf16[9,32,128]{2,1,0:T(8,128)(2,1)S(1)}, u32[]{:S(2)}, u32[]{:S(2)}) collective-permute-start(bf16[9,32,128]{2,1,0:T(8,128)(2,1)S(1)} %get-tuple-element.10), channel_id=1, source_target_pairs={{4,0},{5,1},{6,2},{7,3},{8,4},{9,5},{10,6},{11,7},{12,8},{13,9},{1... | collective-permute-start | bytes 221192 | tf_op jit(solution)/shard_map/ppermute | solution.py:388
  9.7 13.4 %collective-permute-start = (bf16[2,96,128]{2,1,0:T(8,128)(2,1)S(1)}, bf16[2,96,128]{2,1,0:T(8,128)(2,1)S(1)}, u32[]{:S(2)}, u32[]{:S(2)}) collective-permute-start(bf16[2,96,128]{2,1,0:T(8,128)(2,1)S(1)} %get-tuple-element.8), channel_id=1, source_target_pairs={{0,1},{1,2},{2,3},{4,5},{5,6},{6,7},{8,9},{9,10},{10,11},{12,13},{... | collective-permute-start | bytes 147464 | tf_op jit(solution)/shard_map/ppermute | solution.py:388
  13.2 8.5 %collective-permute-start.3 = (bf16[2,32,128]{2,1,0:T(8,128)(2,1)S(1)}, bf16[2,32,128]{2,1,0:T(8,128)(2,1)S(1)}, u32[]{:S(2)}, u32[]{:S(2)}) collective-permute-start(bf16[2,32,128]{2,1,0:T(8,128)(2,1)S(1)} %get-tuple-element.11), channel_id=1, source_target_pairs={{0,5},{1,6},{2,7},{4,9},{5,10},{6,11},{8,13},{9,14},{10,15},{12,17... | collective-permute-start | bytes 49160 | tf_op jit(solution)/shard_map/ppermute | solution.py:388
  15.0 8.1 %collective-permute-start.4 = (bf16[2,32,128]{2,1,0:T(8,128)(2,1)S(1)}, bf16[2,32,128]{2,1,0:T(8,128)(2,1)S(1)}, u32[]{:S(2)}, u32[]{:S(2)}) collective-permute-start(bf16[2,32,128]{2,1,0:T(8,128)(2,1)S(1)} %get-tuple-element.12), channel_id=1, source_target_pairs={{4,1},{5,2},{6,3},{8,5},{9,6},{10,7},{12,9},{13,10},{14,11},{16,13... | collective-permute-start | bytes 49160 | tf_op jit(solution)/shard_map/ppermute | solution.py:388
  23.2 1.0 %copy-start.2 = (bf16[2,256,256]{2,1,0:T(8,128)(2,1)S(1)}, bf16[2,256,256]{2,1,0:T(8,128)(2,1)}, u32[]{:S(2)}) copy-start(bf16[2,256,256]{2,1,0:T(8,128)(2,1)} %constant.15.clone.zl) | copy-start | bytes 786436
  24.1 0.9 %copy-start.4 = (bf16[288,160]{1,0:T(8,128)(2,1)S(1)}, bf16[288,160]{1,0:T(8,128)(2,1)}, u32[]{:S(2)}) copy-start(bf16[288,160]{1,0:T(8,128)(2,1)} %constant.13.clone.xl) | copy-start | bytes 276484
  25.0 0.8 %copy-start.5 = (bf16[256,128]{1,0:T(8,128)(2,1)S(1)}, bf16[256,128]{1,0:T(8,128)(2,1)}, u32[]{:S(2)}) copy-start(bf16[256,128]{1,0:T(8,128)(2,1)} %constant.17.clone.sz) | copy-start | bytes 196612
  25.9 0.7 %copy-start.10 = (bf16[32,144]{1,0:T(8,128)(2,1)S(1)}, bf16[32,144]{1,0:T(8,128)(2,1)}, u32[]{:S(2)}) copy-start(bf16[32,144]{1,0:T(8,128)(2,1)} %constant.16.clone.sx) | copy-start | bytes 27652
  32.1 3.4 %copy-start.12 = (s32[3,2]{0,1:T(2,128)S(1)}, s32[3,2]{0,1:T(2,128)}, u32[]{:S(2)}) copy-start(s32[3,2]{0,1:T(2,128)} %param.15) | copy-start | bytes 76
  32.1 9.0 %copy-start.7 = (f32[6,128]{1,0:T(8,128)S(1)}, f32[6,128]{1,0:T(8,128)}, u32[]{:S(2)}) copy-start(f32[6,128]{1,0:T(8,128)} %temp_in.1) | copy-start | bytes 9220
  32.1 9.0 %copy-start.9 = (f32[6,128]{1,0:T(8,128)S(1)}, f32[6,128]{1,0:T(8,128)}, u32[]{:S(2)}) copy-start(f32[6,128]{1,0:T(8,128)} %cure_in.1) | copy-start | bytes 9220
  32.1 9.0 %all-to-all-start = ((f32[4,16,128]{2,1,0:T(8,128)}), f32[4,16,128]{2,1,0:T(8,128)S(1)}, u32[]{:S(2)}, u32[]{:S(2)}) async-start(f32[4,16,128]{2,1,0:T(8,128)} %tensor.1), calls=%async_computation | async-start | bytes 65536 | tf_op jit(solution)/shard_map/all_to_all | solution.py:418
  35.5 5.6 %copy-start.11 = (f32[8]{0:T(128)S(1)}, f32[8]{0:T(128)}, u32[]{:S(2)}) copy-start(f32[8]{0:T(128)} %levels.1) | copy-start | bytes 100

commit v2 on v1

v2 whole, which is shorter than its diff:
```python
import functools

import jax
import jax.numpy as jnp
import ml_dtypes
import numpy as np
from jax import lax
from jax.experimental import pallas as pl
from jax.experimental.pallas import tpu as pltpu
from jax.sharding import PartitionSpec as P

ROWS = 8
R1 = 6
R2 = 10
COARSE = 4
STEPS = 3

sigma_grad = 2.0
sigma_tensor = 3.3
conduct_matrix = 0.3
conduct_fiber = 1.5
time_step = 0.25
heat_release = 0.4
rate_first = 0.15
rate_second = 0.6
energy_first = 30.0
energy_second = 25.0
reference_temp = 4.2
tensor_eps = 1e-06

EDGE = 32
RIM = R1 + R2
LANES = 128
HALO = 2
GHOST = 3
BEFORE = EDGE // 2 // COARSE
FIRST = 16
ROW_KINDS = (1, 0, 0)
X_KINDS = (0, 1, 0)
DEPTH_KINDS = (0, 0, 1)


def smooth_taps(radius, sigma):
    offsets = np.arange(-radius, radius + 1) * 1.0
    weights = np.exp(-0.5 * offsets * offsets / (sigma * sigma))
    return weights / weights.sum()


def slope_taps(radius, sigma):
    offsets = np.arange(-radius, radius + 1) * 1.0
    weights = np.exp(-0.5 * offsets * offsets / (sigma * sigma))
    return offsets * weights / np.sum(offsets * offsets * weights)


def row_weights(count, radius, sigma):
    taps = smooth_taps(radius, sigma)
    result = np.zeros(count)
    for source in range(count):
        for target in range(count):
            offset = target - source
            if abs(offset) <= radius:
                result[source] += taps[offset + radius]
    return result


def rounded(taps):
    best = None
    for factor in np.linspace(1.0, 2.0, 20001)[:-1]:
        near = (taps * factor).astype(np.float32).astype(ml_dtypes.bfloat16).astype(np.float64)
        error = np.abs(near / factor - taps).sum()
        if best is None or error < best[0]:
            best = (error, near, factor)
    return best[1], best[2]


def as_bfloat16(matrix):
    return matrix.astype(np.float32).astype(ml_dtypes.bfloat16)


def sizes(width, depth):
    columns = width // COARSE + 2 * HALO
    cells = depth // COARSE + BEFORE
    span_x = columns * COARSE + 2 * R2
    pad_x = -(-span_x // 16) * 16
    return columns, cells, span_x, pad_x


GRAD_TAPS = tuple(
    rounded(taps(R1, sigma_grad)) for taps in (smooth_taps, slope_taps)
)
GRAD_FACTOR = GRAD_TAPS[0][1] ** 2 * GRAD_TAPS[1][1]


def grad_taps(kind):
    return GRAD_TAPS[kind][0]


def tap(taps, offset):
    radius = (len(taps) - 1) // 2
    return float(taps[offset + radius]) if abs(offset) <= radius else 0.0


def x_bands(width, depth):
    columns, cells, span_x, pad_x = sizes(width, depth)
    bands = np.zeros((2, pad_x, width + 2 * EDGE))
    first = EDGE - HALO * COARSE - R2 - R1
    for kind in range(2):
        for out in range(span_x):
            bands[kind, out, out + first : out + first + 2 * R1 + 1] = grad_taps(kind)
    return bands.reshape(2 * pad_x, -1)


def packed_lane(row, place):
    return (row % 2) * LANES + (row // 2) * EDGE + EDGE + place


def row_bands(rows, size):
    lane = packed_lane if size == EDGE else lambda row, place: row * size + place + EDGE
    bands = np.zeros((2, rows * size, rows * size))
    for kind in range(2):
        for source in range(rows):
            for target in range(rows):
                for place in range(-EDGE, size - EDGE):
                    at = (lane(source, place), lane(target, place))
                    bands[kind][at] = tap(grad_taps(kind), source - target)
    return bands


def low_bands(rows):
    bands = np.zeros((2, 3 * LANES, 2 * LANES))
    for kind in range(2):
        for row in range(rows):
            for place in range(-BEFORE * COARSE - R2, 0):
                for near in range(place - R1, place + R1 + 1):
                    own = 2 * LANES + row * FIRST + near
                    lane = packed_lane(row, near) if near < 0 else own
                    value = tap(grad_taps(kind), near - place)
                    bands[kind, lane, packed_lane(row, place)] = value
    return bands


def depth_bands(rows, depth):
    bands = np.zeros((2, rows // 2, 2 * LANES, LANES))
    for kind in range(2):
        for place in range(depth):
            for near in range(place - R1, min(place + R1 + 1, depth)):
                value = tap(grad_taps(kind), near - place)
                for block in range(rows // 2):
                    lane = near if near >= 0 else LANES + packed_lane(2 * block, near)
                    bands[kind, block, lane, place] = value
    return bands


def product_weights(rows):
    return row_weights(rows, R2, sigma_tensor) / (255.0 * GRAD_FACTOR) ** 2


def coarse_depth_bands(rows, depth):
    taps = smooth_taps(R2, sigma_tensor)
    weights = product_weights(rows)
    columns, cells, span_x, pad_x = sizes(0, depth)
    bands = np.zeros((3 * LANES, LANES))
    for cell in range(cells):
        for voxel in range(COARSE):
            place = (cell - BEFORE) * COARSE + voxel
            for near in range(place - R2, min(place + R2 + 1, depth)):
                value = tap(taps, near - place)
                if near >= 0:
                    bands[near, cell] += value
                else:
                    for row in range(rows):
                        bands[LANES + packed_lane(row, near), cell] += weights[row] * value
    return bands


def coarse_x_bands(count, padded_in, padded_out):
    taps = smooth_taps(R2, sigma_tensor)
    bands = np.zeros((padded_out, padded_in))
    for cell in range(count):
        for voxel in range(COARSE):
            start = cell * COARSE + voxel
            bands[cell, start : start + 2 * R2 + 1] += taps
    return bands


def three_parts(values):
    high = values.astype(jnp.bfloat16).astype(jnp.float32)
    rest = values - high
    middle = rest.astype(jnp.bfloat16).astype(jnp.float32)
    return high, middle, (rest - middle).astype(jnp.bfloat16).astype(jnp.float32)


def column_slot(temp_ref, cure_ref, first):
    pad = jnp.zeros((8 - 2 * GHOST, temp_ref.shape[1]), jnp.float32)
    rows = pl.ds(first, GHOST)
    both = jnp.concatenate([temp_ref[rows, :], cure_ref[rows, :], pad], axis=0)
    high, middle, low = three_parts(both)
    return jnp.concatenate([high, middle, low, jnp.zeros_like(high)], axis=0).astype(jnp.bfloat16)


def pack_kernel(intensity, temp_hbm, cure_hbm, to_left, to_right, own, grey, temp, cure, sems):
    rows, width, depth = intensity.shape
    copies = [
        pltpu.make_async_copy(intensity, grey, sems.at[0]),
        pltpu.make_async_copy(temp_hbm, temp, sems.at[1]),
        pltpu.make_async_copy(cure_hbm, cure, sems.at[2]),
    ]
    for copy in copies:
        copy.start()
    for copy in copies:
        copy.wait()
    for row in range(rows):
        values = grey[row].astype(jnp.float32).astype(jnp.bfloat16)
        own[row] = values
        to_left[row] = values[:EDGE]
        to_right[row] = values[width - EDGE :]
    count = temp.shape[0]
    left, right = column_slot(temp, cure, 0), column_slot(temp, cure, count - GHOST)
    for slot in range(temp.shape[1] // LANES):
        to_left[rows + slot] = left[:, slot * LANES : (slot + 1) * LANES]
        to_right[rows + slot] = right[:, slot * LANES : (slot + 1) * LANES]


def packed_rows(values, size, first):
    depth = values[0].shape[1]
    lane = lax.broadcasted_iota(jnp.int32, values[0].shape, 1)
    packed = None
    for block, value in enumerate(values):
        shift = (size * block - first) % depth
        moved = value if shift == 0 else pltpu.roll(value, shift, 1)
        packed = moved if block == 0 else jnp.where(lane >= size * block, moved, packed)
    return packed


def window_kernel(own, from_left, from_right, window, up):
    rows, width, depth = own.shape
    values = []
    for row in range(rows):
        half = (row % 2) * depth
        whole = jnp.concatenate([from_left[row], own[row], from_right[row]], axis=0)
        window[row // 2, :, half : half + depth] = whole
        values.append(whole.astype(jnp.float32))
    for pair in range(2):
        up[pair] = packed_rows(values[pair::2], EDGE, depth - EDGE).astype(jnp.bfloat16)


def joined_columns(ref, rows):
    slots = [ref[slot].astype(jnp.float32) for slot in range(rows, ref.shape[0])]
    parts = jnp.concatenate(slots, axis=1)
    return (parts[0:8] + parts[8:16]) + parts[16:24]


def product(first, second):
    return jnp.dot(first, second, preferred_element_type=jnp.float32)


def along_rows(kind, values, row):
    total = None
    for source, value in enumerate(values):
        weight = tap(grad_taps(kind), source - row)
        if weight != 0.0:
            total = weight * value if total is None else total + weight * value
    return total


def own_kernel(window, x_parts, filtered, first_flat, first_steep, across):
    pairs, height, double = window.shape
    rows, depth = 2 * pairs, double // 2
    pad_x = x_parts.shape[0] // 2
    for pair in range(pairs):
        result = product(x_parts[...], window[pair])
        across[2 * pair] = result[:, :depth]
        across[2 * pair + 1] = result[:, depth:]

    values = [
        window[row // 2, :, (row % 2) * depth : (row % 2 + 1) * depth].astype(jnp.float32)
        for row in range(rows)
    ]
    result = product(x_parts[...], packed_rows(values, FIRST, 0).astype(jnp.bfloat16))
    first_flat[...] = result[:pad_x].astype(jnp.bfloat16)
    first_steep[...] = result[pad_x:].astype(jnp.bfloat16)

    def filter_rows(group, carry):
        start = pl.multiple_of(group * 16, 16)
        kinds = [
            [across[row, pl.ds(kind * pad_x + start, 16), :] for row in range(rows)]
            for kind in range(2)
        ]
        for part in range(3):
            for row in range(rows):
                result = along_rows(ROW_KINDS[part], kinds[X_KINDS[part]], row)
                filtered[part, row, pl.ds(start, 16), :] = result.astype(jnp.bfloat16)
        return carry

    lax.fori_loop(0, pad_x // 16, filter_rows, 0)


def tensor_kernel(
    width, temp, cure, below, from_left, from_right, filtered, first_flat, first_steep,
    x_parts, wide, narrow, sx, out, grads, low, products,
):
    parts, rows, pad_x, depth = filtered.shape
    columns, cells, span_x, pad_x = sizes(width, depth)
    planes, depths = lax.axis_size("plane"), lax.axis_size("depth")
    plane, layer = lax.axis_index("plane"), lax.axis_index("depth")

    edge = jnp.concatenate([below[0], below[1]], axis=1)
    result = product(x_parts[...], edge).astype(jnp.bfloat16)
    kinds = (result[:pad_x], result[pad_x:])
    firsts = (first_flat[...], first_steep[...])
    at_first = rows * 2 * LANES + 3 * LANES
    for part in range(3):
        kind, row_kind, depth_kind = X_KINDS[part], ROW_KINDS[part], DEPTH_KINDS[part]
        at = 5 * LANES * row_kind
        edge_rows = product(kinds[kind], wide[at : at + 2 * LANES, :]).astype(jnp.bfloat16)
        at = at_first + row_kind * LANES
        first_rows = product(firsts[kind], narrow[at : at + LANES, :]).astype(jnp.bfloat16)
        at = 5 * LANES * depth_kind + 2 * LANES
        both = jnp.concatenate([edge_rows, first_rows], axis=1)
        low[part] = product(both, wide[at : at + 3 * LANES, :])
        for row in range(rows):
            half = (row % 2) * LANES
            both = jnp.concatenate(
                [filtered[part, row], edge_rows[:, half : half + LANES]], axis=1
            )
            at = (depth_kind * (rows // 2) + row // 2) * 2 * LANES
            grads[part, row] = product(both, narrow[at : at + 2 * LANES, :])

    weights = product_weights(rows)
    pairs = ((0, 0), (1, 1), (2, 2), (0, 1), (0, 2), (1, 2))
    has_below = jnp.where(layer > 0, 1.0, 0.0)

    def multiply(group, carry):
        start = pl.multiple_of(group * 16, 16)
        x_at = plane * width - HALO * COARSE - R2 + start
        x_at = x_at + lax.broadcasted_iota(jnp.int32, (16, LANES), 0)
        inside = jnp.where((x_at >= 0) & (x_at < planes * width), 1.0, 0.0)
        place = pl.ds(start, 16)
        totals = [None] * 6
        for row in range(rows):
            three = [grads[part, row, place, :] for part in range(3)]
            weighted = [float(weights[row]) * value for value in three]
            for index, (first, second) in enumerate(pairs):
                term = weighted[first] * three[second]
                totals[index] = term if row == 0 else totals[index] + term
        for index in range(6):
            products[index, place, 0:LANES] = (totals[index] * inside).astype(jnp.bfloat16)
        inside = inside * has_below
        for tile in range(2):
            lanes = slice(tile * LANES, (tile + 1) * LANES)
            three = [low[part, place, lanes] for part in range(3)]
            masked = [value * inside for value in three]
            for index, (first, second) in enumerate(pairs):
                term = masked[first] * three[second]
                products[index, place, LANES + tile * LANES : 2 * LANES + tile * LANES] = (
                    term.astype(jnp.bfloat16)
                )
        return carry

    lax.fori_loop(0, pad_x // 16, multiply, 0)

    coarse = narrow[rows * 2 * LANES : rows * 2 * LANES + 3 * LANES, :]
    sums = []
    for index in range(6):
        part = product(products[index], coarse).astype(jnp.bfloat16)
        sums.append(product(sx[...], part))
    trace = sums[0] + sums[1] + sums[2]
    scale = (conduct_fiber - conduct_matrix) / (2.0 * trace + tensor_eps)
    xx = conduct_matrix + scale * (trace - sums[1])
    xz = -scale * sums[5]
    zz = conduct_matrix + scale * (trace - sums[2])
    lane = lax.broadcasted_iota(jnp.int32, xx.shape, 1)
    joined = jnp.where(
        lane < cells,
        xx,
        jnp.where(lane < 2 * cells, pltpu.roll(xz, cells, 1), pltpu.roll(zz, 2 * cells, 1)),
    )

    count = temp.shape[0]
    lanes = temp.shape[1]
    pad = jnp.zeros((8 - 2 * GHOST, lanes), jnp.float32)
    own_first = jnp.concatenate([temp[0:GHOST, :], cure[0:GHOST, :], pad], axis=0)
    own_last = jnp.concatenate([temp[count - GHOST :, :], cure[count - GHOST :, :], pad], axis=0)
    left, right = joined_columns(from_left, rows), joined_columns(from_right, rows)
    height = count + 2 * HALO
    for target in range(out.shape[0]):
        piece = jnp.where(layer == target - 1, own_last, 0.0)
        piece = jnp.where(layer == target + 1, own_first, piece)
        if target == 0:
            piece = jnp.where(layer == depths - 1, left, piece)
        if target == out.shape[0] - 1:
            piece = jnp.where(layer == 0, right, piece)
        out[target, 0:height, 0:LANES] = joined[count * target : count * target + height]
        if lanes > LANES:
            out[target, 0:height, LANES:] = jnp.zeros((height, lanes - LANES), jnp.float32)
        out[target, height : height + 2 * GHOST, :] = piece[0 : 2 * GHOST]
        spare = out.shape[1] - height - 2 * GHOST
        if spare:
            out[target, height + 2 * GHOST :, :] = jnp.zeros((spare, lanes), jnp.float32)


def cure_kernel(cells, chunks, temp_in, cure_in, levels, plan, temp_out, cure_out, conduct_out):
    count, lanes = temp_in.shape
    parts = chunks.shape[0]
    planes, depths = lax.axis_size("plane"), lax.axis_size("depth")
    plane, layer = lax.axis_index("plane"), lax.axis_index("depth")
    height = count + 2 * HALO
    own = cells - BEFORE
    lane = lax.broadcasted_iota(jnp.int32, (16, lanes), 1)
    row = lax.broadcasted_iota(jnp.int32, (16, lanes), 0)

    conduct = [jnp.zeros((16, lanes), jnp.float32) for _ in range(3)]
    for part in range(parts):
        chunk = chunks[part, 0:16, :]
        here = lane >= own * part - BEFORE
        for kind in range(3):
            shift = (own * part - BEFORE - kind * cells) % lanes
            moved = chunk if shift == 0 else pltpu.roll(chunk, shift, 1)
            conduct[kind] = jnp.where(here, moved, conduct[kind])
    for kind in range(3):
        conduct_out[kind] = conduct[kind][HALO : HALO + count]

    before = chunks[lax.rem(layer + parts - 1, parts)][height : height + 2 * GHOST]
    after = chunks[lax.rem(layer + 1, parts)][height : height + 2 * GHOST]
    spare = jnp.full((16 - count - 2 * GHOST, lanes), 0.5, jnp.float32)
    temp = jnp.concatenate([before[:GHOST], temp_in[...], after[:GHOST], 8.0 * spare], axis=0)
    cure = jnp.concatenate([before[GHOST:], cure_in[...], after[GHOST:], spare], axis=0)
    gap = GHOST - HALO
    xx, xz, zz = [pltpu.roll(part, gap, 0) for part in conduct]

    first = (plane == 0) & (layer == 0)
    last = (plane == planes - 1) & (layer == depths - 1)
    for step in range(STEPS):
        top, bottom = levels[plan[step, 0]], levels[plan[step, 1]]
        temp = jnp.where((row < GHOST) & first, temp[GHOST : GHOST + 1], temp)
        temp = jnp.where(
            (row >= GHOST + count) & last, temp[GHOST + count - 1 : GHOST + count], temp
        )
        cooler = jnp.where(lane == 0, top, pltpu.roll(temp, 1, 1))
        later = jnp.where(lane == lanes - 1, bottom, pltpu.roll(temp, lanes - 1, 1))
        slant = later - cooler
        second_x = pltpu.roll(temp, 15, 0) - 2.0 * temp + pltpu.roll(temp, 1, 0)
        second_z = later - 2.0 * temp + cooler
        cross = 0.25 * (pltpu.roll(slant, 15, 0) - pltpu.roll(slant, 1, 0))
        spread = xx * second_x + 2.0 * xz * cross + zz * second_z
        inverse = 1.0 / reference_temp - 1.0 / temp
        left = 1.0 - cure
        rate = rate_first * jnp.exp(energy_first * inverse) + rate_second * jnp.exp(
            energy_second * inverse
        ) * jnp.sqrt(cure)
        rate = rate * (left * jnp.sqrt(left))
        temp = temp + time_step * (spread + heat_release * rate)
        cure = cure + time_step * rate
    temp_out[...] = temp[GHOST : GHOST + count]
    cure_out[...] = cure[GHOST : GHOST + count]


def on_device(intensity, temp_start, cure_start, tool_levels, plan):
    rows, width, depth = intensity.shape
    count, lanes = temp_start.shape
    planes, depths = lax.axis_size("plane"), lax.axis_size("depth")
    columns, cells, span_x, pad_x = sizes(width, depth)
    bf16 = jnp.bfloat16
    slots = rows + lanes // LANES
    params = pltpu.CompilerParams(vmem_limit_bytes=24 * 1024 * 1024)
    vmem = pl.BlockSpec(memory_space=pltpu.VMEM)
    smem = pl.BlockSpec(memory_space=pltpu.SMEM)
    stay = pl.BlockSpec(memory_space=pltpu.HBM)

    to_left, to_right, own = pl.pallas_call(
        pack_kernel,
        name="pack",
        out_shape=(
            jax.ShapeDtypeStruct((slots, EDGE, depth), bf16),
            jax.ShapeDtypeStruct((slots, EDGE, depth), bf16),
            jax.ShapeDtypeStruct((rows, width, depth), bf16),
        ),
        in_specs=[stay, stay, stay],
        scratch_shapes=[
            pltpu.VMEM((rows, width, depth), jnp.int32),
            pltpu.VMEM((count, lanes), jnp.float32),
            pltpu.VMEM((count, lanes), jnp.float32),
            pltpu.SemaphoreType.DMA((3,)),
        ],
        compiler_params=params,
    )(*[pltpu.with_memory_space_constraint(x, pltpu.HBM) for x in (intensity, temp_start, cure_start)])

    def shifted(values, by_plane, by_depth):
        pairs = []
        for p in range(planes):
            for d in range(depths):
                q, e = p + by_plane, d + by_depth
                if 0 <= q < planes and 0 <= e < depths:
                    pairs.append((p * depths + d, q * depths + e))
        return lax.ppermute(values, ("plane", "depth"), pairs)

    from_left = shifted(to_right, 1, 0)
    from_right = shifted(to_left, -1, 0)

    span = width + 2 * EDGE
    window, up = pl.pallas_call(
        window_kernel,
        name="window",
        out_shape=(
            jax.ShapeDtypeStruct((rows // 2, span, 2 * depth), bf16),
            jax.ShapeDtypeStruct((2, span, depth), bf16),
        ),
        compiler_params=params,
    )(own, from_left, from_right)
    below = shifted(up, 0, 1)

    x_parts = jnp.asarray(as_bfloat16(x_bands(width, depth)))
    filtered, first_flat, first_steep = pl.pallas_call(
        own_kernel,
        name="own",
        out_shape=(
            jax.ShapeDtypeStruct((3, rows, pad_x, depth), bf16),
            jax.ShapeDtypeStruct((pad_x, depth), bf16),
            jax.ShapeDtypeStruct((pad_x, depth), bf16),
        ),
        scratch_shapes=[pltpu.VMEM((rows, 2 * pad_x, depth), jnp.float32)],
        cost_estimate=pl.CostEstimate(
            flops=2 * rows * 2 * pad_x * span * depth, bytes_accessed=4_000_000, transcendentals=0
        ),
        compiler_params=params,
    )(window, x_parts)

    wide, narrow = [], [*depth_bands(rows, depth).reshape(rows, 2 * LANES, LANES)]
    for edge_rows, low in zip(row_bands(rows, EDGE), low_bands(rows)):
        wide += [edge_rows, low]
    narrow += [coarse_depth_bands(rows, depth), *row_bands(rows, FIRST)]
    wide, narrow = [jnp.asarray(as_bfloat16(np.concatenate(bands))) for bands in (wide, narrow)]
    sx = jnp.asarray(as_bfloat16(coarse_x_bands(columns, pad_x, -(-columns // 16) * 16)))
    height = -(-(count + 2 * HALO + 2 * GHOST) // 8) * 8
    chunks = pl.pallas_call(
        functools.partial(tensor_kernel, width),
        name="tensor",
        out_shape=jax.ShapeDtypeStruct((depths, height, lanes), jnp.float32),
        scratch_shapes=[
            pltpu.VMEM((3, rows, pad_x, depth), jnp.float32),
            pltpu.VMEM((3, pad_x, 2 * LANES), jnp.float32),
            pltpu.VMEM((6, pad_x, 3 * LANES), bf16),
        ],
        compiler_params=params,
    )(
        temp_start, cure_start, below, from_left, from_right, filtered, first_flat, first_steep,
        x_parts, wide, narrow, sx,
    )

    chunks = lax.all_to_all(chunks, "depth", split_axis=0, concat_axis=0, tiled=True)

    return pl.pallas_call(
        functools.partial(cure_kernel, cells),
        name="cure",
        out_shape=(
            jax.ShapeDtypeStruct((count, lanes), jnp.float32),
            jax.ShapeDtypeStruct((count, lanes), jnp.float32),
            jax.ShapeDtypeStruct((3, count, lanes), jnp.float32),
        ),
        in_specs=[vmem, vmem, vmem, smem, smem],
        out_specs=(vmem, vmem, vmem),
        compiler_params=params,
    )(chunks, temp_start, cure_start, tool_levels, plan)


def solution(mesh):
    return jax.shard_map(
        on_device,
        mesh=mesh,
        in_specs=(
            P(None, "plane", "depth"),
            P(("plane", "depth"), None),
            P(("plane", "depth"), None),
            P(),
            P(),
        ),
        out_specs=(
            P(("plane", "depth"), None),
            P(("plane", "depth"), None),
            P(None, ("plane", "depth"), None),
        ),
        check_vma=False,
    )
```

time: 43.2 us -> 34 us (0.79)
  starting transfers between devices: 22 us -> 15.7 us
  local copies, waits for them, and re-layouts: 5.89 us -> 2.3 us
  waiting for transfers between devices: 6.93 us -> 8 us
    ppermute x5 -> x3, starting transfers between devices: 18.6 us -> 9.95 us  [shifted(): return lax.ppermute(values, ('plane', 'depth'), pairs)]
    unnamed x27 -> x19, local copies, waits for them, and re-layouts: 5.89 us -> 2.3 us
    all_to_all x1, starting transfers between devices: 3.39 us -> 5.74 us  [on_device(): lax.all_to_all(chunks, 'depth', split_axis=0, concat_axis=0, tiled=True)]
    pallas_call x1 -> x3, Pallas kernels: 5.52 us -> 4.41 us  [the longest x1 3.08 us: on_device(): pl.pallas_call(functools.partial(tensor_kernel, width), name='tensor', ou...]
    pallas_call x1, Pallas kernels: 0.11 us -> 1.13 us  [on_device(): pl.pallas_call(pack_kernel, name='pack', out_shape=(jax.ShapeDtypeStruct(...]
    ppermute x5 -> x3, waiting for transfers between devices: 1.43 us -> 2.44 us  [shifted(): return lax.ppermute(values, ('plane', 'depth'), pairs)]
  transfers between devices with their start and end apart: 6 -> 4, of which waited for: 2 -> 4; matrix products, arithmetic and copies ran while one was open for 0% -> 0% of each run, Pallas kernels for 0% -> 4%
where the time goes in v2:
time: 34 us; the launch traced here: 33.7 us
  starting transfers between devices  15.7 us (46%)
  waiting for transfers between devices  8 us (24%)
  Pallas kernels  6.97 us (20%)
  local copies, waits for them, and re-layouts  2.3 us (7%)
  between operations  0.71 us (2%)
    ppermute x3, starting transfers between devices, shifted(): return lax.ppermute(values, ('plane', 'depth'), pairs)  9.95 us
    all_to_all x1, starting transfers between devices, on_device(): lax.all_to_all(chunks, 'depth', split_axis=0, concat_axis=0, tiled=True)  5.74 us
    all_to_all x1, waiting for transfers between devices, on_device(): lax.all_to_all(chunks, 'depth', split_axis=0, concat_axis=0, tiled=True)  5.56 us
    pallas_call x1, Pallas kernels, on_device(): pl.pallas_call(functools.partial(tensor_kernel, width), name='tensor', ou...  3.08 us
    ppermute x3, waiting for transfers between devices, shifted(): return lax.ppermute(values, ('plane', 'depth'), pairs)  2.44 us
    unnamed x19, local copies, waits for them, and re-layouts  2.3 us
    pallas_call x1, Pallas kernels, on_device(): pl.pallas_call(functools.partial(cure_kernel, cells), name='cure', out_sh...  1.44 us
    pallas_call x1, Pallas kernels, on_device(): pl.pallas_call(own_kernel, name='own', out_shape=(jax.ShapeDtypeStruct((3...  1.19 us
  transfers between devices with their start and end apart: 4, of which 4 were waited for; matrix products, arithmetic and copies ran while one was open for 0% of the time, Pallas kernels for 4%

profile of v2, /device:TPU:4, one launch (start us, length us, event | category | flops | bytes accessed | tf_op | source)
XLA Modules:
  0.0 33.7 jit_solution(17679496696335255228)
XLA Ops:
  0.6 0.0 copy-start
  0.6 1.1 %pack.1 = (bf16[9,32,128]{2,1,0:T(8,128)(2,1)S(1)}, bf16[9,32,128]{2,1,0:T(8,128)(2,1)S(1)}, bf16[8,96,128]{2,1,0:T(8,128)(2,1)S(1)}) custom-call(s32[8,96,128]{2,1,0:T(8,128)} %intensity.1, f32[6,128]{1,0:T(8,128)} %temp_in.1, f32[6,128]{1,0:T(8,128)} %cure_in.1), custom_call_target="tpu_custom_call" | custom-call | tf_op jit(solution)/shard_map/pack/pallas_call | solution.py:470
  1.8 1.9 %collective-permute-start = (bf16[9,32,128]{2,1,0:T(8,128)(2,1)S(1)}, bf16[9,32,128]{2,1,0:T(8,128)(2,1)S(1)}, u32[]{:S(2)}, u32[]{:S(2)}) collective-permute-start(bf16[9,32,128]{2,1,0:T(8,128)(2,1)S(1)} %get-tuple-element.12), channel_id=1, source_target_pairs={{0,4},{1,5},{2,6},{3,7},{4,8},{5,9},{6,10},{7,11},{8,12},{9,13},{1... | collective-permute-start | bytes 221192 | tf_op jit(solution)/shard_map/ppermute | solution.py:495
  3.7 4.5 %collective-permute-start.1 = (bf16[9,32,128]{2,1,0:T(8,128)(2,1)S(1)}, bf16[9,32,128]{2,1,0:T(8,128)(2,1)S(1)}, u32[]{:S(2)}, u32[]{:S(2)}) collective-permute-start(bf16[9,32,128]{2,1,0:T(8,128)(2,1)S(1)} %get-tuple-element.13), channel_id=1, source_target_pairs={{4,0},{5,1},{6,2},{7,3},{8,4},{9,5},{10,6},{11,7},{12,8},{13,9},{1... | collective-permute-start | bytes 221192 | tf_op jit(solution)/shard_map/ppermute | solution.py:495
  8.3 0.1 collective-permute-done.from_left
  8.3 1.9 %collective-permute-done.1.from_right = bf16[9,32,128]{2,1,0:T(8,128)(2,1)S(1)} collective-permute-done((bf16[9,32,128]{2,1,0:T(8,128)(2,1)S(1)}, bf16[9,32,128]{2,1,0:T(8,128)(2,1)S(1)}, u32[]{:S(2)}, u32[]{:S(2)}) %collective-permute-start.1) | collective-permute-done | bytes 73760 | tf_op jit(solution)/shard_map/ppermute | solution.py:495
  10.2 0.1 window.1
  10.4 3.5 %collective-permute-start.2 = (bf16[2,160,128]{2,1,0:T(8,128)(2,1)S(1)}, bf16[2,160,128]{2,1,0:T(8,128)(2,1)S(1)}, u32[]{:S(2)}, u32[]{:S(2)}) collective-permute-start(bf16[2,160,128]{2,1,0:T(8,128)(2,1)S(1)} %get-tuple-element.14), channel_id=1, source_target_pairs={{0,1},{1,2},{2,3},{4,5},{5,6},{6,7},{8,9},{9,10},{10,11},{12,13},{... | collective-permute-start | bytes 245768 | tf_op jit(solution)/shard_map/ppermute | solution.py:495
  13.8 0.0 copy-start.2
  13.9 0.9 %copy-done.2 = bf16[288,160]{1,0:T(8,128)(2,1)S(1)} copy-done((bf16[288,160]{1,0:T(8,128)(2,1)S(1)}, bf16[288,160]{1,0:T(8,128)(2,1)}, u32[]{:S(2)}) %copy-start.2) | copy-done | bytes 92184
  14.8 1.2 %own.1 = (bf16[3,8,144,128]{3,2,1,0:T(8,128)(2,1)S(1)}, bf16[144,128]{1,0:T(8,128)(2,1)S(1)}, bf16[144,128]{1,0:T(8,128)(2,1)S(1)}) custom-call(bf16[4,160,256]{2,1,0:T(8,128)(2,1)S(1)} %get-tuple-element.15.window, bf16[288,160]{1,0:T(8,128)(2,1)S(1)} %copy-done.2), custom_call_target="tpu_custom_call" | custom-call | flops 94371840 | bytes 4000000 | tf_op jit(solution)/shard_map/own/pallas_call | solution.py:513
  16.0 0.0 copy-start.4
  16.0 0.5 %collective-permute-done.2.below = bf16[2,160,128]{2,1,0:T(8,128)(2,1)S(1)} collective-permute-done((bf16[2,160,128]{2,1,0:T(8,128)(2,1)S(1)}, bf16[2,160,128]{2,1,0:T(8,128)(2,1)S(1)}, u32[]{:S(2)}, u32[]{:S(2)}) %collective-permute-start.2) | collective-permute-done | bytes 81952 | tf_op jit(solution)/shard_map/ppermute | solution.py:495
  16.5 0.0 copy-done
  16.5 0.0 copy-done.3
  16.5 0.0 copy-done.5
  16.5 0.0 copy-done.6
  16.5 0.2 copy-done.4
  16.7 1.1 %copy-done.1 = bf16[1280,256]{1,0:T(8,128)(2,1)S(1)} copy-done((bf16[1280,256]{1,0:T(8,128)(2,1)S(1)}, bf16[1280,256]{1,0:T(8,128)(2,1)}, u32[]{:S(2)}) %copy-start.1) | copy-done | bytes 655384
  17.7 3.1 %tensor.1 = f32[4,16,128]{2,1,0:T(8,128)} custom-call(f32[6,128]{1,0:T(8,128)S(1)} %copy-done.4, f32[6,128]{1,0:T(8,128)S(1)} %copy-done.5, bf16[2,160,128]{2,1,0:T(8,128)(2,1)S(1)} %collective-permute-done.2.below, bf16[9,32,128]{2,1,0:T(8,128)(2,1)S(1)} %collective-permute-done.from_left, bf16[9,32,128]{2,1,0:T(8,128)(2,1)S(1)} %collective-permute-done.1.from_right, ...), custom_call_target="tpu_custom_call" | custom-call | tf_op jit(solution)/shard_map/tensor/pallas_call | solution.py:535
  20.8 5.7 %all-to-all-start = ((f32[4,16,128]{2,1,0:T(8,128)}), f32[4,16,128]{2,1,0:T(8,128)S(1)}, u32[]{:S(2)}, u32[]{:S(2)}) async-start(f32[4,16,128]{2,1,0:T(8,128)} %tensor.1), calls=%async_computation | async-start | bytes 65536 | tf_op jit(solution)/shard_map/all_to_all | solution.py:550
  26.6 0.1 copy.12.plan
  26.7 5.6 %all-to-all-done.chunks = f32[4,16,128]{2,1,0:T(8,128)S(1)} async-done(((f32[4,16,128]{2,1,0:T(8,128)}), f32[4,16,128]{2,1,0:T(8,128)S(1)}, u32[]{:S(2)}, u32[]{:S(2)}) %all-to-all-start) | async-done | bytes 32800 | tf_op jit(solution)/shard_map/all_to_all | solution.py:550
  32.2 1.4 %cure.3 = (f32[6,128]{1,0:T(8,128)}, f32[6,128]{1,0:T(8,128)}, f32[3,6,128]{2,1,0:T(8,128)}) custom-call(f32[4,16,128]{2,1,0:T(8,128)S(1)} %all-to-all-done.chunks, f32[6,128]{1,0:T(8,128)S(1)} %copy-done.4, f32[6,128]{1,0:T(8,128)S(1)} %copy-done.5, f32[8]{0:T(128)S(1)} %copy-done.7, s32[3,2]{1,0:T(4,128)S(1)} %copy.12.plan), custom_call_target="tpu_custom_call" | custom-call | tf_op jit(solution)/shard_map/cure/pallas_call | solution.py:552
  (8 shorter events, 0.0 us)
Async XLA Ops:
  0.6 15.8 %copy-start = (bf16[2688,128]{1,0:T(8,128)(2,1)S(1)}, bf16[2688,128]{1,0:T(8,128)(2,1)}, u32[]{:S(2)}) copy-start(bf16[2688,128]{1,0:T(8,128)(2,1)} %constant.10.clone.narrow) | copy-start | bytes 2064388
  1.8 6.6 %collective-permute-start = (bf16[9,32,128]{2,1,0:T(8,128)(2,1)S(1)}, bf16[9,32,128]{2,1,0:T(8,128)(2,1)S(1)}, u32[]{:S(2)}, u32[]{:S(2)}) collective-permute-start(bf16[9,32,128]{2,1,0:T(8,128)(2,1)S(1)} %get-tuple-element.12), channel_id=1, source_target_pairs={{0,4},{1,5},{2,6},{3,7},{4,8},{5,9},{6,10},{7,11},{8,12},{9,13},{1... | collective-permute-start | bytes 221192 | tf_op jit(solution)/shard_map/ppermute | solution.py:495
  3.7 6.5 %collective-permute-start.1 = (bf16[9,32,128]{2,1,0:T(8,128)(2,1)S(1)}, bf16[9,32,128]{2,1,0:T(8,128)(2,1)S(1)}, u32[]{:S(2)}, u32[]{:S(2)}) collective-permute-start(bf16[9,32,128]{2,1,0:T(8,128)(2,1)S(1)} %get-tuple-element.13), channel_id=1, source_target_pairs={{4,0},{5,1},{6,2},{7,3},{8,4},{9,5},{10,6},{11,7},{12,8},{13,9},{1... | collective-permute-start | bytes 221192 | tf_op jit(solution)/shard_map/ppermute | solution.py:495
  10.4 6.1 %collective-permute-start.2 = (bf16[2,160,128]{2,1,0:T(8,128)(2,1)S(1)}, bf16[2,160,128]{2,1,0:T(8,128)(2,1)S(1)}, u32[]{:S(2)}, u32[]{:S(2)}) collective-permute-start(bf16[2,160,128]{2,1,0:T(8,128)(2,1)S(1)} %get-tuple-element.14), channel_id=1, source_target_pairs={{0,1},{1,2},{2,3},{4,5},{5,6},{6,7},{8,9},{9,10},{10,11},{12,13},{... | collective-permute-start | bytes 245768 | tf_op jit(solution)/shard_map/ppermute | solution.py:495
  13.8 0.9 %copy-start.2 = (bf16[288,160]{1,0:T(8,128)(2,1)S(1)}, bf16[288,160]{1,0:T(8,128)(2,1)}, u32[]{:S(2)}) copy-start(bf16[288,160]{1,0:T(8,128)(2,1)} %constant.8.clone.x_parts) | copy-start | bytes 276484
  14.8 1.7 %copy-start.3 = (bf16[288,160]{1,0:T(8,128)(2,1)S(1)}, bf16[288,160]{1,0:T(8,128)(2,1)}, u32[]{:S(2)}) copy-start(bf16[288,160]{1,0:T(8,128)(2,1)} %constant.8.clone.x_parts) | copy-start | bytes 276484
  14.8 1.7 %copy-start.5 = (f32[6,128]{1,0:T(8,128)S(1)}, f32[6,128]{1,0:T(8,128)}, u32[]{:S(2)}) copy-start(f32[6,128]{1,0:T(8,128)} %cure_in.1) | copy-start | bytes 9220
  14.8 1.7 %copy-start.6 = (bf16[32,144]{1,0:T(8,128)(2,1)S(1)}, bf16[32,144]{1,0:T(8,128)(2,1)}, u32[]{:S(2)}) copy-start(bf16[32,144]{1,0:T(8,128)(2,1)} %constant.11.clone.sx) | copy-start | bytes 27652
  16.0 0.7 %copy-start.4 = (f32[6,128]{1,0:T(8,128)S(1)}, f32[6,128]{1,0:T(8,128)}, u32[]{:S(2)}) copy-start(f32[6,128]{1,0:T(8,128)} %temp_in.1) | copy-start | bytes 9220
  16.7 1.1 %copy-start.1 = (bf16[1280,256]{1,0:T(8,128)(2,1)S(1)}, bf16[1280,256]{1,0:T(8,128)(2,1)}, u32[]{:S(2)}) copy-start(bf16[1280,256]{1,0:T(8,128)(2,1)} %constant.9.clone.wide) | copy-start | bytes 1966084
  20.8 5.7 %copy-start.8 = (s32[3,2]{0,1:T(2,128)S(1)}, s32[3,2]{0,1:T(2,128)}, u32[]{:S(2)}) copy-start(s32[3,2]{0,1:T(2,128)} %param.13) | copy-start | bytes 76
  20.8 11.4 %all-to-all-start = ((f32[4,16,128]{2,1,0:T(8,128)}), f32[4,16,128]{2,1,0:T(8,128)S(1)}, u32[]{:S(2)}, u32[]{:S(2)}) async-start(f32[4,16,128]{2,1,0:T(8,128)} %tensor.1), calls=%async_computation | async-start | bytes 65536 | tf_op jit(solution)/shard_map/all_to_all | solution.py:550
  26.6 5.7 %copy-start.7 = (f32[8]{0:T(128)S(1)}, f32[8]{0:T(128)}, u32[]{:S(2)}) copy-start(f32[8]{0:T(128)} %levels.1) | copy-start | bytes 100

commit v3 on v2

--- a/solution.py
+++ b/solution.py
@@ -198,27 +198,46 @@
     return jnp.concatenate([high, middle, low, jnp.zeros_like(high)], axis=0).astype(jnp.bfloat16)
 
 
-def pack_kernel(intensity, temp_hbm, cure_hbm, to_left, to_right, own, grey, temp, cure, sems):
+def is_odd():
+    return lax.rem(lax.axis_index("plane"), 2) == 1
+
+
+def pack_kernel(
+    intensity, temp_hbm, cure_hbm, x_hbm, far, near, own, x_parts, grey, temp, cure, sems
+):
     rows, width, depth = intensity.shape
     copies = [
         pltpu.make_async_copy(intensity, grey, sems.at[0]),
         pltpu.make_async_copy(temp_hbm, temp, sems.at[1]),
         pltpu.make_async_copy(cure_hbm, cure, sems.at[2]),
+        pltpu.make_async_copy(x_hbm, x_parts, sems.at[3]),
     ]
     for copy in copies:
         copy.start()
     for copy in copies:
         copy.wait()
+    odd = is_odd()
+    count = temp.shape[0]
+    sides = (column_slot(temp, cure, 0), column_slot(temp, cure, count - GHOST))
+
+    def send(left, right):
+        for row in range(rows):
+            left[row] = grey[row, :EDGE, :].astype(jnp.float32).astype(jnp.bfloat16)
+            right[row] = grey[row, width - EDGE :, :].astype(jnp.float32).astype(jnp.bfloat16)
+        for slot in range(temp.shape[1] // LANES):
+            left[rows + slot] = sides[0][:, slot * LANES : (slot + 1) * LANES]
+            right[rows + slot] = sides[1][:, slot * LANES : (slot + 1) * LANES]
+
+    @pl.when(odd)
+    def _():
+        send(near, far)
+
+    @pl.when(jnp.logical_not(odd))
+    def _():
+        send(far, near)
+
     for row in range(rows):
-        values = grey[row].astype(jnp.float32).astype(jnp.bfloat16)
-        own[row] = values
-        to_left[row] = values[:EDGE]
-        to_right[row] = values[width - EDGE :]
-    count = temp.shape[0]
-    left, right = column_slot(temp, cure, 0), column_slot(temp, cure, count - GHOST)
-    for slot in range(temp.shape[1] // LANES):
-        to_left[rows + slot] = left[:, slot * LANES : (slot + 1) * LANES]
-        to_right[rows + slot] = right[:, slot * LANES : (slot + 1) * LANES]
+        own[row] = grey[row].astype(jnp.float32).astype(jnp.bfloat16)
 
 
 def packed_rows(values, size, first):
@@ -232,16 +251,27 @@
     return packed
 
 
-def window_kernel(own, from_left, from_right, window, up):
+def window_kernel(own, far, near, window, up):
     rows, width, depth = own.shape
-    values = []
-    for row in range(rows):
-        half = (row % 2) * depth
-        whole = jnp.concatenate([from_left[row], own[row], from_right[row]], axis=0)
-        window[row // 2, :, half : half + depth] = whole
-        values.append(whole.astype(jnp.float32))
-    for pair in range(2):
-        up[pair] = packed_rows(values[pair::2], EDGE, depth - EDGE).astype(jnp.bfloat16)
+    odd = is_odd()
+
+    def fill(from_left, from_right):
+        values = []
+        for row in range(rows):
+            half = (row % 2) * depth
+            whole = jnp.concatenate([from_left[row], own[row], from_right[row]], axis=0)
+            window[row // 2, :, half : half + depth] = whole
+            values.append(whole.astype(jnp.float32))
+        for pair in range(2):
+            up[pair] = packed_rows(values[pair::2], EDGE, depth - EDGE).astype(jnp.bfloat16)
+
+    @pl.when(odd)
+    def _():
+        fill(near, far)
+
+    @pl.when(jnp.logical_not(odd))
+    def _():
+        fill(far, near)
 
 
 def joined_columns(ref, rows):
@@ -263,7 +293,16 @@
     return total
 
 
-def own_kernel(window, x_parts, filtered, first_flat, first_steep, across):
+def own_kernel(
+    window, x_parts, wide_hbm, narrow_hbm, filtered, first_flat, first_steep, wide, narrow,
+    across, sems,
+):
+    copies = [
+        pltpu.make_async_copy(wide_hbm, wide, sems.at[0]),
+        pltpu.make_async_copy(narrow_hbm, narrow, sems.at[1]),
+    ]
+    for copy in copies:
+        copy.start()
     pairs, height, double = window.shape
     rows, depth = 2 * pairs, double // 2
     pad_x = x_parts.shape[0] // 2
@@ -293,10 +332,12 @@
         return carry
 
     lax.fori_loop(0, pad_x // 16, filter_rows, 0)
+    for copy in copies:
+        copy.wait()
 
 
 def tensor_kernel(
-    width, temp, cure, below, from_left, from_right, filtered, first_flat, first_steep,
+    width, temp, cure, below, far, near, filtered, first_flat, first_steep,
     x_parts, wide, narrow, sx, out, grads, low, products,
 ):
     parts, rows, pad_x, depth = filtered.shape
@@ -381,7 +422,9 @@
     pad = jnp.zeros((8 - 2 * GHOST, lanes), jnp.float32)
     own_first = jnp.concatenate([temp[0:GHOST, :], cure[0:GHOST, :], pad], axis=0)
     own_last = jnp.concatenate([temp[count - GHOST :, :], cure[count - GHOST :, :], pad], axis=0)
-    left, right = joined_columns(from_left, rows), joined_columns(from_right, rows)
+    odd = is_odd()
+    outer, inner = joined_columns(far, rows), joined_columns(near, rows)
+    left, right = jnp.where(odd, inner, outer), jnp.where(odd, outer, inner)
     height = count + 2 * HALO
     for target in range(out.shape[0]):
         piece = jnp.where(layer == target - 1, own_last, 0.0)
@@ -467,35 +510,38 @@
     smem = pl.BlockSpec(memory_space=pltpu.SMEM)
     stay = pl.BlockSpec(memory_space=pltpu.HBM)
 
-    to_left, to_right, own = pl.pallas_call(
+    fixed = lambda values: pltpu.with_memory_space_constraint(values, pltpu.HBM)
+    x_hbm = jnp.asarray(as_bfloat16(x_bands(width, depth)))
+    far, near, own, x_parts = pl.pallas_call(
         pack_kernel,
         name="pack",
         out_shape=(
-            jax.ShapeDtypeStruct((slots, EDGE, depth), bf16),
-            jax.ShapeDtypeStruct((slots, EDGE, depth), bf16),
-            jax.ShapeDtypeStruct((rows, width, depth), bf16),
+            pltpu.VMEM((slots, EDGE, depth), bf16),
+            pltpu.VMEM((slots, EDGE, depth), bf16),
+            pltpu.VMEM((rows, width, depth), bf16),
+            pltpu.VMEM(x_hbm.shape, bf16),
         ),
-        in_specs=[stay, stay, stay],
+        in_specs=[stay] * 4,
         scratch_shapes=[
             pltpu.VMEM((rows, width, depth), jnp.int32),
             pltpu.VMEM((count, lanes), jnp.float32),
             pltpu.VMEM((count, lanes), jnp.float32),
-            pltpu.SemaphoreType.DMA((3,)),
+            pltpu.SemaphoreType.DMA((4,)),
         ],
         compiler_params=params,
-    )(*[pltpu.with_memory_space_constraint(x, pltpu.HBM) for x in (intensity, temp_start, cure_start)])
-
-    def shifted(values, by_plane, by_depth):
-        pairs = []
-        for p in range(planes):
-            for d in range(depths):
-                q, e = p + by_plane, d + by_depth
-                if 0 <= q < planes and 0 <= e < depths:
-                    pairs.append((p * depths + d, q * depths + e))
-        return lax.ppermute(values, ("plane", "depth"), pairs)
-
-    from_left = shifted(to_right, 1, 0)
-    from_right = shifted(to_left, -1, 0)
+    )(*[fixed(values) for values in (intensity, temp_start, cure_start, x_hbm)])
+
+    def moved(values, pairs):
+        index = [(p * depths + d, q * depths + e) for (p, d), (q, e) in pairs]
+        return lax.ppermute(values, ("plane", "depth"), index)
+
+    def swapped(values, first):
+        pairs = [(p, p + 1) for p in range(first, planes - 1, 2)]
+        pairs += [(q, p) for p, q in pairs]
+        return moved(values, [((p, d), (q, d)) for p, q in pairs for d in range(depths)])
+
+    far = swapped(far, 1)
+    near = swapped(near, 0)
 
     span = width + 2 * EDGE
     window, up = pl.pallas_call(
@@ -506,36 +552,42 @@
             jax.ShapeDtypeStruct((2, span, depth), bf16),
         ),
         compiler_params=params,
-    )(own, from_left, from_right)
-    below = shifted(up, 0, 1)
-
-    x_parts = jnp.asarray(as_bfloat16(x_bands(width, depth)))
-    filtered, first_flat, first_steep = pl.pallas_call(
+    )(own, far, near)
+    below = moved(up, [((p, d), (p, d + 1)) for p in range(planes) for d in range(depths - 1)])
+
+    wide, narrow = [], [*depth_bands(rows, depth).reshape(rows, 2 * LANES, LANES)]
+    for edge_rows, low in zip(row_bands(rows, EDGE), low_bands(rows)):
+        wide += [edge_rows, low]
+    narrow += [coarse_depth_bands(rows, depth), *row_bands(rows, FIRST)]
+    wide, narrow = [jnp.asarray(as_bfloat16(np.concatenate(bands))) for bands in (wide, narrow)]
+    wide_hbm, narrow_hbm = wide, narrow
+    sx = jnp.asarray(as_bfloat16(coarse_x_bands(columns, pad_x, -(-columns // 16) * 16)))
+    filtered, first_flat, first_steep, wide, narrow = pl.pallas_call(
         own_kernel,
         name="own",
         out_shape=(
             jax.ShapeDtypeStruct((3, rows, pad_x, depth), bf16),
             jax.ShapeDtypeStruct((pad_x, depth), bf16),
             jax.ShapeDtypeStruct((pad_x, depth), bf16),
+            pltpu.VMEM(wide_hbm.shape, bf16),
+            pltpu.VMEM(narrow_hbm.shape, bf16),
         ),
-        scratch_shapes=[pltpu.VMEM((rows, 2 * pad_x, depth), jnp.float32)],
+        in_specs=[vmem, vmem, stay, stay],
+        scratch_shapes=[
+            pltpu.VMEM((rows, 2 * pad_x, depth), jnp.float32),
+            pltpu.SemaphoreType.DMA((2,)),
+        ],
         cost_estimate=pl.CostEstimate(
             flops=2 * rows * 2 * pad_x * span * depth, bytes_accessed=4_000_000, transcendentals=0
         ),
         compiler_params=params,
-    )(window, x_parts)
-
-    wide, narrow = [], [*depth_bands(rows, depth).reshape(rows, 2 * LANES, LANES)]
-    for edge_rows, low in zip(row_bands(rows, EDGE), low_bands(rows)):
-        wide += [edge_rows, low]
-    narrow += [coarse_depth_bands(rows, depth), *row_bands(rows, FIRST)]
-    wide, narrow = [jnp.asarray(as_bfloat16(np.concatenate(bands))) for bands in (wide, narrow)]
-    sx = jnp.asarray(as_bfloat16(coarse_x_bands(columns, pad_x, -(-columns // 16) * 16)))
+    )(window, x_parts, fixed(wide_hbm), fixed(narrow_hbm))
+
     height = -(-(count + 2 * HALO + 2 * GHOST) // 8) * 8
     chunks = pl.pallas_call(
         functools.partial(tensor_kernel, width),
         name="tensor",
-        out_shape=jax.ShapeDtypeStruct((depths, height, lanes), jnp.float32),
+        out_shape=pltpu.VMEM((depths, height, lanes), jnp.float32),
         scratch_shapes=[
             pltpu.VMEM((3, rows, pad_x, depth), jnp.float32),
             pltpu.VMEM((3, pad_x, 2 * LANES), jnp.float32),
@@ -543,7 +595,7 @@
         ],
         compiler_params=params,
     )(
-        temp_start, cure_start, below, from_left, from_right, filtered, first_flat, first_steep,
+        temp_start, cure_start, below, far, near, filtered, first_flat, first_steep,
         x_parts, wide, narrow, sx,
     )
 

time: 34 us -> 31.2 us (0.918)
  the two profiles are of different devices: /device:TPU:4 before, /device:TPU:0 now
where the time goes in v3:
time: 31.2 us; the launch traced here: 30.9 us
  starting transfers between devices  14.4 us (46%)
  waiting for transfers between devices  7.77 us (25%)
  Pallas kernels  7.22 us (23%)
  local copies, waits for them, and re-layouts  0.8 us (3%)
  between operations  0.68 us (2%)
    ppermute x3, starting transfers between devices, moved(): return lax.ppermute(values, ('plane', 'depth'), index)  8.51 us
    all_to_all x1, starting transfers between devices, on_device(): lax.all_to_all(chunks, 'depth', split_axis=0, concat_axis=0, tiled=True)  5.91 us
    all_to_all x1, waiting for transfers between devices, on_device(): lax.all_to_all(chunks, 'depth', split_axis=0, concat_axis=0, tiled=True)  5.56 us
    pallas_call x1, Pallas kernels, on_device(): pl.pallas_call(functools.partial(tensor_kernel, width), name='tensor', ou...  3.09 us
    ppermute x3, waiting for transfers between devices, moved(): return lax.ppermute(values, ('plane', 'depth'), index)  2.21 us
    pallas_call x1, Pallas kernels, on_device(): pl.pallas_call(functools.partial(cure_kernel, cells), name='cure', out_sh...  1.44 us
    pallas_call x1, Pallas kernels, on_device(): pl.pallas_call(own_kernel, name='own', out_shape=(jax.ShapeDtypeStruct((3...  1.41 us
    pallas_call x1, Pallas kernels, on_device(): pl.pallas_call(pack_kernel, name='pack', out_shape=(pltpu.VMEM((slots, ED...  1.14 us
  transfers between devices with their start and end apart: 4, of which 3 were waited for; matrix products, arithmetic and copies ran while one was open for 0% of the time, Pallas kernels for 5%

profile of v3, /device:TPU:0, one launch (start us, length us, event | category | flops | bytes accessed | tf_op | source)
XLA Modules:
  0.0 30.9 jit_solution(8276455276686911382)
XLA Ops:
  0.6 1.1 %pack.1 = (bf16[9,32,128]{2,1,0:T(8,128)(2,1)S(1)}, bf16[9,32,128]{2,1,0:T(8,128)(2,1)S(1)}, bf16[8,96,128]{2,1,0:T(8,128)(2,1)S(1)}, bf16[288,160]{1,0:T(8,128)(2,1)S(1)}) custom-call(s32[8,96,128]{2,1,0:T(8,128)} %intensity.1, f32[6,128]{1,0:T(8,128)} %temp_in.1, f32[6,128]{1,0:T(8,128)} %cure_in.1, bf16[288,160]{1,0:T(8,128)(2,1)} %constant.8.clone.x_hbm), custom_call_target="tpu_custom_call" | custom-call | tf_op jit(solution)/shard_map/pack/pallas_call | solution.py:515
  1.8 0.7 %collective-permute-start = (bf16[9,32,128]{2,1,0:T(8,128)(2,1)S(1)}, bf16[9,32,128]{2,1,0:T(8,128)(2,1)S(1)}, u32[]{:S(2)}, u32[]{:S(2)}) collective-permute-start(bf16[9,32,128]{2,1,0:T(8,128)(2,1)S(1)} %get-tuple-element.15), channel_id=1, source_target_pairs={{4,8},{5,9},{6,10},{7,11},{12,16},{13,17},{14,18},{15,19},{20,24},... | collective-permute-start | bytes 221192 | tf_op jit(solution)/shard_map/ppermute | solution.py:536
  2.5 4.4 %collective-permute-start.1 = (bf16[9,32,128]{2,1,0:T(8,128)(2,1)S(1)}, bf16[9,32,128]{2,1,0:T(8,128)(2,1)S(1)}, u32[]{:S(2)}, u32[]{:S(2)}) collective-permute-start(bf16[9,32,128]{2,1,0:T(8,128)(2,1)S(1)} %get-tuple-element.16), channel_id=1, source_target_pairs={{0,4},{1,5},{2,6},{3,7},{8,12},{9,13},{10,14},{11,15},{16,20},{17,... | collective-permute-start | bytes 221192 | tf_op jit(solution)/shard_map/ppermute | solution.py:536
  6.8 0.0 collective-permute-done.far
  6.8 0.9 %collective-permute-done.1.near = bf16[9,32,128]{2,1,0:T(8,128)(2,1)S(1)} collective-permute-done((bf16[9,32,128]{2,1,0:T(8,128)(2,1)S(1)}, bf16[9,32,128]{2,1,0:T(8,128)(2,1)S(1)}, u32[]{:S(2)}, u32[]{:S(2)}) %collective-permute-start.1) | collective-permute-done | bytes 73760 | tf_op jit(solution)/shard_map/ppermute | solution.py:536
  7.7 0.1 window.1
  7.9 3.5 %collective-permute-start.2 = (bf16[2,160,128]{2,1,0:T(8,128)(2,1)S(1)}, bf16[2,160,128]{2,1,0:T(8,128)(2,1)S(1)}, u32[]{:S(2)}, u32[]{:S(2)}) collective-permute-start(bf16[2,160,128]{2,1,0:T(8,128)(2,1)S(1)} %get-tuple-element.17), channel_id=1, source_target_pairs={{0,1},{1,2},{2,3},{4,5},{5,6},{6,7},{8,9},{9,10},{10,11},{12,13},{... | collective-permute-start | bytes 245768 | tf_op jit(solution)/shard_map/ppermute | solution.py:536
  11.4 0.0 copy-start.2
  11.4 1.4 %own.1 = (bf16[3,8,144,128]{3,2,1,0:T(8,128)(2,1)S(1)}, bf16[144,128]{1,0:T(8,128)(2,1)S(1)}, bf16[144,128]{1,0:T(8,128)(2,1)S(1)}, bf16[1280,256]{1,0:T(8,128)(2,1)S(1)}, bf16[2688,128]{1,0:T(8,128)(2,1)S(1)}) custom-call(bf16[4,160,256]{2,1,0:T(8,128)(2,1)S(1)} %get-tuple-element.18.window, bf16[288,160]{1,0:T(8,128)(2,1)S(1)} %get-tuple-element.19.x_parts, ...), custom_call_target="tpu_custom_call" | custom-call | flops 94371840 | bytes 4000000 | tf_op jit(solution)/shard_map/own/pallas_call | solution.py:565
  12.8 1.3 %collective-permute-done.2.below = bf16[2,160,128]{2,1,0:T(8,128)(2,1)S(1)} collective-permute-done((bf16[2,160,128]{2,1,0:T(8,128)(2,1)S(1)}, bf16[2,160,128]{2,1,0:T(8,128)(2,1)S(1)}, u32[]{:S(2)}, u32[]{:S(2)}) %collective-permute-start.2) | collective-permute-done | bytes 81952 | tf_op jit(solution)/shard_map/ppermute | solution.py:536
  14.1 0.0 copy-start.1
  14.1 0.0 copy-start
  14.1 0.0 copy-done.2
  14.1 0.7 %copy-done.1 = f32[6,128]{1,0:T(8,128)S(1)} copy-done((f32[6,128]{1,0:T(8,128)S(1)}, f32[6,128]{1,0:T(8,128)}, u32[]{:S(2)}) %copy-start.1) | copy-done | bytes 3096
  14.8 0.0 copy-done
  14.8 3.1 %tensor.1 = f32[4,16,128]{2,1,0:T(8,128)} custom-call(f32[6,128]{1,0:T(8,128)S(1)} %copy-done, f32[6,128]{1,0:T(8,128)S(1)} %copy-done.1, bf16[2,160,128]{2,1,0:T(8,128)(2,1)S(1)} %collective-permute-done.2.below, bf16[9,32,128]{2,1,0:T(8,128)(2,1)S(1)} %collective-permute-done.far, bf16[9,32,128]{2,1,0:T(8,128)(2,1)S(1)} %collective-permute-done.1.near, ...), custom_call_target="tpu_custom_call" | custom-call | tf_op jit(solution)/shard_map/tensor/pallas_call | solution.py:587
  17.9 0.0 copy-start.4
  17.9 5.9 %all-to-all-start = ((f32[4,16,128]{2,1,0:T(8,128)}), f32[4,16,128]{2,1,0:T(8,128)S(1)}, u32[]{:S(2)}, u32[]{:S(2)}) async-start(f32[4,16,128]{2,1,0:T(8,128)} %tensor.1), calls=%async_computation | async-start | bytes 65536 | tf_op jit(solution)/shard_map/all_to_all | solution.py:602
  23.8 0.0 copy-done.4
  23.8 0.0 copy-start.3
  23.8 0.1 copy.12.plan
  23.9 5.6 %all-to-all-done.chunks = f32[4,16,128]{2,1,0:T(8,128)S(1)} async-done(((f32[4,16,128]{2,1,0:T(8,128)}), f32[4,16,128]{2,1,0:T(8,128)S(1)}, u32[]{:S(2)}, u32[]{:S(2)}) %all-to-all-start) | async-done | bytes 32800 | tf_op jit(solution)/shard_map/all_to_all | solution.py:602
  29.5 0.0 copy-done.3
  29.5 1.4 %cure.3 = (f32[6,128]{1,0:T(8,128)}, f32[6,128]{1,0:T(8,128)}, f32[3,6,128]{2,1,0:T(8,128)}) custom-call(f32[4,16,128]{2,1,0:T(8,128)S(1)} %all-to-all-done.chunks, f32[6,128]{1,0:T(8,128)S(1)} %copy-done, f32[6,128]{1,0:T(8,128)S(1)} %copy-done.1, f32[8]{0:T(128)S(1)} %copy-done.3, s32[3,2]{1,0:T(4,128)S(1)} %copy.12.plan), custom_call_target="tpu_custom_call" | custom-call | tf_op jit(solution)/shard_map/cure/pallas_call | solution.py:604
Async XLA Ops:
  1.8 5.0 %collective-permute-start = (bf16[9,32,128]{2,1,0:T(8,128)(2,1)S(1)}, bf16[9,32,128]{2,1,0:T(8,128)(2,1)S(1)}, u32[]{:S(2)}, u32[]{:S(2)}) collective-permute-start(bf16[9,32,128]{2,1,0:T(8,128)(2,1)S(1)} %get-tuple-element.15), channel_id=1, source_target_pairs={{4,8},{5,9},{6,10},{7,11},{12,16},{13,17},{14,18},{15,19},{20,24},... | collective-permute-start | bytes 221192 | tf_op jit(solution)/shard_map/ppermute | solution.py:536
  2.5 5.3 %collective-permute-start.1 = (bf16[9,32,128]{2,1,0:T(8,128)(2,1)S(1)}, bf16[9,32,128]{2,1,0:T(8,128)(2,1)S(1)}, u32[]{:S(2)}, u32[]{:S(2)}) collective-permute-start(bf16[9,32,128]{2,1,0:T(8,128)(2,1)S(1)} %get-tuple-element.16), channel_id=1, source_target_pairs={{0,4},{1,5},{2,6},{3,7},{8,12},{9,13},{10,14},{11,15},{16,20},{17,... | collective-permute-start | bytes 221192 | tf_op jit(solution)/shard_map/ppermute | solution.py:536
  7.9 6.2 %collective-permute-start.2 = (bf16[2,160,128]{2,1,0:T(8,128)(2,1)S(1)}, bf16[2,160,128]{2,1,0:T(8,128)(2,1)S(1)}, u32[]{:S(2)}, u32[]{:S(2)}) collective-permute-start(bf16[2,160,128]{2,1,0:T(8,128)(2,1)S(1)} %get-tuple-element.17), channel_id=1, source_target_pairs={{0,1},{1,2},{2,3},{4,5},{5,6},{6,7},{8,9},{9,10},{10,11},{12,13},{... | collective-permute-start | bytes 245768 | tf_op jit(solution)/shard_map/ppermute | solution.py:536
  11.4 2.7 %copy-start.2 = (bf16[32,144]{1,0:T(8,128)(2,1)S(1)}, bf16[32,144]{1,0:T(8,128)(2,1)}, u32[]{:S(2)}) copy-start(bf16[32,144]{1,0:T(8,128)(2,1)} %constant.11.clone.sx) | copy-start | bytes 27652
  14.1 0.7 %copy-start.1 = (f32[6,128]{1,0:T(8,128)S(1)}, f32[6,128]{1,0:T(8,128)}, u32[]{:S(2)}) copy-start(f32[6,128]{1,0:T(8,128)} %cure_in.1) | copy-start | bytes 9220
  14.1 0.7 %copy-start = (f32[6,128]{1,0:T(8,128)S(1)}, f32[6,128]{1,0:T(8,128)}, u32[]{:S(2)}) copy-start(f32[6,128]{1,0:T(8,128)} %temp_in.1) | copy-start | bytes 9220
  17.9 5.9 %copy-start.4 = (s32[3,2]{0,1:T(2,128)S(1)}, s32[3,2]{0,1:T(2,128)}, u32[]{:S(2)}) copy-start(s32[3,2]{0,1:T(2,128)} %param.13) | copy-start | bytes 76
  17.9 11.6 %all-to-all-start = ((f32[4,16,128]{2,1,0:T(8,128)}), f32[4,16,128]{2,1,0:T(8,128)S(1)}, u32[]{:S(2)}, u32[]{:S(2)}) async-start(f32[4,16,128]{2,1,0:T(8,128)} %tensor.1), calls=%async_computation | async-start | bytes 65536 | tf_op jit(solution)/shard_map/all_to_all | solution.py:602
  23.8 5.7 %copy-start.3 = (f32[8]{0:T(128)S(1)}, f32[8]{0:T(128)}, u32[]{:S(2)}) copy-start(f32[8]{0:T(128)} %levels.1) | copy-start | bytes 100

commit v4 on v3

--- a/solution.py
+++ b/solution.py
@@ -29,12 +29,14 @@
 tensor_eps = 1e-06
 
 EDGE = 32
-RIM = R1 + R2
 LANES = 128
 HALO = 2
 GHOST = 3
-BEFORE = EDGE // 2 // COARSE
 FIRST = 16
+START = 8
+BEFORE = -(-(R1 + R2) // COARSE)
+AFTER = 1
+HALF = LANES // 2
 ROW_KINDS = (1, 0, 0)
 X_KINDS = (0, 1, 0)
 DEPTH_KINDS = (0, 0, 1)
@@ -77,9 +79,14 @@
     return matrix.astype(np.float32).astype(ml_dtypes.bfloat16)
 
 
+def halves(matrix):
+    high = as_bfloat16(matrix)
+    return high, as_bfloat16(matrix - high.astype(np.float64))
+
+
 def sizes(width, depth):
     columns = width // COARSE + 2 * HALO
-    cells = depth // COARSE + BEFORE
+    cells = depth // COARSE + BEFORE + AFTER
     span_x = columns * COARSE + 2 * R2
     pad_x = -(-span_x // 16) * 16
     return columns, cells, span_x, pad_x
@@ -110,44 +117,27 @@
     return bands.reshape(2 * pad_x, -1)
 
 
-def packed_lane(row, place):
-    return (row % 2) * LANES + (row // 2) * EDGE + EDGE + place
-
-
-def row_bands(rows, size):
-    lane = packed_lane if size == EDGE else lambda row, place: row * size + place + EDGE
-    bands = np.zeros((2, rows * size, rows * size))
-    for kind in range(2):
+def edge_bands(rows):
+    bands = np.zeros((2, 3, rows * FIRST, rows * FIRST))
+    for part in range(3):
+        row_taps, depth_taps = grad_taps(ROW_KINDS[part]), grad_taps(DEPTH_KINDS[part])
         for source in range(rows):
             for target in range(rows):
-                for place in range(-EDGE, size - EDGE):
-                    at = (lane(source, place), lane(target, place))
-                    bands[kind][at] = tap(grad_taps(kind), source - target)
+                row_tap = tap(row_taps, source - target)
+                for near in range(-FIRST, FIRST):
+                    side, lane = int(near >= 0), source * FIRST + near % FIRST
+                    for place in range(-R1, START):
+                        value = row_tap * tap(depth_taps, near - place)
+                        bands[side, part, lane, target * FIRST + START + place] = value
     return bands
 
 
-def low_bands(rows):
-    bands = np.zeros((2, 3 * LANES, 2 * LANES))
-    for kind in range(2):
-        for row in range(rows):
-            for place in range(-BEFORE * COARSE - R2, 0):
-                for near in range(place - R1, place + R1 + 1):
-                    own = 2 * LANES + row * FIRST + near
-                    lane = packed_lane(row, near) if near < 0 else own
-                    value = tap(grad_taps(kind), near - place)
-                    bands[kind, lane, packed_lane(row, place)] = value
-    return bands
-
-
-def depth_bands(rows, depth):
-    bands = np.zeros((2, rows // 2, 2 * LANES, LANES))
+def depth_bands(depth):
+    bands = np.zeros((2, depth, depth))
     for kind in range(2):
         for place in range(depth):
-            for near in range(place - R1, min(place + R1 + 1, depth)):
-                value = tap(grad_taps(kind), near - place)
-                for block in range(rows // 2):
-                    lane = near if near >= 0 else LANES + packed_lane(2 * block, near)
-                    bands[kind, block, lane, place] = value
+            for near in range(max(place - R1, 0), min(place + R1 + 1, depth)):
+                bands[kind, near, place] = tap(grad_taps(kind), near - place)
     return bands
 
 
@@ -159,17 +149,17 @@
     taps = smooth_taps(R2, sigma_tensor)
     weights = product_weights(rows)
     columns, cells, span_x, pad_x = sizes(0, depth)
-    bands = np.zeros((3 * LANES, LANES))
+    bands = np.zeros((2, depth, LANES))
     for cell in range(cells):
         for voxel in range(COARSE):
             place = (cell - BEFORE) * COARSE + voxel
-            for near in range(place - R2, min(place + R2 + 1, depth)):
+            for near in range(max(place - R2, -R1), min(place + R2 + 1, depth)):
                 value = tap(taps, near - place)
-                if near >= 0:
-                    bands[near, cell] += value
+                if near >= START:
+                    bands[0, near, cell] += value
                 else:
                     for row in range(rows):
-                        bands[LANES + packed_lane(row, near), cell] += weights[row] * value
+                        bands[1, row * FIRST + START + near, cell] += weights[row] * value
     return bands
 
 
@@ -203,7 +193,7 @@
 
 
 def pack_kernel(
-    intensity, temp_hbm, cure_hbm, x_hbm, far, near, own, x_parts, grey, temp, cure, sems
+    intensity, temp_hbm, cure_hbm, x_hbm, far, near, own, x_parts, temp, cure, grey, sems
 ):
     rows, width, depth = intensity.shape
     copies = [
@@ -262,8 +252,7 @@
             whole = jnp.concatenate([from_left[row], own[row], from_right[row]], axis=0)
             window[row // 2, :, half : half + depth] = whole
             values.append(whole.astype(jnp.float32))
-        for pair in range(2):
-            up[pair] = packed_rows(values[pair::2], EDGE, depth - EDGE).astype(jnp.bfloat16)
+        up[...] = packed_rows(values, FIRST, depth - FIRST).astype(jnp.bfloat16)
 
     @pl.when(odd)
     def _():
@@ -293,31 +282,38 @@
     return total
 
 
+def weighted_products(three, weight):
+    pairs = ((0, 0), (1, 1), (2, 2), (0, 1), (0, 2), (1, 2))
+    first = [weight * value for value in three]
+    return [first[a] * three[b] for a, b in pairs]
+
+
+def inside_x(start, count, width):
+    place = lax.axis_index("plane") * width - HALO * COARSE - R2 + start
+    place = place + lax.broadcasted_iota(jnp.int32, (count, LANES), 0)
+    inside = (place >= 0) & (place < lax.axis_size("plane") * width)
+    return jnp.where(inside, 1.0, 0.0)
+
+
+def block_sums(products, coarse, sx, index):
+    part = product(products[index], coarse).astype(jnp.bfloat16)
+    return product(sx, part)
+
+
 def own_kernel(
-    window, x_parts, wide_hbm, narrow_hbm, filtered, first_flat, first_steep, wide, narrow,
-    across, sems,
+    window, x_parts, bands_hbm, sums, edge, bands, across, filtered, grads, products, sem
 ):
-    copies = [
-        pltpu.make_async_copy(wide_hbm, wide, sems.at[0]),
-        pltpu.make_async_copy(narrow_hbm, narrow, sems.at[1]),
-    ]
-    for copy in copies:
-        copy.start()
     pairs, height, double = window.shape
     rows, depth = 2 * pairs, double // 2
-    pad_x = x_parts.shape[0] // 2
+    width = height - 2 * EDGE
+    columns, cells, span_x, pad_x = sizes(width, depth)
+    copy = pltpu.make_async_copy(bands_hbm, bands, sem.at[0])
+    copy.start()
+    x_bands_of = x_parts[: 2 * pad_x, :]
     for pair in range(pairs):
-        result = product(x_parts[...], window[pair])
+        result = product(x_bands_of, window[pair])
         across[2 * pair] = result[:, :depth]
         across[2 * pair + 1] = result[:, depth:]
-
-    values = [
-        window[row // 2, :, (row % 2) * depth : (row % 2 + 1) * depth].astype(jnp.float32)
-        for row in range(rows)
-    ]
-    result = product(x_parts[...], packed_rows(values, FIRST, 0).astype(jnp.bfloat16))
-    first_flat[...] = result[:pad_x].astype(jnp.bfloat16)
-    first_steep[...] = result[pad_x:].astype(jnp.bfloat16)
 
     def filter_rows(group, carry):
         start = pl.multiple_of(group * 16, 16)
@@ -332,90 +328,81 @@
         return carry
 
     lax.fori_loop(0, pad_x // 16, filter_rows, 0)
-    for copy in copies:
-        copy.wait()
-
-
-def tensor_kernel(
-    width, temp, cure, below, far, near, filtered, first_flat, first_steep,
-    x_parts, wide, narrow, sx, out, grads, low, products,
-):
-    parts, rows, pad_x, depth = filtered.shape
-    columns, cells, span_x, pad_x = sizes(width, depth)
-    planes, depths = lax.axis_size("plane"), lax.axis_size("depth")
-    plane, layer = lax.axis_index("plane"), lax.axis_index("depth")
-
-    edge = jnp.concatenate([below[0], below[1]], axis=1)
-    result = product(x_parts[...], edge).astype(jnp.bfloat16)
-    kinds = (result[:pad_x], result[pad_x:])
-    firsts = (first_flat[...], first_steep[...])
-    at_first = rows * 2 * LANES + 3 * LANES
+
+    values = [
+        window[row // 2, :, (row % 2) * depth : (row % 2 + 1) * depth].astype(jnp.float32)
+        for row in range(rows)
+    ]
+    first = product(x_bands_of, packed_rows(values, FIRST, 0).astype(jnp.bfloat16))
+    first = first.astype(jnp.bfloat16)
+    copy.wait()
     for part in range(3):
-        kind, row_kind, depth_kind = X_KINDS[part], ROW_KINDS[part], DEPTH_KINDS[part]
-        at = 5 * LANES * row_kind
-        edge_rows = product(kinds[kind], wide[at : at + 2 * LANES, :]).astype(jnp.bfloat16)
-        at = at_first + row_kind * LANES
-        first_rows = product(firsts[kind], narrow[at : at + LANES, :]).astype(jnp.bfloat16)
-        at = 5 * LANES * depth_kind + 2 * LANES
-        both = jnp.concatenate([edge_rows, first_rows], axis=1)
-        low[part] = product(both, wide[at : at + 3 * LANES, :])
+        at = DEPTH_KINDS[part] * depth
         for row in range(rows):
-            half = (row % 2) * LANES
-            both = jnp.concatenate(
-                [filtered[part, row], edge_rows[:, half : half + LANES]], axis=1
-            )
-            at = (depth_kind * (rows // 2) + row // 2) * 2 * LANES
-            grads[part, row] = product(both, narrow[at : at + 2 * LANES, :])
+            grads[part, row] = product(filtered[part, row], bands[at : at + depth, :])
+        at = (4 + 2 * part) * depth
+        kind = X_KINDS[part]
+        values = first[kind * pad_x : (kind + 1) * pad_x]
+        edge[part] = product(values, bands[at : at + depth, :]) + product(
+            values, bands[at + depth : at + 2 * depth, :]
+        )
 
     weights = product_weights(rows)
-    pairs = ((0, 0), (1, 1), (2, 2), (0, 1), (0, 2), (1, 2))
-    has_below = jnp.where(layer > 0, 1.0, 0.0)
+    is_last = lax.axis_index("depth") == lax.axis_size("depth") - 1
+    place = lax.broadcasted_iota(jnp.int32, (16, depth), 1)
+    complete = jnp.where((place < depth - R1) | is_last, 1.0, 0.0)
 
     def multiply(group, carry):
         start = pl.multiple_of(group * 16, 16)
-        x_at = plane * width - HALO * COARSE - R2 + start
-        x_at = x_at + lax.broadcasted_iota(jnp.int32, (16, LANES), 0)
-        inside = jnp.where((x_at >= 0) & (x_at < planes * width), 1.0, 0.0)
-        place = pl.ds(start, 16)
-        totals = [None] * 6
+        inside = inside_x(start, 16, width) * complete
+        totals = None
         for row in range(rows):
-            three = [grads[part, row, place, :] for part in range(3)]
-            weighted = [float(weights[row]) * value for value in three]
-            for index, (first, second) in enumerate(pairs):
-                term = weighted[first] * three[second]
-                totals[index] = term if row == 0 else totals[index] + term
+            three = [grads[part, row, pl.ds(start, 16), :] for part in range(3)]
+            terms = weighted_products(three, float(weights[row]))
+            totals = terms if row == 0 else [a + b for a, b in zip(totals, terms)]
         for index in range(6):
-            products[index, place, 0:LANES] = (totals[index] * inside).astype(jnp.bfloat16)
-        inside = inside * has_below
-        for tile in range(2):
-            lanes = slice(tile * LANES, (tile + 1) * LANES)
-            three = [low[part, place, lanes] for part in range(3)]
-            masked = [value * inside for value in three]
-            for index, (first, second) in enumerate(pairs):
-                term = masked[first] * three[second]
-                products[index, place, LANES + tile * LANES : 2 * LANES + tile * LANES] = (
-                    term.astype(jnp.bfloat16)
-                )
+            products[index, pl.ds(start, 16), :] = (totals[index] * inside).astype(jnp.bfloat16)
         return carry
 
     lax.fori_loop(0, pad_x // 16, multiply, 0)
-
-    coarse = narrow[rows * 2 * LANES : rows * 2 * LANES + 3 * LANES, :]
-    sums = []
+    sx = x_parts[2 * pad_x :, :pad_x]
     for index in range(6):
-        part = product(products[index], coarse).astype(jnp.bfloat16)
-        sums.append(product(sx[...], part))
-    trace = sums[0] + sums[1] + sums[2]
-    scale = (conduct_fiber - conduct_matrix) / (2.0 * trace + tensor_eps)
-    xx = conduct_matrix + scale * (trace - sums[1])
-    xz = -scale * sums[5]
-    zz = conduct_matrix + scale * (trace - sums[2])
-    lane = lax.broadcasted_iota(jnp.int32, xx.shape, 1)
-    joined = jnp.where(
-        lane < cells,
-        xx,
-        jnp.where(lane < 2 * cells, pltpu.roll(xz, cells, 1), pltpu.roll(zz, 2 * cells, 1)),
-    )
+        sums[index] = block_sums(products, bands[2 * depth : 3 * depth, :], sx, index)
+
+
+def edge_kernel(
+    width, temp, cure, below, far, near, sums, edge, x_parts, bands, out, products
+):
+    rows = below.shape[1] // FIRST
+    depth = LANES
+    columns, cells, span_x, pad_x = sizes(width, depth)
+    depths, layer = lax.axis_size("depth"), lax.axis_index("depth")
+    result = product(x_parts[: 2 * pad_x, :], below[...]).astype(jnp.bfloat16)
+    three = []
+    for part in range(3):
+        at = (10 + 2 * part) * depth
+        kind = X_KINDS[part]
+        values = result[kind * pad_x : (kind + 1) * pad_x]
+        three.append(
+            edge[part]
+            + product(values, bands[at : at + depth, :])
+            + product(values, bands[at + depth : at + 2 * depth, :])
+        )
+    place = lax.rem(lax.broadcasted_iota(jnp.int32, (pad_x, LANES), 1), FIRST) - START
+    inside = inside_x(0, pad_x, width) * jnp.where((place >= 0) | (layer > 0), 1.0, 0.0)
+    for index, term in enumerate(weighted_products(three, inside)):
+        products[index] = term.astype(jnp.bfloat16)
+    sx = x_parts[2 * pad_x :, :pad_x]
+    total = [
+        sums[index] + block_sums(products, bands[3 * depth : 4 * depth, :], sx, index)
+        for index in range(6)
+    ]
+    trace = total[0] + total[1] + total[2]
+    lane = lax.broadcasted_iota(jnp.int32, trace.shape, 1)
+    joined = [
+        jnp.where(lane < HALF, a, pltpu.roll(b, HALF, 1))
+        for a, b in ((trace, total[1]), (total[2], total[5]))
+    ]
 
     count = temp.shape[0]
     lanes = temp.shape[1]
@@ -433,13 +420,14 @@
             piece = jnp.where(layer == depths - 1, left, piece)
         if target == out.shape[0] - 1:
             piece = jnp.where(layer == 0, right, piece)
-        out[target, 0:height, 0:LANES] = joined[count * target : count * target + height]
+        parts = [values[count * target : count * target + height] for values in joined]
+        spare = out.shape[1] - 2 * height - 2 * GHOST
+        out[target, 0 : 2 * height, 0:LANES] = jnp.concatenate(parts, axis=0)
         if lanes > LANES:
-            out[target, 0:height, LANES:] = jnp.zeros((height, lanes - LANES), jnp.float32)
-        out[target, height : height + 2 * GHOST, :] = piece[0 : 2 * GHOST]
-        spare = out.shape[1] - height - 2 * GHOST
+            out[target, 0 : 2 * height, LANES:] = jnp.zeros((2 * height, lanes - LANES), jnp.float32)
+        out[target, 2 * height : 2 * height + 2 * GHOST, :] = piece[0 : 2 * GHOST]
         if spare:
-            out[target, height + 2 * GHOST :, :] = jnp.zeros((spare, lanes), jnp.float32)
+            out[target, 2 * height + 2 * GHOST :, :] = jnp.zeros((spare, lanes), jnp.float32)
 
 
 def cure_kernel(cells, chunks, temp_in, cure_in, levels, plan, temp_out, cure_out, conduct_out):
@@ -448,23 +436,32 @@
     planes, depths = lax.axis_size("plane"), lax.axis_size("depth")
     plane, layer = lax.axis_index("plane"), lax.axis_index("depth")
     height = count + 2 * HALO
-    own = cells - BEFORE
+    own = cells - BEFORE - AFTER
     lane = lax.broadcasted_iota(jnp.int32, (16, lanes), 1)
     row = lax.broadcasted_iota(jnp.int32, (16, lanes), 0)
 
-    conduct = [jnp.zeros((16, lanes), jnp.float32) for _ in range(3)]
+    sums = [jnp.zeros((16, lanes), jnp.float32) for _ in range(4)]
     for part in range(parts):
-        chunk = chunks[part, 0:16, :]
-        here = lane >= own * part - BEFORE
-        for kind in range(3):
-            shift = (own * part - BEFORE - kind * cells) % lanes
+        first_cell = own * part - BEFORE
+        here = (lane >= first_cell) & (lane < first_cell + cells)
+        for index in range(4):
+            at = (index // 2) * height
+            chunk = chunks[part, at : at + 16, :]
+            shift = (first_cell - (index % 2) * HALF) % lanes
             moved = chunk if shift == 0 else pltpu.roll(chunk, shift, 1)
-            conduct[kind] = jnp.where(here, moved, conduct[kind])
+            sums[index] = sums[index] + jnp.where(here, moved, 0.0)
+    trace = sums[0]
+    scale = (conduct_fiber - conduct_matrix) / (2.0 * trace + tensor_eps)
+    conduct = [
+        conduct_matrix + scale * (trace - sums[1]),
+        -scale * sums[3],
+        conduct_matrix + scale * (trace - sums[2]),
+    ]
     for kind in range(3):
         conduct_out[kind] = conduct[kind][HALO : HALO + count]
 
-    before = chunks[lax.rem(layer + parts - 1, parts)][height : height + 2 * GHOST]
-    after = chunks[lax.rem(layer + 1, parts)][height : height + 2 * GHOST]
+    before = chunks[lax.rem(layer + parts - 1, parts)][2 * height : 2 * height + 2 * GHOST]
+    after = chunks[lax.rem(layer + 1, parts)][2 * height : 2 * height + 2 * GHOST]
     spare = jnp.full((16 - count - 2 * GHOST, lanes), 0.5, jnp.float32)
     temp = jnp.concatenate([before[:GHOST], temp_in[...], after[:GHOST], 8.0 * spare], axis=0)
     cure = jnp.concatenate([before[GHOST:], cure_in[...], after[GHOST:], spare], axis=0)
@@ -511,8 +508,9 @@
     stay = pl.BlockSpec(memory_space=pltpu.HBM)
 
     fixed = lambda values: pltpu.with_memory_space_constraint(values, pltpu.HBM)
-    x_hbm = jnp.asarray(as_bfloat16(x_bands(width, depth)))
-    far, near, own, x_parts = pl.pallas_call(
+    coarse_x = coarse_x_bands(columns, width + 2 * EDGE, -(-columns // 16) * 16)
+    x_hbm = jnp.asarray(as_bfloat16(np.concatenate([x_bands(width, depth), coarse_x])))
+    far, near, own, x_parts, temp, cure = pl.pallas_call(
         pack_kernel,
         name="pack",
         out_shape=(
@@ -520,12 +518,12 @@
             pltpu.VMEM((slots, EDGE, depth), bf16),
             pltpu.VMEM((rows, width, depth), bf16),
             pltpu.VMEM(x_hbm.shape, bf16),
+            pltpu.VMEM((count, lanes), jnp.float32),
+            pltpu.VMEM((count, lanes), jnp.float32),
         ),
         in_specs=[stay] * 4,
         scratch_shapes=[
             pltpu.VMEM((rows, width, depth), jnp.int32),
-            pltpu.VMEM((count, lanes), jnp.float32),
-            pltpu.VMEM((count, lanes), jnp.float32),
             pltpu.SemaphoreType.DMA((4,)),
         ],
         compiler_params=params,
@@ -548,56 +546,48 @@
         window_kernel,
         name="window",
         out_shape=(
-            jax.ShapeDtypeStruct((rows // 2, span, 2 * depth), bf16),
-            jax.ShapeDtypeStruct((2, span, depth), bf16),
+            pltpu.VMEM((rows // 2, span, 2 * depth), bf16),
+            pltpu.VMEM((span, depth), bf16),
         ),
         compiler_params=params,
     )(own, far, near)
     below = moved(up, [((p, d), (p, d + 1)) for p in range(planes) for d in range(depths - 1)])
 
-    wide, narrow = [], [*depth_bands(rows, depth).reshape(rows, 2 * LANES, LANES)]
-    for edge_rows, low in zip(row_bands(rows, EDGE), low_bands(rows)):
-        wide += [edge_rows, low]
-    narrow += [coarse_depth_bands(rows, depth), *row_bands(rows, FIRST)]
-    wide, narrow = [jnp.asarray(as_bfloat16(np.concatenate(bands))) for bands in (wide, narrow)]
-    wide_hbm, narrow_hbm = wide, narrow
-    sx = jnp.asarray(as_bfloat16(coarse_x_bands(columns, pad_x, -(-columns // 16) * 16)))
-    filtered, first_flat, first_steep, wide, narrow = pl.pallas_call(
+    pieces = [*depth_bands(depth), *coarse_depth_bands(rows, depth)]
+    for side in edge_bands(rows)[::-1]:
+        for part in side:
+            pieces += halves(part)
+    bands_hbm = jnp.asarray(np.concatenate([as_bfloat16(piece) for piece in pieces]))
+    sums, edge, bands = pl.pallas_call(
         own_kernel,
         name="own",
         out_shape=(
-            jax.ShapeDtypeStruct((3, rows, pad_x, depth), bf16),
-            jax.ShapeDtypeStruct((pad_x, depth), bf16),
-            jax.ShapeDtypeStruct((pad_x, depth), bf16),
-            pltpu.VMEM(wide_hbm.shape, bf16),
-            pltpu.VMEM(narrow_hbm.shape, bf16),
+            pltpu.VMEM((6, x_hbm.shape[0] - 2 * pad_x, LANES), jnp.float32),
+            pltpu.VMEM((3, pad_x, LANES), jnp.float32),
+            pltpu.VMEM(bands_hbm.shape, bf16),
         ),
-        in_specs=[vmem, vmem, stay, stay],
+        in_specs=[vmem, vmem, stay],
         scratch_shapes=[
             pltpu.VMEM((rows, 2 * pad_x, depth), jnp.float32),
-            pltpu.SemaphoreType.DMA((2,)),
+            pltpu.VMEM((3, rows, pad_x, depth), bf16),
+            pltpu.VMEM((3, rows, pad_x, depth), jnp.float32),
+            pltpu.VMEM((6, pad_x, depth), bf16),
+            pltpu.SemaphoreType.DMA((1,)),
         ],
         cost_estimate=pl.CostEstimate(
-            flops=2 * rows * 2 * pad_x * span * depth, bytes_accessed=4_000_000, transcendentals=0
+            flops=4 * rows * pad_x * span * depth, bytes_accessed=4_000_000, transcendentals=0
         ),
         compiler_params=params,
-    )(window, x_parts, fixed(wide_hbm), fixed(narrow_hbm))
-
-    height = -(-(count + 2 * HALO + 2 * GHOST) // 8) * 8
+    )(window, x_parts, fixed(bands_hbm))
+
+    height = -(-(2 * (count + 2 * HALO) + 2 * GHOST) // 8) * 8
     chunks = pl.pallas_call(
-        functools.partial(tensor_kernel, width),
-        name="tensor",
+        functools.partial(edge_kernel, width),
+        name="edge",
         out_shape=pltpu.VMEM((depths, height, lanes), jnp.float32),
-        scratch_shapes=[
-            pltpu.VMEM((3, rows, pad_x, depth), jnp.float32),
-            pltpu.VMEM((3, pad_x, 2 * LANES), jnp.float32),
-            pltpu.VMEM((6, pad_x, 3 * LANES), bf16),
-        ],
+        scratch_shapes=[pltpu.VMEM((6, pad_x, depth), bf16)],
         compiler_params=params,
-    )(
-        temp_start, cure_start, below, far, near, filtered, first_flat, first_steep,
-        x_parts, wide, narrow, sx,
-    )
+    )(temp, cure, below, far, near, sums, edge, x_parts, bands)
 
     chunks = lax.all_to_all(chunks, "depth", split_axis=0, concat_axis=0, tiled=True)
 
@@ -612,7 +602,7 @@
         in_specs=[vmem, vmem, vmem, smem, smem],
         out_specs=(vmem, vmem, vmem),
         compiler_params=params,
-    )(chunks, temp_start, cure_start, tool_levels, plan)
+    )(chunks, temp, cure, tool_levels, plan)
 
 
 def solution(mesh):

time: 31.2 us -> 29.1 us (0.933)
  the two profiles are of different devices: /device:TPU:0 before, /device:TPU:4 now
where the time goes in v4:
time: 29.1 us; the launch traced here: 28.8 us
  starting transfers between devices  11.1 us (38%)
  waiting for transfers between devices  8.63 us (30%)
  Pallas kernels  8.29 us (28%)
  between operations  0.68 us (2%)
    ppermute x3, starting transfers between devices, moved(): return lax.ppermute(values, ('plane', 'depth'), index)  7.06 us
    all_to_all x1, waiting for transfers between devices, on_device(): lax.all_to_all(chunks, 'depth', split_axis=0, concat_axis=0, tiled=True)  5.65 us
    all_to_all x1, starting transfers between devices, on_device(): lax.all_to_all(chunks, 'depth', split_axis=0, concat_axis=0, tiled=True)  3.99 us
    pallas_call x1, Pallas kernels, on_device(): pl.pallas_call(own_kernel, name='own', out_shape=(pltpu.VMEM((6, x_hbm.sh...  3.75 us
    ppermute x3, waiting for transfers between devices, moved(): return lax.ppermute(values, ('plane', 'depth'), index)  2.99 us
    pallas_call x1, Pallas kernels, on_device(): pl.pallas_call(functools.partial(edge_kernel, width), name='edge', out_sh...  1.8 us
    pallas_call x1, Pallas kernels, on_device(): pl.pallas_call(functools.partial(cure_kernel, cells), name='cure', out_sh...  1.44 us
    pallas_call x1, Pallas kernels, on_device(): pl.pallas_call(pack_kernel, name='pack', out_shape=(pltpu.VMEM((slots, ED...  1.15 us
  transfers between devices with their start and end apart: 4, of which 2 were waited for; matrix products, arithmetic and copies ran while one was open for 0% of the time, Pallas kernels for 13%

profile of v4, /device:TPU:4, one launch (start us, length us, event | category | flops | bytes accessed | tf_op | source)
XLA Modules:
  0.0 28.8 jit_solution(6300322258563850881)
XLA Ops:
  0.6 1.2 %pack.1 = (bf16[9,32,128]{2,1,0:T(8,128)(2,1)S(1)}, bf16[9,32,128]{2,1,0:T(8,128)(2,1)S(1)}, bf16[8,96,128]{2,1,0:T(8,128)(2,1)S(1)}, bf16[320,160]{1,0:T(8,128)...) custom-call(s32[8,96,128]{2,1,0:T(8,128)} %intensity.1, f32[6,128]{1,0:T(8,128)} %temp_hbm.1, f32[6,128]{1,0:T(8,128)} %cure_hbm.1, ...), custom_call_target="tpu_custom_call" | custom-call | tf_op jit(solution)/shard_map/pack/pallas_call | solution.py:513
  1.8 2.8 %collective-permute-start = (bf16[9,32,128]{2,1,0:T(8,128)(2,1)S(1)}, bf16[9,32,128]{2,1,0:T(8,128)(2,1)S(1)}, u32[]{:S(2)}, u32[]{:S(2)}) collective-permute-start(bf16[9,32,128]{2,1,0:T(8,128)(2,1)S(1)} %get-tuple-element.17), channel_id=1, source_target_pairs={{4,8},{5,9},{6,10},{7,11},{12,16},{13,17},{14,18},{15,19},{20,24},... | collective-permute-start | bytes 221192 | tf_op jit(solution)/shard_map/ppermute | solution.py:534
  4.6 0.8 %collective-permute-start.1 = (bf16[9,32,128]{2,1,0:T(8,128)(2,1)S(1)}, bf16[9,32,128]{2,1,0:T(8,128)(2,1)S(1)}, u32[]{:S(2)}, u32[]{:S(2)}) collective-permute-start(bf16[9,32,128]{2,1,0:T(8,128)(2,1)S(1)} %get-tuple-element.18), channel_id=1, source_target_pairs={{0,4},{1,5},{2,6},{3,7},{8,12},{9,13},{10,14},{11,15},{16,20},{17,... | collective-permute-start | bytes 221192 | tf_op jit(solution)/shard_map/ppermute | solution.py:534
  5.4 3.0 %collective-permute-done.far = bf16[9,32,128]{2,1,0:T(8,128)(2,1)S(1)} collective-permute-done((bf16[9,32,128]{2,1,0:T(8,128)(2,1)S(1)}, bf16[9,32,128]{2,1,0:T(8,128)(2,1)S(1)}, u32[]{:S(2)}, u32[]{:S(2)}) %collective-permute-start) | collective-permute-done | bytes 73760 | tf_op jit(solution)/shard_map/ppermute | solution.py:534
  8.4 0.0 collective-permute-done.1.near
  8.4 0.1 window.1
  8.5 3.5 %collective-permute-start.2 = (bf16[160,128]{1,0:T(8,128)(2,1)S(1)}, bf16[160,128]{1,0:T(8,128)(2,1)S(1)}, u32[]{:S(2)}, u32[]{:S(2)}) collective-permute-start(bf16[160,128]{1,0:T(8,128)(2,1)S(1)} %get-tuple-element.19), channel_id=1, source_target_pairs={{0,1},{1,2},{2,3},{4,5},{5,6},{6,7},{8,9},{9,10},{10,11},{12,13},{... | collective-permute-start | bytes 122888 | tf_op jit(solution)/shard_map/ppermute | solution.py:534
  12.0 3.7 %own.1 = (f32[6,32,128]{2,1,0:T(8,128)S(1)}, f32[3,144,128]{2,1,0:T(8,128)S(1)}, bf16[2048,128]{1,0:T(8,128)(2,1)S(1)}) custom-call(bf16[4,160,256]{2,1,0:T(8,128)(2,1)S(1)} %get-tuple-element.20.window, bf16[320,160]{1,0:T(8,128)(2,1)S(1)} %get-tuple-element.21.x_parts, bf16[2048,128]{1,0:T(8,128)(2,1)} %constant.5.clone.bands_hbm), custom_call_target="tpu_custom_call" | custom-call | flops 94371840 | bytes 4000000 | tf_op jit(solution)/shard_map/own/pallas_call | solution.py:561
  15.8 0.0 collective-permute-done.2.below
  15.8 1.8 %edge.1 = f32[4,32,128]{2,1,0:T(8,128)} custom-call(f32[6,128]{1,0:T(8,128)S(1)} %get-tuple-element.14.temp.temp_in, f32[6,128]{1,0:T(8,128)S(1)} %get-tuple-element.15.cure.cure_in, bf16[160,128]{1,0:T(8,128)(2,1)S(1)} %collective-permute-done.2.below, bf16[9,32,128]{2,1,0:T(8,128)(2,1)S(1)} %collective-permute-done.far, ...), custom_call_target="tpu_custom_call" | custom-call | tf_op jit(solution)/shard_map/edge/pallas_call | solution.py:584
  17.6 0.0 copy-start.1
  17.6 4.0 %all-to-all-start = ((f32[4,32,128]{2,1,0:T(8,128)}), f32[4,32,128]{2,1,0:T(8,128)S(1)}, u32[]{:S(2)}, u32[]{:S(2)}) async-start(f32[4,32,128]{2,1,0:T(8,128)} %edge.1), calls=%async_computation | async-start | bytes 131072 | tf_op jit(solution)/shard_map/all_to_all | solution.py:592
  21.6 0.0 copy-done.1
  21.6 0.0 copy-start
  21.6 0.1 copy.10.plan
  21.7 5.6 %all-to-all-done.chunks = f32[4,32,128]{2,1,0:T(8,128)S(1)} async-done(((f32[4,32,128]{2,1,0:T(8,128)}), f32[4,32,128]{2,1,0:T(8,128)S(1)}, u32[]{:S(2)}, u32[]{:S(2)}) %all-to-all-start) | async-done | bytes 65568 | tf_op jit(solution)/shard_map/all_to_all | solution.py:592
  27.3 0.0 copy-done
  27.3 1.4 %cure.1 = (f32[6,128]{1,0:T(8,128)}, f32[6,128]{1,0:T(8,128)}, f32[3,6,128]{2,1,0:T(8,128)}) custom-call(f32[4,32,128]{2,1,0:T(8,128)S(1)} %all-to-all-done.chunks, f32[6,128]{1,0:T(8,128)S(1)} %get-tuple-element.14.temp.temp_in, f32[6,128]{1,0:T(8,128)S(1)} %get-tuple-element.15.cure.cure_in, f32[8]{0:T(128)S(1)} %copy-done, s32[3,2]{1,0:T(4,128)S(1)} %copy.10.plan), custom_call_target="tpu_custom_call" | custom-call | tf_op jit(solution)/shard_map/cure/pallas_call | solution.py:594
Async XLA Ops:
  1.8 6.6 %collective-permute-start = (bf16[9,32,128]{2,1,0:T(8,128)(2,1)S(1)}, bf16[9,32,128]{2,1,0:T(8,128)(2,1)S(1)}, u32[]{:S(2)}, u32[]{:S(2)}) collective-permute-start(bf16[9,32,128]{2,1,0:T(8,128)(2,1)S(1)} %get-tuple-element.17), channel_id=1, source_target_pairs={{4,8},{5,9},{6,10},{7,11},{12,16},{13,17},{14,18},{15,19},{20,24},... | collective-permute-start | bytes 221192 | tf_op jit(solution)/shard_map/ppermute | solution.py:534
  4.6 3.8 %collective-permute-start.1 = (bf16[9,32,128]{2,1,0:T(8,128)(2,1)S(1)}, bf16[9,32,128]{2,1,0:T(8,128)(2,1)S(1)}, u32[]{:S(2)}, u32[]{:S(2)}) collective-permute-start(bf16[9,32,128]{2,1,0:T(8,128)(2,1)S(1)} %get-tuple-element.18), channel_id=1, source_target_pairs={{0,4},{1,5},{2,6},{3,7},{8,12},{9,13},{10,14},{11,15},{16,20},{17,... | collective-permute-start | bytes 221192 | tf_op jit(solution)/shard_map/ppermute | solution.py:534
  8.5 7.2 %collective-permute-start.2 = (bf16[160,128]{1,0:T(8,128)(2,1)S(1)}, bf16[160,128]{1,0:T(8,128)(2,1)S(1)}, u32[]{:S(2)}, u32[]{:S(2)}) collective-permute-start(bf16[160,128]{1,0:T(8,128)(2,1)S(1)} %get-tuple-element.19), channel_id=1, source_target_pairs={{0,1},{1,2},{2,3},{4,5},{5,6},{6,7},{8,9},{9,10},{10,11},{12,13},{... | collective-permute-start | bytes 122888 | tf_op jit(solution)/shard_map/ppermute | solution.py:534
  17.6 4.0 %copy-start.1 = (s32[3,2]{0,1:T(2,128)S(1)}, s32[3,2]{0,1:T(2,128)}, u32[]{:S(2)}) copy-start(s32[3,2]{0,1:T(2,128)} %param.11) | copy-start | bytes 76
  17.6 9.7 %all-to-all-start = ((f32[4,32,128]{2,1,0:T(8,128)}), f32[4,32,128]{2,1,0:T(8,128)S(1)}, u32[]{:S(2)}, u32[]{:S(2)}) async-start(f32[4,32,128]{2,1,0:T(8,128)} %edge.1), calls=%async_computation | async-start | bytes 131072 | tf_op jit(solution)/shard_map/all_to_all | solution.py:592
  21.6 5.7 %copy-start = (f32[8]{0:T(128)S(1)}, f32[8]{0:T(128)}, u32[]{:S(2)}) copy-start(f32[8]{0:T(128)} %levels.1) | copy-start | bytes 100

commit v5 on v4

--- a/solution.py
+++ b/solution.py
@@ -412,22 +412,15 @@
     odd = is_odd()
     outer, inner = joined_columns(far, rows), joined_columns(near, rows)
     left, right = jnp.where(odd, inner, outer), jnp.where(odd, outer, inner)
-    height = count + 2 * HALO
-    for target in range(out.shape[0]):
-        piece = jnp.where(layer == target - 1, own_last, 0.0)
-        piece = jnp.where(layer == target + 1, own_first, piece)
-        if target == 0:
-            piece = jnp.where(layer == depths - 1, left, piece)
-        if target == out.shape[0] - 1:
-            piece = jnp.where(layer == 0, right, piece)
-        parts = [values[count * target : count * target + height] for values in joined]
-        spare = out.shape[1] - 2 * height - 2 * GHOST
-        out[target, 0 : 2 * height, 0:LANES] = jnp.concatenate(parts, axis=0)
+    relay = jnp.where(layer == 0, right, left)
+    half = joined[0].shape[0]
+    for index, values in enumerate(joined):
+        at = slice(index * half, (index + 1) * half)
+        out[at, 0:LANES] = values
         if lanes > LANES:
-            out[target, 0 : 2 * height, LANES:] = jnp.zeros((2 * height, lanes - LANES), jnp.float32)
-        out[target, 2 * height : 2 * height + 2 * GHOST, :] = piece[0 : 2 * GHOST]
-        if spare:
-            out[target, 2 * height + 2 * GHOST :, :] = jnp.zeros((spare, lanes), jnp.float32)
+            out[at, LANES:] = jnp.zeros((half, lanes - LANES), jnp.float32)
+    for index, values in enumerate((own_last, own_first, relay)):
+        out[2 * half + 8 * index : 2 * half + 8 * index + 8, :] = values
 
 
 def cure_kernel(cells, chunks, temp_in, cure_in, levels, plan, temp_out, cure_out, conduct_out):
@@ -437,6 +430,7 @@
     plane, layer = lax.axis_index("plane"), lax.axis_index("depth")
     height = count + 2 * HALO
     own = cells - BEFORE - AFTER
+    half = (chunks.shape[1] - 24) // 2
     lane = lax.broadcasted_iota(jnp.int32, (16, lanes), 1)
     row = lax.broadcasted_iota(jnp.int32, (16, lanes), 0)
 
@@ -445,8 +439,8 @@
         first_cell = own * part - BEFORE
         here = (lane >= first_cell) & (lane < first_cell + cells)
         for index in range(4):
-            at = (index // 2) * height
-            chunk = chunks[part, at : at + 16, :]
+            chunk = chunks[part, (index // 2) * half : (index // 2 + 1) * half, :]
+            chunk = pltpu.roll(chunk, lax.rem(half - layer * count, half), 0)[0:16]
             shift = (first_cell - (index % 2) * HALF) % lanes
             moved = chunk if shift == 0 else pltpu.roll(chunk, shift, 1)
             sums[index] = sums[index] + jnp.where(here, moved, 0.0)
@@ -460,11 +454,15 @@
     for kind in range(3):
         conduct_out[kind] = conduct[kind][HALO : HALO + count]
 
-    before = chunks[lax.rem(layer + parts - 1, parts)][2 * height : 2 * height + 2 * GHOST]
-    after = chunks[lax.rem(layer + 1, parts)][2 * height : 2 * height + 2 * GHOST]
+    rank = (layer + parts - 1, layer + 1)
+    start = (jnp.where(layer == 0, 16, 0), jnp.where(layer == parts - 1, 16, 8))
+    before, after = [
+        chunks[lax.rem(rank[side], parts), pl.ds(pl.multiple_of(2 * half + start[side], 8), 8), :]
+        for side in range(2)
+    ]
     spare = jnp.full((16 - count - 2 * GHOST, lanes), 0.5, jnp.float32)
     temp = jnp.concatenate([before[:GHOST], temp_in[...], after[:GHOST], 8.0 * spare], axis=0)
-    cure = jnp.concatenate([before[GHOST:], cure_in[...], after[GHOST:], spare], axis=0)
+    cure = jnp.concatenate([before[GHOST : 2 * GHOST], cure_in[...], after[GHOST : 2 * GHOST], spare], axis=0)
     gap = GHOST - HALO
     xx, xz, zz = [pltpu.roll(part, gap, 0) for part in conduct]
 
@@ -580,16 +578,16 @@
         compiler_params=params,
     )(window, x_parts, fixed(bands_hbm))
 
-    height = -(-(2 * (count + 2 * HALO) + 2 * GHOST) // 8) * 8
+    height = 2 * (x_hbm.shape[0] - 2 * pad_x) + 24
     chunks = pl.pallas_call(
         functools.partial(edge_kernel, width),
         name="edge",
-        out_shape=pltpu.VMEM((depths, height, lanes), jnp.float32),
+        out_shape=jax.ShapeDtypeStruct((height, lanes), jnp.float32),
         scratch_shapes=[pltpu.VMEM((6, pad_x, depth), bf16)],
         compiler_params=params,
     )(temp, cure, below, far, near, sums, edge, x_parts, bands)
 
-    chunks = lax.all_to_all(chunks, "depth", split_axis=0, concat_axis=0, tiled=True)
+    chunks = lax.all_gather(chunks, "depth")
 
     return pl.pallas_call(
         functools.partial(cure_kernel, cells),

time: 29.1 us -> 33.4 us (1.15)
  blocking collectives: 0 us -> 14 us
  waiting for transfers between devices: 8.63 us -> 2.99 us
  starting transfers between devices: 11.1 us -> 7.06 us
  local copies, waits for them, and re-layouts: 0.1 us -> 0.76 us
  Pallas kernels: 8.29 us -> 7.67 us
    all_gather x0 -> x1, blocking collectives: none -> 14 us  [on_device(): chunks = lax.all_gather(chunks, 'depth')]
    all_to_all x1 -> x0, waiting for transfers between devices: 5.65 us -> none  [on_device(): lax.all_to_all(chunks, 'depth', split_axis=0, concat_axis=0, tiled=True)]
    all_to_all x1 -> x0, starting transfers between devices: 3.99 us -> none  [on_device(): lax.all_to_all(chunks, 'depth', split_axis=0, concat_axis=0, tiled=True)]
    unnamed x5, local copies, waits for them, and re-layouts: 0.1 us -> 0.76 us
    pallas_call x1, Pallas kernels: 1.8 us -> 1.17 us  [on_device(): pl.pallas_call(functools.partial(edge_kernel, width), name='edge', out_sh...]
  transfers between devices with their start and end apart: 4 -> 3, of which waited for: 2 -> 1; matrix products, arithmetic and copies ran while one was open for 0% -> 0% of each run, Pallas kernels for 13% -> 11%
where the time goes in v5:
time: 33.4 us; the launch traced here: 33.2 us
  blocking collectives  14 us (42%)
  Pallas kernels  7.67 us (23%)
  starting transfers between devices  7.06 us (21%)
  waiting for transfers between devices  2.99 us (9%)
  local copies, waits for them, and re-layouts  0.76 us (2%)
  between operations  0.7 us (2%)
    all_gather x1, blocking collectives, on_device(): chunks = lax.all_gather(chunks, 'depth')  14 us
    ppermute x3, starting transfers between devices, moved(): return lax.ppermute(values, ('plane', 'depth'), index)  7.06 us
    pallas_call x1, Pallas kernels, on_device(): pl.pallas_call(own_kernel, name='own', out_shape=(pltpu.VMEM((6, x_hbm.sh...  3.74 us
    ppermute x3, waiting for transfers between devices, moved(): return lax.ppermute(values, ('plane', 'depth'), index)  2.99 us
    pallas_call x1, Pallas kernels, on_device(): pl.pallas_call(functools.partial(cure_kernel, cells), name='cure', out_sh...  1.46 us
    pallas_call x1, Pallas kernels, on_device(): pl.pallas_call(functools.partial(edge_kernel, width), name='edge', out_sh...  1.17 us
    pallas_call x1, Pallas kernels, on_device(): pl.pallas_call(pack_kernel, name='pack', out_shape=(pltpu.VMEM((slots, ED...  1.15 us
    unnamed x5, local copies, waits for them, and re-layouts  0.76 us
  transfers between devices with their start and end apart: 3, of which 1 were waited for; matrix products, arithmetic and copies ran while one was open for 0% of the time, Pallas kernels for 11%

profile of v5, /device:TPU:4, one launch (start us, length us, event | category | flops | bytes accessed | tf_op | source)
XLA Modules:
  0.0 33.2 jit_solution(14367981955328662324)
XLA Ops:
  0.6 1.2 %pack.1 = (bf16[9,32,128]{2,1,0:T(8,128)(2,1)S(1)}, bf16[9,32,128]{2,1,0:T(8,128)(2,1)S(1)}, bf16[8,96,128]{2,1,0:T(8,128)(2,1)S(1)}, bf16[320,160]{1,0:T(8,128)...) custom-call(s32[8,96,128]{2,1,0:T(8,128)} %intensity.1, f32[6,128]{1,0:T(8,128)} %temp_hbm.1, f32[6,128]{1,0:T(8,128)} %cure_hbm.1, ...), custom_call_target="tpu_custom_call" | custom-call | tf_op jit(solution)/shard_map/pack/pallas_call | solution.py:511
  1.8 2.8 %collective-permute-start = (bf16[9,32,128]{2,1,0:T(8,128)(2,1)S(1)}, bf16[9,32,128]{2,1,0:T(8,128)(2,1)S(1)}, u32[]{:S(2)}, u32[]{:S(2)}) collective-permute-start(bf16[9,32,128]{2,1,0:T(8,128)(2,1)S(1)} %get-tuple-element.17), channel_id=1, source_target_pairs={{4,8},{5,9},{6,10},{7,11},{12,16},{13,17},{14,18},{15,19},{20,24},... | collective-permute-start | bytes 221192 | tf_op jit(solution)/shard_map/ppermute | solution.py:532
  4.6 0.8 %collective-permute-start.1 = (bf16[9,32,128]{2,1,0:T(8,128)(2,1)S(1)}, bf16[9,32,128]{2,1,0:T(8,128)(2,1)S(1)}, u32[]{:S(2)}, u32[]{:S(2)}) collective-permute-start(bf16[9,32,128]{2,1,0:T(8,128)(2,1)S(1)} %get-tuple-element.18), channel_id=1, source_target_pairs={{0,4},{1,5},{2,6},{3,7},{8,12},{9,13},{10,14},{11,15},{16,20},{17,... | collective-permute-start | bytes 221192 | tf_op jit(solution)/shard_map/ppermute | solution.py:532
  5.4 3.0 %collective-permute-done.far = bf16[9,32,128]{2,1,0:T(8,128)(2,1)S(1)} collective-permute-done((bf16[9,32,128]{2,1,0:T(8,128)(2,1)S(1)}, bf16[9,32,128]{2,1,0:T(8,128)(2,1)S(1)}, u32[]{:S(2)}, u32[]{:S(2)}) %collective-permute-start) | collective-permute-done | bytes 73760 | tf_op jit(solution)/shard_map/ppermute | solution.py:532
  8.4 0.0 collective-permute-done.1.near
  8.4 0.1 window.1
  8.5 0.0 copy-start.1
  8.5 3.5 %collective-permute-start.2 = (bf16[160,128]{1,0:T(8,128)(2,1)S(1)}, bf16[160,128]{1,0:T(8,128)(2,1)S(1)}, u32[]{:S(2)}, u32[]{:S(2)}) collective-permute-start(bf16[160,128]{1,0:T(8,128)(2,1)S(1)} %get-tuple-element.19), channel_id=1, source_target_pairs={{0,1},{1,2},{2,3},{4,5},{5,6},{6,7},{8,9},{9,10},{10,11},{12,13},{... | collective-permute-start | bytes 122888 | tf_op jit(solution)/shard_map/ppermute | solution.py:532
  12.0 0.0 copy-done.1
  12.0 0.1 copy.10.plan
  12.1 3.7 %own.1 = (f32[6,32,128]{2,1,0:T(8,128)S(1)}, f32[3,144,128]{2,1,0:T(8,128)S(1)}, bf16[2048,128]{1,0:T(8,128)(2,1)S(1)}) custom-call(bf16[4,160,256]{2,1,0:T(8,128)(2,1)S(1)} %get-tuple-element.20.window, bf16[320,160]{1,0:T(8,128)(2,1)S(1)} %get-tuple-element.21.x_parts, bf16[2048,128]{1,0:T(8,128)(2,1)} %constant.5.clone.bands_hbm), custom_call_target="tpu_custom_call" | custom-call | flops 94371840 | bytes 4000000 | tf_op jit(solution)/shard_map/own/pallas_call | solution.py:559
  15.9 0.0 collective-permute-done.2.below
  15.9 1.2 %edge.1 = f32[88,128]{1,0:T(8,128)S(1)} custom-call(f32[6,128]{1,0:T(8,128)S(1)} %get-tuple-element.14.temp.temp_in, f32[6,128]{1,0:T(8,128)S(1)} %get-tuple-element.15.cure.cure_in, bf16[160,128]{1,0:T(8,128)(2,1)S(1)} %collective-permute-done.2.below, bf16[9,32,128]{2,1,0:T(8,128)(2,1)S(1)} %collective-permute-done.far, ...), custom_call_target="tpu_custom_call" | custom-call | tf_op jit(solution)/shard_map/edge/pallas_call | solution.py:582
  17.1 14.0 %all-gather = f32[352,128]{1,0:T(8,128)S(1)} all-gather(f32[88,128]{1,0:T(8,128)S(1)} %edge.1), channel_id=2, replica_groups=mesh['plane'=8,'depth'=4] {'depth'}, dimensions={0}, use_global_device_ids=true | all-gather | bytes 225280 | tf_op jit(solution)/shard_map/all_gather | solution.py:590
  31.1 0.0 copy-start
  31.1 0.7 %copy-done = f32[8]{0:T(128)S(1)} copy-done((f32[8]{0:T(128)S(1)}, f32[8]{0:T(128)}, u32[]{:S(2)}) %copy-start) | copy-done | bytes 56
  31.7 1.5 %cure.1 = (f32[6,128]{1,0:T(8,128)}, f32[6,128]{1,0:T(8,128)}, f32[3,6,128]{2,1,0:T(8,128)}) custom-call(f32[4,88,128]{2,1,0:T(8,128)S(1)} %bitcast.1, f32[6,128]{1,0:T(8,128)S(1)} %get-tuple-element.14.temp.temp_in, f32[6,128]{1,0:T(8,128)S(1)} %get-tuple-element.15.cure.cure_in, f32[8]{0:T(128)S(1)} %copy-done, s32[3,2]{1,0:T(4,128)S(1)} %copy.10.plan), custom_call_target="tpu_custom_call" | custom-call | tf_op jit(solution)/shard_map/cure/pallas_call | solution.py:592
Async XLA Ops:
  1.8 6.6 %collective-permute-start = (bf16[9,32,128]{2,1,0:T(8,128)(2,1)S(1)}, bf16[9,32,128]{2,1,0:T(8,128)(2,1)S(1)}, u32[]{:S(2)}, u32[]{:S(2)}) collective-permute-start(bf16[9,32,128]{2,1,0:T(8,128)(2,1)S(1)} %get-tuple-element.17), channel_id=1, source_target_pairs={{4,8},{5,9},{6,10},{7,11},{12,16},{13,17},{14,18},{15,19},{20,24},... | collective-permute-start | bytes 221192 | tf_op jit(solution)/shard_map/ppermute | solution.py:532
  4.6 3.8 %collective-permute-start.1 = (bf16[9,32,128]{2,1,0:T(8,128)(2,1)S(1)}, bf16[9,32,128]{2,1,0:T(8,128)(2,1)S(1)}, u32[]{:S(2)}, u32[]{:S(2)}) collective-permute-start(bf16[9,32,128]{2,1,0:T(8,128)(2,1)S(1)} %get-tuple-element.18), channel_id=1, source_target_pairs={{0,4},{1,5},{2,6},{3,7},{8,12},{9,13},{10,14},{11,15},{16,20},{17,... | collective-permute-start | bytes 221192 | tf_op jit(solution)/shard_map/ppermute | solution.py:532
  8.5 3.5 %copy-start.1 = (s32[3,2]{0,1:T(2,128)S(1)}, s32[3,2]{0,1:T(2,128)}, u32[]{:S(2)}) copy-start(s32[3,2]{0,1:T(2,128)} %param.11) | copy-start | bytes 76
  8.5 7.3 %collective-permute-start.2 = (bf16[160,128]{1,0:T(8,128)(2,1)S(1)}, bf16[160,128]{1,0:T(8,128)(2,1)S(1)}, u32[]{:S(2)}, u32[]{:S(2)}) collective-permute-start(bf16[160,128]{1,0:T(8,128)(2,1)S(1)} %get-tuple-element.19), channel_id=1, source_target_pairs={{0,1},{1,2},{2,3},{4,5},{5,6},{6,7},{8,9},{9,10},{10,11},{12,13},{... | collective-permute-start | bytes 122888 | tf_op jit(solution)/shard_map/ppermute | solution.py:532
  31.1 0.7 %copy-start = (f32[8]{0:T(128)S(1)}, f32[8]{0:T(128)}, u32[]{:S(2)}) copy-start(f32[8]{0:T(128)} %levels.1) | copy-start | bytes 100

commit v6 on v4

--- a/solution.py
+++ b/solution.py
@@ -32,10 +32,10 @@
 LANES = 128
 HALO = 2
 GHOST = 3
-FIRST = 16
-START = 8
-BEFORE = -(-(R1 + R2) // COARSE)
-AFTER = 1
+PACK = 16
+BACK = 8
+BEFORE = 1
+AFTER = -(-(R1 + R2) // COARSE)
 HALF = LANES // 2
 ROW_KINDS = (1, 0, 0)
 X_KINDS = (0, 1, 0)
@@ -87,9 +87,16 @@
 def sizes(width, depth):
     columns = width // COARSE + 2 * HALO
     cells = depth // COARSE + BEFORE + AFTER
-    span_x = columns * COARSE + 2 * R2
-    pad_x = -(-span_x // 16) * 16
-    return columns, cells, span_x, pad_x
+    side = HALO * COARSE + R2 + R1
+    inner = -(-(width - 2 * R1) // 16) * 16
+    return columns, cells, side, inner
+
+
+def product_rows(width):
+    columns, cells, side, inner = sizes(width, 0)
+    places = [R1 + i if R1 + i < width - R1 else None for i in range(inner)]
+    places += [R1 - side + i for i in range(side)] + [width - R1 + i for i in range(side)]
+    return places
 
 
 GRAD_TAPS = tuple(
@@ -107,37 +114,39 @@
     return float(taps[offset + radius]) if abs(offset) <= radius else 0.0
 
 
-def x_bands(width, depth):
-    columns, cells, span_x, pad_x = sizes(width, depth)
-    bands = np.zeros((2, pad_x, width + 2 * EDGE))
-    first = EDGE - HALO * COARSE - R2 - R1
+def x_bands(width):
+    places = product_rows(width)
+    bands = np.zeros((2, len(places), width + 2 * EDGE))
     for kind in range(2):
-        for out in range(span_x):
-            bands[kind, out, out + first : out + first + 2 * R1 + 1] = grad_taps(kind)
-    return bands.reshape(2 * pad_x, -1)
-
-
-def edge_bands(rows):
-    bands = np.zeros((2, 3, rows * FIRST, rows * FIRST))
+        for row, place in enumerate(places):
+            if place is not None:
+                first = place + EDGE - R1
+                bands[kind, row, first : first + 2 * R1 + 1] = grad_taps(kind)
+    return bands
+
+
+def edge_bands(rows, depth):
+    bands = np.zeros((2, 3, rows * PACK, rows * PACK))
     for part in range(3):
         row_taps, depth_taps = grad_taps(ROW_KINDS[part]), grad_taps(DEPTH_KINDS[part])
         for source in range(rows):
             for target in range(rows):
                 row_tap = tap(row_taps, source - target)
-                for near in range(-FIRST, FIRST):
-                    side, lane = int(near >= 0), source * FIRST + near % FIRST
-                    for place in range(-R1, START):
+                for near in range(-PACK, PACK):
+                    side, lane = int(near >= 0), source * PACK + near % PACK
+                    for place in range(-BACK, R1):
                         value = row_tap * tap(depth_taps, near - place)
-                        bands[side, part, lane, target * FIRST + START + place] = value
+                        bands[side, part, lane, target * PACK + BACK + place] = value
     return bands
 
 
 def depth_bands(depth):
-    bands = np.zeros((2, depth, depth))
+    bands = np.zeros((2, 2 * depth, 2 * depth))
     for kind in range(2):
         for place in range(depth):
             for near in range(max(place - R1, 0), min(place + R1 + 1, depth)):
-                bands[kind, near, place] = tap(grad_taps(kind), near - place)
+                value = tap(grad_taps(kind), near - place)
+                bands[kind, near, place] = bands[kind, depth + near, depth + place] = value
     return bands
 
 
@@ -148,29 +157,57 @@
 def coarse_depth_bands(rows, depth):
     taps = smooth_taps(R2, sigma_tensor)
     weights = product_weights(rows)
-    columns, cells, span_x, pad_x = sizes(0, depth)
+    columns, cells, side, inner = sizes(0, depth)
     bands = np.zeros((2, depth, LANES))
     for cell in range(cells):
         for voxel in range(COARSE):
             place = (cell - BEFORE) * COARSE + voxel
-            for near in range(max(place - R2, -R1), min(place + R2 + 1, depth)):
+            for near in range(max(place - R2, 0), min(place + R2 + 1, depth + R1)):
                 value = tap(taps, near - place)
-                if near >= START:
+                if near < depth - BACK:
                     bands[0, near, cell] += value
                 else:
                     for row in range(rows):
-                        bands[1, row * FIRST + START + near, cell] += weights[row] * value
+                        lane = row * PACK + near - depth + BACK
+                        bands[1, lane, cell] += weights[row] * value
     return bands
 
 
-def coarse_x_bands(count, padded_in, padded_out):
+def coarse_x_bands(width):
     taps = smooth_taps(R2, sigma_tensor)
-    bands = np.zeros((padded_out, padded_in))
-    for cell in range(count):
+    places = product_rows(width)
+    columns, cells, side, inner = sizes(width, 0)
+    bands = np.zeros((-(-columns // 16) * 16, len(places)))
+    for column in range(columns):
         for voxel in range(COARSE):
-            start = cell * COARSE + voxel
-            bands[cell, start : start + 2 * R2 + 1] += taps
+            middle = (column - HALO) * COARSE + voxel
+            for row, place in enumerate(places):
+                if place is not None:
+                    bands[column, row] += tap(taps, place - middle)
     return bands
+
+
+def x_constants(width):
+    columns, cells, side, inner = sizes(width, 0)
+    bands, coarse = x_bands(width), coarse_x_bands(width)
+    pieces = [
+        bands[:, :inner].reshape(2 * inner, -1),
+        bands[:, inner:].reshape(4 * side, -1),
+        bands[:, :inner, EDGE : EDGE + width].reshape(2 * inner, -1),
+        coarse,
+        coarse[:, inner:],
+    ]
+    widest = max(piece.shape[1] for piece in pieces)
+    padded = [np.pad(piece, ((0, 0), (0, widest - piece.shape[1]))) for piece in pieces]
+    return as_bfloat16(np.concatenate(padded)), [len(piece) for piece in pieces]
+
+
+def depth_constants(rows, depth):
+    above = [[np.concatenate(halves(part)) for part in side] for side in edge_bands(rows, depth)]
+    wide = [*depth_bands(depth)]
+    wide += [np.concatenate([side[0], side[2]], axis=1) for side in above]
+    narrow = [*coarse_depth_bands(rows, depth)] + [side[1] for side in above]
+    return [np.concatenate([as_bfloat16(piece) for piece in pieces]) for pieces in (wide, narrow)]
 
 
 def three_parts(values):
@@ -227,7 +264,8 @@
         send(far, near)
 
     for row in range(rows):
-        own[row] = grey[row].astype(jnp.float32).astype(jnp.bfloat16)
+        half = (row % 2) * depth
+        own[row // 2, :, half : half + depth] = grey[row].astype(jnp.float32).astype(jnp.bfloat16)
 
 
 def packed_rows(values, size, first):
@@ -241,18 +279,20 @@
     return packed
 
 
-def window_kernel(own, far, near, window, up):
-    rows, width, depth = own.shape
+def window_kernel(own, far, near, inner_sums, window, down):
+    pairs, width, double = own.shape
+    rows, depth = 2 * pairs, double // 2
     odd = is_odd()
 
     def fill(from_left, from_right):
         values = []
         for row in range(rows):
             half = (row % 2) * depth
-            whole = jnp.concatenate([from_left[row], own[row], from_right[row]], axis=0)
+            middle = own[row // 2, :, half : half + depth]
+            whole = jnp.concatenate([from_left[row], middle, from_right[row]], axis=0)
             window[row // 2, :, half : half + depth] = whole
             values.append(whole.astype(jnp.float32))
-        up[...] = packed_rows(values, FIRST, depth - FIRST).astype(jnp.bfloat16)
+        down[...] = packed_rows(values, PACK, 0).astype(jnp.bfloat16)
 
     @pl.when(odd)
     def _():
@@ -288,115 +328,153 @@
     return [first[a] * three[b] for a, b in pairs]
 
 
-def inside_x(start, count, width):
-    place = lax.axis_index("plane") * width - HALO * COARSE - R2 + start
-    place = place + lax.broadcasted_iota(jnp.int32, (count, LANES), 0)
+def side_mask(side, width):
+    row = lax.broadcasted_iota(jnp.int32, (2 * side, LANES), 0)
+    place = jnp.where(row < side, row + R1 - side, row + width - R1 - side)
+    place = place + lax.axis_index("plane") * width
     inside = (place >= 0) & (place < lax.axis_size("plane") * width)
     return jnp.where(inside, 1.0, 0.0)
 
 
-def block_sums(products, coarse, sx, index):
-    part = product(products[index], coarse).astype(jnp.bfloat16)
-    return product(sx, part)
-
-
-def own_kernel(
-    window, x_parts, bands_hbm, sums, edge, bands, across, filtered, grads, products, sem
-):
+def all_sums(products, coarse, sx):
+    kinds, count, lanes = products.shape
+    along = product(products[...].reshape(kinds * count, lanes), coarse).astype(jnp.bfloat16)
+    parts = [along[index * count : (index + 1) * count] for index in range(kinds)]
+    return product(sx, jnp.concatenate(parts, axis=1))
+
+
+def tensor_sums(window, bands, sx, mask, ready, wide, narrow, across, filtered, grads, products):
     pairs, height, double = window.shape
     rows, depth = 2 * pairs, double // 2
-    width = height - 2 * EDGE
-    columns, cells, span_x, pad_x = sizes(width, depth)
-    copy = pltpu.make_async_copy(bands_hbm, bands, sem.at[0])
-    copy.start()
-    x_bands_of = x_parts[: 2 * pad_x, :]
+    count = bands.shape[0] // 2
     for pair in range(pairs):
-        result = product(x_bands_of, window[pair])
-        across[2 * pair] = result[:, :depth]
-        across[2 * pair + 1] = result[:, depth:]
+        across[pair] = product(bands, window[pair])
 
     def filter_rows(group, carry):
         start = pl.multiple_of(group * 16, 16)
         kinds = [
-            [across[row, pl.ds(kind * pad_x + start, 16), :] for row in range(rows)]
+            [
+                across[row // 2, pl.ds(kind * count + start, 16), pl.ds((row % 2) * depth, depth)]
+                for row in range(rows)
+            ]
             for kind in range(2)
         ]
         for part in range(3):
             for row in range(rows):
                 result = along_rows(ROW_KINDS[part], kinds[X_KINDS[part]], row)
-                filtered[part, row, pl.ds(start, 16), :] = result.astype(jnp.bfloat16)
+                lanes = pl.ds((row % 2) * depth, depth)
+                filtered[part, row // 2, pl.ds(start, 16), lanes] = result.astype(jnp.bfloat16)
         return carry
 
-    lax.fori_loop(0, pad_x // 16, filter_rows, 0)
-
-    values = [
-        window[row // 2, :, (row % 2) * depth : (row % 2 + 1) * depth].astype(jnp.float32)
-        for row in range(rows)
-    ]
-    first = product(x_bands_of, packed_rows(values, FIRST, 0).astype(jnp.bfloat16))
-    first = first.astype(jnp.bfloat16)
-    copy.wait()
+    lax.fori_loop(0, count // 16, filter_rows, 0)
+    ready()
     for part in range(3):
-        at = DEPTH_KINDS[part] * depth
-        for row in range(rows):
-            grads[part, row] = product(filtered[part, row], bands[at : at + depth, :])
-        at = (4 + 2 * part) * depth
-        kind = X_KINDS[part]
-        values = first[kind * pad_x : (kind + 1) * pad_x]
-        edge[part] = product(values, bands[at : at + depth, :]) + product(
-            values, bands[at + depth : at + 2 * depth, :]
-        )
+        at = DEPTH_KINDS[part] * double
+        for pair in range(pairs):
+            grads[part, pair] = product(filtered[part, pair], wide[at : at + double, :])
 
     weights = product_weights(rows)
-    is_last = lax.axis_index("depth") == lax.axis_size("depth") - 1
+    first = lax.axis_index("depth") == 0
     place = lax.broadcasted_iota(jnp.int32, (16, depth), 1)
-    complete = jnp.where((place < depth - R1) | is_last, 1.0, 0.0)
+    complete = jnp.where((place >= R1) | first, 1.0, 0.0)
 
     def multiply(group, carry):
         start = pl.multiple_of(group * 16, 16)
-        inside = inside_x(start, 16, width) * complete
+        inside = complete if mask is None else complete * mask[pl.ds(start, 16), :]
         totals = None
         for row in range(rows):
-            three = [grads[part, row, pl.ds(start, 16), :] for part in range(3)]
+            lanes = pl.ds((row % 2) * depth, depth)
+            three = [grads[part, row // 2, pl.ds(start, 16), lanes] for part in range(3)]
             terms = weighted_products(three, float(weights[row]))
             totals = terms if row == 0 else [a + b for a, b in zip(totals, terms)]
         for index in range(6):
             products[index, pl.ds(start, 16), :] = (totals[index] * inside).astype(jnp.bfloat16)
         return carry
 
-    lax.fori_loop(0, pad_x // 16, multiply, 0)
-    sx = x_parts[2 * pad_x :, :pad_x]
-    for index in range(6):
-        sums[index] = block_sums(products, bands[2 * depth : 3 * depth, :], sx, index)
+    lax.fori_loop(0, count // 16, multiply, 0)
+    return all_sums(products, narrow[0:depth, :], sx)
+
+
+def inner_kernel(
+    starts, own, x_parts, wide_hbm, narrow_hbm, sums, wide, narrow, across, filtered, grads,
+    products, sems,
+):
+    copies = [
+        pltpu.make_async_copy(wide_hbm, wide, sems.at[0]),
+        pltpu.make_async_copy(narrow_hbm, narrow, sems.at[1]),
+    ]
+    for copy in copies:
+        copy.start()
+
+    def ready():
+        for copy in copies:
+            copy.wait()
+
+    width, count = own.shape[1], across.shape[1] // 2
+    bands = x_parts[starts[2] : starts[3], :width]
+    sx = x_parts[starts[3] : starts[4], :count]
+    sums[...] = tensor_sums(
+        own, bands, sx, None, ready, wide, narrow, across, filtered, grads, products
+    )
+
+
+def side_kernel(
+    starts, window, x_parts, wide, narrow, inner_sums, sums, edge, across, filtered, grads,
+    products, mask,
+):
+    pairs, height, double = window.shape
+    rows, depth = 2 * pairs, double // 2
+    count = across.shape[1] // 2
+    mask[...] = side_mask(count // 2, height - 2 * EDGE)
+    bands = x_parts[starts[1] : starts[2], :]
+    sx = x_parts[starts[4] : starts[5], :count]
+    sums[...] = inner_sums[...] + tensor_sums(
+        window, bands, sx, mask, lambda: None, wide, narrow, across, filtered, grads, products
+    )
+    values = [
+        window[row // 2, :, (row % 2) * depth : (row % 2 + 1) * depth].astype(jnp.float32)
+        for row in range(rows)
+    ]
+    last = packed_rows(values, PACK, depth - PACK).astype(jnp.bfloat16)
+    results = edge_gradients(starts, last, x_parts, wide, narrow, 0)
+    for part in range(3):
+        edge[part] = results[part]
+
+
+def edge_gradients(starts, packed, x_parts, wide, narrow, side):
+    result = product(x_parts[: starts[2], :], packed).astype(jnp.bfloat16)
+    inner, outer = starts[1] // 2, (starts[2] - starts[1]) // 2
+    kinds = []
+    for kind in range(2):
+        at, after = kind * inner, starts[1] + kind * outer
+        both = jnp.concatenate([result[at : at + inner], result[after : after + outer]], axis=0)
+        kinds.append(jnp.concatenate([both, both], axis=1))
+    lanes = packed.shape[1]
+    at = (4 + 2 * side) * lanes
+    flat = product(kinds[0], wide[at : at + 2 * lanes, :])
+    at = (2 + 2 * side) * lanes
+    steep = product(kinds[1], narrow[at : at + 2 * lanes, :])
+    return flat[:, :lanes], steep, flat[:, lanes:]
 
 
 def edge_kernel(
-    width, temp, cure, below, far, near, sums, edge, x_parts, bands, out, products
+    starts, width, temp, cure, above, far, near, sums, edge, x_parts, wide, narrow, out, products
 ):
-    rows = below.shape[1] // FIRST
-    depth = LANES
-    columns, cells, span_x, pad_x = sizes(width, depth)
+    kinds, pad_x, depth = edge.shape
+    rows = depth // PACK
     depths, layer = lax.axis_size("depth"), lax.axis_index("depth")
-    result = product(x_parts[: 2 * pad_x, :], below[...]).astype(jnp.bfloat16)
-    three = []
-    for part in range(3):
-        at = (10 + 2 * part) * depth
-        kind = X_KINDS[part]
-        values = result[kind * pad_x : (kind + 1) * pad_x]
-        three.append(
-            edge[part]
-            + product(values, bands[at : at + depth, :])
-            + product(values, bands[at + depth : at + 2 * depth, :])
-        )
-    place = lax.rem(lax.broadcasted_iota(jnp.int32, (pad_x, LANES), 1), FIRST) - START
-    inside = inside_x(0, pad_x, width) * jnp.where((place >= 0) | (layer > 0), 1.0, 0.0)
+    side = (starts[2] - starts[1]) // 4
+    results = edge_gradients(starts, above[...], x_parts, wide, narrow, 1)
+    three = [edge[part] + results[part] for part in range(3)]
+    place = lax.rem(lax.broadcasted_iota(jnp.int32, (pad_x, LANES), 1), PACK) - BACK
+    inside = jnp.where((place < 0) | (layer < depths - 1), 1.0, 0.0)
+    inner = jnp.ones((pad_x - 2 * side, LANES), jnp.float32)
+    inside = inside * jnp.concatenate([inner, side_mask(side, width)], axis=0)
     for index, term in enumerate(weighted_products(three, inside)):
         products[index] = term.astype(jnp.bfloat16)
-    sx = x_parts[2 * pad_x :, :pad_x]
-    total = [
-        sums[index] + block_sums(products, bands[3 * depth : 4 * depth, :], sx, index)
-        for index in range(6)
-    ]
+    sx = x_parts[starts[3] : starts[4], :pad_x]
+    total = sums[...] + all_sums(products, narrow[depth : 2 * depth, :], sx)
+    total = [total[:, index * LANES : (index + 1) * LANES] for index in range(6)]
     trace = total[0] + total[1] + total[2]
     lane = lax.broadcasted_iota(jnp.int32, trace.shape, 1)
     joined = [
@@ -420,17 +498,23 @@
             piece = jnp.where(layer == depths - 1, left, piece)
         if target == out.shape[0] - 1:
             piece = jnp.where(layer == 0, right, piece)
-        parts = [values[count * target : count * target + height] for values in joined]
-        spare = out.shape[1] - 2 * height - 2 * GHOST
-        out[target, 0 : 2 * height, 0:LANES] = jnp.concatenate(parts, axis=0)
+        for index, values in enumerate(joined):
+            at = index * height
+            out[target, at : at + height, 0:LANES] = values[
+                count * target : count * target + height
+            ]
         if lanes > LANES:
             out[target, 0 : 2 * height, LANES:] = jnp.zeros((2 * height, lanes - LANES), jnp.float32)
         out[target, 2 * height : 2 * height + 2 * GHOST, :] = piece[0 : 2 * GHOST]
+        spare = out.shape[1] - 2 * height - 2 * GHOST
         if spare:
             out[target, 2 * height + 2 * GHOST :, :] = jnp.zeros((spare, lanes), jnp.float32)
 
 
-def cure_kernel(cells, chunks, temp_in, cure_in, levels, plan, temp_out, cure_out, conduct_out):
+def cure_kernel(
+    cells, chunks, temp_in, cure_in, levels, plan, temp_hbm, cure_hbm, conduct_hbm, temp_out,
+    cure_out, conduct_out, sems,
+):
     count, lanes = temp_in.shape
     parts = chunks.shape[0]
     planes, depths = lax.axis_size("plane"), lax.axis_size("depth")
@@ -459,6 +543,12 @@
     ]
     for kind in range(3):
         conduct_out[kind] = conduct[kind][HALO : HALO + count]
+    copies = [
+        pltpu.make_async_copy(conduct_out, conduct_hbm, sems.at[0]),
+        pltpu.make_async_copy(temp_out, temp_hbm, sems.at[1]),
+        pltpu.make_async_copy(cure_out, cure_hbm, sems.at[2]),
+    ]
+    copies[0].start()
 
     before = chunks[lax.rem(layer + parts - 1, parts)][2 * height : 2 * height + 2 * GHOST]
     after = chunks[lax.rem(layer + 1, parts)][2 * height : 2 * height + 2 * GHOST]
@@ -493,13 +583,17 @@
         cure = cure + time_step * rate
     temp_out[...] = temp[GHOST : GHOST + count]
     cure_out[...] = cure[GHOST : GHOST + count]
+    for copy in copies[1:]:
+        copy.start()
+    for copy in copies:
+        copy.wait()
 
 
 def on_device(intensity, temp_start, cure_start, tool_levels, plan):
     rows, width, depth = intensity.shape
     count, lanes = temp_start.shape
     planes, depths = lax.axis_size("plane"), lax.axis_size("depth")
-    columns, cells, span_x, pad_x = sizes(width, depth)
+    columns, cells, side, inner = sizes(width, depth)
     bf16 = jnp.bfloat16
     slots = rows + lanes // LANES
     params = pltpu.CompilerParams(vmem_limit_bytes=24 * 1024 * 1024)
@@ -508,15 +602,16 @@
     stay = pl.BlockSpec(memory_space=pltpu.HBM)
 
     fixed = lambda values: pltpu.with_memory_space_constraint(values, pltpu.HBM)
-    coarse_x = coarse_x_bands(columns, width + 2 * EDGE, -(-columns // 16) * 16)
-    x_hbm = jnp.asarray(as_bfloat16(np.concatenate([x_bands(width, depth), coarse_x])))
+    x_constant, lengths = x_constants(width)
+    x_hbm = jnp.asarray(x_constant)
+    starts = tuple(int(start) for start in np.cumsum([0] + lengths))
     far, near, own, x_parts, temp, cure = pl.pallas_call(
         pack_kernel,
         name="pack",
         out_shape=(
             pltpu.VMEM((slots, EDGE, depth), bf16),
             pltpu.VMEM((slots, EDGE, depth), bf16),
-            pltpu.VMEM((rows, width, depth), bf16),
+            pltpu.VMEM((rows // 2, width, 2 * depth), bf16),
             pltpu.VMEM(x_hbm.shape, bf16),
             pltpu.VMEM((count, lanes), jnp.float32),
             pltpu.VMEM((count, lanes), jnp.float32),
@@ -541,8 +636,40 @@
     far = swapped(far, 1)
     near = swapped(near, 0)
 
+    wide_hbm, narrow_hbm = [jnp.asarray(values) for values in depth_constants(rows, depth)]
+    high = starts[4] - starts[3]
+
+    def scratch(count):
+        return [
+            pltpu.VMEM((rows // 2, 2 * count, 2 * depth), jnp.float32),
+            pltpu.VMEM((3, rows // 2, count, 2 * depth), bf16),
+            pltpu.VMEM((3, rows // 2, count, 2 * depth), jnp.float32),
+            pltpu.VMEM((6, count, depth), bf16),
+        ]
+
+    def cost(count):
+        return pl.CostEstimate(
+            flops=2 * rows * (2 * count) * 160 * depth * 4,
+            bytes_accessed=4_000_000,
+            transcendentals=0,
+        )
+
+    inner_sums, wide, narrow = pl.pallas_call(
+        functools.partial(inner_kernel, starts),
+        name="inner",
+        out_shape=(
+            pltpu.VMEM((high, 6 * LANES), jnp.float32),
+            pltpu.VMEM(wide_hbm.shape, bf16),
+            pltpu.VMEM(narrow_hbm.shape, bf16),
+        ),
+        in_specs=[vmem, vmem, stay, stay],
+        scratch_shapes=scratch(inner) + [pltpu.SemaphoreType.DMA((2,))],
+        cost_estimate=cost(inner),
+        compiler_params=params,
+    )(own, x_parts, fixed(wide_hbm), fixed(narrow_hbm))
+
     span = width + 2 * EDGE
-    window, up = pl.pallas_call(
+    window, down = pl.pallas_call(
         window_kernel,
         name="window",
         out_shape=(
@@ -550,44 +677,29 @@
             pltpu.VMEM((span, depth), bf16),
         ),
         compiler_params=params,
-    )(own, far, near)
-    below = moved(up, [((p, d), (p, d + 1)) for p in range(planes) for d in range(depths - 1)])
-
-    pieces = [*depth_bands(depth), *coarse_depth_bands(rows, depth)]
-    for side in edge_bands(rows)[::-1]:
-        for part in side:
-            pieces += halves(part)
-    bands_hbm = jnp.asarray(np.concatenate([as_bfloat16(piece) for piece in pieces]))
-    sums, edge, bands = pl.pallas_call(
-        own_kernel,
-        name="own",
+    )(own, far, near, inner_sums)
+    above = moved(down, [((p, d + 1), (p, d)) for p in range(planes) for d in range(depths - 1)])
+
+    sums, edge = pl.pallas_call(
+        functools.partial(side_kernel, starts),
+        name="side",
         out_shape=(
-            pltpu.VMEM((6, x_hbm.shape[0] - 2 * pad_x, LANES), jnp.float32),
-            pltpu.VMEM((3, pad_x, LANES), jnp.float32),
-            pltpu.VMEM(bands_hbm.shape, bf16),
+            pltpu.VMEM((high, 6 * LANES), jnp.float32),
+            pltpu.VMEM((3, inner + 2 * side, LANES), jnp.float32),
         ),
-        in_specs=[vmem, vmem, stay],
-        scratch_shapes=[
-            pltpu.VMEM((rows, 2 * pad_x, depth), jnp.float32),
-            pltpu.VMEM((3, rows, pad_x, depth), bf16),
-            pltpu.VMEM((3, rows, pad_x, depth), jnp.float32),
-            pltpu.VMEM((6, pad_x, depth), bf16),
-            pltpu.SemaphoreType.DMA((1,)),
-        ],
-        cost_estimate=pl.CostEstimate(
-            flops=4 * rows * pad_x * span * depth, bytes_accessed=4_000_000, transcendentals=0
-        ),
+        scratch_shapes=scratch(2 * side) + [pltpu.VMEM((2 * side, LANES), jnp.float32)],
+        cost_estimate=cost(2 * side),
         compiler_params=params,
-    )(window, x_parts, fixed(bands_hbm))
+    )(window, x_parts, wide, narrow, inner_sums)
 
     height = -(-(2 * (count + 2 * HALO) + 2 * GHOST) // 8) * 8
     chunks = pl.pallas_call(
-        functools.partial(edge_kernel, width),
+        functools.partial(edge_kernel, starts, width),
         name="edge",
         out_shape=pltpu.VMEM((depths, height, lanes), jnp.float32),
-        scratch_shapes=[pltpu.VMEM((6, pad_x, depth), bf16)],
+        scratch_shapes=[pltpu.VMEM((6, inner + 2 * side, depth), bf16)],
         compiler_params=params,
-    )(temp, cure, below, far, near, sums, edge, x_parts, bands)
+    )(temp, cure, above, far, near, sums, edge, x_parts, wide, narrow)
 
     chunks = lax.all_to_all(chunks, "depth", split_axis=0, concat_axis=0, tiled=True)
 
@@ -595,12 +707,18 @@
         functools.partial(cure_kernel, cells),
         name="cure",
         out_shape=(
-            jax.ShapeDtypeStruct((count, lanes), jnp.float32),
-            jax.ShapeDtypeStruct((count, lanes), jnp.float32),
-            jax.ShapeDtypeStruct((3, count, lanes), jnp.float32),
+            pltpu.HBM((count, lanes), jnp.float32),
+            pltpu.HBM((count, lanes), jnp.float32),
+            pltpu.HBM((3, count, lanes), jnp.float32),
         ),
         in_specs=[vmem, vmem, vmem, smem, smem],
-        out_specs=(vmem, vmem, vmem),
+        out_specs=(stay, stay, stay),
+        scratch_shapes=[
+            pltpu.VMEM((count, lanes), jnp.float32),
+            pltpu.VMEM((count, lanes), jnp.float32),
+            pltpu.VMEM((3, count, lanes), jnp.float32),
+            pltpu.SemaphoreType.DMA((3,)),
+        ],
         compiler_params=params,
     )(chunks, temp, cure, tool_levels, plan)
 

time: 29.1 us -> 27.9 us (0.959)
  the two profiles are of different devices: /device:TPU:4 before, /device:TPU:0 now
where the time goes in v6:
time: 27.9 us; the launch traced here: 27.6 us
  starting transfers between devices  10.3 us (37%)
  waiting for transfers between devices  8.72 us (31%)
  Pallas kernels  7.79 us (28%)
  between operations  0.7 us (3%)
    ppermute x3, starting transfers between devices, moved(): return lax.ppermute(values, ('plane', 'depth'), index)  6.32 us
    all_to_all x1, waiting for transfers between devices, on_device(): lax.all_to_all(chunks, 'depth', split_axis=0, concat_axis=0, tiled=True)  5.65 us
    all_to_all x1, starting transfers between devices, on_device(): lax.all_to_all(chunks, 'depth', split_axis=0, concat_axis=0, tiled=True)  3.99 us
    ppermute x3, waiting for transfers between devices, moved(): return lax.ppermute(values, ('plane', 'depth'), index)  3.07 us
    pallas_call x1, Pallas kernels, on_device(): pl.pallas_call(functools.partial(inner_kernel, starts), name='inner', out...  2.07 us
    pallas_call x1, Pallas kernels, on_device(): pl.pallas_call(functools.partial(side_kernel, starts), name='side', out_s...  1.52 us
    pallas_call x1, Pallas kernels, on_device(): pl.pallas_call(functools.partial(cure_kernel, cells), name='cure', out_sh...  1.46 us
    pallas_call x1, Pallas kernels, on_device(): pl.pallas_call(functools.partial(edge_kernel, starts, width), name='edge'...  1.38 us
  transfers between devices with their start and end apart: 4, of which 2 were waited for; matrix products, arithmetic and copies ran while one was open for 0% of the time, Pallas kernels for 13%

profile of v6, /device:TPU:0, one launch (start us, length us, event | category | flops | bytes accessed | tf_op | source)
XLA Modules:
  0.0 27.6 jit_solution(17993636196715569795)
XLA Ops:
  0.6 1.2 %pack.1 = (bf16[9,32,128]{2,1,0:T(8,128)(2,1)S(1)}, bf16[9,32,128]{2,1,0:T(8,128)(2,1)S(1)}, bf16[4,96,256]{2,1,0:T(8,128)(2,1)S(1)}, bf16[544,160]{1,0:T(8,128)...) custom-call(s32[8,96,128]{2,1,0:T(8,128)} %intensity.1, f32[6,128]{1,0:T(8,128)} %temp_hbm.1, f32[6,128]{1,0:T(8,128)} %cure_hbm.1, ...), custom_call_target="tpu_custom_call" | custom-call | tf_op jit(solution)/shard_map/pack/pallas_call | solution.py:608
  1.8 0.7 %collective-permute-start = (bf16[9,32,128]{2,1,0:T(8,128)(2,1)S(1)}, bf16[9,32,128]{2,1,0:T(8,128)(2,1)S(1)}, u32[]{:S(2)}, u32[]{:S(2)}) collective-permute-start(bf16[9,32,128]{2,1,0:T(8,128)(2,1)S(1)} %get-tuple-element.19), channel_id=1, source_target_pairs={{4,8},{5,9},{6,10},{7,11},{12,16},{13,17},{14,18},{15,19},{20,24},... | collective-permute-start | bytes 221192 | tf_op jit(solution)/shard_map/ppermute | solution.py:629
  2.5 4.4 %collective-permute-start.1 = (bf16[9,32,128]{2,1,0:T(8,128)(2,1)S(1)}, bf16[9,32,128]{2,1,0:T(8,128)(2,1)S(1)}, u32[]{:S(2)}, u32[]{:S(2)}) collective-permute-start(bf16[9,32,128]{2,1,0:T(8,128)(2,1)S(1)} %get-tuple-element.20), channel_id=1, source_target_pairs={{0,4},{1,5},{2,6},{3,7},{8,12},{9,13},{10,14},{11,15},{16,20},{17,... | collective-permute-start | bytes 221192 | tf_op jit(solution)/shard_map/ppermute | solution.py:629
  6.9 2.1 %inner.1 = (f32[32,768]{1,0:T(8,128)S(1)}, bf16[1024,256]{1,0:T(8,128)(2,1)S(1)}, bf16[768,128]{1,0:T(8,128)(2,1)S(1)}) custom-call(bf16[4,96,256]{2,1,0:T(8,128)(2,1)S(1)} %get-tuple-element.18.own, bf16[544,160]{1,0:T(8,128)(2,1)S(1)} %get-tuple-element.21.x_parts, bf16[1024,256]{1,0:T(8,128)(2,1)} %constant.7.clone.wide_hbm, ...), custom_call_target="tpu_custom_call" | custom-call | flops 251658240 | bytes 4000000 | tf_op jit(solution)/shard_map/inner/pallas_call | solution.py:657
  9.0 0.0 collective-permute-done.far
  9.0 0.0 collective-permute-done.1.near
  9.0 0.2 window.1
  9.1 1.3 %collective-permute-start.2 = (bf16[160,128]{1,0:T(8,128)(2,1)S(1)}, bf16[160,128]{1,0:T(8,128)(2,1)S(1)}, u32[]{:S(2)}, u32[]{:S(2)}) collective-permute-start(bf16[160,128]{1,0:T(8,128)(2,1)S(1)} %get-tuple-element.23), channel_id=1, source_target_pairs={{1,0},{2,1},{3,2},{5,4},{6,5},{7,6},{9,8},{10,9},{11,10},{13,12},{... | collective-permute-start | bytes 122888 | tf_op jit(solution)/shard_map/ppermute | solution.py:629
  10.4 1.5 %side.1 = (f32[32,768]{1,0:T(8,128)S(1)}, f32[3,144,128]{2,1,0:T(8,128)S(1)}) custom-call(bf16[4,160,256]{2,1,0:T(8,128)(2,1)S(1)} %get-tuple-element.24.window, bf16[544,160]{1,0:T(8,128)(2,1)S(1)} %get-tuple-element.21.x_parts, bf16[1024,256]{1,0:T(8,128)(2,1)S(1)} %get-tuple-element.25.wide, bf16[768,128]{1,0:T(8,128)(2,1)S(1)} %get-tuple-element.26.narrow, ...), custom_call_target="tpu_custom_call" | custom-call | flops 125829120 | bytes 4000000 | tf_op jit(solution)/shard_map/side/pallas_call | solution.py:683
  12.0 3.1 %collective-permute-done.2.above = bf16[160,128]{1,0:T(8,128)(2,1)S(1)} collective-permute-done((bf16[160,128]{1,0:T(8,128)(2,1)S(1)}, bf16[160,128]{1,0:T(8,128)(2,1)S(1)}, u32[]{:S(2)}, u32[]{:S(2)}) %collective-permute-start.2) | collective-permute-done | bytes 40992 | tf_op jit(solution)/shard_map/ppermute | solution.py:629
  15.0 1.4 %edge.1 = f32[4,32,128]{2,1,0:T(8,128)} custom-call(f32[6,128]{1,0:T(8,128)S(1)} %get-tuple-element.16.temp.temp_in, f32[6,128]{1,0:T(8,128)S(1)} %get-tuple-element.17.cure.cure_in, bf16[160,128]{1,0:T(8,128)(2,1)S(1)} %collective-permute-done.2.above, bf16[9,32,128]{2,1,0:T(8,128)(2,1)S(1)} %collective-permute-done.far, ...), custom_call_target="tpu_custom_call" | custom-call | tf_op jit(solution)/shard_map/edge/pallas_call | solution.py:696
  16.4 0.0 copy-start.1
  16.4 4.0 %all-to-all-start = ((f32[4,32,128]{2,1,0:T(8,128)}), f32[4,32,128]{2,1,0:T(8,128)S(1)}, u32[]{:S(2)}, u32[]{:S(2)}) async-start(f32[4,32,128]{2,1,0:T(8,128)} %edge.1), calls=%async_computation | async-start | bytes 131072 | tf_op jit(solution)/shard_map/all_to_all | solution.py:704
  20.4 0.0 copy-done.1
  20.4 0.0 copy-start
  20.4 0.1 copy.11.plan
  20.5 5.6 %all-to-all-done.chunks = f32[4,32,128]{2,1,0:T(8,128)S(1)} async-done(((f32[4,32,128]{2,1,0:T(8,128)}), f32[4,32,128]{2,1,0:T(8,128)S(1)}, u32[]{:S(2)}, u32[]{:S(2)}) %all-to-all-start) | async-done | bytes 65568 | tf_op jit(solution)/shard_map/all_to_all | solution.py:704
  26.2 0.0 copy-done
  26.2 1.5 %cure.1 = (f32[6,128]{1,0:T(8,128)}, f32[6,128]{1,0:T(8,128)}, f32[3,6,128]{2,1,0:T(8,128)}) custom-call(f32[4,32,128]{2,1,0:T(8,128)S(1)} %all-to-all-done.chunks, f32[6,128]{1,0:T(8,128)S(1)} %get-tuple-element.16.temp.temp_in, f32[6,128]{1,0:T(8,128)S(1)} %get-tuple-element.17.cure.cure_in, f32[8]{0:T(128)S(1)} %copy-done, s32[3,2]{1,0:T(4,128)S(1)} %copy.11.plan), custom_call_target="tpu_custom_call" | custom-call | tf_op jit(solution)/shard_map/cure/pallas_call | solution.py:706
Async XLA Ops:
  1.8 7.1 %collective-permute-start = (bf16[9,32,128]{2,1,0:T(8,128)(2,1)S(1)}, bf16[9,32,128]{2,1,0:T(8,128)(2,1)S(1)}, u32[]{:S(2)}, u32[]{:S(2)}) collective-permute-start(bf16[9,32,128]{2,1,0:T(8,128)(2,1)S(1)} %get-tuple-element.19), channel_id=1, source_target_pairs={{4,8},{5,9},{6,10},{7,11},{12,16},{13,17},{14,18},{15,19},{20,24},... | collective-permute-start | bytes 221192 | tf_op jit(solution)/shard_map/ppermute | solution.py:629
  2.5 6.5 %collective-permute-start.1 = (bf16[9,32,128]{2,1,0:T(8,128)(2,1)S(1)}, bf16[9,32,128]{2,1,0:T(8,128)(2,1)S(1)}, u32[]{:S(2)}, u32[]{:S(2)}) collective-permute-start(bf16[9,32,128]{2,1,0:T(8,128)(2,1)S(1)} %get-tuple-element.20), channel_id=1, source_target_pairs={{0,4},{1,5},{2,6},{3,7},{8,12},{9,13},{10,14},{11,15},{16,20},{17,... | collective-permute-start | bytes 221192 | tf_op jit(solution)/shard_map/ppermute | solution.py:629
  9.1 5.9 %collective-permute-start.2 = (bf16[160,128]{1,0:T(8,128)(2,1)S(1)}, bf16[160,128]{1,0:T(8,128)(2,1)S(1)}, u32[]{:S(2)}, u32[]{:S(2)}) collective-permute-start(bf16[160,128]{1,0:T(8,128)(2,1)S(1)} %get-tuple-element.23), channel_id=1, source_target_pairs={{1,0},{2,1},{3,2},{5,4},{6,5},{7,6},{9,8},{10,9},{11,10},{13,12},{... | collective-permute-start | bytes 122888 | tf_op jit(solution)/shard_map/ppermute | solution.py:629
  16.4 4.0 %copy-start.1 = (s32[3,2]{0,1:T(2,128)S(1)}, s32[3,2]{0,1:T(2,128)}, u32[]{:S(2)}) copy-start(s32[3,2]{0,1:T(2,128)} %param.12) | copy-start | bytes 76
  16.4 9.7 %all-to-all-start = ((f32[4,32,128]{2,1,0:T(8,128)}), f32[4,32,128]{2,1,0:T(8,128)S(1)}, u32[]{:S(2)}, u32[]{:S(2)}) async-start(f32[4,32,128]{2,1,0:T(8,128)} %edge.1), calls=%async_computation | async-start | bytes 131072 | tf_op jit(solution)/shard_map/all_to_all | solution.py:704
  20.4 5.7 %copy-start = (f32[8]{0:T(128)S(1)}, f32[8]{0:T(128)}, u32[]{:S(2)}) copy-start(f32[8]{0:T(128)} %levels.1) | copy-start | bytes 100

commit v7 on v6

--- a/solution.py
+++ b/solution.py
@@ -28,9 +28,10 @@
 reference_temp = 4.2
 tensor_eps = 1e-06
 
-EDGE = 32
 LANES = 128
 HALO = 2
+EDGE = HALO * COARSE + R1 + R2
+EARLY = 48
 GHOST = 3
 PACK = 16
 BACK = 8
@@ -87,16 +88,12 @@
 def sizes(width, depth):
     columns = width // COARSE + 2 * HALO
     cells = depth // COARSE + BEFORE + AFTER
-    side = HALO * COARSE + R2 + R1
-    inner = -(-(width - 2 * R1) // 16) * 16
-    return columns, cells, side, inner
+    return columns, cells
 
 
 def product_rows(width):
-    columns, cells, side, inner = sizes(width, 0)
-    places = [R1 + i if R1 + i < width - R1 else None for i in range(inner)]
-    places += [R1 - side + i for i in range(side)] + [width - R1 + i for i in range(side)]
-    return places
+    places = [*range(R1, width - R1), *range(R1 - EDGE, R1), *range(width - R1, width + EDGE - R1)]
+    return places + [None] * (-len(places) % 16)
 
 
 GRAD_TAPS = tuple(
@@ -157,7 +154,7 @@
 def coarse_depth_bands(rows, depth):
     taps = smooth_taps(R2, sigma_tensor)
     weights = product_weights(rows)
-    columns, cells, side, inner = sizes(0, depth)
+    columns, cells = sizes(0, depth)
     bands = np.zeros((2, depth, LANES))
     for cell in range(cells):
         for voxel in range(COARSE):
@@ -176,7 +173,7 @@
 def coarse_x_bands(width):
     taps = smooth_taps(R2, sigma_tensor)
     places = product_rows(width)
-    columns, cells, side, inner = sizes(width, 0)
+    columns, cells = sizes(width, 0)
     bands = np.zeros((-(-columns // 16) * 16, len(places)))
     for column in range(columns):
         for voxel in range(COARSE):
@@ -188,14 +185,13 @@
 
 
 def x_constants(width):
-    columns, cells, side, inner = sizes(width, 0)
     bands, coarse = x_bands(width), coarse_x_bands(width)
     pieces = [
-        bands[:, :inner].reshape(2 * inner, -1),
-        bands[:, inner:].reshape(4 * side, -1),
-        bands[:, :inner, EDGE : EDGE + width].reshape(2 * inner, -1),
+        bands[:, :EARLY].reshape(2 * EARLY, -1),
+        bands[:, EARLY:].reshape(2 * (bands.shape[1] - EARLY), -1),
+        bands[:, :EARLY, EDGE : EDGE + width].reshape(2 * EARLY, -1),
         coarse,
-        coarse[:, inner:],
+        coarse[:, EARLY:],
     ]
     widest = max(piece.shape[1] for piece in pieces)
     padded = [np.pad(piece, ((0, 0), (0, widest - piece.shape[1]))) for piece in pieces]
@@ -248,12 +244,15 @@
     sides = (column_slot(temp, cure, 0), column_slot(temp, cure, count - GHOST))
 
     def send(left, right):
-        for row in range(rows):
-            left[row] = grey[row, :EDGE, :].astype(jnp.float32).astype(jnp.bfloat16)
-            right[row] = grey[row, width - EDGE :, :].astype(jnp.float32).astype(jnp.bfloat16)
+        for place, target in ((0, left), (width - EDGE, right)):
+            for pair in range(rows // 2):
+                two = [grey[2 * pair + i, place : place + EDGE, :] for i in range(2)]
+                two = jnp.concatenate(two, axis=0).astype(jnp.float32)
+                target[2 * EDGE * pair : 2 * EDGE * (pair + 1), :] = two.astype(jnp.bfloat16)
         for slot in range(temp.shape[1] // LANES):
-            left[rows + slot] = sides[0][:, slot * LANES : (slot + 1) * LANES]
-            right[rows + slot] = sides[1][:, slot * LANES : (slot + 1) * LANES]
+            at = rows * EDGE + 32 * slot
+            left[at : at + 32, :] = sides[0][:, slot * LANES : (slot + 1) * LANES]
+            right[at : at + 32, :] = sides[1][:, slot * LANES : (slot + 1) * LANES]
 
     @pl.when(odd)
     def _():
@@ -279,19 +278,26 @@
     return packed
 
 
-def window_kernel(own, far, near, inner_sums, window, down):
+def window_kernel(own, far, near, early_sums, window, down):
     pairs, width, double = own.shape
     rows, depth = 2 * pairs, double // 2
     odd = is_odd()
 
+    def edges_of(ref):
+        two = [
+            ref[2 * EDGE * pair : 2 * EDGE * (pair + 1), :].astype(jnp.float32)
+            for pair in range(pairs)
+        ]
+        return [two[row // 2][row % 2 * EDGE : (row % 2 + 1) * EDGE] for row in range(rows)]
+
     def fill(from_left, from_right):
-        values = []
+        lefts, rights, values = edges_of(from_left), edges_of(from_right), []
         for row in range(rows):
             half = (row % 2) * depth
-            middle = own[row // 2, :, half : half + depth]
-            whole = jnp.concatenate([from_left[row], middle, from_right[row]], axis=0)
-            window[row // 2, :, half : half + depth] = whole
-            values.append(whole.astype(jnp.float32))
+            middle = own[row // 2, :, half : half + depth].astype(jnp.float32)
+            whole = jnp.concatenate([lefts[row], middle, rights[row]], axis=0)
+            window[row // 2, :, half : half + depth] = whole.astype(jnp.bfloat16)
+            values.append(whole)
         down[...] = packed_rows(values, PACK, 0).astype(jnp.bfloat16)
 
     @pl.when(odd)
@@ -304,8 +310,9 @@
 
 
 def joined_columns(ref, rows):
-    slots = [ref[slot].astype(jnp.float32) for slot in range(rows, ref.shape[0])]
-    parts = jnp.concatenate(slots, axis=1)
+    slots = range(rows * EDGE, ref.shape[0], 32)
+    parts = [ref[at : at + 32, :].astype(jnp.float32) for at in slots]
+    parts = jnp.concatenate(parts, axis=1)
     return (parts[0:8] + parts[8:16]) + parts[16:24]
 
 
@@ -328,12 +335,13 @@
     return [first[a] * three[b] for a, b in pairs]
 
 
-def side_mask(side, width):
-    row = lax.broadcasted_iota(jnp.int32, (2 * side, LANES), 0)
-    place = jnp.where(row < side, row + R1 - side, row + width - R1 - side)
+def late_mask(count, width):
+    row = lax.broadcasted_iota(jnp.int32, (count, LANES), 0)
+    left = width - 2 * R1 - EARLY
+    place = jnp.where(row < left + EDGE, row - left + R1 - EDGE, row - left - EDGE + width - R1)
     place = place + lax.axis_index("plane") * width
     inside = (place >= 0) & (place < lax.axis_size("plane") * width)
-    return jnp.where(inside, 1.0, 0.0)
+    return jnp.where(inside | (row < left), 1.0, 0.0)
 
 
 def all_sums(products, coarse, sx):
@@ -395,7 +403,7 @@
     return all_sums(products, narrow[0:depth, :], sx)
 
 
-def inner_kernel(
+def early_kernel(
     starts, own, x_parts, wide_hbm, narrow_hbm, sums, wide, narrow, across, filtered, grads,
     products, sems,
 ):
@@ -418,17 +426,17 @@
     )
 
 
-def side_kernel(
-    starts, window, x_parts, wide, narrow, inner_sums, sums, edge, across, filtered, grads,
+def late_kernel(
+    starts, window, x_parts, wide, narrow, early_sums, sums, edge, across, filtered, grads,
     products, mask,
 ):
     pairs, height, double = window.shape
     rows, depth = 2 * pairs, double // 2
     count = across.shape[1] // 2
-    mask[...] = side_mask(count // 2, height - 2 * EDGE)
-    bands = x_parts[starts[1] : starts[2], :]
+    mask[...] = late_mask(count, height - 2 * EDGE)
+    bands = x_parts[starts[1] : starts[2], :height]
     sx = x_parts[starts[4] : starts[5], :count]
-    sums[...] = inner_sums[...] + tensor_sums(
+    sums[...] = early_sums[...] + tensor_sums(
         window, bands, sx, mask, lambda: None, wide, narrow, across, filtered, grads, products
     )
     values = [
@@ -442,7 +450,7 @@
 
 
 def edge_gradients(starts, packed, x_parts, wide, narrow, side):
-    result = product(x_parts[: starts[2], :], packed).astype(jnp.bfloat16)
+    result = product(x_parts[: starts[2], : packed.shape[0]], packed).astype(jnp.bfloat16)
     inner, outer = starts[1] // 2, (starts[2] - starts[1]) // 2
     kinds = []
     for kind in range(2):
@@ -463,13 +471,12 @@
     kinds, pad_x, depth = edge.shape
     rows = depth // PACK
     depths, layer = lax.axis_size("depth"), lax.axis_index("depth")
-    side = (starts[2] - starts[1]) // 4
     results = edge_gradients(starts, above[...], x_parts, wide, narrow, 1)
     three = [edge[part] + results[part] for part in range(3)]
     place = lax.rem(lax.broadcasted_iota(jnp.int32, (pad_x, LANES), 1), PACK) - BACK
     inside = jnp.where((place < 0) | (layer < depths - 1), 1.0, 0.0)
-    inner = jnp.ones((pad_x - 2 * side, LANES), jnp.float32)
-    inside = inside * jnp.concatenate([inner, side_mask(side, width)], axis=0)
+    mask = [jnp.ones((EARLY, LANES), jnp.float32), late_mask(pad_x - EARLY, width)]
+    inside = inside * jnp.concatenate(mask, axis=0)
     for index, term in enumerate(weighted_products(three, inside)):
         products[index] = term.astype(jnp.bfloat16)
     sx = x_parts[starts[3] : starts[4], :pad_x]
@@ -512,7 +519,7 @@
 
 
 def cure_kernel(
-    cells, chunks, temp_in, cure_in, levels, plan, temp_hbm, cure_hbm, conduct_hbm, temp_out,
+    cells, chunks, temp_in, cure_in, tools, temp_hbm, cure_hbm, conduct_hbm, temp_out,
     cure_out, conduct_out, sems,
 ):
     count, lanes = temp_in.shape
@@ -561,7 +568,7 @@
     first = (plane == 0) & (layer == 0)
     last = (plane == planes - 1) & (layer == depths - 1)
     for step in range(STEPS):
-        top, bottom = levels[plan[step, 0]], levels[plan[step, 1]]
+        top, bottom = tools[2 * step : 2 * step + 1, :], tools[2 * step + 1 : 2 * step + 2, :]
         temp = jnp.where((row < GHOST) & first, temp[GHOST : GHOST + 1], temp)
         temp = jnp.where(
             (row >= GHOST + count) & last, temp[GHOST + count - 1 : GHOST + count], temp
@@ -593,12 +600,11 @@
     rows, width, depth = intensity.shape
     count, lanes = temp_start.shape
     planes, depths = lax.axis_size("plane"), lax.axis_size("depth")
-    columns, cells, side, inner = sizes(width, depth)
+    columns, cells = sizes(width, depth)
     bf16 = jnp.bfloat16
-    slots = rows + lanes // LANES
+    slots = rows * EDGE + 32 * (lanes // LANES)
     params = pltpu.CompilerParams(vmem_limit_bytes=24 * 1024 * 1024)
     vmem = pl.BlockSpec(memory_space=pltpu.VMEM)
-    smem = pl.BlockSpec(memory_space=pltpu.SMEM)
     stay = pl.BlockSpec(memory_space=pltpu.HBM)
 
     fixed = lambda values: pltpu.with_memory_space_constraint(values, pltpu.HBM)
@@ -609,8 +615,8 @@
         pack_kernel,
         name="pack",
         out_shape=(
-            pltpu.VMEM((slots, EDGE, depth), bf16),
-            pltpu.VMEM((slots, EDGE, depth), bf16),
+            pltpu.VMEM((slots, depth), bf16),
+            pltpu.VMEM((slots, depth), bf16),
             pltpu.VMEM((rows // 2, width, 2 * depth), bf16),
             pltpu.VMEM(x_hbm.shape, bf16),
             pltpu.VMEM((count, lanes), jnp.float32),
@@ -638,6 +644,7 @@
 
     wide_hbm, narrow_hbm = [jnp.asarray(values) for values in depth_constants(rows, depth)]
     high = starts[4] - starts[3]
+    late = (starts[2] - starts[1]) // 2
 
     def scratch(count):
         return [
@@ -654,17 +661,17 @@
             transcendentals=0,
         )
 
-    inner_sums, wide, narrow = pl.pallas_call(
-        functools.partial(inner_kernel, starts),
-        name="inner",
+    early_sums, wide, narrow = pl.pallas_call(
+        functools.partial(early_kernel, starts),
+        name="early",
         out_shape=(
             pltpu.VMEM((high, 6 * LANES), jnp.float32),
             pltpu.VMEM(wide_hbm.shape, bf16),
             pltpu.VMEM(narrow_hbm.shape, bf16),
         ),
         in_specs=[vmem, vmem, stay, stay],
-        scratch_shapes=scratch(inner) + [pltpu.SemaphoreType.DMA((2,))],
-        cost_estimate=cost(inner),
+        scratch_shapes=scratch(EARLY) + [pltpu.SemaphoreType.DMA((2,))],
+        cost_estimate=cost(EARLY),
         compiler_params=params,
     )(own, x_parts, fixed(wide_hbm), fixed(narrow_hbm))
 
@@ -677,29 +684,33 @@
             pltpu.VMEM((span, depth), bf16),
         ),
         compiler_params=params,
-    )(own, far, near, inner_sums)
+    )(own, far, near, early_sums)
     above = moved(down, [((p, d + 1), (p, d)) for p in range(planes) for d in range(depths - 1)])
 
     sums, edge = pl.pallas_call(
-        functools.partial(side_kernel, starts),
-        name="side",
+        functools.partial(late_kernel, starts),
+        name="late",
         out_shape=(
             pltpu.VMEM((high, 6 * LANES), jnp.float32),
-            pltpu.VMEM((3, inner + 2 * side, LANES), jnp.float32),
+            pltpu.VMEM((3, EARLY + late, LANES), jnp.float32),
         ),
-        scratch_shapes=scratch(2 * side) + [pltpu.VMEM((2 * side, LANES), jnp.float32)],
-        cost_estimate=cost(2 * side),
+        scratch_shapes=scratch(late) + [pltpu.VMEM((late, LANES), jnp.float32)],
+        cost_estimate=cost(late),
         compiler_params=params,
-    )(window, x_parts, wide, narrow, inner_sums)
+    )(window, x_parts, wide, narrow, early_sums)
 
     height = -(-(2 * (count + 2 * HALO) + 2 * GHOST) // 8) * 8
     chunks = pl.pallas_call(
         functools.partial(edge_kernel, starts, width),
         name="edge",
         out_shape=pltpu.VMEM((depths, height, lanes), jnp.float32),
-        scratch_shapes=[pltpu.VMEM((6, inner + 2 * side, depth), bf16)],
+        scratch_shapes=[pltpu.VMEM((6, EARLY + late, depth), bf16)],
         compiler_params=params,
     )(temp, cure, above, far, near, sums, edge, x_parts, wide, narrow)
+
+    faces = plan.reshape(2 * STEPS, 1) == jnp.arange(tool_levels.shape[0], dtype=jnp.int32)
+    tools = jnp.sum(jnp.where(faces, tool_levels, jnp.zeros_like(tool_levels)), axis=1)
+    tools = jnp.broadcast_to(tools[:, None], (2 * STEPS, lanes))
 
     chunks = lax.all_to_all(chunks, "depth", split_axis=0, concat_axis=0, tiled=True)
 
@@ -711,7 +722,7 @@
             pltpu.HBM((count, lanes), jnp.float32),
             pltpu.HBM((3, count, lanes), jnp.float32),
         ),
-        in_specs=[vmem, vmem, vmem, smem, smem],
+        in_specs=[vmem, vmem, vmem, vmem],
         out_specs=(stay, stay, stay),
         scratch_shapes=[
             pltpu.VMEM((count, lanes), jnp.float32),
@@ -720,7 +731,7 @@
             pltpu.SemaphoreType.DMA((3,)),
         ],
         compiler_params=params,
-    )(chunks, temp, cure, tool_levels, plan)
+    )(chunks, temp, cure, tools)
 
 
 def solution(mesh):

time: 27.9 us -> 27.2 us (0.975)
  waiting for transfers between devices: 8.72 us -> 7.9 us
    ppermute x3, waiting for transfers between devices: 3.07 us -> 2.34 us  [moved(): return lax.ppermute(values, ('plane', 'depth'), index)]
    pallas_call x1, Pallas kernels: 1.46 us -> 0.89 us  [on_device(): pl.pallas_call(functools.partial(cure_kernel, cells), name='cure', out_sh...]
    pallas_call x3, Pallas kernels: 4.79 us -> 5.1 us  [the longest x1 2.02 us: on_device(): pl.pallas_call(functools.partial(late_kernel, starts), name='late', out_s...]
  transfers between devices with their start and end apart: 4 -> 4, of which waited for: 2 -> 2; matrix products, arithmetic and copies ran while one was open for 0% -> 1% of each run, Pallas kernels for 13% -> 15%
where the time goes in v7:
time: 27.2 us; the launch traced here: 26.9 us
  starting transfers between devices  10.3 us (38%)
  waiting for transfers between devices  7.9 us (29%)
  Pallas kernels  7.54 us (28%)
  between operations  0.72 us (3%)
    ppermute x3, starting transfers between devices, moved(): return lax.ppermute(values, ('plane', 'depth'), index)  6.32 us
    all_to_all x1, waiting for transfers between devices, on_device(): lax.all_to_all(chunks, 'depth', split_axis=0, concat_axis=0, tiled=True)  5.56 us
    all_to_all x1, starting transfers between devices, on_device(): lax.all_to_all(chunks, 'depth', split_axis=0, concat_axis=0, tiled=True)  3.99 us
    ppermute x3, waiting for transfers between devices, moved(): return lax.ppermute(values, ('plane', 'depth'), index)  2.34 us
    pallas_call x1, Pallas kernels, on_device(): pl.pallas_call(functools.partial(late_kernel, starts), name='late', out_s...  2.02 us
    pallas_call x1, Pallas kernels, on_device(): pl.pallas_call(functools.partial(early_kernel, starts), name='early', out...  1.9 us
    pallas_call x1, Pallas kernels, on_device(): pl.pallas_call(functools.partial(edge_kernel, starts, width), name='edge'...  1.4 us
    pallas_call x1, Pallas kernels, on_device(): pl.pallas_call(pack_kernel, name='pack', out_shape=(pltpu.VMEM((slots, de...  1.18 us
  transfers between devices with their start and end apart: 4, of which 2 were waited for; matrix products, arithmetic and copies ran while one was open for 1% of the time, Pallas kernels for 15%

profile of v7, /device:TPU:0, one launch (start us, length us, event | category | flops | bytes accessed | tf_op | source)
XLA Modules:
  0.0 26.9 jit_solution(6592394152561749773)
XLA Ops:
  0.6 1.2 %pack.1 = (bf16[224,128]{1,0:T(8,128)(2,1)S(1)}, bf16[224,128]{1,0:T(8,128)(2,1)S(1)}, bf16[4,96,256]{2,1,0:T(8,128)(2,1)S(1)}, bf16[448,144]{1,0:T(8,128)(2,1)S...) custom-call(s32[8,96,128]{2,1,0:T(8,128)} %intensity.1, f32[6,128]{1,0:T(8,128)} %temp_hbm.1, f32[6,128]{1,0:T(8,128)} %cure_hbm.1, ...), custom_call_target="tpu_custom_call" | custom-call | tf_op jit(solution)/shard_map/pack/pallas_call | solution.py:614
  1.8 0.7 %collective-permute-start = (bf16[224,128]{1,0:T(8,128)(2,1)S(1)}, bf16[224,128]{1,0:T(8,128)(2,1)S(1)}, u32[]{:S(2)}, u32[]{:S(2)}) collective-permute-start(bf16[224,128]{1,0:T(8,128)(2,1)S(1)} %get-tuple-element.19), channel_id=1, source_target_pairs={{4,8},{5,9},{6,10},{7,11},{12,16},{13,17},{14,18},{15,19},{20,24},... | collective-permute-start | bytes 172040 | tf_op jit(solution)/shard_map/ppermute | solution.py:635
  2.5 4.4 %collective-permute-start.1 = (bf16[224,128]{1,0:T(8,128)(2,1)S(1)}, bf16[224,128]{1,0:T(8,128)(2,1)S(1)}, u32[]{:S(2)}, u32[]{:S(2)}) collective-permute-start(bf16[224,128]{1,0:T(8,128)(2,1)S(1)} %get-tuple-element.20), channel_id=1, source_target_pairs={{0,4},{1,5},{2,6},{3,7},{8,12},{9,13},{10,14},{11,15},{16,20},{17,... | collective-permute-start | bytes 172040 | tf_op jit(solution)/shard_map/ppermute | solution.py:635
  6.8 1.9 %early.1 = (f32[32,768]{1,0:T(8,128)S(1)}, bf16[1024,256]{1,0:T(8,128)(2,1)S(1)}, bf16[768,128]{1,0:T(8,128)(2,1)S(1)}) custom-call(bf16[4,96,256]{2,1,0:T(8,128)(2,1)S(1)} %get-tuple-element.18.own, bf16[448,144]{1,0:T(8,128)(2,1)S(1)} %get-tuple-element.21.x_parts, bf16[1024,256]{1,0:T(8,128)(2,1)} %constant.10.clone.wide_hbm, ...), custom_call_target="tpu_custom_call" | custom-call | flops 125829120 | bytes 4000000 | tf_op jit(solution)/shard_map/early/pallas_call | solution.py:664
  8.8 0.0 collective-permute-done.far
  8.8 0.0 collective-permute-done.1.near
  8.8 0.2 window.1
  8.9 0.0 copy-start
  9.0 1.3 %collective-permute-start.2 = (bf16[144,128]{1,0:T(8,128)(2,1)S(1)}, bf16[144,128]{1,0:T(8,128)(2,1)S(1)}, u32[]{:S(2)}, u32[]{:S(2)}) collective-permute-start(bf16[144,128]{1,0:T(8,128)(2,1)S(1)} %get-tuple-element.23), channel_id=1, source_target_pairs={{1,0},{2,1},{3,2},{5,4},{6,5},{7,6},{9,8},{10,9},{11,10},{13,12},{... | collective-permute-start | bytes 110600 | tf_op jit(solution)/shard_map/ppermute | solution.py:635
  10.3 0.0 copy-done
  10.3 0.1 copy.13
  10.4 0.1 eq.15
  10.4 2.0 %late.1 = (f32[32,768]{1,0:T(8,128)S(1)}, f32[3,144,128]{2,1,0:T(8,128)S(1)}) custom-call(bf16[4,144,256]{2,1,0:T(8,128)(2,1)S(1)} %get-tuple-element.24.window, bf16[448,144]{1,0:T(8,128)(2,1)S(1)} %get-tuple-element.21.x_parts, bf16[1024,256]{1,0:T(8,128)(2,1)S(1)} %get-tuple-element.25.wide, bf16[768,128]{1,0:T(8,128)(2,1)S(1)} %get-tuple-element.26.narrow, ...), custom_call_target="tpu_custom_call" | custom-call | flops 251658240 | bytes 4000000 | tf_op jit(solution)/shard_map/late/pallas_call | solution.py:690
  12.5 2.3 %collective-permute-done.2.above = bf16[144,128]{1,0:T(8,128)(2,1)S(1)} collective-permute-done((bf16[144,128]{1,0:T(8,128)(2,1)S(1)}, bf16[144,128]{1,0:T(8,128)(2,1)S(1)}, u32[]{:S(2)}, u32[]{:S(2)}) %collective-permute-start.2) | collective-permute-done | bytes 36896 | tf_op jit(solution)/shard_map/ppermute | solution.py:635
  14.8 1.4 %edge.1 = f32[4,32,128]{2,1,0:T(8,128)} custom-call(f32[6,128]{1,0:T(8,128)S(1)} %get-tuple-element.16.temp.temp_in, f32[6,128]{1,0:T(8,128)S(1)} %get-tuple-element.17.cure.cure_in, bf16[144,128]{1,0:T(8,128)(2,1)S(1)} %collective-permute-done.2.above, bf16[224,128]{1,0:T(8,128)(2,1)S(1)} %collective-permute-done.far, ...), custom_call_target="tpu_custom_call" | custom-call | tf_op jit(solution)/shard_map/edge/pallas_call | solution.py:703
  16.2 0.0 copy-start.1
  16.2 4.0 %all-to-all-start = ((f32[4,32,128]{2,1,0:T(8,128)}), f32[4,32,128]{2,1,0:T(8,128)S(1)}, u32[]{:S(2)}, u32[]{:S(2)}) async-start(f32[4,32,128]{2,1,0:T(8,128)} %edge.1), calls=%async_computation | async-start | bytes 131072 | tf_op jit(solution)/shard_map/all_to_all | solution.py:715
  20.2 0.0 copy-done.1
  20.2 0.2 select_reduce_fusion
  20.4 5.6 %all-to-all-done.chunks = f32[4,32,128]{2,1,0:T(8,128)S(1)} async-done(((f32[4,32,128]{2,1,0:T(8,128)}), f32[4,32,128]{2,1,0:T(8,128)S(1)}, u32[]{:S(2)}, u32[]{:S(2)}) %all-to-all-start) | async-done | bytes 65568 | tf_op jit(solution)/shard_map/all_to_all | solution.py:715
  25.9 0.1 broadcast_in_dim.17.tools
  26.0 0.9 %cure.1 = (f32[6,128]{1,0:T(8,128)}, f32[6,128]{1,0:T(8,128)}, f32[3,6,128]{2,1,0:T(8,128)}) custom-call(f32[4,32,128]{2,1,0:T(8,128)S(1)} %all-to-all-done.chunks, f32[6,128]{1,0:T(8,128)S(1)} %get-tuple-element.16.temp.temp_in, f32[6,128]{1,0:T(8,128)S(1)} %get-tuple-element.17.cure.cure_in, f32[6,128]{1,0:T(8,128)S(1)} %broadcast_in_dim.17.tools), custom_call_target="tpu_custom_call" | custom-call | tf_op jit(solution)/shard_map/cure/pallas_call | solution.py:717
Async XLA Ops:
  1.8 6.9 %collective-permute-start = (bf16[224,128]{1,0:T(8,128)(2,1)S(1)}, bf16[224,128]{1,0:T(8,128)(2,1)S(1)}, u32[]{:S(2)}, u32[]{:S(2)}) collective-permute-start(bf16[224,128]{1,0:T(8,128)(2,1)S(1)} %get-tuple-element.19), channel_id=1, source_target_pairs={{4,8},{5,9},{6,10},{7,11},{12,16},{13,17},{14,18},{15,19},{20,24},... | collective-permute-start | bytes 172040 | tf_op jit(solution)/shard_map/ppermute | solution.py:635
  2.5 6.3 %collective-permute-start.1 = (bf16[224,128]{1,0:T(8,128)(2,1)S(1)}, bf16[224,128]{1,0:T(8,128)(2,1)S(1)}, u32[]{:S(2)}, u32[]{:S(2)}) collective-permute-start(bf16[224,128]{1,0:T(8,128)(2,1)S(1)} %get-tuple-element.20), channel_id=1, source_target_pairs={{0,4},{1,5},{2,6},{3,7},{8,12},{9,13},{10,14},{11,15},{16,20},{17,... | collective-permute-start | bytes 172040 | tf_op jit(solution)/shard_map/ppermute | solution.py:635
  8.9 1.3 %copy-start = (s32[3,2]{0,1:T(2,128)S(1)}, s32[3,2]{0,1:T(2,128)}, u32[]{:S(2)}) copy-start(s32[3,2]{0,1:T(2,128)} %param.12) | copy-start | bytes 76
  9.0 5.9 %collective-permute-start.2 = (bf16[144,128]{1,0:T(8,128)(2,1)S(1)}, bf16[144,128]{1,0:T(8,128)(2,1)S(1)}, u32[]{:S(2)}, u32[]{:S(2)}) collective-permute-start(bf16[144,128]{1,0:T(8,128)(2,1)S(1)} %get-tuple-element.23), channel_id=1, source_target_pairs={{1,0},{2,1},{3,2},{5,4},{6,5},{7,6},{9,8},{10,9},{11,10},{13,12},{... | collective-permute-start | bytes 110600 | tf_op jit(solution)/shard_map/ppermute | solution.py:635
  16.2 4.0 %copy-start.1 = (f32[8]{0:T(128)S(1)}, f32[8]{0:T(128)}, u32[]{:S(2)}) copy-start(f32[8]{0:T(128)} %param.11) | copy-start | bytes 100
  16.2 9.7 %all-to-all-start = ((f32[4,32,128]{2,1,0:T(8,128)}), f32[4,32,128]{2,1,0:T(8,128)S(1)}, u32[]{:S(2)}, u32[]{:S(2)}) async-start(f32[4,32,128]{2,1,0:T(8,128)} %edge.1), calls=%async_computation | async-start | bytes 131072 | tf_op jit(solution)/shard_map/all_to_all | solution.py:715

commit v8 on v7

--- a/solution.py
+++ b/solution.py
@@ -138,12 +138,11 @@
 
 
 def depth_bands(depth):
-    bands = np.zeros((2, 2 * depth, 2 * depth))
+    bands = np.zeros((2, depth, depth))
     for kind in range(2):
         for place in range(depth):
             for near in range(max(place - R1, 0), min(place + R1 + 1, depth)):
-                value = tap(grad_taps(kind), near - place)
-                bands[kind, near, place] = bands[kind, depth + near, depth + place] = value
+                bands[kind, near, place] = tap(grad_taps(kind), near - place)
     return bands
 
 
@@ -199,11 +198,11 @@
 
 
 def depth_constants(rows, depth):
+    own = [*depth_bands(depth), *coarse_depth_bands(rows, depth)]
     above = [[np.concatenate(halves(part)) for part in side] for side in edge_bands(rows, depth)]
-    wide = [*depth_bands(depth)]
-    wide += [np.concatenate([side[0], side[2]], axis=1) for side in above]
-    narrow = [*coarse_depth_bands(rows, depth)] + [side[1] for side in above]
-    return [np.concatenate([as_bfloat16(piece) for piece in pieces]) for pieces in (wide, narrow)]
+    wide = [np.concatenate([side[0], side[2]], axis=1) for side in above]
+    narrow = [side[1] for side in above]
+    return [as_bfloat16(np.concatenate(pieces)) for pieces in (own, wide, narrow)]
 
 
 def three_parts(values):
@@ -226,7 +225,8 @@
 
 
 def pack_kernel(
-    intensity, temp_hbm, cure_hbm, x_hbm, far, near, own, x_parts, temp, cure, grey, sems
+    intensity, temp_hbm, cure_hbm, x_hbm, z_hbm, far, near, own, x_parts, z_parts, temp, cure,
+    grey, sems,
 ):
     rows, width, depth = intensity.shape
     copies = [
@@ -234,6 +234,7 @@
         pltpu.make_async_copy(temp_hbm, temp, sems.at[1]),
         pltpu.make_async_copy(cure_hbm, cure, sems.at[2]),
         pltpu.make_async_copy(x_hbm, x_parts, sems.at[3]),
+        pltpu.make_async_copy(z_hbm, z_parts, sems.at[4]),
     ]
     for copy in copies:
         copy.start()
@@ -346,12 +347,13 @@
 
 def all_sums(products, coarse, sx):
     kinds, count, lanes = products.shape
-    along = product(products[...].reshape(kinds * count, lanes), coarse).astype(jnp.bfloat16)
-    parts = [along[index * count : (index + 1) * count] for index in range(kinds)]
-    return product(sx, jnp.concatenate(parts, axis=1))
-
-
-def tensor_sums(window, bands, sx, mask, ready, wide, narrow, across, filtered, grads, products):
+    side_by_side = jnp.concatenate([products[index] for index in range(kinds)], axis=1)
+    along = product(sx, side_by_side).astype(jnp.bfloat16)
+    parts = [along[:, index * lanes : (index + 1) * lanes] for index in range(kinds)]
+    return product(jnp.concatenate(parts, axis=0), coarse)
+
+
+def tensor_sums(window, bands, sx, mask, diagonal, z_parts, across, filtered, grads, products):
     pairs, height, double = window.shape
     rows, depth = 2 * pairs, double // 2
     count = bands.shape[0] // 2
@@ -375,11 +377,10 @@
         return carry
 
     lax.fori_loop(0, count // 16, filter_rows, 0)
-    ready()
     for part in range(3):
         at = DEPTH_KINDS[part] * double
         for pair in range(pairs):
-            grads[part, pair] = product(filtered[part, pair], wide[at : at + double, :])
+            grads[part, pair] = product(filtered[part, pair], diagonal[at : at + double, :])
 
     weights = product_weights(rows)
     first = lax.axis_index("depth") == 0
@@ -400,50 +401,54 @@
         return carry
 
     lax.fori_loop(0, count // 16, multiply, 0)
-    return all_sums(products, narrow[0:depth, :], sx)
+    return all_sums(products, z_parts[double : double + depth, :], sx)
 
 
 def early_kernel(
-    starts, own, x_parts, wide_hbm, narrow_hbm, sums, wide, narrow, across, filtered, grads,
-    products, sems,
+    starts, own, x_parts, z_parts, sums, diagonal, across, filtered, grads, products
 ):
+    pairs, width, double = own.shape
+    depth = double // 2
+    empty = jnp.zeros((depth, depth), jnp.bfloat16)
+    for kind in range(2):
+        for half in range(2):
+            at = pl.ds(kind * double + half * depth, depth)
+            band = z_parts[kind * depth : (kind + 1) * depth, :]
+            diagonal[at, half * depth : (half + 1) * depth] = band
+            diagonal[at, (1 - half) * depth : (2 - half) * depth] = empty
+    bands = x_parts[starts[2] : starts[3], :width]
+    sx = x_parts[starts[3] : starts[4], :EARLY]
+    sums[...] = tensor_sums(
+        own, bands, sx, None, diagonal, z_parts, across, filtered, grads, products
+    )
+
+
+def late_kernel(
+    starts, window, x_parts, z_parts, diagonal, early_sums, wide_hbm, narrow_hbm, sums, edge,
+    wide, narrow, across, filtered, grads, products, mask, sems,
+):
+    pairs, height, double = window.shape
+    rows, depth = 2 * pairs, double // 2
     copies = [
         pltpu.make_async_copy(wide_hbm, wide, sems.at[0]),
         pltpu.make_async_copy(narrow_hbm, narrow, sems.at[1]),
     ]
     for copy in copies:
         copy.start()
-
-    def ready():
-        for copy in copies:
-            copy.wait()
-
-    width, count = own.shape[1], across.shape[1] // 2
-    bands = x_parts[starts[2] : starts[3], :width]
-    sx = x_parts[starts[3] : starts[4], :count]
-    sums[...] = tensor_sums(
-        own, bands, sx, None, ready, wide, narrow, across, filtered, grads, products
-    )
-
-
-def late_kernel(
-    starts, window, x_parts, wide, narrow, early_sums, sums, edge, across, filtered, grads,
-    products, mask,
-):
-    pairs, height, double = window.shape
-    rows, depth = 2 * pairs, double // 2
     count = across.shape[1] // 2
     mask[...] = late_mask(count, height - 2 * EDGE)
     bands = x_parts[starts[1] : starts[2], :height]
     sx = x_parts[starts[4] : starts[5], :count]
     sums[...] = early_sums[...] + tensor_sums(
-        window, bands, sx, mask, lambda: None, wide, narrow, across, filtered, grads, products
+        window, bands, sx, mask, diagonal, z_parts, across, filtered, grads, products
     )
     values = [
         window[row // 2, :, (row % 2) * depth : (row % 2 + 1) * depth].astype(jnp.float32)
         for row in range(rows)
     ]
     last = packed_rows(values, PACK, depth - PACK).astype(jnp.bfloat16)
+    for copy in copies:
+        copy.wait()
     results = edge_gradients(starts, last, x_parts, wide, narrow, 0)
     for part in range(3):
         edge[part] = results[part]
@@ -458,15 +463,15 @@
         both = jnp.concatenate([result[at : at + inner], result[after : after + outer]], axis=0)
         kinds.append(jnp.concatenate([both, both], axis=1))
     lanes = packed.shape[1]
-    at = (4 + 2 * side) * lanes
+    at = 2 * side * lanes
     flat = product(kinds[0], wide[at : at + 2 * lanes, :])
-    at = (2 + 2 * side) * lanes
     steep = product(kinds[1], narrow[at : at + 2 * lanes, :])
     return flat[:, :lanes], steep, flat[:, lanes:]
 
 
 def edge_kernel(
-    starts, width, temp, cure, above, far, near, sums, edge, x_parts, wide, narrow, out, products
+    starts, width, temp, cure, above, far, near, sums, edge, x_parts, z_parts, wide, narrow, out,
+    products,
 ):
     kinds, pad_x, depth = edge.shape
     rows = depth // PACK
@@ -480,8 +485,9 @@
     for index, term in enumerate(weighted_products(three, inside)):
         products[index] = term.astype(jnp.bfloat16)
     sx = x_parts[starts[3] : starts[4], :pad_x]
-    total = sums[...] + all_sums(products, narrow[depth : 2 * depth, :], sx)
-    total = [total[:, index * LANES : (index + 1) * LANES] for index in range(6)]
+    total = sums[...] + all_sums(products, z_parts[3 * depth : 4 * depth, :], sx)
+    high = sx.shape[0]
+    total = [total[index * high : (index + 1) * high] for index in range(6)]
     trace = total[0] + total[1] + total[2]
     lane = lax.broadcasted_iota(jnp.int32, trace.shape, 1)
     joined = [
@@ -611,7 +617,9 @@
     x_constant, lengths = x_constants(width)
     x_hbm = jnp.asarray(x_constant)
     starts = tuple(int(start) for start in np.cumsum([0] + lengths))
-    far, near, own, x_parts, temp, cure = pl.pallas_call(
+    constants = [jnp.asarray(values) for values in depth_constants(rows, depth)]
+    z_hbm, wide_hbm, narrow_hbm = constants
+    far, near, own, x_parts, z_parts, temp, cure = pl.pallas_call(
         pack_kernel,
         name="pack",
         out_shape=(
@@ -619,16 +627,17 @@
             pltpu.VMEM((slots, depth), bf16),
             pltpu.VMEM((rows // 2, width, 2 * depth), bf16),
             pltpu.VMEM(x_hbm.shape, bf16),
+            pltpu.VMEM(z_hbm.shape, bf16),
             pltpu.VMEM((count, lanes), jnp.float32),
             pltpu.VMEM((count, lanes), jnp.float32),
         ),
-        in_specs=[stay] * 4,
+        in_specs=[stay] * 5,
         scratch_shapes=[
             pltpu.VMEM((rows, width, depth), jnp.int32),
-            pltpu.SemaphoreType.DMA((4,)),
+            pltpu.SemaphoreType.DMA((5,)),
         ],
         compiler_params=params,
-    )(*[fixed(values) for values in (intensity, temp_start, cure_start, x_hbm)])
+    )(*[fixed(values) for values in (intensity, temp_start, cure_start, x_hbm, z_hbm)])
 
     def moved(values, pairs):
         index = [(p * depths + d, q * depths + e) for (p, d), (q, e) in pairs]
@@ -642,7 +651,6 @@
     far = swapped(far, 1)
     near = swapped(near, 0)
 
-    wide_hbm, narrow_hbm = [jnp.asarray(values) for values in depth_constants(rows, depth)]
     high = starts[4] - starts[3]
     late = (starts[2] - starts[1]) // 2
 
@@ -661,19 +669,17 @@
             transcendentals=0,
         )
 
-    early_sums, wide, narrow = pl.pallas_call(
+    early_sums, diagonal = pl.pallas_call(
         functools.partial(early_kernel, starts),
         name="early",
         out_shape=(
-            pltpu.VMEM((high, 6 * LANES), jnp.float32),
-            pltpu.VMEM(wide_hbm.shape, bf16),
-            pltpu.VMEM(narrow_hbm.shape, bf16),
+            pltpu.VMEM((6 * high, LANES), jnp.float32),
+            pltpu.VMEM((4 * depth, 2 * depth), bf16),
         ),
-        in_specs=[vmem, vmem, stay, stay],
-        scratch_shapes=scratch(EARLY) + [pltpu.SemaphoreType.DMA((2,))],
+        scratch_shapes=scratch(EARLY),
         cost_estimate=cost(EARLY),
         compiler_params=params,
-    )(own, x_parts, fixed(wide_hbm), fixed(narrow_hbm))
+    )(own, x_parts, z_parts)
 
     span = width + 2 * EDGE
     window, down = pl.pallas_call(
@@ -687,17 +693,21 @@
     )(own, far, near, early_sums)
     above = moved(down, [((p, d + 1), (p, d)) for p in range(planes) for d in range(depths - 1)])
 
-    sums, edge = pl.pallas_call(
+    sums, edge, wide, narrow = pl.pallas_call(
         functools.partial(late_kernel, starts),
         name="late",
         out_shape=(
-            pltpu.VMEM((high, 6 * LANES), jnp.float32),
+            pltpu.VMEM((6 * high, LANES), jnp.float32),
             pltpu.VMEM((3, EARLY + late, LANES), jnp.float32),
+            pltpu.VMEM(wide_hbm.shape, bf16),
+            pltpu.VMEM(narrow_hbm.shape, bf16),
         ),
-        scratch_shapes=scratch(late) + [pltpu.VMEM((late, LANES), jnp.float32)],
+        in_specs=[vmem] * 5 + [stay] * 2,
+        scratch_shapes=scratch(late)
+        + [pltpu.VMEM((late, LANES), jnp.float32), pltpu.SemaphoreType.DMA((2,))],
         cost_estimate=cost(late),
         compiler_params=params,
-    )(window, x_parts, wide, narrow, early_sums)
+    )(window, x_parts, z_parts, diagonal, early_sums, fixed(wide_hbm), fixed(narrow_hbm))
 
     height = -(-(2 * (count + 2 * HALO) + 2 * GHOST) // 8) * 8
     chunks = pl.pallas_call(
@@ -706,7 +716,7 @@
         out_shape=pltpu.VMEM((depths, height, lanes), jnp.float32),
         scratch_shapes=[pltpu.VMEM((6, EARLY + late, depth), bf16)],
         compiler_params=params,
-    )(temp, cure, above, far, near, sums, edge, x_parts, wide, narrow)
+    )(temp, cure, above, far, near, sums, edge, x_parts, z_parts, wide, narrow)
 
     faces = plan.reshape(2 * STEPS, 1) == jnp.arange(tool_levels.shape[0], dtype=jnp.int32)
     tools = jnp.sum(jnp.where(faces, tool_levels, jnp.zeros_like(tool_levels)), axis=1)

time: 27.2 us -> 26.6 us (0.978)
  Pallas kernels: 7.54 us -> 7.03 us
    pallas_call x1, Pallas kernels: 1.9 us -> 1.27 us  [on_device(): pl.pallas_call(functools.partial(early_kernel, starts), name='early', out...]
  transfers between devices with their start and end apart: 4 -> 4, of which waited for: 2 -> 2; matrix products, arithmetic and copies ran while one was open for 1% -> 1% of each run, Pallas kernels for 15% -> 13%
where the time goes in v8:
time: 26.6 us; the launch traced here: 26.3 us
  starting transfers between devices  10.3 us (39%)
  waiting for transfers between devices  7.79 us (29%)
  Pallas kernels  7.03 us (26%)
  between operations  0.72 us (3%)
    ppermute x3, starting transfers between devices, moved(): return lax.ppermute(values, ('plane', 'depth'), index)  6.32 us
    all_to_all x1, waiting for transfers between devices, on_device(): lax.all_to_all(chunks, 'depth', split_axis=0, concat_axis=0, tiled=True)  5.56 us
    all_to_all x1, starting transfers between devices, on_device(): lax.all_to_all(chunks, 'depth', split_axis=0, concat_axis=0, tiled=True)  3.99 us
    ppermute x3, waiting for transfers between devices, moved(): return lax.ppermute(values, ('plane', 'depth'), index)  2.23 us
    pallas_call x1, Pallas kernels, on_device(): pl.pallas_call(functools.partial(late_kernel, starts), name='late', out_s...  2.13 us
    pallas_call x1, Pallas kernels, on_device(): pl.pallas_call(functools.partial(edge_kernel, starts, width), name='edge'...  1.32 us
    pallas_call x1, Pallas kernels, on_device(): pl.pallas_call(functools.partial(early_kernel, starts), name='early', out...  1.27 us
    pallas_call x1, Pallas kernels, on_device(): pl.pallas_call(pack_kernel, name='pack', out_shape=(pltpu.VMEM((slots, de...  1.26 us
  transfers between devices with their start and end apart: 4, of which 2 were waited for; matrix products, arithmetic and copies ran while one was open for 1% of the time, Pallas kernels for 13%

profile of v8, /device:TPU:0, one launch (start us, length us, event | category | flops | bytes accessed | tf_op | source)
XLA Modules:
  0.0 26.3 jit_solution(11869124476381815789)
XLA Ops:
  0.6 1.3 %pack.1 = (bf16[224,128]{1,0:T(8,128)(2,1)S(1)}, bf16[224,128]{1,0:T(8,128)(2,1)S(1)}, bf16[4,96,256]{2,1,0:T(8,128)(2,1)S(1)}, bf16[448,144]{1,0:T(8,128)(2,1)S...) custom-call(s32[8,96,128]{2,1,0:T(8,128)} %intensity.1, f32[6,128]{1,0:T(8,128)} %temp_hbm.1, ...), custom_call_target="tpu_custom_call" | custom-call | tf_op jit(solution)/shard_map/pack/pallas_call | solution.py:622
  1.9 0.7 %collective-permute-start = (bf16[224,128]{1,0:T(8,128)(2,1)S(1)}, bf16[224,128]{1,0:T(8,128)(2,1)S(1)}, u32[]{:S(2)}, u32[]{:S(2)}) collective-permute-start(bf16[224,128]{1,0:T(8,128)(2,1)S(1)} %get-tuple-element.21), channel_id=1, source_target_pairs={{4,8},{5,9},{6,10},{7,11},{12,16},{13,17},{14,18},{15,19},{20,24},... | collective-permute-start | bytes 172040 | tf_op jit(solution)/shard_map/ppermute | solution.py:644
  2.6 4.4 %collective-permute-start.1 = (bf16[224,128]{1,0:T(8,128)(2,1)S(1)}, bf16[224,128]{1,0:T(8,128)(2,1)S(1)}, u32[]{:S(2)}, u32[]{:S(2)}) collective-permute-start(bf16[224,128]{1,0:T(8,128)(2,1)S(1)} %get-tuple-element.22), channel_id=1, source_target_pairs={{0,4},{1,5},{2,6},{3,7},{8,12},{9,13},{10,14},{11,15},{16,20},{17,... | collective-permute-start | bytes 172040 | tf_op jit(solution)/shard_map/ppermute | solution.py:644
  6.9 1.3 %early.1 = (f32[192,128]{1,0:T(8,128)S(1)}, bf16[512,256]{1,0:T(8,128)(2,1)S(1)}) custom-call(bf16[4,96,256]{2,1,0:T(8,128)(2,1)S(1)} %get-tuple-element.20.own, bf16[448,144]{1,0:T(8,128)(2,1)S(1)} %get-tuple-element.23.x_parts, bf16[512,128]{1,0:T(8,128)(2,1)S(1)} %get-tuple-element.24.z_parts), custom_call_target="tpu_custom_call" | custom-call | flops 125829120 | bytes 4000000 | tf_op jit(solution)/shard_map/early/pallas_call | solution.py:672
  8.2 0.0 collective-permute-done.far
  8.2 0.0 collective-permute-done.1.near
  8.2 0.2 window.1
  8.4 0.0 copy-start
  8.4 1.3 %collective-permute-start.2 = (bf16[144,128]{1,0:T(8,128)(2,1)S(1)}, bf16[144,128]{1,0:T(8,128)(2,1)S(1)}, u32[]{:S(2)}, u32[]{:S(2)}) collective-permute-start(bf16[144,128]{1,0:T(8,128)(2,1)S(1)} %get-tuple-element.26), channel_id=1, source_target_pairs={{1,0},{2,1},{3,2},{5,4},{6,5},{7,6},{9,8},{10,9},{11,10},{13,12},{... | collective-permute-start | bytes 110600 | tf_op jit(solution)/shard_map/ppermute | solution.py:644
  9.7 0.0 copy-done
  9.7 0.1 copy.14
  9.8 0.1 eq.15
  9.9 2.1 %late.1 = (f32[192,128]{1,0:T(8,128)S(1)}, f32[3,144,128]{2,1,0:T(8,128)S(1)}, bf16[512,256]{1,0:T(8,128)(2,1)S(1)}, bf16[512,128]{1,0:T(8,128)(2,1)S(1)}) custom-call(bf16[4,144,256]{2,1,0:T(8,128)(2,1)S(1)} %get-tuple-element.27.window, bf16[448,144]{1,0:T(8,128)(2,1)S(1)} %get-tuple-element.23.x_parts, bf16[512,128]{1,0:T(8,128)(2,1)S(1)} %get-tuple-element.24.z_parts, ...), custom_call_target="tpu_custom_call" | custom-call | flops 251658240 | bytes 4000000 | tf_op jit(solution)/shard_map/late/pallas_call | solution.py:696
  12.0 2.2 %collective-permute-done.2.above = bf16[144,128]{1,0:T(8,128)(2,1)S(1)} collective-permute-done((bf16[144,128]{1,0:T(8,128)(2,1)S(1)}, bf16[144,128]{1,0:T(8,128)(2,1)S(1)}, u32[]{:S(2)}, u32[]{:S(2)}) %collective-permute-start.2) | collective-permute-done | bytes 36896 | tf_op jit(solution)/shard_map/ppermute | solution.py:644
  14.3 1.3 %edge.1 = f32[4,32,128]{2,1,0:T(8,128)} custom-call(f32[6,128]{1,0:T(8,128)S(1)} %get-tuple-element.18.temp.temp_in, f32[6,128]{1,0:T(8,128)S(1)} %get-tuple-element.19.cure.cure_in, bf16[144,128]{1,0:T(8,128)(2,1)S(1)} %collective-permute-done.2.above, bf16[224,128]{1,0:T(8,128)(2,1)S(1)} %collective-permute-done.far, ...), custom_call_target="tpu_custom_call" | custom-call | tf_op jit(solution)/shard_map/edge/pallas_call | solution.py:713
  15.6 0.0 copy-start.1
  15.6 4.0 %all-to-all-start = ((f32[4,32,128]{2,1,0:T(8,128)}), f32[4,32,128]{2,1,0:T(8,128)S(1)}, u32[]{:S(2)}, u32[]{:S(2)}) async-start(f32[4,32,128]{2,1,0:T(8,128)} %edge.1), calls=%async_computation | async-start | bytes 131072 | tf_op jit(solution)/shard_map/all_to_all | solution.py:725
  19.6 0.0 copy-done.1
  19.6 0.2 select_reduce_fusion
  19.8 5.6 %all-to-all-done.chunks = f32[4,32,128]{2,1,0:T(8,128)S(1)} async-done(((f32[4,32,128]{2,1,0:T(8,128)}), f32[4,32,128]{2,1,0:T(8,128)S(1)}, u32[]{:S(2)}, u32[]{:S(2)}) %all-to-all-start) | async-done | bytes 65568 | tf_op jit(solution)/shard_map/all_to_all | solution.py:725
  25.3 0.1 broadcast_in_dim.17.tools
  25.4 0.9 %cure.1 = (f32[6,128]{1,0:T(8,128)}, f32[6,128]{1,0:T(8,128)}, f32[3,6,128]{2,1,0:T(8,128)}) custom-call(f32[4,32,128]{2,1,0:T(8,128)S(1)} %all-to-all-done.chunks, f32[6,128]{1,0:T(8,128)S(1)} %get-tuple-element.18.temp.temp_in, f32[6,128]{1,0:T(8,128)S(1)} %get-tuple-element.19.cure.cure_in, f32[6,128]{1,0:T(8,128)S(1)} %broadcast_in_dim.17.tools), custom_call_target="tpu_custom_call" | custom-call | tf_op jit(solution)/shard_map/cure/pallas_call | solution.py:727
Async XLA Ops:
  1.9 6.3 %collective-permute-start = (bf16[224,128]{1,0:T(8,128)(2,1)S(1)}, bf16[224,128]{1,0:T(8,128)(2,1)S(1)}, u32[]{:S(2)}, u32[]{:S(2)}) collective-permute-start(bf16[224,128]{1,0:T(8,128)(2,1)S(1)} %get-tuple-element.21), channel_id=1, source_target_pairs={{4,8},{5,9},{6,10},{7,11},{12,16},{13,17},{14,18},{15,19},{20,24},... | collective-permute-start | bytes 172040 | tf_op jit(solution)/shard_map/ppermute | solution.py:644
  2.6 5.7 %collective-permute-start.1 = (bf16[224,128]{1,0:T(8,128)(2,1)S(1)}, bf16[224,128]{1,0:T(8,128)(2,1)S(1)}, u32[]{:S(2)}, u32[]{:S(2)}) collective-permute-start(bf16[224,128]{1,0:T(8,128)(2,1)S(1)} %get-tuple-element.22), channel_id=1, source_target_pairs={{0,4},{1,5},{2,6},{3,7},{8,12},{9,13},{10,14},{11,15},{16,20},{17,... | collective-permute-start | bytes 172040 | tf_op jit(solution)/shard_map/ppermute | solution.py:644
  8.4 1.3 %copy-start = (s32[3,2]{0,1:T(2,128)S(1)}, s32[3,2]{0,1:T(2,128)}, u32[]{:S(2)}) copy-start(s32[3,2]{0,1:T(2,128)} %param.13) | copy-start | bytes 76
  8.4 5.9 %collective-permute-start.2 = (bf16[144,128]{1,0:T(8,128)(2,1)S(1)}, bf16[144,128]{1,0:T(8,128)(2,1)S(1)}, u32[]{:S(2)}, u32[]{:S(2)}) collective-permute-start(bf16[144,128]{1,0:T(8,128)(2,1)S(1)} %get-tuple-element.26), channel_id=1, source_target_pairs={{1,0},{2,1},{3,2},{5,4},{6,5},{7,6},{9,8},{10,9},{11,10},{13,12},{... | collective-permute-start | bytes 110600 | tf_op jit(solution)/shard_map/ppermute | solution.py:644
  15.6 4.0 %copy-start.1 = (f32[8]{0:T(128)S(1)}, f32[8]{0:T(128)}, u32[]{:S(2)}) copy-start(f32[8]{0:T(128)} %param.12) | copy-start | bytes 100
  15.6 9.7 %all-to-all-start = ((f32[4,32,128]{2,1,0:T(8,128)}), f32[4,32,128]{2,1,0:T(8,128)S(1)}, u32[]{:S(2)}, u32[]{:S(2)}) async-start(f32[4,32,128]{2,1,0:T(8,128)} %edge.1), calls=%async_computation | async-start | bytes 131072 | tf_op jit(solution)/shard_map/all_to_all | solution.py:725

commit v9 on v8

--- a/solution.py
+++ b/solution.py
@@ -31,12 +31,11 @@
 LANES = 128
 HALO = 2
 EDGE = HALO * COARSE + R1 + R2
-EARLY = 48
+EARLY = 64
 GHOST = 3
-PACK = 16
-BACK = 8
-BEFORE = 1
-AFTER = -(-(R1 + R2) // COARSE)
+RIM = 2 * R1
+BEFORE = -(-(R2 - R1) // COARSE)
+AFTER = BEFORE
 HALF = LANES // 2
 ROW_KINDS = (1, 0, 0)
 X_KINDS = (0, 1, 0)
@@ -122,19 +121,61 @@
     return bands
 
 
-def edge_bands(rows, depth):
-    bands = np.zeros((2, 3, rows * PACK, rows * PACK))
+def rim_bands(rows):
+    bands = np.zeros((3, 3 * LANES, LANES))
     for part in range(3):
         row_taps, depth_taps = grad_taps(ROW_KINDS[part]), grad_taps(DEPTH_KINDS[part])
         for source in range(rows):
             for target in range(rows):
                 row_tap = tap(row_taps, source - target)
-                for near in range(-PACK, PACK):
-                    side, lane = int(near >= 0), source * PACK + near % PACK
-                    for place in range(-BACK, R1):
+                for near in range(-RIM, RIM):
+                    lane = source * RIM + near % RIM
+                    if near >= 0:
+                        lane += rows * RIM + LANES
+                    for place in range(-R1, R1):
                         value = row_tap * tap(depth_taps, near - place)
-                        bands[side, part, lane, target * PACK + BACK + place] = value
+                        bands[part, lane, target * 2 * R1 + R1 + place] = value
     return bands
+
+
+def rim_cells(rows, depth, blocks):
+    taps = smooth_taps(R2, sigma_tensor)
+    weights = product_weights(rows)
+    bands = np.zeros((blocks - 1, LANES, blocks * depth // COARSE))
+    for boundary in range(blocks - 1):
+        middle = (boundary + 1) * depth
+        for cell in range(bands.shape[2]):
+            for voxel in range(cell * COARSE, (cell + 1) * COARSE):
+                for place in range(-R1, R1):
+                    value = tap(taps, middle + place - voxel)
+                    for row in range(rows):
+                        bands[boundary, row * 2 * R1 + R1 + place, cell] += weights[row] * value
+    return bands.reshape(-1, bands.shape[2])
+
+
+def own_columns(count):
+    products = (count + 2 * HALO) * COARSE + 2 * R2
+    voxels = products + 2 * R1
+    return -(-products // 16) * 16, -(-voxels // 8) * 8
+
+
+def fold(voxels):
+    return -(-voxels // 16) * 8
+
+
+def rim_x_bands(count):
+    products, voxels = own_columns(count)
+    bands = np.zeros((2, products, -(-voxels // 16) * 16))
+    valid = (count + 2 * HALO) * COARSE + 2 * R2
+    for kind in range(2):
+        for row in range(valid):
+            bands[kind, row, row : row + 2 * R1 + 1] = grad_taps(kind)
+    taps = smooth_taps(R2, sigma_tensor)
+    coarse = np.zeros((16, products))
+    for column in range(count + 2 * HALO):
+        for voxel in range(column * COARSE, (column + 1) * COARSE):
+            coarse[column, voxel : voxel + 2 * R2 + 1] += taps
+    return bands.reshape(2 * products, -1), coarse
 
 
 def depth_bands(depth):
@@ -150,22 +191,15 @@
     return row_weights(rows, R2, sigma_tensor) / (255.0 * GRAD_FACTOR) ** 2
 
 
-def coarse_depth_bands(rows, depth):
+def coarse_depth_bands(depth):
     taps = smooth_taps(R2, sigma_tensor)
-    weights = product_weights(rows)
     columns, cells = sizes(0, depth)
-    bands = np.zeros((2, depth, LANES))
+    bands = np.zeros((depth, LANES))
     for cell in range(cells):
         for voxel in range(COARSE):
             place = (cell - BEFORE) * COARSE + voxel
-            for near in range(max(place - R2, 0), min(place + R2 + 1, depth + R1)):
-                value = tap(taps, near - place)
-                if near < depth - BACK:
-                    bands[0, near, cell] += value
-                else:
-                    for row in range(rows):
-                        lane = row * PACK + near - depth + BACK
-                        bands[1, lane, cell] += weights[row] * value
+            for near in range(max(place - R2, 0), min(place + R2 + 1, depth)):
+                bands[near, cell] += tap(taps, near - place)
     return bands
 
 
@@ -183,41 +217,28 @@
     return bands
 
 
-def x_constants(width):
-    bands, coarse = x_bands(width), coarse_x_bands(width)
-    pieces = [
-        bands[:, :EARLY].reshape(2 * EARLY, -1),
-        bands[:, EARLY:].reshape(2 * (bands.shape[1] - EARLY), -1),
-        bands[:, :EARLY, EDGE : EDGE + width].reshape(2 * EARLY, -1),
-        coarse,
-        coarse[:, EARLY:],
-    ]
+def stacked(*pieces):
     widest = max(piece.shape[1] for piece in pieces)
     padded = [np.pad(piece, ((0, 0), (0, widest - piece.shape[1]))) for piece in pieces]
-    return as_bfloat16(np.concatenate(padded)), [len(piece) for piece in pieces]
-
-
-def depth_constants(rows, depth):
-    own = [*depth_bands(depth), *coarse_depth_bands(rows, depth)]
-    above = [[np.concatenate(halves(part)) for part in side] for side in edge_bands(rows, depth)]
-    wide = [np.concatenate([side[0], side[2]], axis=1) for side in above]
-    narrow = [side[1] for side in above]
-    return [as_bfloat16(np.concatenate(pieces)) for pieces in (own, wide, narrow)]
-
-
-def three_parts(values):
+    starts = np.cumsum([0] + [len(piece) for piece in pieces])
+    return jnp.asarray(as_bfloat16(np.concatenate(padded))), tuple(int(start) for start in starts)
+
+
+def two_parts(values):
     high = values.astype(jnp.bfloat16).astype(jnp.float32)
-    rest = values - high
-    middle = rest.astype(jnp.bfloat16).astype(jnp.float32)
-    return high, middle, (rest - middle).astype(jnp.bfloat16).astype(jnp.float32)
-
-
-def column_slot(temp_ref, cure_ref, first):
-    pad = jnp.zeros((8 - 2 * GHOST, temp_ref.shape[1]), jnp.float32)
-    rows = pl.ds(first, GHOST)
-    both = jnp.concatenate([temp_ref[rows, :], cure_ref[rows, :], pad], axis=0)
-    high, middle, low = three_parts(both)
-    return jnp.concatenate([high, middle, low, jnp.zeros_like(high)], axis=0).astype(jnp.bfloat16)
+    return jnp.concatenate([high, (values - high).astype(jnp.bfloat16).astype(jnp.float32)], axis=0)
+
+
+def joined(parts):
+    half = parts.shape[0] // 2
+    return parts[:half] + parts[half:]
+
+
+def column_rows(temp, cure, first):
+    pad = jnp.zeros((8 - 2 * GHOST, temp.shape[1]), jnp.float32)
+    return jnp.concatenate(
+        [temp[first : first + GHOST, :], cure[first : first + GHOST, :], pad], axis=0
+    )
 
 
 def is_odd():
@@ -242,18 +263,20 @@
         copy.wait()
     odd = is_odd()
     count = temp.shape[0]
-    sides = (column_slot(temp, cure, 0), column_slot(temp, cure, count - GHOST))
+    sides = [
+        two_parts(column_rows(temp, cure, first)).astype(jnp.bfloat16)
+        for first in (0, count - GHOST)
+    ]
 
     def send(left, right):
-        for place, target in ((0, left), (width - EDGE, right)):
+        for place, target, columns in ((0, left, sides[0]), (width - EDGE, right, sides[1])):
             for pair in range(rows // 2):
                 two = [grey[2 * pair + i, place : place + EDGE, :] for i in range(2)]
                 two = jnp.concatenate(two, axis=0).astype(jnp.float32)
                 target[2 * EDGE * pair : 2 * EDGE * (pair + 1), :] = two.astype(jnp.bfloat16)
-        for slot in range(temp.shape[1] // LANES):
-            at = rows * EDGE + 32 * slot
-            left[at : at + 32, :] = sides[0][:, slot * LANES : (slot + 1) * LANES]
-            right[at : at + 32, :] = sides[1][:, slot * LANES : (slot + 1) * LANES]
+            for slot in range(temp.shape[1] // LANES):
+                at = rows * EDGE + 16 * slot
+                target[at : at + 16, :] = columns[:, slot * LANES : (slot + 1) * LANES]
 
     @pl.when(odd)
     def _():
@@ -279,42 +302,15 @@
     return packed
 
 
-def window_kernel(own, far, near, early_sums, window, down):
-    pairs, width, double = own.shape
-    rows, depth = 2 * pairs, double // 2
-    odd = is_odd()
-
-    def edges_of(ref):
-        two = [
-            ref[2 * EDGE * pair : 2 * EDGE * (pair + 1), :].astype(jnp.float32)
-            for pair in range(pairs)
-        ]
-        return [two[row // 2][row % 2 * EDGE : (row % 2 + 1) * EDGE] for row in range(rows)]
-
-    def fill(from_left, from_right):
-        lefts, rights, values = edges_of(from_left), edges_of(from_right), []
-        for row in range(rows):
-            half = (row % 2) * depth
-            middle = own[row // 2, :, half : half + depth].astype(jnp.float32)
-            whole = jnp.concatenate([lefts[row], middle, rights[row]], axis=0)
-            window[row // 2, :, half : half + depth] = whole.astype(jnp.bfloat16)
-            values.append(whole)
-        down[...] = packed_rows(values, PACK, 0).astype(jnp.bfloat16)
-
-    @pl.when(odd)
-    def _():
-        fill(near, far)
-
-    @pl.when(jnp.logical_not(odd))
-    def _():
-        fill(far, near)
-
-
-def joined_columns(ref, rows):
-    slots = range(rows * EDGE, ref.shape[0], 32)
-    parts = [ref[at : at + 32, :].astype(jnp.float32) for at in slots]
-    parts = jnp.concatenate(parts, axis=1)
-    return (parts[0:8] + parts[8:16]) + parts[16:24]
+def edges_of(ref, rows):
+    two = [
+        ref[2 * EDGE * pair : 2 * EDGE * (pair + 1), :].astype(jnp.float32)
+        for pair in range(rows // 2)
+    ]
+    voxels = [two[row // 2][row % 2 * EDGE : (row % 2 + 1) * EDGE] for row in range(rows)]
+    slots = range(rows * EDGE, ref.shape[0], 16)
+    columns = [joined(ref[at : at + 16, :].astype(jnp.float32)) for at in slots]
+    return voxels, jnp.concatenate(columns, axis=1)
 
 
 def product(first, second):
@@ -383,9 +379,11 @@
             grads[part, pair] = product(filtered[part, pair], diagonal[at : at + double, :])
 
     weights = product_weights(rows)
-    first = lax.axis_index("depth") == 0
+    layer = lax.axis_index("depth")
+    first, last = layer == 0, layer == lax.axis_size("depth") - 1
     place = lax.broadcasted_iota(jnp.int32, (16, depth), 1)
-    complete = jnp.where((place >= R1) | first, 1.0, 0.0)
+    complete = ((place >= R1) | first) & ((place < depth - R1) | last)
+    complete = jnp.where(complete, 1.0, 0.0)
 
     def multiply(group, carry):
         start = pl.multiple_of(group * 16, 16)
@@ -404,9 +402,17 @@
     return all_sums(products, z_parts[double : double + depth, :], sx)
 
 
-def early_kernel(
-    starts, own, x_parts, z_parts, sums, diagonal, across, filtered, grads, products
-):
+def early_kernel(*refs):
+    starts, own, x_parts, z_parts, *rest = refs
+    count = (len(rest) - 7) // 2
+    constants, (sums, diagonal), held = rest[:count], rest[count : count + 2], rest[count + 2 : -5]
+    across, filtered, grads, products, sems = rest[-5:]
+    copies = [
+        pltpu.make_async_copy(source, target, sems.at[index])
+        for index, (source, target) in enumerate(zip(constants, held))
+    ]
+    for copy in copies:
+        copy.start()
     pairs, width, double = own.shape
     depth = double // 2
     empty = jnp.zeros((depth, depth), jnp.bfloat16)
@@ -416,117 +422,139 @@
             band = z_parts[kind * depth : (kind + 1) * depth, :]
             diagonal[at, half * depth : (half + 1) * depth] = band
             diagonal[at, (1 - half) * depth : (2 - half) * depth] = empty
-    bands = x_parts[starts[2] : starts[3], :width]
-    sx = x_parts[starts[3] : starts[4], :EARLY]
+    bands = x_parts[starts[0] : starts[1], :width]
+    sx = x_parts[starts[1] : starts[2], :EARLY]
     sums[...] = tensor_sums(
         own, bands, sx, None, diagonal, z_parts, across, filtered, grads, products
     )
+    for copy in copies:
+        copy.wait()
 
 
 def late_kernel(
-    starts, window, x_parts, z_parts, diagonal, early_sums, wide_hbm, narrow_hbm, sums, edge,
-    wide, narrow, across, filtered, grads, products, mask, sems,
+    starts, own, far, near, x_late, z_parts, diagonal, early_sums, temp, cure, out,
+    window, across, filtered, grads, products, mask,
 ):
-    pairs, height, double = window.shape
+    pairs, width, double = own.shape
     rows, depth = 2 * pairs, double // 2
-    copies = [
-        pltpu.make_async_copy(wide_hbm, wide, sems.at[0]),
-        pltpu.make_async_copy(narrow_hbm, narrow, sems.at[1]),
-    ]
-    for copy in copies:
-        copy.start()
-    count = across.shape[1] // 2
-    mask[...] = late_mask(count, height - 2 * EDGE)
-    bands = x_parts[starts[1] : starts[2], :height]
-    sx = x_parts[starts[4] : starts[5], :count]
-    sums[...] = early_sums[...] + tensor_sums(
+    count, lanes = temp.shape
+    odd = is_odd()
+    depths, layer = lax.axis_size("depth"), lax.axis_index("depth")
+    outer, outer_columns = edges_of(far, rows)
+    inner, inner_columns = edges_of(near, rows)
+    values = []
+    for row in range(rows):
+        half = (row % 2) * depth
+        middle = own[row // 2, :, half : half + depth].astype(jnp.float32)
+        left = jnp.where(odd, inner[row], outer[row])
+        right = jnp.where(odd, outer[row], inner[row])
+        whole = jnp.concatenate([left, middle, right], axis=0)
+        window[row // 2, :, half : half + depth] = whole.astype(jnp.bfloat16)
+        values.append(whole)
+    left = jnp.where(odd, inner_columns, outer_columns)
+    right = jnp.where(odd, outer_columns, inner_columns)
+
+    products_x, voxels = own_columns(count)
+    folded, stride = fold(voxels), COARSE * count
+    below = packed_rows(values, RIM, depth - RIM)
+    above = pltpu.roll(packed_rows(values, RIM, 0), rows * RIM, 1)
+    lane = lax.broadcasted_iota(jnp.int32, below.shape, 1)
+    tiles = [jnp.where(lane < rows * RIM, below, above), above, pltpu.roll(above, HALF, 1)]
+    missing = stride * (depths - 1) + voxels - below.shape[0]
+    if missing > 0:
+        spare = jnp.zeros((-(-missing // 8) * 8, LANES), jnp.float32)
+        tiles = [jnp.concatenate([tile, spare], axis=0) for tile in tiles]
+
+    late = across.shape[1] // 2
+    mask[...] = late_mask(late, width)
+    bands = x_late[starts[0] : starts[1], :]
+    sx = x_late[starts[1] : starts[2], :late]
+    sums = early_sums[...] + tensor_sums(
         window, bands, sx, mask, diagonal, z_parts, across, filtered, grads, products
     )
-    values = [
-        window[row // 2, :, (row % 2) * depth : (row % 2 + 1) * depth].astype(jnp.float32)
-        for row in range(rows)
-    ]
-    last = packed_rows(values, PACK, depth - PACK).astype(jnp.bfloat16)
-    for copy in copies:
-        copy.wait()
-    results = edge_gradients(starts, last, x_parts, wide, narrow, 0)
-    for part in range(3):
-        edge[part] = results[part]
-
-
-def edge_gradients(starts, packed, x_parts, wide, narrow, side):
-    result = product(x_parts[: starts[2], : packed.shape[0]], packed).astype(jnp.bfloat16)
-    inner, outer = starts[1] // 2, (starts[2] - starts[1]) // 2
-    kinds = []
-    for kind in range(2):
-        at, after = kind * inner, starts[1] + kind * outer
-        both = jnp.concatenate([result[at : at + inner], result[after : after + outer]], axis=0)
-        kinds.append(jnp.concatenate([both, both], axis=1))
-    lanes = packed.shape[1]
-    at = 2 * side * lanes
-    flat = product(kinds[0], wide[at : at + 2 * lanes, :])
-    steep = product(kinds[1], narrow[at : at + 2 * lanes, :])
-    return flat[:, :lanes], steep, flat[:, lanes:]
-
-
-def edge_kernel(
-    starts, width, temp, cure, above, far, near, sums, edge, x_parts, z_parts, wide, narrow, out,
-    products,
-):
-    kinds, pad_x, depth = edge.shape
-    rows = depth // PACK
-    depths, layer = lax.axis_size("depth"), lax.axis_index("depth")
-    results = edge_gradients(starts, above[...], x_parts, wide, narrow, 1)
-    three = [edge[part] + results[part] for part in range(3)]
-    place = lax.rem(lax.broadcasted_iota(jnp.int32, (pad_x, LANES), 1), PACK) - BACK
-    inside = jnp.where((place < 0) | (layer < depths - 1), 1.0, 0.0)
-    mask = [jnp.ones((EARLY, LANES), jnp.float32), late_mask(pad_x - EARLY, width)]
-    inside = inside * jnp.concatenate(mask, axis=0)
-    for index, term in enumerate(weighted_products(three, inside)):
-        products[index] = term.astype(jnp.bfloat16)
-    sx = x_parts[starts[3] : starts[4], :pad_x]
-    total = sums[...] + all_sums(products, z_parts[3 * depth : 4 * depth, :], sx)
     high = sx.shape[0]
-    total = [total[index * high : (index + 1) * high] for index in range(6)]
+    total = [sums[index * high : (index + 1) * high] for index in range(6)]
     trace = total[0] + total[1] + total[2]
     lane = lax.broadcasted_iota(jnp.int32, trace.shape, 1)
-    joined = [
+    both = [
         jnp.where(lane < HALF, a, pltpu.roll(b, HALF, 1))
         for a, b in ((trace, total[1]), (total[2], total[5]))
     ]
 
-    count = temp.shape[0]
-    lanes = temp.shape[1]
-    pad = jnp.zeros((8 - 2 * GHOST, lanes), jnp.float32)
-    own_first = jnp.concatenate([temp[0:GHOST, :], cure[0:GHOST, :], pad], axis=0)
-    own_last = jnp.concatenate([temp[count - GHOST :, :], cure[count - GHOST :, :], pad], axis=0)
-    odd = is_odd()
-    outer, inner = joined_columns(far, rows), joined_columns(near, rows)
-    left, right = jnp.where(odd, inner, outer), jnp.where(odd, outer, inner)
+    own_first, own_last = column_rows(temp, cure, 0), column_rows(temp, cure, count - GHOST)
     height = count + 2 * HALO
+    half_lane = lax.broadcasted_iota(jnp.int32, (folded, LANES), 1) < HALF
     for target in range(out.shape[0]):
+        at = stride * target
+        second = jnp.where(
+            half_lane,
+            tiles[1][at : at + folded],
+            tiles[2][at + voxels - folded : at + voxels],
+        )
+        rims = jnp.concatenate([tiles[0][at : at + voxels], second], axis=0)
         piece = jnp.where(layer == target - 1, own_last, 0.0)
         piece = jnp.where(layer == target + 1, own_first, piece)
         if target == 0:
             piece = jnp.where(layer == depths - 1, left, piece)
         if target == out.shape[0] - 1:
             piece = jnp.where(layer == 0, right, piece)
-        for index, values in enumerate(joined):
-            at = index * height
-            out[target, at : at + height, 0:LANES] = values[
-                count * target : count * target + height
-            ]
-        if lanes > LANES:
-            out[target, 0 : 2 * height, LANES:] = jnp.zeros((2 * height, lanes - LANES), jnp.float32)
-        out[target, 2 * height : 2 * height + 2 * GHOST, :] = piece[0 : 2 * GHOST]
-        spare = out.shape[1] - 2 * height - 2 * GHOST
-        if spare:
-            out[target, 2 * height + 2 * GHOST :, :] = jnp.zeros((spare, lanes), jnp.float32)
+        pieces = [values[count * target : count * target + height] for values in both]
+        for slot in range(lanes // LANES):
+            pieces.append(piece[0 : 2 * GHOST, slot * LANES : (slot + 1) * LANES])
+        filled = sum(part.shape[0] for part in pieces)
+        pieces.append(jnp.zeros((32 - filled, LANES), jnp.float32))
+        sent = jnp.concatenate([rims, two_parts(jnp.concatenate(pieces, axis=0))], axis=0)
+        out[target] = sent.astype(jnp.bfloat16)
+
+
+def rim_sums(chunks, count, starts, flat, steep, cells):
+    parts = chunks.shape[0]
+    rows_x, voxels = own_columns(count)
+    folded = fold(voxels)
+    tall = -(-voxels // 16) * 16
+    spare = [jnp.zeros((tall - voxels, LANES), jnp.float32)] if tall > voxels else []
+    tiles = []
+    for part in range(parts):
+        rims = chunks[part, 0 : voxels + folded, :].astype(jnp.float32)
+        second = rims[voxels:]
+        second = [second[: voxels - folded], pltpu.roll(second, HALF, 1)]
+        for tile in ([rims[:voxels]], second):
+            tiles.append(jnp.concatenate(tile + spare, axis=0).astype(jnp.bfloat16))
+    result = product(
+        steep[starts[1] : starts[2], :tall], jnp.concatenate(tiles, axis=1)
+    ).astype(jnp.bfloat16)
+    kinds = []
+    for kind in range(2):
+        values = result[kind * rows_x : (kind + 1) * rows_x]
+        tile = lambda index: values[:, index * LANES : (index + 1) * LANES]
+        stack = [
+            jnp.concatenate([tile(2 * part), tile(2 * part + 2), tile(2 * part + 3)], axis=1)
+            for part in range(parts - 1)
+        ]
+        kinds.append(jnp.concatenate(stack, axis=0))
+    both = product(kinds[0], flat[...])
+    three = (both[:, :LANES], product(kinds[1], steep[starts[0] : starts[1], :]), both[:, LANES:])
+
+    index = lax.axis_index("plane") * lax.axis_size("depth") + lax.axis_index("depth")
+    total = lax.axis_size("plane") * lax.axis_size("depth") * count * COARSE
+    place = lax.rem(lax.broadcasted_iota(jnp.int32, three[0].shape, 0), rows_x)
+    place = place + (index * count - HALO) * COARSE - R2
+    inside = jnp.where((place >= 0) & (place < total), 1.0, 0.0)
+    wide = []
+    for term in weighted_products(three, inside):
+        term = term.astype(jnp.bfloat16)
+        wide += [term[part * rows_x : (part + 1) * rows_x] for part in range(parts - 1)]
+    sx = steep[starts[2] : starts[3], :rows_x]
+    along = product(sx, jnp.concatenate(wide, axis=1)).astype(jnp.bfloat16)
+    step = (parts - 1) * LANES
+    along = [along[:, kind * step : (kind + 1) * step] for kind in range(6)]
+    sums = product(jnp.concatenate(along, axis=0), cells[...])
+    return [sums[kind * 16 : (kind + 1) * 16] for kind in range(6)]
 
 
 def cure_kernel(
-    cells, chunks, temp_in, cure_in, tools, temp_hbm, cure_hbm, conduct_hbm, temp_out,
-    cure_out, conduct_out, sems,
+    cells, starts, chunks, temp_in, cure_in, tools, flat, steep, rim_bands, temp_hbm, cure_hbm,
+    conduct_hbm, temp_out, cure_out, conduct_out, sems,
 ):
     count, lanes = temp_in.shape
     parts = chunks.shape[0]
@@ -536,14 +564,20 @@
     own = cells - BEFORE - AFTER
     lane = lax.broadcasted_iota(jnp.int32, (16, lanes), 1)
     row = lax.broadcasted_iota(jnp.int32, (16, lanes), 0)
-
-    sums = [jnp.zeros((16, lanes), jnp.float32) for _ in range(4)]
+    at_sums = chunks.shape[1] - 64
+
+    near = rim_sums(chunks, count, starts, flat, steep, rim_bands)
+    sums = [near[0] + near[1] + near[2], near[1], near[2], near[5]]
     for part in range(parts):
         first_cell = own * part - BEFORE
         here = (lane >= first_cell) & (lane < first_cell + cells)
+        values = joined(chunks[part, at_sums:, :].astype(jnp.float32))
         for index in range(4):
             at = (index // 2) * height
-            chunk = chunks[part, at : at + 16, :]
+            chunk = values[at : at + 16]
+            if lanes > LANES:
+                spare = jnp.zeros((16, lanes - LANES), jnp.float32)
+                chunk = jnp.concatenate([chunk, spare], axis=1)
             shift = (first_cell - (index % 2) * HALF) % lanes
             moved = chunk if shift == 0 else pltpu.roll(chunk, shift, 1)
             sums[index] = sums[index] + jnp.where(here, moved, 0.0)
@@ -563,8 +597,13 @@
     ]
     copies[0].start()
 
-    before = chunks[lax.rem(layer + parts - 1, parts)][2 * height : 2 * height + 2 * GHOST]
-    after = chunks[lax.rem(layer + 1, parts)][2 * height : 2 * height + 2 * GHOST]
+    def columns_of(part):
+        values = joined(chunks[part, at_sums:, :].astype(jnp.float32))
+        slots = range(2 * height, 2 * height + 2 * GHOST * (lanes // LANES), 2 * GHOST)
+        return jnp.concatenate([values[at : at + 2 * GHOST] for at in slots], axis=1)
+
+    before = columns_of(lax.rem(layer + parts - 1, parts))
+    after = columns_of(lax.rem(layer + 1, parts))
     spare = jnp.full((16 - count - 2 * GHOST, lanes), 0.5, jnp.float32)
     temp = jnp.concatenate([before[:GHOST], temp_in[...], after[:GHOST], 8.0 * spare], axis=0)
     cure = jnp.concatenate([before[GHOST:], cure_in[...], after[GHOST:], spare], axis=0)
@@ -608,17 +647,23 @@
     planes, depths = lax.axis_size("plane"), lax.axis_size("depth")
     columns, cells = sizes(width, depth)
     bf16 = jnp.bfloat16
-    slots = rows * EDGE + 32 * (lanes // LANES)
+    slots = rows * EDGE + 16 * (lanes // LANES)
     params = pltpu.CompilerParams(vmem_limit_bytes=24 * 1024 * 1024)
     vmem = pl.BlockSpec(memory_space=pltpu.VMEM)
     stay = pl.BlockSpec(memory_space=pltpu.HBM)
 
     fixed = lambda values: pltpu.with_memory_space_constraint(values, pltpu.HBM)
-    x_constant, lengths = x_constants(width)
-    x_hbm = jnp.asarray(x_constant)
-    starts = tuple(int(start) for start in np.cumsum([0] + lengths))
-    constants = [jnp.asarray(values) for values in depth_constants(rows, depth)]
-    z_hbm, wide_hbm, narrow_hbm = constants
+    bands, coarse = x_bands(width), coarse_x_bands(width)
+    late = bands.shape[1] - EARLY
+    middle = bands[:, :EARLY, EDGE : EDGE + width]
+    x_hbm, early_starts = stacked(middle.reshape(2 * EARLY, -1), coarse[:, :EARLY])
+    z_hbm, _ = stacked(*depth_bands(depth), coarse_depth_bands(depth))
+    x_late, late_starts = stacked(bands[:, EARLY:].reshape(2 * late, -1), coarse[:, EARLY:])
+    rims = rim_bands(rows)
+    flat, _ = stacked(np.concatenate([rims[0], rims[2]], axis=1))
+    steep, rim_starts = stacked(rims[1], *rim_x_bands(count))
+    cell_bands, _ = stacked(rim_cells(rows, depth, depths))
+    constants = (x_late, flat, steep, cell_bands)
     far, near, own, x_parts, z_parts, temp, cure = pl.pallas_call(
         pack_kernel,
         name="pack",
@@ -651,8 +696,7 @@
     far = swapped(far, 1)
     near = swapped(near, 0)
 
-    high = starts[4] - starts[3]
-    late = (starts[2] - starts[1]) // 2
+    high = coarse.shape[0]
 
     def scratch(count):
         return [
@@ -669,54 +713,31 @@
             transcendentals=0,
         )
 
-    early_sums, diagonal = pl.pallas_call(
-        functools.partial(early_kernel, starts),
+    early_sums, diagonal, x_late, flat, steep, cell_bands = pl.pallas_call(
+        functools.partial(early_kernel, early_starts),
         name="early",
         out_shape=(
             pltpu.VMEM((6 * high, LANES), jnp.float32),
             pltpu.VMEM((4 * depth, 2 * depth), bf16),
+            *[pltpu.VMEM(values.shape, bf16) for values in constants],
         ),
-        scratch_shapes=scratch(EARLY),
+        in_specs=[vmem] * 3 + [stay] * len(constants),
+        scratch_shapes=scratch(EARLY) + [pltpu.SemaphoreType.DMA((len(constants),))],
         cost_estimate=cost(EARLY),
         compiler_params=params,
-    )(own, x_parts, z_parts)
-
-    span = width + 2 * EDGE
-    window, down = pl.pallas_call(
-        window_kernel,
-        name="window",
-        out_shape=(
-            pltpu.VMEM((rows // 2, span, 2 * depth), bf16),
-            pltpu.VMEM((span, depth), bf16),
-        ),
-        compiler_params=params,
-    )(own, far, near, early_sums)
-    above = moved(down, [((p, d + 1), (p, d)) for p in range(planes) for d in range(depths - 1)])
-
-    sums, edge, wide, narrow = pl.pallas_call(
-        functools.partial(late_kernel, starts),
+    )(own, x_parts, z_parts, *[fixed(values) for values in constants])
+
+    products_x, voxels = own_columns(count)
+    chunks = pl.pallas_call(
+        functools.partial(late_kernel, late_starts),
         name="late",
-        out_shape=(
-            pltpu.VMEM((6 * high, LANES), jnp.float32),
-            pltpu.VMEM((3, EARLY + late, LANES), jnp.float32),
-            pltpu.VMEM(wide_hbm.shape, bf16),
-            pltpu.VMEM(narrow_hbm.shape, bf16),
-        ),
-        in_specs=[vmem] * 5 + [stay] * 2,
-        scratch_shapes=scratch(late)
-        + [pltpu.VMEM((late, LANES), jnp.float32), pltpu.SemaphoreType.DMA((2,))],
+        out_shape=pltpu.VMEM((depths, voxels + fold(voxels) + 64, LANES), bf16),
+        scratch_shapes=[pltpu.VMEM((rows // 2, width + 2 * EDGE, 2 * depth), bf16)]
+        + scratch(late)
+        + [pltpu.VMEM((late, LANES), jnp.float32)],
         cost_estimate=cost(late),
         compiler_params=params,
-    )(window, x_parts, z_parts, diagonal, early_sums, fixed(wide_hbm), fixed(narrow_hbm))
-
-    height = -(-(2 * (count + 2 * HALO) + 2 * GHOST) // 8) * 8
-    chunks = pl.pallas_call(
-        functools.partial(edge_kernel, starts, width),
-        name="edge",
-        out_shape=pltpu.VMEM((depths, height, lanes), jnp.float32),
-        scratch_shapes=[pltpu.VMEM((6, EARLY + late, depth), bf16)],
-        compiler_params=params,
-    )(temp, cure, above, far, near, sums, edge, x_parts, z_parts, wide, narrow)
+    )(own, far, near, x_late, z_parts, diagonal, early_sums, temp, cure)
 
     faces = plan.reshape(2 * STEPS, 1) == jnp.arange(tool_levels.shape[0], dtype=jnp.int32)
     tools = jnp.sum(jnp.where(faces, tool_levels, jnp.zeros_like(tool_levels)), axis=1)
@@ -725,14 +746,14 @@
     chunks = lax.all_to_all(chunks, "depth", split_axis=0, concat_axis=0, tiled=True)
 
     return pl.pallas_call(
-        functools.partial(cure_kernel, cells),
+        functools.partial(cure_kernel, cells, rim_starts),
         name="cure",
         out_shape=(
             pltpu.HBM((count, lanes), jnp.float32),
             pltpu.HBM((count, lanes), jnp.float32),
             pltpu.HBM((3, count, lanes), jnp.float32),
         ),
-        in_specs=[vmem, vmem, vmem, vmem],
+        in_specs=[vmem] * 7,
         out_specs=(stay, stay, stay),
         scratch_shapes=[
             pltpu.VMEM((count, lanes), jnp.float32),
@@ -741,7 +762,7 @@
             pltpu.SemaphoreType.DMA((3,)),
         ],
         compiler_params=params,
-    )(chunks, temp, cure, tools)
+    )(chunks, temp, cure, tools, flat, steep, cell_bands)
 
 
 def solution(mesh):

time: 26.6 us -> 25.2 us (0.947)
  waiting for transfers between devices: 7.79 us -> 6.61 us
  local copies, waits for them, and re-layouts: 0.26 us -> 0.82 us
  Pallas kernels: 7.03 us -> 6.66 us
  starting transfers between devices: 10.3 us -> 10 us
    ppermute x3 -> x2, waiting for transfers between devices: 2.23 us -> 0.01 us  [moved(): return lax.ppermute(values, ('plane', 'depth'), index)]
    ppermute x3 -> x2, starting transfers between devices: 6.32 us -> 5.03 us  [moved(): return lax.ppermute(values, ('plane', 'depth'), index)]
    all_to_all x1, waiting for transfers between devices: 5.56 us -> 6.6 us  [on_device(): lax.all_to_all(chunks, 'depth', split_axis=0, concat_axis=0, tiled=True)]
    all_to_all x1, starting transfers between devices: 3.99 us -> 5 us  [on_device(): lax.all_to_all(chunks, 'depth', split_axis=0, concat_axis=0, tiled=True)]
    unnamed x5, local copies, waits for them, and re-layouts: 0.1 us -> 0.67 us
    pallas_call x5 -> x3, Pallas kernels: 5.77 us -> 5.5 us  [the longest x1 2.51 us: on_device(): pl.pallas_call(functools.partial(late_kernel, late_starts), name='late',...]
  transfers between devices with their start and end apart: 4 -> 3, of which waited for: 2 -> 1; matrix products, arithmetic and copies ran while one was open for 1% -> 1% of each run, Pallas kernels for 13% -> 6%
where the time goes in v9:
time: 25.2 us; the launch traced here: 25 us
  starting transfers between devices  10 us (40%)
  Pallas kernels  6.66 us (26%)
  waiting for transfers between devices  6.61 us (26%)
  local copies, waits for them, and re-layouts  0.82 us (3%)
  between operations  0.68 us (3%)
    all_to_all x1, waiting for transfers between devices, on_device(): lax.all_to_all(chunks, 'depth', split_axis=0, concat_axis=0, tiled=True)  6.6 us
    ppermute x2, starting transfers between devices, moved(): return lax.ppermute(values, ('plane', 'depth'), index)  5.03 us
    all_to_all x1, starting transfers between devices, on_device(): lax.all_to_all(chunks, 'depth', split_axis=0, concat_axis=0, tiled=True)  5 us
    pallas_call x1, Pallas kernels, on_device(): pl.pallas_call(functools.partial(late_kernel, late_starts), name='late',...  2.51 us
    pallas_call x1, Pallas kernels, on_device(): pl.pallas_call(functools.partial(cure_kernel, cells, rim_starts), name='c...  1.52 us
    pallas_call x1, Pallas kernels, on_device(): pl.pallas_call(functools.partial(early_kernel, early_starts), name='early...  1.46 us
    pallas_call x1, Pallas kernels, on_device(): pl.pallas_call(pack_kernel, name='pack', out_shape=(pltpu.VMEM((slots, de...  1.16 us
    unnamed x5, local copies, waits for them, and re-layouts  0.67 us
  transfers between devices with their start and end apart: 3, of which 1 were waited for; matrix products, arithmetic and copies ran while one was open for 1% of the time, Pallas kernels for 6%

profile of v9, /device:TPU:0, one launch (start us, length us, event | category | flops | bytes accessed | tf_op | source)
XLA Modules:
  0.0 25.0 jit_solution(86863945831448760)
XLA Ops:
  0.6 1.2 %pack.1 = (bf16[208,128]{1,0:T(8,128)(2,1)S(1)}, bf16[208,128]{1,0:T(8,128)(2,1)S(1)}, bf16[4,96,256]{2,1,0:T(8,128)(2,1)S(1)}, bf16[160,96]{1,0:T(8,128)(2,1)S(...) custom-call(s32[8,96,128]{2,1,0:T(8,128)} %intensity.1, f32[6,128]{1,0:T(8,128)} %temp_hbm.1, ...), custom_call_target="tpu_custom_call" | custom-call | tf_op jit(solution)/shard_map/pack/pallas_call | solution.py:667
  1.8 0.7 %collective-permute-start = (bf16[208,128]{1,0:T(8,128)(2,1)S(1)}, bf16[208,128]{1,0:T(8,128)(2,1)S(1)}, u32[]{:S(2)}, u32[]{:S(2)}) collective-permute-start(bf16[208,128]{1,0:T(8,128)(2,1)S(1)} %get-tuple-element.17), channel_id=1, source_target_pairs={{4,8},{5,9},{6,10},{7,11},{12,16},{13,17},{14,18},{15,19},{20,24},... | collective-permute-start | bytes 159752 | tf_op jit(solution)/shard_map/ppermute | solution.py:689
  2.5 4.4 %collective-permute-start.1 = (bf16[208,128]{1,0:T(8,128)(2,1)S(1)}, bf16[208,128]{1,0:T(8,128)(2,1)S(1)}, u32[]{:S(2)}, u32[]{:S(2)}) collective-permute-start(bf16[208,128]{1,0:T(8,128)(2,1)S(1)} %get-tuple-element.18), channel_id=1, source_target_pairs={{0,4},{1,5},{2,6},{3,7},{8,12},{9,13},{10,14},{11,15},{16,20},{17,... | collective-permute-start | bytes 159752 | tf_op jit(solution)/shard_map/ppermute | solution.py:689
  6.8 1.5 %early.1 = (f32[192,128]{1,0:T(8,128)S(1)}, bf16[512,256]{1,0:T(8,128)(2,1)S(1)}, bf16[192,144]{1,0:T(8,128)(2,1)S(1)}, bf16[384,256]{1,0:T(8,128)(2,1)S(1)}, bf...) custom-call(bf16[4,96,256]{2,1,0:T(8,128)(2,1)S(1)} %get-tuple-element.16.refs_0_.own, ...), custom_call_target="tpu_custom_call" | custom-call | flops 167772160 | bytes 4000000 | tf_op jit(solution)/shard_map/early/pallas_call | solution.py:716
  8.3 0.0 collective-permute-done.far
  8.3 0.0 collective-permute-done.1.near
  8.3 2.5 %late.1 = bf16[4,176,128]{2,1,0:T(8,128)(2,1)} custom-call(bf16[4,96,256]{2,1,0:T(8,128)(2,1)S(1)} %get-tuple-element.16.refs_0_.own, bf16[208,128]{1,0:T(8,128)(2,1)S(1)} %collective-permute-done.far, bf16[208,128]{1,0:T(8,128)(2,1)S(1)} %collective-permute-done.1.near, bf16[192,144]{1,0:T(8,128)(2,1)S(1)} %get-tuple-element.21.x_late, ...), custom_call_target="tpu_custom_call" | custom-call | flops 209715200 | bytes 4000000 | tf_op jit(solution)/shard_map/late/pallas_call | solution.py:731
  10.8 0.0 copy-start
  10.8 5.0 %all-to-all-start = ((bf16[4,176,128]{2,1,0:T(8,128)(2,1)}), bf16[4,176,128]{2,1,0:T(8,128)(2,1)S(1)}, u32[]{:S(2)}, u32[]{:S(2)}) async-start(bf16[4,176,128]{2,1,0:T(8,128)(2,1)} %late.1), calls=%async_computation | async-start | bytes 360448 | tf_op jit(solution)/shard_map/all_to_all | solution.py:746
  15.8 0.0 copy-done
  15.8 0.1 copy.16
  15.9 0.0 copy-start.1
  15.9 0.1 eq.15
  16.0 0.6 %copy-done.1 = f32[8]{0:T(128)S(1)} copy-done((f32[8]{0:T(128)S(1)}, f32[8]{0:T(128)}, u32[]{:S(2)}) %copy-start.1) | copy-done | bytes 56
  16.6 0.2 select_reduce_fusion
  16.8 6.6 %all-to-all-done.chunks = bf16[4,176,128]{2,1,0:T(8,128)(2,1)S(1)} async-done(((bf16[4,176,128]{2,1,0:T(8,128)(2,1)}), bf16[4,176,128]{2,1,0:T(8,128)(2,1)S(1)}, u32[]{:S(2)}, u32[]{:S(2)}) %all-to-all-start) | async-done | bytes 180256 | tf_op jit(solution)/shard_map/all_to_all | solution.py:746
  23.4 0.1 broadcast_in_dim.17.tools
  23.4 1.5 %cure.1 = (f32[6,128]{1,0:T(8,128)}, f32[6,128]{1,0:T(8,128)}, f32[3,6,128]{2,1,0:T(8,128)}) custom-call(bf16[4,176,128]{2,1,0:T(8,128)(2,1)S(1)} %all-to-all-done.chunks, f32[6,128]{1,0:T(8,128)S(1)} %get-tuple-element.24.temp.temp_in, f32[6,128]{1,0:T(8,128)S(1)} %get-tuple-element.25.cure.cure_in, f32[6,128]{1,0:T(8,128)S(1)} %broadcast_in_dim.17.tools, ...), custom_call_target="tpu_custom_call" | custom-call | tf_op jit(solution)/shard_map/cure/pallas_call | solution.py:748
Async XLA Ops:
  1.8 6.5 %collective-permute-start = (bf16[208,128]{1,0:T(8,128)(2,1)S(1)}, bf16[208,128]{1,0:T(8,128)(2,1)S(1)}, u32[]{:S(2)}, u32[]{:S(2)}) collective-permute-start(bf16[208,128]{1,0:T(8,128)(2,1)S(1)} %get-tuple-element.17), channel_id=1, source_target_pairs={{4,8},{5,9},{6,10},{7,11},{12,16},{13,17},{14,18},{15,19},{20,24},... | collective-permute-start | bytes 159752 | tf_op jit(solution)/shard_map/ppermute | solution.py:689
  2.5 5.8 %collective-permute-start.1 = (bf16[208,128]{1,0:T(8,128)(2,1)S(1)}, bf16[208,128]{1,0:T(8,128)(2,1)S(1)}, u32[]{:S(2)}, u32[]{:S(2)}) collective-permute-start(bf16[208,128]{1,0:T(8,128)(2,1)S(1)} %get-tuple-element.18), channel_id=1, source_target_pairs={{0,4},{1,5},{2,6},{3,7},{8,12},{9,13},{10,14},{11,15},{16,20},{17,... | collective-permute-start | bytes 159752 | tf_op jit(solution)/shard_map/ppermute | solution.py:689
  10.8 5.0 %copy-start = (s32[3,2]{0,1:T(2,128)S(1)}, s32[3,2]{0,1:T(2,128)}, u32[]{:S(2)}) copy-start(s32[3,2]{0,1:T(2,128)} %param.15) | copy-start | bytes 76
  10.8 12.5 %all-to-all-start = ((bf16[4,176,128]{2,1,0:T(8,128)(2,1)}), bf16[4,176,128]{2,1,0:T(8,128)(2,1)S(1)}, u32[]{:S(2)}, u32[]{:S(2)}) async-start(bf16[4,176,128]{2,1,0:T(8,128)(2,1)} %late.1), calls=%async_computation | async-start | bytes 360448 | tf_op jit(solution)/shard_map/all_to_all | solution.py:746
  15.9 0.7 %copy-start.1 = (f32[8]{0:T(128)S(1)}, f32[8]{0:T(128)}, u32[]{:S(2)}) copy-start(f32[8]{0:T(128)} %param.14) | copy-start | bytes 100

commit v10 on v9

--- a/solution.py
+++ b/solution.py
@@ -31,12 +31,13 @@
 LANES = 128
 HALO = 2
 EDGE = HALO * COARSE + R1 + R2
-EARLY = 64
+EARLY = 80
 GHOST = 3
 RIM = 2 * R1
 BEFORE = -(-(R2 - R1) // COARSE)
 AFTER = BEFORE
 HALF = LANES // 2
+SLOT = 40
 ROW_KINDS = (1, 0, 0)
 X_KINDS = (0, 1, 0)
 DEPTH_KINDS = (0, 0, 1)
@@ -317,13 +318,21 @@
     return jnp.dot(first, second, preferred_element_type=jnp.float32)
 
 
-def along_rows(kind, values, row):
-    total = None
-    for source, value in enumerate(values):
-        weight = tap(grad_taps(kind), source - row)
-        if weight != 0.0:
+def mirrored_filter(kind, values, even):
+    rows = len(values)
+    use_sum = even == (kind == 0)
+    sign = 1.0 if use_sum else -1.0
+    half = [values[row] + sign * values[rows - 1 - row] for row in range(rows // 2)]
+    results = []
+    for row in range(rows // 2):
+        total = None
+        for source, value in enumerate(half):
+            near = tap(grad_taps(kind), source - row)
+            far = tap(grad_taps(kind), rows - 1 - source - row)
+            weight = 0.5 * (near + sign * far)
             total = weight * value if total is None else total + weight * value
-    return total
+        results.append(total)
+    return results
 
 
 def weighted_products(three, weight):
@@ -366,8 +375,10 @@
             for kind in range(2)
         ]
         for part in range(3):
-            for row in range(rows):
-                result = along_rows(ROW_KINDS[part], kinds[X_KINDS[part]], row)
+            values = kinds[X_KINDS[part]]
+            results = mirrored_filter(ROW_KINDS[part], values, True)
+            results += mirrored_filter(ROW_KINDS[part], values, False)
+            for row, result in enumerate(results):
                 lanes = pl.ds((row % 2) * depth, depth)
                 filtered[part, row // 2, pl.ds(start, 16), lanes] = result.astype(jnp.bfloat16)
         return carry
@@ -392,7 +403,7 @@
         for row in range(rows):
             lanes = pl.ds((row % 2) * depth, depth)
             three = [grads[part, row // 2, pl.ds(start, 16), lanes] for part in range(3)]
-            terms = weighted_products(three, float(weights[row]))
+            terms = weighted_products(three, 2.0 * float(weights[row % (rows // 2)]))
             totals = terms if row == 0 else [a + b for a, b in zip(totals, terms)]
         for index in range(6):
             products[index, pl.ds(start, 16), :] = (totals[index] * inside).astype(jnp.bfloat16)
@@ -432,8 +443,8 @@
 
 
 def late_kernel(
-    starts, own, far, near, x_late, z_parts, diagonal, early_sums, temp, cure, out,
-    window, across, filtered, grads, products, mask,
+    starts, own, far, near, x_late, z_parts, diagonal, early_sums, temp, cure, out_hbm,
+    window, across, filtered, grads, products, mask, out, sems,
 ):
     pairs, width, double = own.shape
     rows, depth = 2 * pairs, double // 2
@@ -465,6 +476,24 @@
         spare = jnp.zeros((-(-missing // 8) * 8, LANES), jnp.float32)
         tiles = [jnp.concatenate([tile, spare], axis=0) for tile in tiles]
 
+    height = count + 2 * HALO
+    half_lane = lax.broadcasted_iota(jnp.int32, (folded, LANES), 1) < HALF
+    for target in range(out.shape[0]):
+        at = stride * target
+        second = jnp.where(
+            half_lane,
+            tiles[1][at : at + folded],
+            tiles[2][at + voxels - folded : at + voxels],
+        )
+        rims = jnp.concatenate([tiles[0][at : at + voxels], second], axis=0)
+        out[target, 0 : voxels + folded, :] = rims.astype(jnp.bfloat16)
+    split = (pl.ds(0, voxels + folded), pl.ds(voxels + folded, out.shape[1] - voxels - folded))
+    copies = [
+        pltpu.make_async_copy(out.at[:, part, :], out_hbm.at[:, part, :], sems.at[index])
+        for index, part in enumerate(split)
+    ]
+    copies[0].start()
+
     late = across.shape[1] // 2
     mask[...] = late_mask(late, width)
     bands = x_late[starts[0] : starts[1], :]
@@ -476,35 +505,38 @@
     total = [sums[index * high : (index + 1) * high] for index in range(6)]
     trace = total[0] + total[1] + total[2]
     lane = lax.broadcasted_iota(jnp.int32, trace.shape, 1)
-    both = [
-        jnp.where(lane < HALF, a, pltpu.roll(b, HALF, 1))
-        for a, b in ((trace, total[1]), (total[2], total[5]))
-    ]
+    three = jnp.where(lane < SLOT, trace, pltpu.roll(total[1], SLOT, 1))
+    three = jnp.where(lane < 2 * SLOT, three, pltpu.roll(total[2], 2 * SLOT, 1))
+    xz = [total[5]] + [pltpu.roll(total[5], index * SLOT, 1) for index in range(1, 3)]
 
     own_first, own_last = column_rows(temp, cure, 0), column_rows(temp, cure, count - GHOST)
-    height = count + 2 * HALO
-    half_lane = lax.broadcasted_iota(jnp.int32, (folded, LANES), 1) < HALF
     for target in range(out.shape[0]):
-        at = stride * target
-        second = jnp.where(
-            half_lane,
-            tiles[1][at : at + folded],
-            tiles[2][at + voxels - folded : at + voxels],
-        )
-        rims = jnp.concatenate([tiles[0][at : at + voxels], second], axis=0)
         piece = jnp.where(layer == target - 1, own_last, 0.0)
         piece = jnp.where(layer == target + 1, own_first, piece)
         if target == 0:
             piece = jnp.where(layer == depths - 1, left, piece)
         if target == out.shape[0] - 1:
             piece = jnp.where(layer == 0, right, piece)
-        pieces = [values[count * target : count * target + height] for values in both]
+        at = count * target
+        pieces = [three[at : at + height], jnp.zeros((4, LANES), jnp.float32)]
+        for index in range(3):
+            size = min(4, height - 4 * index)
+            if size > 0:
+                part = xz[index][at + 4 * index : at + 4 * index + size]
+                if size < 4:
+                    spare = jnp.zeros((4 - size, LANES), jnp.float32)
+                    part = jnp.concatenate([part, spare], axis=0)
+                pieces[1] = jnp.where(lane[:4] < index * SLOT, pieces[1], part)
         for slot in range(lanes // LANES):
             pieces.append(piece[0 : 2 * GHOST, slot * LANES : (slot + 1) * LANES])
         filled = sum(part.shape[0] for part in pieces)
-        pieces.append(jnp.zeros((32 - filled, LANES), jnp.float32))
-        sent = jnp.concatenate([rims, two_parts(jnp.concatenate(pieces, axis=0))], axis=0)
-        out[target] = sent.astype(jnp.bfloat16)
+        if filled < 24:
+            pieces.append(jnp.zeros((24 - filled, LANES), jnp.float32))
+        sent = two_parts(jnp.concatenate(pieces, axis=0))
+        out[target, voxels + folded :, :] = sent.astype(jnp.bfloat16)
+    copies[1].start()
+    for copy in copies:
+        copy.wait()
 
 
 def rim_sums(chunks, count, starts, flat, steep, cells):
@@ -564,7 +596,7 @@
     own = cells - BEFORE - AFTER
     lane = lax.broadcasted_iota(jnp.int32, (16, lanes), 1)
     row = lax.broadcasted_iota(jnp.int32, (16, lanes), 0)
-    at_sums = chunks.shape[1] - 64
+    at_sums = chunks.shape[1] - 48
 
     near = rim_sums(chunks, count, starts, flat, steep, rim_bands)
     sums = [near[0] + near[1] + near[2], near[1], near[2], near[5]]
@@ -572,13 +604,16 @@
         first_cell = own * part - BEFORE
         here = (lane >= first_cell) & (lane < first_cell + cells)
         values = joined(chunks[part, at_sums:, :].astype(jnp.float32))
+        xz = values[height : height + 4]
+        xz = [xz] + [pltpu.roll(xz, LANES - index * SLOT, 1) for index in range(1, 3)]
+        spare = jnp.zeros((4, LANES), jnp.float32)
+        xz = jnp.concatenate([*xz, spare], axis=0)
         for index in range(4):
-            at = (index // 2) * height
-            chunk = values[at : at + 16]
+            chunk = values[0:16] if index < 3 else xz
             if lanes > LANES:
                 spare = jnp.zeros((16, lanes - LANES), jnp.float32)
                 chunk = jnp.concatenate([chunk, spare], axis=1)
-            shift = (first_cell - (index % 2) * HALF) % lanes
+            shift = (first_cell - (index % 3) * SLOT) % lanes
             moved = chunk if shift == 0 else pltpu.roll(chunk, shift, 1)
             sums[index] = sums[index] + jnp.where(here, moved, 0.0)
     trace = sums[0]
@@ -599,7 +634,7 @@
 
     def columns_of(part):
         values = joined(chunks[part, at_sums:, :].astype(jnp.float32))
-        slots = range(2 * height, 2 * height + 2 * GHOST * (lanes // LANES), 2 * GHOST)
+        slots = range(height + 4, height + 4 + 2 * GHOST * (lanes // LANES), 2 * GHOST)
         return jnp.concatenate([values[at : at + 2 * GHOST] for at in slots], axis=1)
 
     before = columns_of(lax.rem(layer + parts - 1, parts))
@@ -728,20 +763,28 @@
     )(own, x_parts, z_parts, *[fixed(values) for values in constants])
 
     products_x, voxels = own_columns(count)
+    chunk_shape = (depths, voxels + fold(voxels) + 48, LANES)
     chunks = pl.pallas_call(
         functools.partial(late_kernel, late_starts),
         name="late",
-        out_shape=pltpu.VMEM((depths, voxels + fold(voxels) + 64, LANES), bf16),
+        out_shape=pltpu.HBM(chunk_shape, bf16),
+        in_specs=[vmem] * 9,
+        out_specs=stay,
         scratch_shapes=[pltpu.VMEM((rows // 2, width + 2 * EDGE, 2 * depth), bf16)]
         + scratch(late)
-        + [pltpu.VMEM((late, LANES), jnp.float32)],
+        + [
+            pltpu.VMEM((late, LANES), jnp.float32),
+            pltpu.VMEM(chunk_shape, bf16),
+            pltpu.SemaphoreType.DMA((2,)),
+        ],
         cost_estimate=cost(late),
         compiler_params=params,
     )(own, far, near, x_late, z_parts, diagonal, early_sums, temp, cure)
 
     faces = plan.reshape(2 * STEPS, 1) == jnp.arange(tool_levels.shape[0], dtype=jnp.int32)
-    tools = jnp.sum(jnp.where(faces, tool_levels, jnp.zeros_like(tool_levels)), axis=1)
-    tools = jnp.broadcast_to(tools[:, None], (2 * STEPS, lanes))
+    tools = jnp.sum(
+        jnp.where(faces, tool_levels, jnp.zeros_like(tool_levels)), axis=1, keepdims=True
+    )
 
     chunks = lax.all_to_all(chunks, "depth", split_axis=0, concat_axis=0, tiled=True)
 

time: 25.2 us -> 24 us (0.952)
  waiting for transfers between devices: 6.61 us -> 5.75 us
  Pallas kernels: 6.66 us -> 6.31 us
    all_to_all x1, waiting for transfers between devices: 6.6 us -> 5.75 us  [on_device(): lax.all_to_all(chunks, 'depth', split_axis=0, concat_axis=0, tiled=True)]
    pallas_call x1, Pallas kernels: 2.51 us -> 2.18 us  [on_device(): pl.pallas_call(functools.partial(late_kernel, late_starts), name='late',...]
  transfers between devices with their start and end apart: 3 -> 3, of which waited for: 1 -> 1; matrix products, arithmetic and copies ran while one was open for 1% -> 2% of each run, Pallas kernels for 6% -> 6%
where the time goes in v10:
time: 24 us; the launch traced here: 23.7 us
  starting transfers between devices  9.91 us (41%)
  Pallas kernels  6.31 us (26%)
  waiting for transfers between devices  5.75 us (24%)
  local copies, waits for them, and re-layouts  0.85 us (4%)
  between operations  0.69 us (3%)
    all_to_all x1, waiting for transfers between devices, on_device(): lax.all_to_all(chunks, 'depth', split_axis=0, concat_axis=0, tiled=True)  5.75 us
    ppermute x2, starting transfers between devices, moved(): return lax.ppermute(values, ('plane', 'depth'), index)  5.03 us
    all_to_all x1, starting transfers between devices, on_device(): lax.all_to_all(chunks, 'depth', split_axis=0, concat_axis=0, tiled=True)  4.89 us
    pallas_call x1, Pallas kernels, on_device(): pl.pallas_call(functools.partial(late_kernel, late_starts), name='late',...  2.18 us
    pallas_call x1, Pallas kernels, on_device(): pl.pallas_call(functools.partial(cure_kernel, cells, rim_starts), name='c...  1.53 us
    pallas_call x1, Pallas kernels, on_device(): pl.pallas_call(functools.partial(early_kernel, early_starts), name='early...  1.45 us
    pallas_call x1, Pallas kernels, on_device(): pl.pallas_call(pack_kernel, name='pack', out_shape=(pltpu.VMEM((slots, de...  1.16 us
    unnamed x5, local copies, waits for them, and re-layouts  0.67 us
  transfers between devices with their start and end apart: 3, of which 1 were waited for; matrix products, arithmetic and copies ran while one was open for 2% of the time, Pallas kernels for 6%

profile of v10, /device:TPU:0, one launch (start us, length us, event | category | flops | bytes accessed | tf_op | source)
XLA Modules:
  0.0 23.7 jit_solution(8036936956411558542)
XLA Ops:
  0.6 1.2 %pack.1 = (bf16[208,128]{1,0:T(8,128)(2,1)S(1)}, bf16[208,128]{1,0:T(8,128)(2,1)S(1)}, bf16[4,96,256]{2,1,0:T(8,128)(2,1)S(1)}, bf16[192,96]{1,0:T(8,128)(2,1)S(...) custom-call(s32[8,96,128]{2,1,0:T(8,128)} %intensity.1, f32[6,128]{1,0:T(8,128)} %temp_hbm.1, ...), custom_call_target="tpu_custom_call" | custom-call | tf_op jit(solution)/shard_map/pack/pallas_call | solution.py:702
  1.8 0.7 %collective-permute-start = (bf16[208,128]{1,0:T(8,128)(2,1)S(1)}, bf16[208,128]{1,0:T(8,128)(2,1)S(1)}, u32[]{:S(2)}, u32[]{:S(2)}) collective-permute-start(bf16[208,128]{1,0:T(8,128)(2,1)S(1)} %get-tuple-element.17), channel_id=1, source_target_pairs={{4,8},{5,9},{6,10},{7,11},{12,16},{13,17},{14,18},{15,19},{20,24},... | collective-permute-start | bytes 159752 | tf_op jit(solution)/shard_map/ppermute | solution.py:724
  2.5 4.4 %collective-permute-start.1 = (bf16[208,128]{1,0:T(8,128)(2,1)S(1)}, bf16[208,128]{1,0:T(8,128)(2,1)S(1)}, u32[]{:S(2)}, u32[]{:S(2)}) collective-permute-start(bf16[208,128]{1,0:T(8,128)(2,1)S(1)} %get-tuple-element.18), channel_id=1, source_target_pairs={{0,4},{1,5},{2,6},{3,7},{8,12},{9,13},{10,14},{11,15},{16,20},{17,... | collective-permute-start | bytes 159752 | tf_op jit(solution)/shard_map/ppermute | solution.py:724
  6.8 1.4 %early.1 = (f32[192,128]{1,0:T(8,128)S(1)}, bf16[512,256]{1,0:T(8,128)(2,1)S(1)}, bf16[160,144]{1,0:T(8,128)(2,1)S(1)}, bf16[384,256]{1,0:T(8,128)(2,1)S(1)}, bf...) custom-call(bf16[4,96,256]{2,1,0:T(8,128)(2,1)S(1)} %get-tuple-element.16.refs_0_.own, ...), custom_call_target="tpu_custom_call" | custom-call | flops 209715200 | bytes 4000000 | tf_op jit(solution)/shard_map/early/pallas_call | solution.py:751
  8.3 0.0 collective-permute-done.far
  8.3 0.0 collective-permute-done.1.near
  8.3 2.2 %late.1 = bf16[4,160,128]{2,1,0:T(8,128)(2,1)} custom-call(bf16[4,96,256]{2,1,0:T(8,128)(2,1)S(1)} %get-tuple-element.16.refs_0_.own, bf16[208,128]{1,0:T(8,128)(2,1)S(1)} %collective-permute-done.far, bf16[208,128]{1,0:T(8,128)(2,1)S(1)} %collective-permute-done.1.near, bf16[160,144]{1,0:T(8,128)(2,1)S(1)} %get-tuple-element.21.x_late, ...), custom_call_target="tpu_custom_call" | custom-call | flops 167772160 | bytes 4000000 | tf_op jit(solution)/shard_map/late/pallas_call | solution.py:767
  10.5 0.0 copy-start
  10.5 4.9 %all-to-all-start = ((bf16[4,160,128]{2,1,0:T(8,128)(2,1)}), bf16[4,160,128]{2,1,0:T(8,128)(2,1)S(1)}, u32[]{:S(2)}, u32[]{:S(2)}) async-start(bf16[4,160,128]{2,1,0:T(8,128)(2,1)} %late.1), calls=%async_computation | async-start | bytes 327680 | tf_op jit(solution)/shard_map/all_to_all | solution.py:789
  15.4 0.0 copy-done
  15.4 0.1 copy.18
  15.5 0.0 copy-start.1
  15.5 0.1 eq.15
  15.6 0.6 %copy-done.1 = f32[8]{0:T(128)S(1)} copy-done((f32[8]{0:T(128)S(1)}, f32[8]{0:T(128)}, u32[]{:S(2)}) %copy-start.1) | copy-done | bytes 56
  16.1 0.2 select_reduce_fusion
  16.3 0.1 copy.19.tools
  16.4 5.7 %all-to-all-done.chunks = bf16[4,160,128]{2,1,0:T(8,128)(2,1)S(1)} async-done(((bf16[4,160,128]{2,1,0:T(8,128)(2,1)}), bf16[4,160,128]{2,1,0:T(8,128)(2,1)S(1)}, u32[]{:S(2)}, u32[]{:S(2)}) %all-to-all-start) | async-done | bytes 163872 | tf_op jit(solution)/shard_map/all_to_all | solution.py:789
  22.2 1.5 %cure.1 = (f32[6,128]{1,0:T(8,128)}, f32[6,128]{1,0:T(8,128)}, f32[3,6,128]{2,1,0:T(8,128)}) custom-call(bf16[4,160,128]{2,1,0:T(8,128)(2,1)S(1)} %all-to-all-done.chunks, f32[6,128]{1,0:T(8,128)S(1)} %get-tuple-element.24.temp.temp_in, f32[6,128]{1,0:T(8,128)S(1)} %get-tuple-element.25.cure.cure_in, f32[6,1]{1,0:T(8,128)S(1)} %copy.19.tools, ...), custom_call_target="tpu_custom_call" | custom-call | tf_op jit(solution)/shard_map/cure/pallas_call | solution.py:791
Async XLA Ops:
  1.8 6.5 %collective-permute-start = (bf16[208,128]{1,0:T(8,128)(2,1)S(1)}, bf16[208,128]{1,0:T(8,128)(2,1)S(1)}, u32[]{:S(2)}, u32[]{:S(2)}) collective-permute-start(bf16[208,128]{1,0:T(8,128)(2,1)S(1)} %get-tuple-element.17), channel_id=1, source_target_pairs={{4,8},{5,9},{6,10},{7,11},{12,16},{13,17},{14,18},{15,19},{20,24},... | collective-permute-start | bytes 159752 | tf_op jit(solution)/shard_map/ppermute | solution.py:724
  2.5 5.8 %collective-permute-start.1 = (bf16[208,128]{1,0:T(8,128)(2,1)S(1)}, bf16[208,128]{1,0:T(8,128)(2,1)S(1)}, u32[]{:S(2)}, u32[]{:S(2)}) collective-permute-start(bf16[208,128]{1,0:T(8,128)(2,1)S(1)} %get-tuple-element.18), channel_id=1, source_target_pairs={{0,4},{1,5},{2,6},{3,7},{8,12},{9,13},{10,14},{11,15},{16,20},{17,... | collective-permute-start | bytes 159752 | tf_op jit(solution)/shard_map/ppermute | solution.py:724
  10.5 4.9 %copy-start = (s32[3,2]{0,1:T(2,128)S(1)}, s32[3,2]{0,1:T(2,128)}, u32[]{:S(2)}) copy-start(s32[3,2]{0,1:T(2,128)} %param.15) | copy-start | bytes 76
  10.5 11.7 %all-to-all-start = ((bf16[4,160,128]{2,1,0:T(8,128)(2,1)}), bf16[4,160,128]{2,1,0:T(8,128)(2,1)S(1)}, u32[]{:S(2)}, u32[]{:S(2)}) async-start(bf16[4,160,128]{2,1,0:T(8,128)(2,1)} %late.1), calls=%async_computation | async-start | bytes 327680 | tf_op jit(solution)/shard_map/all_to_all | solution.py:789
  15.5 0.7 %copy-start.1 = (f32[8]{0:T(128)S(1)}, f32[8]{0:T(128)}, u32[]{:S(2)}) copy-start(f32[8]{0:T(128)} %param.14) | copy-start | bytes 100

commit v11 on v10

--- a/solution.py
+++ b/solution.py
@@ -152,6 +152,11 @@
                     for row in range(rows):
                         bands[boundary, row * 2 * R1 + R1 + place, cell] += weights[row] * value
     return bands.reshape(-1, bands.shape[2])
+
+
+def meeting_order(blocks):
+    middle = blocks // 2
+    return [middle, *range(middle + 1, blocks), *range(middle - 1, -1, -1)]
 
 
 def own_columns(count):
@@ -478,7 +483,8 @@
 
     height = count + 2 * HALO
     half_lane = lax.broadcasted_iota(jnp.int32, (folded, LANES), 1) < HALF
-    for target in range(out.shape[0]):
+    order = meeting_order(out.shape[0])
+    for position, target in enumerate(order):
         at = stride * target
         second = jnp.where(
             half_lane,
@@ -486,7 +492,7 @@
             tiles[2][at + voxels - folded : at + voxels],
         )
         rims = jnp.concatenate([tiles[0][at : at + voxels], second], axis=0)
-        out[target, 0 : voxels + folded, :] = rims.astype(jnp.bfloat16)
+        out[position, 0 : voxels + folded, :] = rims.astype(jnp.bfloat16)
     split = (pl.ds(0, voxels + folded), pl.ds(voxels + folded, out.shape[1] - voxels - folded))
     copies = [
         pltpu.make_async_copy(out.at[:, part, :], out_hbm.at[:, part, :], sems.at[index])
@@ -510,7 +516,7 @@
     xz = [total[5]] + [pltpu.roll(total[5], index * SLOT, 1) for index in range(1, 3)]
 
     own_first, own_last = column_rows(temp, cure, 0), column_rows(temp, cure, count - GHOST)
-    for target in range(out.shape[0]):
+    for position, target in enumerate(order):
         piece = jnp.where(layer == target - 1, own_last, 0.0)
         piece = jnp.where(layer == target + 1, own_first, piece)
         if target == 0:
@@ -533,7 +539,7 @@
         if filled < 24:
             pieces.append(jnp.zeros((24 - filled, LANES), jnp.float32))
         sent = two_parts(jnp.concatenate(pieces, axis=0))
-        out[target, voxels + folded :, :] = sent.astype(jnp.bfloat16)
+        out[position, voxels + folded :, :] = sent.astype(jnp.bfloat16)
     copies[1].start()
     for copy in copies:
         copy.wait()
@@ -546,8 +552,9 @@
     tall = -(-voxels // 16) * 16
     spare = [jnp.zeros((tall - voxels, LANES), jnp.float32)] if tall > voxels else []
     tiles = []
+    order = meeting_order(parts)
     for part in range(parts):
-        rims = chunks[part, 0 : voxels + folded, :].astype(jnp.float32)
+        rims = chunks[order.index(part), 0 : voxels + folded, :].astype(jnp.float32)
         second = rims[voxels:]
         second = [second[: voxels - folded], pltpu.roll(second, HALF, 1)]
         for tile in ([rims[:voxels]], second):
@@ -597,13 +604,16 @@
     lane = lax.broadcasted_iota(jnp.int32, (16, lanes), 1)
     row = lax.broadcasted_iota(jnp.int32, (16, lanes), 0)
     at_sums = chunks.shape[1] - 48
+    order = meeting_order(parts)
 
     near = rim_sums(chunks, count, starts, flat, steep, rim_bands)
     sums = [near[0] + near[1] + near[2], near[1], near[2], near[5]]
+    blocks = []
     for part in range(parts):
         first_cell = own * part - BEFORE
         here = (lane >= first_cell) & (lane < first_cell + cells)
-        values = joined(chunks[part, at_sums:, :].astype(jnp.float32))
+        values = joined(chunks[order.index(part), at_sums:, :].astype(jnp.float32))
+        blocks.append(values)
         xz = values[height : height + 4]
         xz = [xz] + [pltpu.roll(xz, LANES - index * SLOT, 1) for index in range(1, 3)]
         spare = jnp.zeros((4, LANES), jnp.float32)
@@ -632,13 +642,14 @@
     ]
     copies[0].start()
 
-    def columns_of(part):
-        values = joined(chunks[part, at_sums:, :].astype(jnp.float32))
-        slots = range(height + 4, height + 4 + 2 * GHOST * (lanes // LANES), 2 * GHOST)
-        return jnp.concatenate([values[at : at + 2 * GHOST] for at in slots], axis=1)
-
-    before = columns_of(lax.rem(layer + parts - 1, parts))
-    after = columns_of(lax.rem(layer + 1, parts))
+    slots = range(height + 4, height + 4 + 2 * GHOST * (lanes // LANES), 2 * GHOST)
+    columns = [
+        jnp.concatenate([values[at : at + 2 * GHOST] for at in slots], axis=1) for values in blocks
+    ]
+    before, after = columns[parts - 1], columns[0]
+    for part in range(parts - 1):
+        before = jnp.where(layer == part + 1, columns[part], before)
+        after = jnp.where(layer == part, columns[part + 1], after)
     spare = jnp.full((16 - count - 2 * GHOST, lanes), 0.5, jnp.float32)
     temp = jnp.concatenate([before[:GHOST], temp_in[...], after[:GHOST], 8.0 * spare], axis=0)
     cure = jnp.concatenate([before[GHOST:], cure_in[...], after[GHOST:], spare], axis=0)
@@ -786,7 +797,14 @@
         jnp.where(faces, tool_levels, jnp.zeros_like(tool_levels)), axis=1, keepdims=True
     )
 
-    chunks = lax.all_to_all(chunks, "depth", split_axis=0, concat_axis=0, tiled=True)
+    chunks = lax.all_to_all(
+        chunks,
+        "depth",
+        split_axis=0,
+        concat_axis=0,
+        tiled=True,
+        axis_index_groups=[meeting_order(depths)],
+    )
 
     return pl.pallas_call(
         functools.partial(cure_kernel, cells, rim_starts),

time: 24 us -> 23.3 us (0.971)
  waiting for transfers between devices: 5.75 us -> 4.11 us
  starting transfers between devices: 9.91 us -> 10.9 us
    all_to_all x1, waiting for transfers between devices: 5.75 us -> 4.1 us  [on_device(): lax.all_to_all(chunks, 'depth', split_axis=0, concat_axis=0, tiled=True,...]
    all_to_all x1, starting transfers between devices: 4.89 us -> 5.92 us  [on_device(): lax.all_to_all(chunks, 'depth', split_axis=0, concat_axis=0, tiled=True,...]
where the time goes in v11:
time: 23.3 us; the launch traced here: 23.1 us
  starting transfers between devices  10.9 us (47%)
  Pallas kernels  6.31 us (27%)
  waiting for transfers between devices  4.11 us (18%)
  local copies, waits for them, and re-layouts  0.85 us (4%)
  between operations  0.69 us (3%)
    all_to_all x1, starting transfers between devices, on_device(): lax.all_to_all(chunks, 'depth', split_axis=0, concat_axis=0, tiled=True,...  5.92 us
    ppermute x2, starting transfers between devices, moved(): return lax.ppermute(values, ('plane', 'depth'), index)  5.03 us
    all_to_all x1, waiting for transfers between devices, on_device(): lax.all_to_all(chunks, 'depth', split_axis=0, concat_axis=0, tiled=True,...  4.1 us
    pallas_call x1, Pallas kernels, on_device(): pl.pallas_call(functools.partial(late_kernel, late_starts), name='late',...  2.18 us
    pallas_call x1, Pallas kernels, on_device(): pl.pallas_call(functools.partial(cure_kernel, cells, rim_starts), name='c...  1.52 us
    pallas_call x1, Pallas kernels, on_device(): pl.pallas_call(functools.partial(early_kernel, early_starts), name='early...  1.45 us
    pallas_call x1, Pallas kernels, on_device(): pl.pallas_call(pack_kernel, name='pack', out_shape=(pltpu.VMEM((slots, de...  1.16 us
    unnamed x5, local copies, waits for them, and re-layouts  0.67 us
  transfers between devices with their start and end apart: 3, of which 1 were waited for; matrix products, arithmetic and copies ran while one was open for 2% of the time, Pallas kernels for 6%

profile of v11, /device:TPU:0, one launch (start us, length us, event | category | flops | bytes accessed | tf_op | source)
XLA Modules:
  0.0 23.1 jit_solution(9929079250191926494)
XLA Ops:
  0.6 1.2 %pack.1 = (bf16[208,128]{1,0:T(8,128)(2,1)S(1)}, bf16[208,128]{1,0:T(8,128)(2,1)S(1)}, bf16[4,96,256]{2,1,0:T(8,128)(2,1)S(1)}, bf16[192,96]{1,0:T(8,128)(2,1)S(...) custom-call(s32[8,96,128]{2,1,0:T(8,128)} %intensity.1, f32[6,128]{1,0:T(8,128)} %temp_hbm.1, ...), custom_call_target="tpu_custom_call" | custom-call | tf_op jit(solution)/shard_map/pack/pallas_call | solution.py:713
  1.8 0.7 %collective-permute-start = (bf16[208,128]{1,0:T(8,128)(2,1)S(1)}, bf16[208,128]{1,0:T(8,128)(2,1)S(1)}, u32[]{:S(2)}, u32[]{:S(2)}) collective-permute-start(bf16[208,128]{1,0:T(8,128)(2,1)S(1)} %get-tuple-element.17), channel_id=1, source_target_pairs={{4,8},{5,9},{6,10},{7,11},{12,16},{13,17},{14,18},{15,19},{20,24},... | collective-permute-start | bytes 159752 | tf_op jit(solution)/shard_map/ppermute | solution.py:735
  2.5 4.4 %collective-permute-start.1 = (bf16[208,128]{1,0:T(8,128)(2,1)S(1)}, bf16[208,128]{1,0:T(8,128)(2,1)S(1)}, u32[]{:S(2)}, u32[]{:S(2)}) collective-permute-start(bf16[208,128]{1,0:T(8,128)(2,1)S(1)} %get-tuple-element.18), channel_id=1, source_target_pairs={{0,4},{1,5},{2,6},{3,7},{8,12},{9,13},{10,14},{11,15},{16,20},{17,... | collective-permute-start | bytes 159752 | tf_op jit(solution)/shard_map/ppermute | solution.py:735
  6.8 1.4 %early.1 = (f32[192,128]{1,0:T(8,128)S(1)}, bf16[512,256]{1,0:T(8,128)(2,1)S(1)}, bf16[160,144]{1,0:T(8,128)(2,1)S(1)}, bf16[384,256]{1,0:T(8,128)(2,1)S(1)}, bf...) custom-call(bf16[4,96,256]{2,1,0:T(8,128)(2,1)S(1)} %get-tuple-element.16.refs_0_.own, ...), custom_call_target="tpu_custom_call" | custom-call | flops 209715200 | bytes 4000000 | tf_op jit(solution)/shard_map/early/pallas_call | solution.py:762
  8.3 0.0 collective-permute-done.far
  8.3 0.0 collective-permute-done.1.near
  8.3 2.2 %late.1 = bf16[4,160,128]{2,1,0:T(8,128)(2,1)} custom-call(bf16[4,96,256]{2,1,0:T(8,128)(2,1)S(1)} %get-tuple-element.16.refs_0_.own, bf16[208,128]{1,0:T(8,128)(2,1)S(1)} %collective-permute-done.far, bf16[208,128]{1,0:T(8,128)(2,1)S(1)} %collective-permute-done.1.near, bf16[160,144]{1,0:T(8,128)(2,1)S(1)} %get-tuple-element.21.x_late, ...), custom_call_target="tpu_custom_call" | custom-call | flops 167772160 | bytes 4000000 | tf_op jit(solution)/shard_map/late/pallas_call | solution.py:778
  10.5 0.0 copy-start
  10.5 5.9 %all-to-all-start = ((bf16[4,160,128]{2,1,0:T(8,128)(2,1)}), bf16[4,160,128]{2,1,0:T(8,128)(2,1)S(1)}, u32[]{:S(2)}, u32[]{:S(2)}) async-start(bf16[4,160,128]{2,1,0:T(8,128)(2,1)} %late.1), calls=%async_computation | async-start | bytes 327680 | tf_op jit(solution)/shard_map/all_to_all | solution.py:800
  16.4 0.0 copy-done
  16.4 0.1 copy.18
  16.5 0.0 copy-start.1
  16.5 0.1 eq.15
  16.6 0.6 %copy-done.1 = f32[8]{0:T(128)S(1)} copy-done((f32[8]{0:T(128)S(1)}, f32[8]{0:T(128)}, u32[]{:S(2)}) %copy-start.1) | copy-done | bytes 56
  17.2 0.2 select_reduce_fusion
  17.4 0.1 copy.19.tools
  17.5 4.1 %all-to-all-done.chunks = bf16[4,160,128]{2,1,0:T(8,128)(2,1)S(1)} async-done(((bf16[4,160,128]{2,1,0:T(8,128)(2,1)}), bf16[4,160,128]{2,1,0:T(8,128)(2,1)S(1)}, u32[]{:S(2)}, u32[]{:S(2)}) %all-to-all-start) | async-done | bytes 163872 | tf_op jit(solution)/shard_map/all_to_all | solution.py:800
  21.6 1.5 %cure.1 = (f32[6,128]{1,0:T(8,128)}, f32[6,128]{1,0:T(8,128)}, f32[3,6,128]{2,1,0:T(8,128)}) custom-call(bf16[4,160,128]{2,1,0:T(8,128)(2,1)S(1)} %all-to-all-done.chunks, f32[6,128]{1,0:T(8,128)S(1)} %get-tuple-element.24.temp.temp_in, f32[6,128]{1,0:T(8,128)S(1)} %get-tuple-element.25.cure.cure_in, f32[6,1]{1,0:T(8,128)S(1)} %copy.19.tools, ...), custom_call_target="tpu_custom_call" | custom-call | tf_op jit(solution)/shard_map/cure/pallas_call | solution.py:809
Async XLA Ops:
  1.8 6.5 %collective-permute-start = (bf16[208,128]{1,0:T(8,128)(2,1)S(1)}, bf16[208,128]{1,0:T(8,128)(2,1)S(1)}, u32[]{:S(2)}, u32[]{:S(2)}) collective-permute-start(bf16[208,128]{1,0:T(8,128)(2,1)S(1)} %get-tuple-element.17), channel_id=1, source_target_pairs={{4,8},{5,9},{6,10},{7,11},{12,16},{13,17},{14,18},{15,19},{20,24},... | collective-permute-start | bytes 159752 | tf_op jit(solution)/shard_map/ppermute | solution.py:735
  2.5 5.8 %collective-permute-start.1 = (bf16[208,128]{1,0:T(8,128)(2,1)S(1)}, bf16[208,128]{1,0:T(8,128)(2,1)S(1)}, u32[]{:S(2)}, u32[]{:S(2)}) collective-permute-start(bf16[208,128]{1,0:T(8,128)(2,1)S(1)} %get-tuple-element.18), channel_id=1, source_target_pairs={{0,4},{1,5},{2,6},{3,7},{8,12},{9,13},{10,14},{11,15},{16,20},{17,... | collective-permute-start | bytes 159752 | tf_op jit(solution)/shard_map/ppermute | solution.py:735
  10.5 5.9 %copy-start = (s32[3,2]{0,1:T(2,128)S(1)}, s32[3,2]{0,1:T(2,128)}, u32[]{:S(2)}) copy-start(s32[3,2]{0,1:T(2,128)} %param.15) | copy-start | bytes 76
  10.5 11.1 %all-to-all-start = ((bf16[4,160,128]{2,1,0:T(8,128)(2,1)}), bf16[4,160,128]{2,1,0:T(8,128)(2,1)S(1)}, u32[]{:S(2)}, u32[]{:S(2)}) async-start(bf16[4,160,128]{2,1,0:T(8,128)(2,1)} %late.1), calls=%async_computation | async-start | bytes 327680 | tf_op jit(solution)/shard_map/all_to_all | solution.py:800
  16.5 0.7 %copy-start.1 = (f32[8]{0:T(128)S(1)}, f32[8]{0:T(128)}, u32[]{:S(2)}) copy-start(f32[8]{0:T(128)} %param.14) | copy-start | bytes 100

commit v12 on v11

--- a/solution.py
+++ b/solution.py
@@ -155,8 +155,7 @@
 
 
 def meeting_order(blocks):
-    middle = blocks // 2
-    return [middle, *range(middle + 1, blocks), *range(middle - 1, -1, -1)]
+    return [*range(blocks - 1, -1, -1)]
 
 
 def own_columns(count):

time: 23.3 us -> 24.3 us (1.043)
  starting transfers between devices: 10.9 us -> 12 us
    all_to_all x1, starting transfers between devices: 5.92 us -> 6.93 us  [on_device(): lax.all_to_all(chunks, 'depth', split_axis=0, concat_axis=0, tiled=True,...]
where the time goes in v12:
time: 24.3 us; the launch traced here: 24.1 us
  starting transfers between devices  12 us (49%)
  Pallas kernels  6.31 us (26%)
  waiting for transfers between devices  4.09 us (17%)
  local copies, waits for them, and re-layouts  0.85 us (3%)
  between operations  0.69 us (3%)
    all_to_all x1, starting transfers between devices, on_device(): lax.all_to_all(chunks, 'depth', split_axis=0, concat_axis=0, tiled=True,...  6.93 us
    ppermute x2, starting transfers between devices, moved(): return lax.ppermute(values, ('plane', 'depth'), index)  5.03 us
    all_to_all x1, waiting for transfers between devices, on_device(): lax.all_to_all(chunks, 'depth', split_axis=0, concat_axis=0, tiled=True,...  4.08 us
    pallas_call x1, Pallas kernels, on_device(): pl.pallas_call(functools.partial(late_kernel, late_starts), name='late',...  2.18 us
    pallas_call x1, Pallas kernels, on_device(): pl.pallas_call(functools.partial(cure_kernel, cells, rim_starts), name='c...  1.52 us
    pallas_call x1, Pallas kernels, on_device(): pl.pallas_call(functools.partial(early_kernel, early_starts), name='early...  1.45 us
    pallas_call x1, Pallas kernels, on_device(): pl.pallas_call(pack_kernel, name='pack', out_shape=(pltpu.VMEM((slots, de...  1.16 us
    unnamed x5, local copies, waits for them, and re-layouts  0.67 us
  transfers between devices with their start and end apart: 3, of which 1 were waited for; matrix products, arithmetic and copies ran while one was open for 2% of the time, Pallas kernels for 6%

profile of v12, /device:TPU:0, one launch (start us, length us, event | category | flops | bytes accessed | tf_op | source)
XLA Modules:
  0.0 24.1 jit_solution(16614599404885789016)
XLA Ops:
  0.6 1.2 %pack.1 = (bf16[208,128]{1,0:T(8,128)(2,1)S(1)}, bf16[208,128]{1,0:T(8,128)(2,1)S(1)}, bf16[4,96,256]{2,1,0:T(8,128)(2,1)S(1)}, bf16[192,96]{1,0:T(8,128)(2,1)S(...) custom-call(s32[8,96,128]{2,1,0:T(8,128)} %intensity.1, f32[6,128]{1,0:T(8,128)} %temp_hbm.1, ...), custom_call_target="tpu_custom_call" | custom-call | tf_op jit(solution)/shard_map/pack/pallas_call | solution.py:712
  1.8 0.7 %collective-permute-start = (bf16[208,128]{1,0:T(8,128)(2,1)S(1)}, bf16[208,128]{1,0:T(8,128)(2,1)S(1)}, u32[]{:S(2)}, u32[]{:S(2)}) collective-permute-start(bf16[208,128]{1,0:T(8,128)(2,1)S(1)} %get-tuple-element.17), channel_id=1, source_target_pairs={{4,8},{5,9},{6,10},{7,11},{12,16},{13,17},{14,18},{15,19},{20,24},... | collective-permute-start | bytes 159752 | tf_op jit(solution)/shard_map/ppermute | solution.py:734
  2.5 4.4 %collective-permute-start.1 = (bf16[208,128]{1,0:T(8,128)(2,1)S(1)}, bf16[208,128]{1,0:T(8,128)(2,1)S(1)}, u32[]{:S(2)}, u32[]{:S(2)}) collective-permute-start(bf16[208,128]{1,0:T(8,128)(2,1)S(1)} %get-tuple-element.18), channel_id=1, source_target_pairs={{0,4},{1,5},{2,6},{3,7},{8,12},{9,13},{10,14},{11,15},{16,20},{17,... | collective-permute-start | bytes 159752 | tf_op jit(solution)/shard_map/ppermute | solution.py:734
  6.8 1.4 %early.1 = (f32[192,128]{1,0:T(8,128)S(1)}, bf16[512,256]{1,0:T(8,128)(2,1)S(1)}, bf16[160,144]{1,0:T(8,128)(2,1)S(1)}, bf16[384,256]{1,0:T(8,128)(2,1)S(1)}, bf...) custom-call(bf16[4,96,256]{2,1,0:T(8,128)(2,1)S(1)} %get-tuple-element.16.refs_0_.own, ...), custom_call_target="tpu_custom_call" | custom-call | flops 209715200 | bytes 4000000 | tf_op jit(solution)/shard_map/early/pallas_call | solution.py:761
  8.3 0.0 collective-permute-done.far
  8.3 0.0 collective-permute-done.1.near
  8.3 2.2 %late.1 = bf16[4,160,128]{2,1,0:T(8,128)(2,1)} custom-call(bf16[4,96,256]{2,1,0:T(8,128)(2,1)S(1)} %get-tuple-element.16.refs_0_.own, bf16[208,128]{1,0:T(8,128)(2,1)S(1)} %collective-permute-done.far, bf16[208,128]{1,0:T(8,128)(2,1)S(1)} %collective-permute-done.1.near, bf16[160,144]{1,0:T(8,128)(2,1)S(1)} %get-tuple-element.21.x_late, ...), custom_call_target="tpu_custom_call" | custom-call | flops 167772160 | bytes 4000000 | tf_op jit(solution)/shard_map/late/pallas_call | solution.py:777
  10.5 0.0 copy-start
  10.5 6.9 %all-to-all-start = ((bf16[4,160,128]{2,1,0:T(8,128)(2,1)}), bf16[4,160,128]{2,1,0:T(8,128)(2,1)S(1)}, u32[]{:S(2)}, u32[]{:S(2)}) async-start(bf16[4,160,128]{2,1,0:T(8,128)(2,1)} %late.1), calls=%async_computation | async-start | bytes 327680 | tf_op jit(solution)/shard_map/all_to_all | solution.py:799
  17.4 0.0 copy-done
  17.4 0.1 copy.18
  17.5 0.0 copy-start.1
  17.5 0.1 eq.15
  17.6 0.6 %copy-done.1 = f32[8]{0:T(128)S(1)} copy-done((f32[8]{0:T(128)S(1)}, f32[8]{0:T(128)}, u32[]{:S(2)}) %copy-start.1) | copy-done | bytes 56
  18.2 0.2 select_reduce_fusion
  18.4 0.1 copy.19.tools
  18.5 4.1 %all-to-all-done.chunks = bf16[4,160,128]{2,1,0:T(8,128)(2,1)S(1)} async-done(((bf16[4,160,128]{2,1,0:T(8,128)(2,1)}), bf16[4,160,128]{2,1,0:T(8,128)(2,1)S(1)}, u32[]{:S(2)}, u32[]{:S(2)}) %all-to-all-start) | async-done | bytes 163872 | tf_op jit(solution)/shard_map/all_to_all | solution.py:799
  22.6 1.5 %cure.1 = (f32[6,128]{1,0:T(8,128)}, f32[6,128]{1,0:T(8,128)}, f32[3,6,128]{2,1,0:T(8,128)}) custom-call(bf16[4,160,128]{2,1,0:T(8,128)(2,1)S(1)} %all-to-all-done.chunks, f32[6,128]{1,0:T(8,128)S(1)} %get-tuple-element.24.temp.temp_in, f32[6,128]{1,0:T(8,128)S(1)} %get-tuple-element.25.cure.cure_in, f32[6,1]{1,0:T(8,128)S(1)} %copy.19.tools, ...), custom_call_target="tpu_custom_call" | custom-call | tf_op jit(solution)/shard_map/cure/pallas_call | solution.py:808
Async XLA Ops:
  1.8 6.5 %collective-permute-start = (bf16[208,128]{1,0:T(8,128)(2,1)S(1)}, bf16[208,128]{1,0:T(8,128)(2,1)S(1)}, u32[]{:S(2)}, u32[]{:S(2)}) collective-permute-start(bf16[208,128]{1,0:T(8,128)(2,1)S(1)} %get-tuple-element.17), channel_id=1, source_target_pairs={{4,8},{5,9},{6,10},{7,11},{12,16},{13,17},{14,18},{15,19},{20,24},... | collective-permute-start | bytes 159752 | tf_op jit(solution)/shard_map/ppermute | solution.py:734
  2.5 5.8 %collective-permute-start.1 = (bf16[208,128]{1,0:T(8,128)(2,1)S(1)}, bf16[208,128]{1,0:T(8,128)(2,1)S(1)}, u32[]{:S(2)}, u32[]{:S(2)}) collective-permute-start(bf16[208,128]{1,0:T(8,128)(2,1)S(1)} %get-tuple-element.18), channel_id=1, source_target_pairs={{0,4},{1,5},{2,6},{3,7},{8,12},{9,13},{10,14},{11,15},{16,20},{17,... | collective-permute-start | bytes 159752 | tf_op jit(solution)/shard_map/ppermute | solution.py:734
  10.5 6.9 %copy-start = (s32[3,2]{0,1:T(2,128)S(1)}, s32[3,2]{0,1:T(2,128)}, u32[]{:S(2)}) copy-start(s32[3,2]{0,1:T(2,128)} %param.15) | copy-start | bytes 76
  10.5 12.0 %all-to-all-start = ((bf16[4,160,128]{2,1,0:T(8,128)(2,1)}), bf16[4,160,128]{2,1,0:T(8,128)(2,1)S(1)}, u32[]{:S(2)}, u32[]{:S(2)}) async-start(bf16[4,160,128]{2,1,0:T(8,128)(2,1)} %late.1), calls=%async_computation | async-start | bytes 327680 | tf_op jit(solution)/shard_map/all_to_all | solution.py:799
  17.5 0.7 %copy-start.1 = (f32[8]{0:T(128)S(1)}, f32[8]{0:T(128)}, u32[]{:S(2)}) copy-start(f32[8]{0:T(128)} %param.14) | copy-start | bytes 100

commit v13 on v11

--- a/solution.py
+++ b/solution.py
@@ -256,16 +256,24 @@
     grey, sems,
 ):
     rows, width, depth = intensity.shape
+    parts = [(0, EDGE), (width - EDGE, EDGE), (EDGE, width - 2 * EDGE)]
     copies = [
-        pltpu.make_async_copy(intensity, grey, sems.at[0]),
-        pltpu.make_async_copy(temp_hbm, temp, sems.at[1]),
-        pltpu.make_async_copy(cure_hbm, cure, sems.at[2]),
-        pltpu.make_async_copy(x_hbm, x_parts, sems.at[3]),
-        pltpu.make_async_copy(z_hbm, z_parts, sems.at[4]),
+        pltpu.make_async_copy(
+            intensity.at[:, pl.ds(*part), :], grey.at[:, pl.ds(*part), :], sems.at[index]
+        )
+        for index, part in enumerate(parts)
+    ]
+    copies[2:2] = [
+        pltpu.make_async_copy(temp_hbm, temp, sems.at[3]),
+        pltpu.make_async_copy(cure_hbm, cure, sems.at[4]),
+    ]
+    copies += [
+        pltpu.make_async_copy(x_hbm, x_parts, sems.at[5]),
+        pltpu.make_async_copy(z_hbm, z_parts, sems.at[6]),
     ]
     for copy in copies:
         copy.start()
-    for copy in copies:
+    for copy in copies[:4]:
         copy.wait()
     odd = is_odd()
     count = temp.shape[0]
@@ -292,6 +300,8 @@
     def _():
         send(far, near)
 
+    for copy in copies[4:]:
+        copy.wait()
     for row in range(rows):
         half = (row % 2) * depth
         own[row // 2, :, half : half + depth] = grey[row].astype(jnp.float32).astype(jnp.bfloat16)
@@ -355,26 +365,35 @@
     return jnp.where(inside | (row < left), 1.0, 0.0)
 
 
+USED = (0, 1, 2, 5)
+UNUSED = (3, 4)
+
+
 def all_sums(products, coarse, sx):
-    kinds, count, lanes = products.shape
-    side_by_side = jnp.concatenate([products[index] for index in range(kinds)], axis=1)
-    along = product(sx, side_by_side).astype(jnp.bfloat16)
-    parts = [along[:, index * lanes : (index + 1) * lanes] for index in range(kinds)]
-    return product(jnp.concatenate(parts, axis=0), coarse)
-
-
-def tensor_sums(window, bands, sx, mask, diagonal, z_parts, across, filtered, grads, products):
+    sums = [None] * 6
+    for kinds in (USED, UNUSED):
+        tiles = [tile for index in kinds for tile in products[index]]
+        along = product(sx, jnp.concatenate(tiles, axis=1)).astype(jnp.bfloat16)
+        step = along.shape[1] // len(kinds)
+        parts = [along[:, index * step : (index + 1) * step] for index in range(len(kinds))]
+        total = product(jnp.concatenate(parts, axis=0), coarse)
+        high = sx.shape[0]
+        for index, kind in enumerate(kinds):
+            sums[kind] = total[index * high : (index + 1) * high]
+    return sums
+
+
+def tensor_sums(window, bands, sx, mask, diagonal, z_parts, across, filtered, grads):
     pairs, height, double = window.shape
     rows, depth = 2 * pairs, double // 2
     count = bands.shape[0] // 2
-    for pair in range(pairs):
-        across[pair] = product(bands, window[pair])
-
-    def filter_rows(group, carry):
-        start = pl.multiple_of(group * 16, 16)
+    whole = jnp.concatenate([window[pair] for pair in range(pairs)], axis=1)
+    across[...] = product(bands, whole)
+
+    for start in range(0, count, 16):
         kinds = [
             [
-                across[row // 2, pl.ds(kind * count + start, 16), pl.ds((row % 2) * depth, depth)]
+                across[kind * count + start : kind * count + start + 16, row * depth : (row + 1) * depth]
                 for row in range(rows)
             ]
             for kind in range(2)
@@ -384,15 +403,13 @@
             results = mirrored_filter(ROW_KINDS[part], values, True)
             results += mirrored_filter(ROW_KINDS[part], values, False)
             for row, result in enumerate(results):
-                lanes = pl.ds((row % 2) * depth, depth)
-                filtered[part, row // 2, pl.ds(start, 16), lanes] = result.astype(jnp.bfloat16)
-        return carry
-
-    lax.fori_loop(0, count // 16, filter_rows, 0)
-    for part in range(3):
-        at = DEPTH_KINDS[part] * double
-        for pair in range(pairs):
-            grads[part, pair] = product(filtered[part, pair], diagonal[at : at + double, :])
+                at = (part * pairs + row // 2) * count + start
+                lanes = slice((row % 2) * depth, (row % 2 + 1) * depth)
+                filtered[at : at + 16, lanes] = result.astype(jnp.bfloat16)
+
+    at = 2 * pairs * count
+    grads[:at] = product(filtered[:at, :], diagonal[0:double, :])
+    grads[at:] = product(filtered[at:, :], diagonal[double : 2 * double, :])
 
     weights = product_weights(rows)
     layer = lax.axis_index("depth")
@@ -400,29 +417,29 @@
     place = lax.broadcasted_iota(jnp.int32, (16, depth), 1)
     complete = ((place >= R1) | first) & ((place < depth - R1) | last)
     complete = jnp.where(complete, 1.0, 0.0)
-
-    def multiply(group, carry):
-        start = pl.multiple_of(group * 16, 16)
-        inside = complete if mask is None else complete * mask[pl.ds(start, 16), :]
+    groups = [[] for _ in range(6)]
+    for start in range(0, count, 16):
+        inside = complete if mask is None else complete * mask[start : start + 16]
         totals = None
         for row in range(rows):
-            lanes = pl.ds((row % 2) * depth, depth)
-            three = [grads[part, row // 2, pl.ds(start, 16), lanes] for part in range(3)]
+            lanes = slice((row % 2) * depth, (row % 2 + 1) * depth)
+            three = []
+            for part in range(3):
+                at = (part * pairs + row // 2) * count + start
+                three.append(grads[at : at + 16, lanes])
             terms = weighted_products(three, 2.0 * float(weights[row % (rows // 2)]))
             totals = terms if row == 0 else [a + b for a, b in zip(totals, terms)]
         for index in range(6):
-            products[index, pl.ds(start, 16), :] = (totals[index] * inside).astype(jnp.bfloat16)
-        return carry
-
-    lax.fori_loop(0, count // 16, multiply, 0)
+            groups[index].append((totals[index] * inside).astype(jnp.bfloat16))
+    products = [[jnp.concatenate(group, axis=0)] for group in groups]
     return all_sums(products, z_parts[double : double + depth, :], sx)
 
 
 def early_kernel(*refs):
     starts, own, x_parts, z_parts, *rest = refs
-    count = (len(rest) - 7) // 2
-    constants, (sums, diagonal), held = rest[:count], rest[count : count + 2], rest[count + 2 : -5]
-    across, filtered, grads, products, sems = rest[-5:]
+    count = (len(rest) - 6) // 2
+    constants, (sums, diagonal), held = rest[:count], rest[count : count + 2], rest[count + 2 : -4]
+    across, filtered, grads, sems = rest[-4:]
     copies = [
         pltpu.make_async_copy(source, target, sems.at[index])
         for index, (source, target) in enumerate(zip(constants, held))
@@ -440,16 +457,16 @@
             diagonal[at, (1 - half) * depth : (2 - half) * depth] = empty
     bands = x_parts[starts[0] : starts[1], :width]
     sx = x_parts[starts[1] : starts[2], :EARLY]
-    sums[...] = tensor_sums(
-        own, bands, sx, None, diagonal, z_parts, across, filtered, grads, products
-    )
+    results = tensor_sums(own, bands, sx, None, diagonal, z_parts, across, filtered, grads)
+    for index, kind in enumerate(USED):
+        sums[index] = results[kind]
     for copy in copies:
         copy.wait()
 
 
 def late_kernel(
     starts, own, far, near, x_late, z_parts, diagonal, early_sums, temp, cure, out_hbm,
-    window, across, filtered, grads, products, mask, out, sems,
+    window, across, filtered, grads, out, sems,
 ):
     pairs, width, double = own.shape
     rows, depth = 2 * pairs, double // 2
@@ -500,20 +517,18 @@
     ]
     copies[0].start()
 
-    late = across.shape[1] // 2
-    mask[...] = late_mask(late, width)
+    late = across.shape[0] // 2
     bands = x_late[starts[0] : starts[1], :]
     sx = x_late[starts[1] : starts[2], :late]
-    sums = early_sums[...] + tensor_sums(
-        window, bands, sx, mask, diagonal, z_parts, across, filtered, grads, products
+    results = tensor_sums(
+        window, bands, sx, late_mask(late, width), diagonal, z_parts, across, filtered, grads
     )
-    high = sx.shape[0]
-    total = [sums[index * high : (index + 1) * high] for index in range(6)]
-    trace = total[0] + total[1] + total[2]
+    yy, xx, zz, xz = [early_sums[index] + results[kind] for index, kind in enumerate(USED)]
+    trace = yy + xx + zz
     lane = lax.broadcasted_iota(jnp.int32, trace.shape, 1)
-    three = jnp.where(lane < SLOT, trace, pltpu.roll(total[1], SLOT, 1))
-    three = jnp.where(lane < 2 * SLOT, three, pltpu.roll(total[2], 2 * SLOT, 1))
-    xz = [total[5]] + [pltpu.roll(total[5], index * SLOT, 1) for index in range(1, 3)]
+    three = jnp.where(lane < SLOT, trace, pltpu.roll(xx, SLOT, 1))
+    three = jnp.where(lane < 2 * SLOT, three, pltpu.roll(zz, 2 * SLOT, 1))
+    xz = [xz] + [pltpu.roll(xz, index * SLOT, 1) for index in range(1, 3)]
 
     own_first, own_last = column_rows(temp, cure, 0), column_rows(temp, cure, count - GHOST)
     for position, target in enumerate(order):
@@ -579,16 +594,14 @@
     place = lax.rem(lax.broadcasted_iota(jnp.int32, three[0].shape, 0), rows_x)
     place = place + (index * count - HALO) * COARSE - R2
     inside = jnp.where((place >= 0) & (place < total), 1.0, 0.0)
-    wide = []
-    for term in weighted_products(three, inside):
-        term = term.astype(jnp.bfloat16)
-        wide += [term[part * rows_x : (part + 1) * rows_x] for part in range(parts - 1)]
-    sx = steep[starts[2] : starts[3], :rows_x]
-    along = product(sx, jnp.concatenate(wide, axis=1)).astype(jnp.bfloat16)
-    step = (parts - 1) * LANES
-    along = [along[:, kind * step : (kind + 1) * step] for kind in range(6)]
-    sums = product(jnp.concatenate(along, axis=0), cells[...])
-    return [sums[kind * 16 : (kind + 1) * 16] for kind in range(6)]
+    products = [
+        [
+            term[part * rows_x : (part + 1) * rows_x].astype(jnp.bfloat16)
+            for part in range(parts - 1)
+        ]
+        for term in weighted_products(three, inside)
+    ]
+    return all_sums(products, cells[...], steep[starts[2] : starts[3], :rows_x])
 
 
 def cure_kernel(
@@ -725,7 +738,7 @@
         in_specs=[stay] * 5,
         scratch_shapes=[
             pltpu.VMEM((rows, width, depth), jnp.int32),
-            pltpu.SemaphoreType.DMA((5,)),
+            pltpu.SemaphoreType.DMA((7,)),
         ],
         compiler_params=params,
     )(*[fixed(values) for values in (intensity, temp_start, cure_start, x_hbm, z_hbm)])
@@ -746,10 +759,9 @@
 
     def scratch(count):
         return [
-            pltpu.VMEM((rows // 2, 2 * count, 2 * depth), jnp.float32),
-            pltpu.VMEM((3, rows // 2, count, 2 * depth), bf16),
-            pltpu.VMEM((3, rows // 2, count, 2 * depth), jnp.float32),
-            pltpu.VMEM((6, count, depth), bf16),
+            pltpu.VMEM((2 * count, rows * depth), jnp.float32),
+            pltpu.VMEM((3 * rows // 2 * count, 2 * depth), bf16),
+            pltpu.VMEM((3 * rows // 2 * count, 2 * depth), jnp.float32),
         ]
 
     def cost(count):
@@ -763,7 +775,7 @@
         functools.partial(early_kernel, early_starts),
         name="early",
         out_shape=(
-            pltpu.VMEM((6 * high, LANES), jnp.float32),
+            pltpu.VMEM((len(USED), high, LANES), jnp.float32),
             pltpu.VMEM((4 * depth, 2 * depth), bf16),
             *[pltpu.VMEM(values.shape, bf16) for values in constants],
         ),
@@ -784,7 +796,6 @@
         scratch_shapes=[pltpu.VMEM((rows // 2, width + 2 * EDGE, 2 * depth), bf16)]
         + scratch(late)
         + [
-            pltpu.VMEM((late, LANES), jnp.float32),
             pltpu.VMEM(chunk_shape, bf16),
             pltpu.SemaphoreType.DMA((2,)),
         ],

time: 23.3 us -> 22.9 us (0.983)
  Pallas kernels: 6.31 us -> 5.59 us
  waiting for transfers between devices: 4.11 us -> 4.36 us
    pallas_call x1, Pallas kernels: 2.18 us -> 1.66 us  [on_device(): pl.pallas_call(functools.partial(late_kernel, late_starts), name='late',...]
    pallas_call x1, Pallas kernels: 1.45 us -> 1.19 us  [on_device(): pl.pallas_call(functools.partial(early_kernel, early_starts), name='early...]
    all_to_all x1, waiting for transfers between devices: 4.1 us -> 4.35 us  [on_device(): lax.all_to_all(chunks, 'depth', split_axis=0, concat_axis=0, tiled=True,...]
  transfers between devices with their start and end apart: 3 -> 3, of which waited for: 1 -> 1; matrix products, arithmetic and copies ran while one was open for 2% -> 2% of each run, Pallas kernels for 6% -> 5%
where the time goes in v13:
time: 22.9 us; the launch traced here: 22.6 us
  starting transfers between devices  10.9 us (48%)
  Pallas kernels  5.59 us (24%)
  waiting for transfers between devices  4.36 us (19%)
  local copies, waits for them, and re-layouts  0.85 us (4%)
  between operations  0.69 us (3%)
    all_to_all x1, starting transfers between devices, on_device(): lax.all_to_all(chunks, 'depth', split_axis=0, concat_axis=0, tiled=True,...  5.92 us
    ppermute x2, starting transfers between devices, moved(): return lax.ppermute(values, ('plane', 'depth'), index)  5.03 us
    all_to_all x1, waiting for transfers between devices, on_device(): lax.all_to_all(chunks, 'depth', split_axis=0, concat_axis=0, tiled=True,...  4.35 us
    pallas_call x1, Pallas kernels, on_device(): pl.pallas_call(functools.partial(late_kernel, late_starts), name='late',...  1.66 us
    pallas_call x1, Pallas kernels, on_device(): pl.pallas_call(functools.partial(cure_kernel, cells, rim_starts), name='c...  1.51 us
    pallas_call x1, Pallas kernels, on_device(): pl.pallas_call(pack_kernel, name='pack', out_shape=(pltpu.VMEM((slots, de...  1.23 us
    pallas_call x1, Pallas kernels, on_device(): pl.pallas_call(functools.partial(early_kernel, early_starts), name='early...  1.19 us
    unnamed x5, local copies, waits for them, and re-layouts  0.67 us
  transfers between devices with their start and end apart: 3, of which 1 were waited for; matrix products, arithmetic and copies ran while one was open for 2% of the time, Pallas kernels for 5%

profile of v13, /device:TPU:0, one launch (start us, length us, event | category | flops | bytes accessed | tf_op | source)
XLA Modules:
  0.0 22.6 jit_solution(5916595870383898433)
XLA Ops:
  0.6 1.2 %pack.1 = (bf16[208,128]{1,0:T(8,128)(2,1)S(1)}, bf16[208,128]{1,0:T(8,128)(2,1)S(1)}, bf16[4,96,256]{2,1,0:T(8,128)(2,1)S(1)}, bf16[192,96]{1,0:T(8,128)(2,1)S(...) custom-call(s32[8,96,128]{2,1,0:T(8,128)} %intensity.1, f32[6,128]{1,0:T(8,128)} %temp_hbm.1, ...), custom_call_target="tpu_custom_call" | custom-call | tf_op jit(solution)/shard_map/pack/pallas_call | solution.py:726
  1.9 0.7 %collective-permute-start = (bf16[208,128]{1,0:T(8,128)(2,1)S(1)}, bf16[208,128]{1,0:T(8,128)(2,1)S(1)}, u32[]{:S(2)}, u32[]{:S(2)}) collective-permute-start(bf16[208,128]{1,0:T(8,128)(2,1)S(1)} %get-tuple-element.17), channel_id=1, source_target_pairs={{4,8},{5,9},{6,10},{7,11},{12,16},{13,17},{14,18},{15,19},{20,24},... | collective-permute-start | bytes 159752 | tf_op jit(solution)/shard_map/ppermute | solution.py:748
  2.5 4.4 %collective-permute-start.1 = (bf16[208,128]{1,0:T(8,128)(2,1)S(1)}, bf16[208,128]{1,0:T(8,128)(2,1)S(1)}, u32[]{:S(2)}, u32[]{:S(2)}) collective-permute-start(bf16[208,128]{1,0:T(8,128)(2,1)S(1)} %get-tuple-element.18), channel_id=1, source_target_pairs={{0,4},{1,5},{2,6},{3,7},{8,12},{9,13},{10,14},{11,15},{16,20},{17,... | collective-permute-start | bytes 159752 | tf_op jit(solution)/shard_map/ppermute | solution.py:748
  6.9 1.2 %early.1 = (f32[4,32,128]{2,1,0:T(8,128)S(1)}, bf16[512,256]{1,0:T(8,128)(2,1)S(1)}, bf16[160,144]{1,0:T(8,128)(2,1)S(1)}, bf16[384,256]{1,0:T(8,128)(2,1)S(1)},...) custom-call(bf16[4,96,256]{2,1,0:T(8,128)(2,1)S(1)} %get-tuple-element.16.refs_0_.own, ...), custom_call_target="tpu_custom_call" | custom-call | flops 209715200 | bytes 4000000 | tf_op jit(solution)/shard_map/early/pallas_call | solution.py:774
  8.1 0.0 collective-permute-done.far
  8.1 0.0 collective-permute-done.1.near
  8.1 1.7 %late.1 = bf16[4,160,128]{2,1,0:T(8,128)(2,1)} custom-call(bf16[4,96,256]{2,1,0:T(8,128)(2,1)S(1)} %get-tuple-element.16.refs_0_.own, bf16[208,128]{1,0:T(8,128)(2,1)S(1)} %collective-permute-done.far, bf16[208,128]{1,0:T(8,128)(2,1)S(1)} %collective-permute-done.1.near, bf16[160,144]{1,0:T(8,128)(2,1)S(1)} %get-tuple-element.21.x_late, ...), custom_call_target="tpu_custom_call" | custom-call | flops 167772160 | bytes 4000000 | tf_op jit(solution)/shard_map/late/pallas_call | solution.py:790
  9.8 0.0 copy-start
  9.8 5.9 %all-to-all-start = ((bf16[4,160,128]{2,1,0:T(8,128)(2,1)}), bf16[4,160,128]{2,1,0:T(8,128)(2,1)S(1)}, u32[]{:S(2)}, u32[]{:S(2)}) async-start(bf16[4,160,128]{2,1,0:T(8,128)(2,1)} %late.1), calls=%async_computation | async-start | bytes 327680 | tf_op jit(solution)/shard_map/all_to_all | solution.py:811
  15.7 0.0 copy-done
  15.7 0.1 copy.18
  15.8 0.0 copy-start.1
  15.8 0.1 eq.15
  15.9 0.6 %copy-done.1 = f32[8]{0:T(128)S(1)} copy-done((f32[8]{0:T(128)S(1)}, f32[8]{0:T(128)}, u32[]{:S(2)}) %copy-start.1) | copy-done | bytes 56
  16.5 0.2 select_reduce_fusion
  16.7 0.1 copy.19.tools
  16.8 4.4 %all-to-all-done.chunks = bf16[4,160,128]{2,1,0:T(8,128)(2,1)S(1)} async-done(((bf16[4,160,128]{2,1,0:T(8,128)(2,1)}), bf16[4,160,128]{2,1,0:T(8,128)(2,1)S(1)}, u32[]{:S(2)}, u32[]{:S(2)}) %all-to-all-start) | async-done | bytes 163872 | tf_op jit(solution)/shard_map/all_to_all | solution.py:811
  21.1 1.5 %cure.1 = (f32[6,128]{1,0:T(8,128)}, f32[6,128]{1,0:T(8,128)}, f32[3,6,128]{2,1,0:T(8,128)}) custom-call(bf16[4,160,128]{2,1,0:T(8,128)(2,1)S(1)} %all-to-all-done.chunks, f32[6,128]{1,0:T(8,128)S(1)} %get-tuple-element.24.temp.temp_in, f32[6,128]{1,0:T(8,128)S(1)} %get-tuple-element.25.cure.cure_in, f32[6,1]{1,0:T(8,128)S(1)} %copy.19.tools, ...), custom_call_target="tpu_custom_call" | custom-call | tf_op jit(solution)/shard_map/cure/pallas_call | solution.py:820
Async XLA Ops:
  1.9 6.2 %collective-permute-start = (bf16[208,128]{1,0:T(8,128)(2,1)S(1)}, bf16[208,128]{1,0:T(8,128)(2,1)S(1)}, u32[]{:S(2)}, u32[]{:S(2)}) collective-permute-start(bf16[208,128]{1,0:T(8,128)(2,1)S(1)} %get-tuple-element.17), channel_id=1, source_target_pairs={{4,8},{5,9},{6,10},{7,11},{12,16},{13,17},{14,18},{15,19},{20,24},... | collective-permute-start | bytes 159752 | tf_op jit(solution)/shard_map/ppermute | solution.py:748
  2.5 5.6 %collective-permute-start.1 = (bf16[208,128]{1,0:T(8,128)(2,1)S(1)}, bf16[208,128]{1,0:T(8,128)(2,1)S(1)}, u32[]{:S(2)}, u32[]{:S(2)}) collective-permute-start(bf16[208,128]{1,0:T(8,128)(2,1)S(1)} %get-tuple-element.18), channel_id=1, source_target_pairs={{0,4},{1,5},{2,6},{3,7},{8,12},{9,13},{10,14},{11,15},{16,20},{17,... | collective-permute-start | bytes 159752 | tf_op jit(solution)/shard_map/ppermute | solution.py:748
  9.8 5.9 %copy-start = (s32[3,2]{0,1:T(2,128)S(1)}, s32[3,2]{0,1:T(2,128)}, u32[]{:S(2)}) copy-start(s32[3,2]{0,1:T(2,128)} %param.15) | copy-start | bytes 76
  9.8 11.3 %all-to-all-start = ((bf16[4,160,128]{2,1,0:T(8,128)(2,1)}), bf16[4,160,128]{2,1,0:T(8,128)(2,1)S(1)}, u32[]{:S(2)}, u32[]{:S(2)}) async-start(bf16[4,160,128]{2,1,0:T(8,128)(2,1)} %late.1), calls=%async_computation | async-start | bytes 327680 | tf_op jit(solution)/shard_map/all_to_all | solution.py:811
  15.8 0.7 %copy-start.1 = (f32[8]{0:T(128)S(1)}, f32[8]{0:T(128)}, u32[]{:S(2)}) copy-start(f32[8]{0:T(128)} %param.14) | copy-start | bytes 100

commit v14 on v13

--- a/solution.py
+++ b/solution.py
@@ -31,13 +31,13 @@
 LANES = 128
 HALO = 2
 EDGE = HALO * COARSE + R1 + R2
-EARLY = 80
+EARLY = 96
 GHOST = 3
+COLUMN_ROWS = 2 * GHOST - 1
 RIM = 2 * R1
 BEFORE = -(-(R2 - R1) // COARSE)
 AFTER = BEFORE
 HALF = LANES // 2
-SLOT = 40
 ROW_KINDS = (1, 0, 0)
 X_KINDS = (0, 1, 0)
 DEPTH_KINDS = (0, 0, 1)
@@ -92,7 +92,9 @@
 
 
 def product_rows(width):
-    places = [*range(R1, width - R1), *range(R1 - EDGE, R1), *range(width - R1, width + EDGE - R1)]
+    places = [*range(R1, width - R1)]
+    places += [None] * max(EARLY - len(places), 0)
+    places += [*range(R1 - EDGE, R1), *range(width - R1, width + EDGE - R1)]
     return places + [None] * (-len(places) % 16)
 
 
@@ -240,11 +242,19 @@
     return parts[:half] + parts[half:]
 
 
-def column_rows(temp, cure, first):
-    pad = jnp.zeros((8 - 2 * GHOST, temp.shape[1]), jnp.float32)
+def column_rows(temp, cure, at_end):
+    count = temp.shape[0]
+    first, second = (count - GHOST, count - GHOST + 1) if at_end else (0, 0)
+    pad = jnp.zeros((8 - COLUMN_ROWS, temp.shape[1]), jnp.float32)
     return jnp.concatenate(
-        [temp[first : first + GHOST, :], cure[first : first + GHOST, :], pad], axis=0
+        [temp[first : first + GHOST, :], cure[second : second + GHOST - 1, :], pad], axis=0
     )
+
+
+def chunk_rows(count, lanes):
+    products, voxels = own_columns(count)
+    held = count + 2 * HALO + 1 + COLUMN_ROWS * (lanes // LANES)
+    return voxels + fold(voxels), -(-held // 8) * 8
 
 
 def is_odd():
@@ -256,30 +266,21 @@
     grey, sems,
 ):
     rows, width, depth = intensity.shape
-    parts = [(0, EDGE), (width - EDGE, EDGE), (EDGE, width - 2 * EDGE)]
     copies = [
-        pltpu.make_async_copy(
-            intensity.at[:, pl.ds(*part), :], grey.at[:, pl.ds(*part), :], sems.at[index]
-        )
-        for index, part in enumerate(parts)
-    ]
-    copies[2:2] = [
-        pltpu.make_async_copy(temp_hbm, temp, sems.at[3]),
-        pltpu.make_async_copy(cure_hbm, cure, sems.at[4]),
-    ]
-    copies += [
-        pltpu.make_async_copy(x_hbm, x_parts, sems.at[5]),
-        pltpu.make_async_copy(z_hbm, z_parts, sems.at[6]),
+        pltpu.make_async_copy(intensity, grey, sems.at[0]),
+        pltpu.make_async_copy(temp_hbm, temp, sems.at[1]),
+        pltpu.make_async_copy(cure_hbm, cure, sems.at[2]),
+        pltpu.make_async_copy(x_hbm, x_parts, sems.at[3]),
+        pltpu.make_async_copy(z_hbm, z_parts, sems.at[4]),
     ]
     for copy in copies:
         copy.start()
-    for copy in copies[:4]:
+    for copy in copies[:3]:
         copy.wait()
     odd = is_odd()
-    count = temp.shape[0]
     sides = [
-        two_parts(column_rows(temp, cure, first)).astype(jnp.bfloat16)
-        for first in (0, count - GHOST)
+        two_parts(column_rows(temp, cure, at_end)).astype(jnp.bfloat16)
+        for at_end in (False, True)
     ]
 
     def send(left, right):
@@ -300,11 +301,11 @@
     def _():
         send(far, near)
 
-    for copy in copies[4:]:
-        copy.wait()
     for row in range(rows):
         half = (row % 2) * depth
         own[row // 2, :, half : half + depth] = grey[row].astype(jnp.float32).astype(jnp.bfloat16)
+    for copy in copies[3:]:
+        copy.wait()
 
 
 def packed_rows(values, size, first):
@@ -358,7 +359,7 @@
 
 def late_mask(count, width):
     row = lax.broadcasted_iota(jnp.int32, (count, LANES), 0)
-    left = width - 2 * R1 - EARLY
+    left = max(width - 2 * R1 - EARLY, 0)
     place = jnp.where(row < left + EDGE, row - left + R1 - EDGE, row - left - EDGE + width - R1)
     place = place + lax.axis_index("plane") * width
     inside = (place >= 0) & (place < lax.axis_size("plane") * width)
@@ -526,11 +527,17 @@
     yy, xx, zz, xz = [early_sums[index] + results[kind] for index, kind in enumerate(USED)]
     trace = yy + xx + zz
     lane = lax.broadcasted_iota(jnp.int32, trace.shape, 1)
-    three = jnp.where(lane < SLOT, trace, pltpu.roll(xx, SLOT, 1))
-    three = jnp.where(lane < 2 * SLOT, three, pltpu.roll(zz, 2 * SLOT, 1))
-    xz = [xz] + [pltpu.roll(xz, index * SLOT, 1) for index in range(1, 3)]
-
-    own_first, own_last = column_rows(temp, cure, 0), column_rows(temp, cure, count - GHOST)
+    columns, cells = sizes(width, depth)
+    tail = 4 * cells - LANES
+    joint = pltpu.roll(xz, 3 * cells, 1)
+    rest = jnp.where(lane < tail, joint, 0.0)
+    rest = pltpu.roll(rest, 0, 1, stride=tail, stride_axis=0)
+    for index, part in ((2, zz), (1, xx), (0, trace)):
+        moved = part if index == 0 else pltpu.roll(part, index * cells, 1)
+        joint = jnp.where(lane < (index + 1) * cells, moved, joint)
+
+    own_first, own_last = column_rows(temp, cure, False), column_rows(temp, cure, True)
+    half = chunk_rows(count, lanes)[1]
     for position, target in enumerate(order):
         piece = jnp.where(layer == target - 1, own_last, 0.0)
         piece = jnp.where(layer == target + 1, own_first, piece)
@@ -538,21 +545,13 @@
             piece = jnp.where(layer == depths - 1, left, piece)
         if target == out.shape[0] - 1:
             piece = jnp.where(layer == 0, right, piece)
-        at = count * target
-        pieces = [three[at : at + height], jnp.zeros((4, LANES), jnp.float32)]
-        for index in range(3):
-            size = min(4, height - 4 * index)
-            if size > 0:
-                part = xz[index][at + 4 * index : at + 4 * index + size]
-                if size < 4:
-                    spare = jnp.zeros((4 - size, LANES), jnp.float32)
-                    part = jnp.concatenate([part, spare], axis=0)
-                pieces[1] = jnp.where(lane[:4] < index * SLOT, pieces[1], part)
+        mine = slice(count * target, count * target + height)
+        pieces = [joint[mine], jnp.sum(rest[mine], axis=0, keepdims=True)]
         for slot in range(lanes // LANES):
-            pieces.append(piece[0 : 2 * GHOST, slot * LANES : (slot + 1) * LANES])
+            pieces.append(piece[0:COLUMN_ROWS, slot * LANES : (slot + 1) * LANES])
         filled = sum(part.shape[0] for part in pieces)
-        if filled < 24:
-            pieces.append(jnp.zeros((24 - filled, LANES), jnp.float32))
+        if filled < half:
+            pieces.append(jnp.zeros((half - filled, LANES), jnp.float32))
         sent = two_parts(jnp.concatenate(pieces, axis=0))
         out[position, voxels + folded :, :] = sent.astype(jnp.bfloat16)
     copies[1].start()
@@ -616,27 +615,39 @@
     own = cells - BEFORE - AFTER
     lane = lax.broadcasted_iota(jnp.int32, (16, lanes), 1)
     row = lax.broadcasted_iota(jnp.int32, (16, lanes), 0)
-    at_sums = chunks.shape[1] - 48
+    at_sums, half = chunk_rows(count, lanes)
+    tail = 4 * cells - LANES
+    narrow_lane = lax.broadcasted_iota(jnp.int32, (16, LANES), 1)
     order = meeting_order(parts)
 
     near = rim_sums(chunks, count, starts, flat, steep, rim_bands)
     sums = [near[0] + near[1] + near[2], near[1], near[2], near[5]]
-    blocks = []
+    blocks = [
+        joined(chunks[order.index(part), at_sums:, :].astype(jnp.float32)) for part in range(parts)
+    ]
+    tails = [block[height : height + 1] for block in blocks]
+    if parts % 8:
+        tails.append(jnp.zeros((-parts % 8, LANES), jnp.float32))
+    tails = jnp.concatenate(tails, axis=0)
+    tails = pltpu.roll(tails, lax.rem(LANES - lax.rem(tail * count * layer, LANES), LANES), 1)
+    narrow_row = lax.broadcasted_iota(jnp.int32, (16, LANES), 0)
+    rests = [jnp.zeros((16, LANES), jnp.float32) for _ in range(parts)]
+    for column in range(height):
+        moved = pltpu.roll(tails, LANES - tail * column, 1) if column else tails
+        for part in range(parts):
+            rests[part] = jnp.where(narrow_row == column, moved[part : part + 1], rests[part])
     for part in range(parts):
         first_cell = own * part - BEFORE
         here = (lane >= first_cell) & (lane < first_cell + cells)
-        values = joined(chunks[order.index(part), at_sums:, :].astype(jnp.float32))
-        blocks.append(values)
-        xz = values[height : height + 4]
-        xz = [xz] + [pltpu.roll(xz, LANES - index * SLOT, 1) for index in range(1, 3)]
-        spare = jnp.zeros((4, LANES), jnp.float32)
-        xz = jnp.concatenate([*xz, spare], axis=0)
+        values = blocks[part]
+        joint = values[0:16]
+        xz = pltpu.roll(jnp.where(narrow_lane < tail, rests[part], joint), LANES - 3 * cells, 1)
         for index in range(4):
-            chunk = values[0:16] if index < 3 else xz
+            chunk = xz if index == 3 else joint
             if lanes > LANES:
                 spare = jnp.zeros((16, lanes - LANES), jnp.float32)
                 chunk = jnp.concatenate([chunk, spare], axis=1)
-            shift = (first_cell - (index % 3) * SLOT) % lanes
+            shift = (first_cell - (index % 3) * cells) % lanes
             moved = chunk if shift == 0 else pltpu.roll(chunk, shift, 1)
             sums[index] = sums[index] + jnp.where(here, moved, 0.0)
     trace = sums[0]
@@ -655,9 +666,9 @@
     ]
     copies[0].start()
 
-    slots = range(height + 4, height + 4 + 2 * GHOST * (lanes // LANES), 2 * GHOST)
+    slots = range(height + 1, height + 1 + COLUMN_ROWS * (lanes // LANES), COLUMN_ROWS)
     columns = [
-        jnp.concatenate([values[at : at + 2 * GHOST] for at in slots], axis=1) for values in blocks
+        jnp.concatenate([values[at : at + COLUMN_ROWS] for at in slots], axis=1) for values in blocks
     ]
     before, after = columns[parts - 1], columns[0]
     for part in range(parts - 1):
@@ -665,7 +676,7 @@
         after = jnp.where(layer == part, columns[part + 1], after)
     spare = jnp.full((16 - count - 2 * GHOST, lanes), 0.5, jnp.float32)
     temp = jnp.concatenate([before[:GHOST], temp_in[...], after[:GHOST], 8.0 * spare], axis=0)
-    cure = jnp.concatenate([before[GHOST:], cure_in[...], after[GHOST:], spare], axis=0)
+    cure = jnp.concatenate([spare[:1], before[GHOST:], cure_in[...], after[GHOST:], spare[:1], spare], axis=0)
     gap = GHOST - HALO
     xx, xz, zz = [pltpu.roll(part, gap, 0) for part in conduct]
 
@@ -738,7 +749,7 @@
         in_specs=[stay] * 5,
         scratch_shapes=[
             pltpu.VMEM((rows, width, depth), jnp.int32),
-            pltpu.SemaphoreType.DMA((7,)),
+            pltpu.SemaphoreType.DMA((5,)),
         ],
         compiler_params=params,
     )(*[fixed(values) for values in (intensity, temp_start, cure_start, x_hbm, z_hbm)])
@@ -786,7 +797,8 @@
     )(own, x_parts, z_parts, *[fixed(values) for values in constants])
 
     products_x, voxels = own_columns(count)
-    chunk_shape = (depths, voxels + fold(voxels) + 48, LANES)
+    at_sums, half = chunk_rows(count, lanes)
+    chunk_shape = (depths, at_sums + 2 * half, LANES)
     chunks = pl.pallas_call(
         functools.partial(late_kernel, late_starts),
         name="late",

time: 22.9 us -> 22.5 us (0.983)
  waiting for transfers between devices: 4.36 us -> 4.1 us
    all_to_all x1, waiting for transfers between devices: 4.35 us -> 4.1 us  [on_device(): lax.all_to_all(chunks, 'depth', split_axis=0, concat_axis=0, tiled=True,...]
where the time goes in v14:
time: 22.5 us; the launch traced here: 22.2 us
  starting transfers between devices  10.9 us (48%)
  Pallas kernels  5.44 us (24%)
  waiting for transfers between devices  4.1 us (18%)
  local copies, waits for them, and re-layouts  0.85 us (4%)
  between operations  0.69 us (3%)
    all_to_all x1, starting transfers between devices, on_device(): lax.all_to_all(chunks, 'depth', split_axis=0, concat_axis=0, tiled=True,...  5.91 us
    ppermute x2, starting transfers between devices, moved(): return lax.ppermute(values, ('plane', 'depth'), index)  5.03 us
    all_to_all x1, waiting for transfers between devices, on_device(): lax.all_to_all(chunks, 'depth', split_axis=0, concat_axis=0, tiled=True,...  4.1 us
    pallas_call x1, Pallas kernels, on_device(): pl.pallas_call(functools.partial(late_kernel, late_starts), name='late',...  1.63 us
    pallas_call x1, Pallas kernels, on_device(): pl.pallas_call(functools.partial(cure_kernel, cells, rim_starts), name='c...  1.5 us
    pallas_call x1, Pallas kernels, on_device(): pl.pallas_call(functools.partial(early_kernel, early_starts), name='early...  1.19 us
    pallas_call x1, Pallas kernels, on_device(): pl.pallas_call(pack_kernel, name='pack', out_shape=(pltpu.VMEM((slots, de...  1.12 us
    unnamed x5, local copies, waits for them, and re-layouts  0.67 us
  transfers between devices with their start and end apart: 3, of which 1 were waited for; matrix products, arithmetic and copies ran while one was open for 2% of the time, Pallas kernels for 5%

profile of v14, /device:TPU:0, one launch (start us, length us, event | category | flops | bytes accessed | tf_op | source)
XLA Modules:
  0.0 22.2 jit_solution(11299871680155269204)
XLA Ops:
  0.6 1.1 %pack.1 = (bf16[208,128]{1,0:T(8,128)(2,1)S(1)}, bf16[208,128]{1,0:T(8,128)(2,1)S(1)}, bf16[4,96,256]{2,1,0:T(8,128)(2,1)S(1)}, bf16[224,96]{1,0:T(8,128)(2,1)S(...) custom-call(s32[8,96,128]{2,1,0:T(8,128)} %intensity.1, f32[6,128]{1,0:T(8,128)} %temp_hbm.1, ...), custom_call_target="tpu_custom_call" | custom-call | tf_op jit(solution)/shard_map/pack/pallas_call | solution.py:737
  1.8 0.7 %collective-permute-start = (bf16[208,128]{1,0:T(8,128)(2,1)S(1)}, bf16[208,128]{1,0:T(8,128)(2,1)S(1)}, u32[]{:S(2)}, u32[]{:S(2)}) collective-permute-start(bf16[208,128]{1,0:T(8,128)(2,1)S(1)} %get-tuple-element.17), channel_id=1, source_target_pairs={{4,8},{5,9},{6,10},{7,11},{12,16},{13,17},{14,18},{15,19},{20,24},... | collective-permute-start | bytes 159752 | tf_op jit(solution)/shard_map/ppermute | solution.py:759
  2.4 4.4 %collective-permute-start.1 = (bf16[208,128]{1,0:T(8,128)(2,1)S(1)}, bf16[208,128]{1,0:T(8,128)(2,1)S(1)}, u32[]{:S(2)}, u32[]{:S(2)}) collective-permute-start(bf16[208,128]{1,0:T(8,128)(2,1)S(1)} %get-tuple-element.18), channel_id=1, source_target_pairs={{0,4},{1,5},{2,6},{3,7},{8,12},{9,13},{10,14},{11,15},{16,20},{17,... | collective-permute-start | bytes 159752 | tf_op jit(solution)/shard_map/ppermute | solution.py:759
  6.8 1.2 %early.1 = (f32[4,32,128]{2,1,0:T(8,128)S(1)}, bf16[512,256]{1,0:T(8,128)(2,1)S(1)}, bf16[128,144]{1,0:T(8,128)(2,1)S(1)}, bf16[384,256]{1,0:T(8,128)(2,1)S(1)},...) custom-call(bf16[4,96,256]{2,1,0:T(8,128)(2,1)S(1)} %get-tuple-element.16.refs_0_.own, ...), custom_call_target="tpu_custom_call" | custom-call | flops 251658240 | bytes 4000000 | tf_op jit(solution)/shard_map/early/pallas_call | solution.py:785
  8.0 0.0 collective-permute-done.far
  8.0 0.0 collective-permute-done.1.near
  8.0 1.6 %late.1 = bf16[4,144,128]{2,1,0:T(8,128)(2,1)} custom-call(bf16[4,96,256]{2,1,0:T(8,128)(2,1)S(1)} %get-tuple-element.16.refs_0_.own, bf16[208,128]{1,0:T(8,128)(2,1)S(1)} %collective-permute-done.far, bf16[208,128]{1,0:T(8,128)(2,1)S(1)} %collective-permute-done.1.near, bf16[128,144]{1,0:T(8,128)(2,1)S(1)} %get-tuple-element.21.x_late, ...), custom_call_target="tpu_custom_call" | custom-call | flops 125829120 | bytes 4000000 | tf_op jit(solution)/shard_map/late/pallas_call | solution.py:802
  9.7 0.0 copy-start
  9.7 5.9 %all-to-all-start = ((bf16[4,144,128]{2,1,0:T(8,128)(2,1)}), bf16[4,144,128]{2,1,0:T(8,128)(2,1)S(1)}, u32[]{:S(2)}, u32[]{:S(2)}) async-start(bf16[4,144,128]{2,1,0:T(8,128)(2,1)} %late.1), calls=%async_computation | async-start | bytes 294912 | tf_op jit(solution)/shard_map/all_to_all | solution.py:823
  15.6 0.0 copy-done
  15.6 0.1 copy.18
  15.7 0.0 copy-start.1
  15.7 0.1 eq.15
  15.8 0.6 %copy-done.1 = f32[8]{0:T(128)S(1)} copy-done((f32[8]{0:T(128)S(1)}, f32[8]{0:T(128)}, u32[]{:S(2)}) %copy-start.1) | copy-done | bytes 56
  16.3 0.2 select_reduce_fusion
  16.5 0.1 copy.19.tools
  16.6 4.1 %all-to-all-done.chunks = bf16[4,144,128]{2,1,0:T(8,128)(2,1)S(1)} async-done(((bf16[4,144,128]{2,1,0:T(8,128)(2,1)}), bf16[4,144,128]{2,1,0:T(8,128)(2,1)S(1)}, u32[]{:S(2)}, u32[]{:S(2)}) %all-to-all-start) | async-done | bytes 147488 | tf_op jit(solution)/shard_map/all_to_all | solution.py:823
  20.7 1.5 %cure.1 = (f32[6,128]{1,0:T(8,128)}, f32[6,128]{1,0:T(8,128)}, f32[3,6,128]{2,1,0:T(8,128)}) custom-call(bf16[4,144,128]{2,1,0:T(8,128)(2,1)S(1)} %all-to-all-done.chunks, f32[6,128]{1,0:T(8,128)S(1)} %get-tuple-element.24.temp.temp_in, f32[6,128]{1,0:T(8,128)S(1)} %get-tuple-element.25.cure.cure_in, f32[6,1]{1,0:T(8,128)S(1)} %copy.19.tools, ...), custom_call_target="tpu_custom_call" | custom-call | tf_op jit(solution)/shard_map/cure/pallas_call | solution.py:832
Async XLA Ops:
  1.8 6.2 %collective-permute-start = (bf16[208,128]{1,0:T(8,128)(2,1)S(1)}, bf16[208,128]{1,0:T(8,128)(2,1)S(1)}, u32[]{:S(2)}, u32[]{:S(2)}) collective-permute-start(bf16[208,128]{1,0:T(8,128)(2,1)S(1)} %get-tuple-element.17), channel_id=1, source_target_pairs={{4,8},{5,9},{6,10},{7,11},{12,16},{13,17},{14,18},{15,19},{20,24},... | collective-permute-start | bytes 159752 | tf_op jit(solution)/shard_map/ppermute | solution.py:759
  2.4 5.6 %collective-permute-start.1 = (bf16[208,128]{1,0:T(8,128)(2,1)S(1)}, bf16[208,128]{1,0:T(8,128)(2,1)S(1)}, u32[]{:S(2)}, u32[]{:S(2)}) collective-permute-start(bf16[208,128]{1,0:T(8,128)(2,1)S(1)} %get-tuple-element.18), channel_id=1, source_target_pairs={{0,4},{1,5},{2,6},{3,7},{8,12},{9,13},{10,14},{11,15},{16,20},{17,... | collective-permute-start | bytes 159752 | tf_op jit(solution)/shard_map/ppermute | solution.py:759
  9.7 5.9 %copy-start = (s32[3,2]{0,1:T(2,128)S(1)}, s32[3,2]{0,1:T(2,128)}, u32[]{:S(2)}) copy-start(s32[3,2]{0,1:T(2,128)} %param.15) | copy-start | bytes 76
  9.7 11.0 %all-to-all-start = ((bf16[4,144,128]{2,1,0:T(8,128)(2,1)}), bf16[4,144,128]{2,1,0:T(8,128)(2,1)S(1)}, u32[]{:S(2)}, u32[]{:S(2)}) async-start(bf16[4,144,128]{2,1,0:T(8,128)(2,1)} %late.1), calls=%async_computation | async-start | bytes 294912 | tf_op jit(solution)/shard_map/all_to_all | solution.py:823
  15.7 0.7 %copy-start.1 = (f32[8]{0:T(128)S(1)}, f32[8]{0:T(128)}, u32[]{:S(2)}) copy-start(f32[8]{0:T(128)} %param.14) | copy-start | bytes 100

commit v15 on v14

--- a/solution.py
+++ b/solution.py
@@ -158,7 +158,9 @@
 
 def meeting_order(blocks):
     middle = blocks // 2
-    return [middle, *range(middle + 1, blocks), *range(middle - 1, -1, -1)]
+    rest = [block for block in range(blocks) if block != middle]
+    ends = [rest.pop(0 if turn % 2 == 0 else -1) for turn in range(blocks - 1)]
+    return [middle, *ends]
 
 
 def own_columns(count):

time: 22.5 us -> 22.1 us (0.982)
  waiting for transfers between devices: 4.1 us -> 3.73 us
    all_to_all x1, waiting for transfers between devices: 4.1 us -> 3.72 us  [on_device(): lax.all_to_all(chunks, 'depth', split_axis=0, concat_axis=0, tiled=True,...]
where the time goes in v15:
time: 22.1 us; the launch traced here: 21.8 us
  starting transfers between devices  10.9 us (49%)
  Pallas kernels  5.45 us (25%)
  waiting for transfers between devices  3.73 us (17%)
  local copies, waits for them, and re-layouts  0.85 us (4%)
  between operations  0.69 us (3%)
    all_to_all x1, starting transfers between devices, on_device(): lax.all_to_all(chunks, 'depth', split_axis=0, concat_axis=0, tiled=True,...  5.9 us
    ppermute x2, starting transfers between devices, moved(): return lax.ppermute(values, ('plane', 'depth'), index)  5.03 us
    all_to_all x1, waiting for transfers between devices, on_device(): lax.all_to_all(chunks, 'depth', split_axis=0, concat_axis=0, tiled=True,...  3.72 us
    pallas_call x1, Pallas kernels, on_device(): pl.pallas_call(functools.partial(late_kernel, late_starts), name='late',...  1.63 us
    pallas_call x1, Pallas kernels, on_device(): pl.pallas_call(functools.partial(cure_kernel, cells, rim_starts), name='c...  1.51 us
    pallas_call x1, Pallas kernels, on_device(): pl.pallas_call(functools.partial(early_kernel, early_starts), name='early...  1.19 us
    pallas_call x1, Pallas kernels, on_device(): pl.pallas_call(pack_kernel, name='pack', out_shape=(pltpu.VMEM((slots, de...  1.12 us
    unnamed x5, local copies, waits for them, and re-layouts  0.67 us
  transfers between devices with their start and end apart: 3, of which 1 were waited for; matrix products, arithmetic and copies ran while one was open for 2% of the time, Pallas kernels for 5%

profile of v15, /device:TPU:0, one launch (start us, length us, event | category | flops | bytes accessed | tf_op | source)
XLA Modules:
  0.0 21.8 jit_solution(10911426841209454999)
XLA Ops:
  0.6 1.1 %pack.1 = (bf16[208,128]{1,0:T(8,128)(2,1)S(1)}, bf16[208,128]{1,0:T(8,128)(2,1)S(1)}, bf16[4,96,256]{2,1,0:T(8,128)(2,1)S(1)}, bf16[224,96]{1,0:T(8,128)(2,1)S(...) custom-call(s32[8,96,128]{2,1,0:T(8,128)} %intensity.1, f32[6,128]{1,0:T(8,128)} %temp_hbm.1, ...), custom_call_target="tpu_custom_call" | custom-call | tf_op jit(solution)/shard_map/pack/pallas_call | solution.py:739
  1.8 0.7 %collective-permute-start = (bf16[208,128]{1,0:T(8,128)(2,1)S(1)}, bf16[208,128]{1,0:T(8,128)(2,1)S(1)}, u32[]{:S(2)}, u32[]{:S(2)}) collective-permute-start(bf16[208,128]{1,0:T(8,128)(2,1)S(1)} %get-tuple-element.17), channel_id=1, source_target_pairs={{4,8},{5,9},{6,10},{7,11},{12,16},{13,17},{14,18},{15,19},{20,24},... | collective-permute-start | bytes 159752 | tf_op jit(solution)/shard_map/ppermute | solution.py:761
  2.4 4.4 %collective-permute-start.1 = (bf16[208,128]{1,0:T(8,128)(2,1)S(1)}, bf16[208,128]{1,0:T(8,128)(2,1)S(1)}, u32[]{:S(2)}, u32[]{:S(2)}) collective-permute-start(bf16[208,128]{1,0:T(8,128)(2,1)S(1)} %get-tuple-element.18), channel_id=1, source_target_pairs={{0,4},{1,5},{2,6},{3,7},{8,12},{9,13},{10,14},{11,15},{16,20},{17,... | collective-permute-start | bytes 159752 | tf_op jit(solution)/shard_map/ppermute | solution.py:761
  6.8 1.2 %early.1 = (f32[4,32,128]{2,1,0:T(8,128)S(1)}, bf16[512,256]{1,0:T(8,128)(2,1)S(1)}, bf16[128,144]{1,0:T(8,128)(2,1)S(1)}, bf16[384,256]{1,0:T(8,128)(2,1)S(1)},...) custom-call(bf16[4,96,256]{2,1,0:T(8,128)(2,1)S(1)} %get-tuple-element.16.refs_0_.own, ...), custom_call_target="tpu_custom_call" | custom-call | flops 251658240 | bytes 4000000 | tf_op jit(solution)/shard_map/early/pallas_call | solution.py:787
  8.0 0.0 collective-permute-done.far
  8.0 0.0 collective-permute-done.1.near
  8.0 1.6 %late.1 = bf16[4,144,128]{2,1,0:T(8,128)(2,1)} custom-call(bf16[4,96,256]{2,1,0:T(8,128)(2,1)S(1)} %get-tuple-element.16.refs_0_.own, bf16[208,128]{1,0:T(8,128)(2,1)S(1)} %collective-permute-done.far, bf16[208,128]{1,0:T(8,128)(2,1)S(1)} %collective-permute-done.1.near, bf16[128,144]{1,0:T(8,128)(2,1)S(1)} %get-tuple-element.21.x_late, ...), custom_call_target="tpu_custom_call" | custom-call | flops 125829120 | bytes 4000000 | tf_op jit(solution)/shard_map/late/pallas_call | solution.py:804
  9.7 0.0 copy-start
  9.7 5.9 %all-to-all-start = ((bf16[4,144,128]{2,1,0:T(8,128)(2,1)}), bf16[4,144,128]{2,1,0:T(8,128)(2,1)S(1)}, u32[]{:S(2)}, u32[]{:S(2)}) async-start(bf16[4,144,128]{2,1,0:T(8,128)(2,1)} %late.1), calls=%async_computation | async-start | bytes 294912 | tf_op jit(solution)/shard_map/all_to_all | solution.py:825
  15.6 0.0 copy-done
  15.6 0.1 copy.18
  15.7 0.0 copy-start.1
  15.7 0.1 eq.15
  15.7 0.6 %copy-done.1 = f32[8]{0:T(128)S(1)} copy-done((f32[8]{0:T(128)S(1)}, f32[8]{0:T(128)}, u32[]{:S(2)}) %copy-start.1) | copy-done | bytes 56
  16.3 0.2 select_reduce_fusion
  16.5 0.1 copy.19.tools
  16.6 3.7 %all-to-all-done.chunks = bf16[4,144,128]{2,1,0:T(8,128)(2,1)S(1)} async-done(((bf16[4,144,128]{2,1,0:T(8,128)(2,1)}), bf16[4,144,128]{2,1,0:T(8,128)(2,1)S(1)}, u32[]{:S(2)}, u32[]{:S(2)}) %all-to-all-start) | async-done | bytes 147488 | tf_op jit(solution)/shard_map/all_to_all | solution.py:825
  20.3 1.5 %cure.1 = (f32[6,128]{1,0:T(8,128)}, f32[6,128]{1,0:T(8,128)}, f32[3,6,128]{2,1,0:T(8,128)}) custom-call(bf16[4,144,128]{2,1,0:T(8,128)(2,1)S(1)} %all-to-all-done.chunks, f32[6,128]{1,0:T(8,128)S(1)} %get-tuple-element.24.temp.temp_in, f32[6,128]{1,0:T(8,128)S(1)} %get-tuple-element.25.cure.cure_in, f32[6,1]{1,0:T(8,128)S(1)} %copy.19.tools, ...), custom_call_target="tpu_custom_call" | custom-call | tf_op jit(solution)/shard_map/cure/pallas_call | solution.py:834
Async XLA Ops:
  1.8 6.2 %collective-permute-start = (bf16[208,128]{1,0:T(8,128)(2,1)S(1)}, bf16[208,128]{1,0:T(8,128)(2,1)S(1)}, u32[]{:S(2)}, u32[]{:S(2)}) collective-permute-start(bf16[208,128]{1,0:T(8,128)(2,1)S(1)} %get-tuple-element.17), channel_id=1, source_target_pairs={{4,8},{5,9},{6,10},{7,11},{12,16},{13,17},{14,18},{15,19},{20,24},... | collective-permute-start | bytes 159752 | tf_op jit(solution)/shard_map/ppermute | solution.py:761
  2.4 5.6 %collective-permute-start.1 = (bf16[208,128]{1,0:T(8,128)(2,1)S(1)}, bf16[208,128]{1,0:T(8,128)(2,1)S(1)}, u32[]{:S(2)}, u32[]{:S(2)}) collective-permute-start(bf16[208,128]{1,0:T(8,128)(2,1)S(1)} %get-tuple-element.18), channel_id=1, source_target_pairs={{0,4},{1,5},{2,6},{3,7},{8,12},{9,13},{10,14},{11,15},{16,20},{17,... | collective-permute-start | bytes 159752 | tf_op jit(solution)/shard_map/ppermute | solution.py:761
  9.7 5.9 %copy-start = (s32[3,2]{0,1:T(2,128)S(1)}, s32[3,2]{0,1:T(2,128)}, u32[]{:S(2)}) copy-start(s32[3,2]{0,1:T(2,128)} %param.15) | copy-start | bytes 76
  9.7 10.7 %all-to-all-start = ((bf16[4,144,128]{2,1,0:T(8,128)(2,1)}), bf16[4,144,128]{2,1,0:T(8,128)(2,1)S(1)}, u32[]{:S(2)}, u32[]{:S(2)}) async-start(bf16[4,144,128]{2,1,0:T(8,128)(2,1)} %late.1), calls=%async_computation | async-start | bytes 294912 | tf_op jit(solution)/shard_map/all_to_all | solution.py:825
  15.7 0.7 %copy-start.1 = (f32[8]{0:T(128)S(1)}, f32[8]{0:T(128)}, u32[]{:S(2)}) copy-start(f32[8]{0:T(128)} %param.14) | copy-start | bytes 100

commit v16 on v15

--- a/solution.py
+++ b/solution.py
@@ -386,13 +386,10 @@
     return sums
 
 
-def tensor_sums(window, bands, sx, mask, diagonal, z_parts, across, filtered, grads):
-    pairs, height, double = window.shape
-    rows, depth = 2 * pairs, double // 2
-    count = bands.shape[0] // 2
-    whole = jnp.concatenate([window[pair] for pair in range(pairs)], axis=1)
-    across[...] = product(bands, whole)
-
+def tensor_sums(across, sx, mask, diagonal, z_parts, filtered, grads):
+    double = diagonal.shape[1]
+    depth, pairs = double // 2, across.shape[1] // double
+    rows, count = 2 * pairs, across.shape[0] // 2
     for start in range(0, count, 16):
         kinds = [
             [
@@ -438,19 +435,22 @@
     return all_sums(products, z_parts[double : double + depth, :], sx)
 
 
-def early_kernel(*refs):
-    starts, own, x_parts, z_parts, *rest = refs
-    count = (len(rest) - 6) // 2
-    constants, (sums, diagonal), held = rest[:count], rest[count : count + 2], rest[count + 2 : -4]
-    across, filtered, grads, sems = rest[-4:]
-    copies = [
-        pltpu.make_async_copy(source, target, sems.at[index])
-        for index, (source, target) in enumerate(zip(constants, held))
-    ]
-    for copy in copies:
-        copy.start()
+def rim_tiles(values):
+    rows, depth = len(values), values[0].shape[1]
+    below = packed_rows(values, RIM, depth - RIM)
+    above = pltpu.roll(packed_rows(values, RIM, 0), rows * RIM, 1)
+    lane = lax.broadcasted_iota(jnp.int32, below.shape, 1)
+    return [jnp.where(lane < rows * RIM, below, above), above, pltpu.roll(above, HALF, 1)]
+
+
+def early_kernel(
+    starts, own, x_parts, z_parts, late_hbm, sums, diagonal, sides, tiles, x_late, across,
+    filtered, grads, sem,
+):
+    copy = pltpu.make_async_copy(late_hbm, x_late, sem.at[0])
+    copy.start()
     pairs, width, double = own.shape
-    depth = double // 2
+    rows, depth = 2 * pairs, double // 2
     empty = jnp.zeros((depth, depth), jnp.bfloat16)
     for kind in range(2):
         for half in range(2):
@@ -458,21 +458,39 @@
             band = z_parts[kind * depth : (kind + 1) * depth, :]
             diagonal[at, half * depth : (half + 1) * depth] = band
             diagonal[at, (1 - half) * depth : (2 - half) * depth] = empty
-    bands = x_parts[starts[0] : starts[1], :width]
-    sx = x_parts[starts[1] : starts[2], :EARLY]
-    results = tensor_sums(own, bands, sx, None, diagonal, z_parts, across, filtered, grads)
+    whole = jnp.concatenate([own[pair] for pair in range(pairs)], axis=1)
+    result = product(x_parts[starts[0] : starts[2], :width], whole)
+    across[...] = result[: starts[1]]
+    sides[...] = result[starts[1] :]
+    sx = x_parts[starts[2] : starts[3], :EARLY]
+    results = tensor_sums(across, sx, None, diagonal, z_parts, filtered, grads)
     for index, kind in enumerate(USED):
         sums[index] = results[kind]
-    for copy in copies:
-        copy.wait()
+    values = [
+        own[row // 2, :, (row % 2) * depth : (row % 2 + 1) * depth].astype(jnp.float32)
+        for row in range(rows)
+    ]
+    for index, tile in enumerate(rim_tiles(values)):
+        tiles[index] = tile
+    copy.wait()
 
 
 def late_kernel(
-    starts, own, far, near, x_late, z_parts, diagonal, early_sums, temp, cure, out_hbm,
-    window, across, filtered, grads, out, sems,
+    starts, width, far, near, x_late, z_parts, diagonal, early_sums, sides, own_tiles, temp, cure,
+    flat_hbm, steep_hbm, cells_hbm, out_hbm, flat, steep, cell_bands, across, filtered, grads,
+    out, sems,
 ):
-    pairs, width, double = own.shape
-    rows, depth = 2 * pairs, double // 2
+    constants = [
+        pltpu.make_async_copy(source, target, sems.at[2 + index])
+        for index, (source, target) in enumerate(
+            ((flat_hbm, flat), (steep_hbm, steep), (cells_hbm, cell_bands))
+        )
+    ]
+    for copy in constants:
+        copy.start()
+    double = diagonal.shape[1]
+    depth = double // 2
+    rows = across.shape[1] // depth
     count, lanes = temp.shape
     odd = is_odd()
     depths, layer = lax.axis_size("depth"), lax.axis_index("depth")
@@ -480,23 +498,23 @@
     inner, inner_columns = edges_of(near, rows)
     values = []
     for row in range(rows):
-        half = (row % 2) * depth
-        middle = own[row // 2, :, half : half + depth].astype(jnp.float32)
         left = jnp.where(odd, inner[row], outer[row])
         right = jnp.where(odd, outer[row], inner[row])
-        whole = jnp.concatenate([left, middle, right], axis=0)
-        window[row // 2, :, half : half + depth] = whole.astype(jnp.bfloat16)
-        values.append(whole)
+        values.append(jnp.concatenate([left, right], axis=0))
     left = jnp.where(odd, inner_columns, outer_columns)
     right = jnp.where(odd, outer_columns, inner_columns)
 
+    late = across.shape[0] // 2
+    halos = jnp.concatenate([value.astype(jnp.bfloat16) for value in values], axis=1)
+    across[...] = sides[...] + product(x_late[starts[0] : starts[1], : 2 * EDGE], halos)
+
     products_x, voxels = own_columns(count)
     folded, stride = fold(voxels), COARSE * count
-    below = packed_rows(values, RIM, depth - RIM)
-    above = pltpu.roll(packed_rows(values, RIM, 0), rows * RIM, 1)
-    lane = lax.broadcasted_iota(jnp.int32, below.shape, 1)
-    tiles = [jnp.where(lane < rows * RIM, below, above), above, pltpu.roll(above, HALF, 1)]
-    missing = stride * (depths - 1) + voxels - below.shape[0]
+    tiles = [
+        jnp.concatenate([tile[:EDGE], own_tiles[index], tile[EDGE:]], axis=0)
+        for index, tile in enumerate(rim_tiles(values))
+    ]
+    missing = stride * (depths - 1) + voxels - tiles[0].shape[0]
     if missing > 0:
         spare = jnp.zeros((-(-missing // 8) * 8, LANES), jnp.float32)
         tiles = [jnp.concatenate([tile, spare], axis=0) for tile in tiles]
@@ -520,11 +538,9 @@
     ]
     copies[0].start()
 
-    late = across.shape[0] // 2
-    bands = x_late[starts[0] : starts[1], :]
     sx = x_late[starts[1] : starts[2], :late]
     results = tensor_sums(
-        window, bands, sx, late_mask(late, width), diagonal, z_parts, across, filtered, grads
+        across, sx, late_mask(late, width), diagonal, z_parts, filtered, grads
     )
     yy, xx, zz, xz = [early_sums[index] + results[kind] for index, kind in enumerate(USED)]
     trace = yy + xx + zz
@@ -557,7 +573,7 @@
         sent = two_parts(jnp.concatenate(pieces, axis=0))
         out[position, voxels + folded :, :] = sent.astype(jnp.bfloat16)
     copies[1].start()
-    for copy in copies:
+    for copy in copies + constants:
         copy.wait()
 
 
@@ -728,14 +744,18 @@
     bands, coarse = x_bands(width), coarse_x_bands(width)
     late = bands.shape[1] - EARLY
     middle = bands[:, :EARLY, EDGE : EDGE + width]
-    x_hbm, early_starts = stacked(middle.reshape(2 * EARLY, -1), coarse[:, :EARLY])
+    sides = bands[:, EARLY:].reshape(2 * late, -1)
+    x_hbm, early_starts = stacked(
+        middle.reshape(2 * EARLY, -1), sides[:, EDGE : EDGE + width], coarse[:, :EARLY]
+    )
     z_hbm, _ = stacked(*depth_bands(depth), coarse_depth_bands(depth))
-    x_late, late_starts = stacked(bands[:, EARLY:].reshape(2 * late, -1), coarse[:, EARLY:])
+    halos = np.concatenate([sides[:, :EDGE], sides[:, EDGE + width :]], axis=1)
+    x_late, late_starts = stacked(halos, coarse[:, EARLY:])
     rims = rim_bands(rows)
     flat, _ = stacked(np.concatenate([rims[0], rims[2]], axis=1))
     steep, rim_starts = stacked(rims[1], *rim_x_bands(count))
     cell_bands, _ = stacked(rim_cells(rows, depth, depths))
-    constants = (x_late, flat, steep, cell_bands)
+    constants = (flat, steep, cell_bands)
     far, near, own, x_parts, z_parts, temp, cure = pl.pallas_call(
         pack_kernel,
         name="pack",
@@ -784,38 +804,42 @@
             transcendentals=0,
         )
 
-    early_sums, diagonal, x_late, flat, steep, cell_bands = pl.pallas_call(
+    early_sums, diagonal, sides, own_tiles, x_late = pl.pallas_call(
         functools.partial(early_kernel, early_starts),
         name="early",
         out_shape=(
             pltpu.VMEM((len(USED), high, LANES), jnp.float32),
             pltpu.VMEM((4 * depth, 2 * depth), bf16),
-            *[pltpu.VMEM(values.shape, bf16) for values in constants],
+            pltpu.VMEM((2 * late, rows * depth), jnp.float32),
+            pltpu.VMEM((3, width, LANES), jnp.float32),
+            pltpu.VMEM(x_late.shape, bf16),
         ),
-        in_specs=[vmem] * 3 + [stay] * len(constants),
-        scratch_shapes=scratch(EARLY) + [pltpu.SemaphoreType.DMA((len(constants),))],
+        in_specs=[vmem] * 3 + [stay],
+        scratch_shapes=scratch(EARLY) + [pltpu.SemaphoreType.DMA((1,))],
         cost_estimate=cost(EARLY),
         compiler_params=params,
-    )(own, x_parts, z_parts, *[fixed(values) for values in constants])
+    )(own, x_parts, z_parts, fixed(x_late))
 
     products_x, voxels = own_columns(count)
     at_sums, half = chunk_rows(count, lanes)
     chunk_shape = (depths, at_sums + 2 * half, LANES)
-    chunks = pl.pallas_call(
-        functools.partial(late_kernel, late_starts),
+    chunks, flat, steep, cell_bands = pl.pallas_call(
+        functools.partial(late_kernel, late_starts, width),
         name="late",
-        out_shape=pltpu.HBM(chunk_shape, bf16),
-        in_specs=[vmem] * 9,
-        out_specs=stay,
-        scratch_shapes=[pltpu.VMEM((rows // 2, width + 2 * EDGE, 2 * depth), bf16)]
-        + scratch(late)
-        + [
-            pltpu.VMEM(chunk_shape, bf16),
-            pltpu.SemaphoreType.DMA((2,)),
-        ],
+        out_shape=(
+            pltpu.HBM(chunk_shape, bf16),
+            *[pltpu.VMEM(values.shape, bf16) for values in constants],
+        ),
+        in_specs=[vmem] * 10 + [stay] * 3,
+        out_specs=(stay, vmem, vmem, vmem),
+        scratch_shapes=scratch(late)
+        + [pltpu.VMEM(chunk_shape, bf16), pltpu.SemaphoreType.DMA((5,))],
         cost_estimate=cost(late),
         compiler_params=params,
-    )(own, far, near, x_late, z_parts, diagonal, early_sums, temp, cure)
+    )(
+        far, near, x_late, z_parts, diagonal, early_sums, sides, own_tiles, temp, cure,
+        *[fixed(values) for values in constants],
+    )
 
     faces = plan.reshape(2 * STEPS, 1) == jnp.arange(tool_levels.shape[0], dtype=jnp.int32)
     tools = jnp.sum(

time: 22.1 us -> 22.3 us (level)
    pallas_call x1, Pallas kernels: 1.63 us -> 1.93 us  [on_device(): pl.pallas_call(functools.partial(late_kernel, late_starts, width), name='...]
where the time goes in v16:
time: 22.3 us; the launch traced here: 22 us
  starting transfers between devices  10.9 us (49%)
  Pallas kernels  5.58 us (25%)
  waiting for transfers between devices  3.81 us (17%)
  local copies, waits for them, and re-layouts  0.85 us (4%)
  between operations  0.69 us (3%)
    all_to_all x1, starting transfers between devices, on_device(): lax.all_to_all(chunks, 'depth', split_axis=0, concat_axis=0, tiled=True,...  5.9 us
    ppermute x2, starting transfers between devices, moved(): return lax.ppermute(values, ('plane', 'depth'), index)  5.03 us
    all_to_all x1, waiting for transfers between devices, on_device(): lax.all_to_all(chunks, 'depth', split_axis=0, concat_axis=0, tiled=True,...  3.81 us
    pallas_call x1, Pallas kernels, on_device(): pl.pallas_call(functools.partial(late_kernel, late_starts, width), name='...  1.93 us
    pallas_call x1, Pallas kernels, on_device(): pl.pallas_call(functools.partial(cure_kernel, cells, rim_starts), name='c...  1.5 us
    pallas_call x1, Pallas kernels, on_device(): pl.pallas_call(pack_kernel, name='pack', out_shape=(pltpu.VMEM((slots, de...  1.13 us
    pallas_call x1, Pallas kernels, on_device(): pl.pallas_call(functools.partial(early_kernel, early_starts), name='early...  1.02 us
    unnamed x5, local copies, waits for them, and re-layouts  0.67 us
  transfers between devices with their start and end apart: 3, of which 1 were waited for; matrix products, arithmetic and copies ran while one was open for 2% of the time, Pallas kernels for 5%

profile of v16, /device:TPU:0, one launch (start us, length us, event | category | flops | bytes accessed | tf_op | source)
XLA Modules:
  0.0 22.0 jit_solution(13474733806182133704)
XLA Ops:
  0.6 1.1 %pack.1 = (bf16[208,128]{1,0:T(8,128)(2,1)S(1)}, bf16[208,128]{1,0:T(8,128)(2,1)S(1)}, bf16[4,96,256]{2,1,0:T(8,128)(2,1)S(1)}, bf16[320,96]{1,0:T(8,128)(2,1)S(...) custom-call(s32[8,96,128]{2,1,0:T(8,128)} %intensity.1, f32[6,128]{1,0:T(8,128)} %temp_hbm.1, ...), custom_call_target="tpu_custom_call" | custom-call | tf_op jit(solution)/shard_map/pack/pallas_call | solution.py:759
  1.8 0.7 %collective-permute-start = (bf16[208,128]{1,0:T(8,128)(2,1)S(1)}, bf16[208,128]{1,0:T(8,128)(2,1)S(1)}, u32[]{:S(2)}, u32[]{:S(2)}) collective-permute-start(bf16[208,128]{1,0:T(8,128)(2,1)S(1)} %get-tuple-element.19), channel_id=1, source_target_pairs={{4,8},{5,9},{6,10},{7,11},{12,16},{13,17},{14,18},{15,19},{20,24},... | collective-permute-start | bytes 159752 | tf_op jit(solution)/shard_map/ppermute | solution.py:781
  2.4 4.4 %collective-permute-start.1 = (bf16[208,128]{1,0:T(8,128)(2,1)S(1)}, bf16[208,128]{1,0:T(8,128)(2,1)S(1)}, u32[]{:S(2)}, u32[]{:S(2)}) collective-permute-start(bf16[208,128]{1,0:T(8,128)(2,1)S(1)} %get-tuple-element.20), channel_id=1, source_target_pairs={{0,4},{1,5},{2,6},{3,7},{8,12},{9,13},{10,14},{11,15},{16,20},{17,... | collective-permute-start | bytes 159752 | tf_op jit(solution)/shard_map/ppermute | solution.py:781
  6.8 1.0 %early.1 = (f32[4,32,128]{2,1,0:T(8,128)S(1)}, bf16[512,256]{1,0:T(8,128)(2,1)S(1)}, f32[96,1024]{1,0:T(8,128)S(1)}, f32[3,96,128]{2,1,0:T(8,128)S(1)}, bf16[128,48]{1,0:T(8,128)(2,1)S(1)}) custom-call(bf16[4,96,256]{2,1,0:T(8,128)(2,1)S(1)} %get-tuple-element.21.own, bf16[320,96]{1,0:T(8,128)(2,1)S(1)} %get-tuple-element.22.x_parts, ...), custom_call_target="tpu_custom_call" | custom-call | flops 251658240 | bytes 4000000 | tf_op jit(solution)/shard_map/early/pallas_call | solution.py:807
  7.8 0.0 collective-permute-done.far
  7.8 0.0 collective-permute-done.1.near
  7.8 1.9 %late.1 = (bf16[4,144,128]{2,1,0:T(8,128)(2,1)}, bf16[384,256]{1,0:T(8,128)(2,1)S(1)}, bf16[528,128]{1,0:T(8,128)(2,1)S(1)}, bf16[384,128]{1,0:T(8,128)(2,1)S(1)}) custom-call(bf16[208,128]{1,0:T(8,128)(2,1)S(1)} %collective-permute-done.far, bf16[208,128]{1,0:T(8,128)(2,1)S(1)} %collective-permute-done.1.near, ...), custom_call_target="tpu_custom_call" | custom-call | flops 125829120 | bytes 4000000 | tf_op jit(solution)/shard_map/late/pallas_call | solution.py:826
  9.8 0.0 copy-start
  9.8 5.9 %all-to-all-start = ((bf16[4,144,128]{2,1,0:T(8,128)(2,1)}), bf16[4,144,128]{2,1,0:T(8,128)(2,1)S(1)}, u32[]{:S(2)}, u32[]{:S(2)}) async-start(bf16[4,144,128]{2,1,0:T(8,128)(2,1)} %get-tuple-element.31), calls=%async_computation | async-start | bytes 294912 | tf_op jit(solution)/shard_map/all_to_all | solution.py:849
  15.7 0.0 copy-done
  15.7 0.1 copy.18
  15.8 0.0 copy-start.1
  15.8 0.1 eq.15
  15.9 0.6 %copy-done.1 = f32[8]{0:T(128)S(1)} copy-done((f32[8]{0:T(128)S(1)}, f32[8]{0:T(128)}, u32[]{:S(2)}) %copy-start.1) | copy-done | bytes 56
  16.5 0.2 select_reduce_fusion
  16.6 0.1 copy.19.tools
  16.7 3.8 %all-to-all-done.chunks = bf16[4,144,128]{2,1,0:T(8,128)(2,1)S(1)} async-done(((bf16[4,144,128]{2,1,0:T(8,128)(2,1)}), bf16[4,144,128]{2,1,0:T(8,128)(2,1)S(1)}, u32[]{:S(2)}, u32[]{:S(2)}) %all-to-all-start) | async-done | bytes 147488 | tf_op jit(solution)/shard_map/all_to_all | solution.py:849
  20.5 1.5 %cure.1 = (f32[6,128]{1,0:T(8,128)}, f32[6,128]{1,0:T(8,128)}, f32[3,6,128]{2,1,0:T(8,128)}) custom-call(bf16[4,144,128]{2,1,0:T(8,128)(2,1)S(1)} %all-to-all-done.chunks, f32[6,128]{1,0:T(8,128)S(1)} %get-tuple-element.29.temp.temp_in, f32[6,128]{1,0:T(8,128)S(1)} %get-tuple-element.30.cure.cure_in, f32[6,1]{1,0:T(8,128)S(1)} %copy.19.tools, ...), custom_call_target="tpu_custom_call" | custom-call | tf_op jit(solution)/shard_map/cure/pallas_call | solution.py:858
Async XLA Ops:
  1.8 6.1 %collective-permute-start = (bf16[208,128]{1,0:T(8,128)(2,1)S(1)}, bf16[208,128]{1,0:T(8,128)(2,1)S(1)}, u32[]{:S(2)}, u32[]{:S(2)}) collective-permute-start(bf16[208,128]{1,0:T(8,128)(2,1)S(1)} %get-tuple-element.19), channel_id=1, source_target_pairs={{4,8},{5,9},{6,10},{7,11},{12,16},{13,17},{14,18},{15,19},{20,24},... | collective-permute-start | bytes 159752 | tf_op jit(solution)/shard_map/ppermute | solution.py:781
  2.4 5.4 %collective-permute-start.1 = (bf16[208,128]{1,0:T(8,128)(2,1)S(1)}, bf16[208,128]{1,0:T(8,128)(2,1)S(1)}, u32[]{:S(2)}, u32[]{:S(2)}) collective-permute-start(bf16[208,128]{1,0:T(8,128)(2,1)S(1)} %get-tuple-element.20), channel_id=1, source_target_pairs={{0,4},{1,5},{2,6},{3,7},{8,12},{9,13},{10,14},{11,15},{16,20},{17,... | collective-permute-start | bytes 159752 | tf_op jit(solution)/shard_map/ppermute | solution.py:781
  9.8 5.9 %copy-start = (s32[3,2]{0,1:T(2,128)S(1)}, s32[3,2]{0,1:T(2,128)}, u32[]{:S(2)}) copy-start(s32[3,2]{0,1:T(2,128)} %param.15) | copy-start | bytes 76
  9.8 10.7 %all-to-all-start = ((bf16[4,144,128]{2,1,0:T(8,128)(2,1)}), bf16[4,144,128]{2,1,0:T(8,128)(2,1)S(1)}, u32[]{:S(2)}, u32[]{:S(2)}) async-start(bf16[4,144,128]{2,1,0:T(8,128)(2,1)} %get-tuple-element.31), calls=%async_computation | async-start | bytes 294912 | tf_op jit(solution)/shard_map/all_to_all | solution.py:849
  15.8 0.7 %copy-start.1 = (f32[8]{0:T(128)S(1)}, f32[8]{0:T(128)}, u32[]{:S(2)}) copy-start(f32[8]{0:T(128)} %param.14) | copy-start | bytes 100

commit v17 on v16

--- a/solution.py
+++ b/solution.py
@@ -477,17 +477,8 @@
 
 def late_kernel(
     starts, width, far, near, x_late, z_parts, diagonal, early_sums, sides, own_tiles, temp, cure,
-    flat_hbm, steep_hbm, cells_hbm, out_hbm, flat, steep, cell_bands, across, filtered, grads,
-    out, sems,
+    out_hbm, across, filtered, grads, out, sems,
 ):
-    constants = [
-        pltpu.make_async_copy(source, target, sems.at[2 + index])
-        for index, (source, target) in enumerate(
-            ((flat_hbm, flat), (steep_hbm, steep), (cells_hbm, cell_bands))
-        )
-    ]
-    for copy in constants:
-        copy.start()
     double = diagonal.shape[1]
     depth = double // 2
     rows = across.shape[1] // depth
@@ -573,7 +564,7 @@
         sent = two_parts(jnp.concatenate(pieces, axis=0))
         out[position, voxels + folded :, :] = sent.astype(jnp.bfloat16)
     copies[1].start()
-    for copy in copies + constants:
+    for copy in copies:
         copy.wait()
 
 
@@ -755,7 +746,6 @@
     flat, _ = stacked(np.concatenate([rims[0], rims[2]], axis=1))
     steep, rim_starts = stacked(rims[1], *rim_x_bands(count))
     cell_bands, _ = stacked(rim_cells(rows, depth, depths))
-    constants = (flat, steep, cell_bands)
     far, near, own, x_parts, z_parts, temp, cure = pl.pallas_call(
         pack_kernel,
         name="pack",
@@ -823,23 +813,17 @@
     products_x, voxels = own_columns(count)
     at_sums, half = chunk_rows(count, lanes)
     chunk_shape = (depths, at_sums + 2 * half, LANES)
-    chunks, flat, steep, cell_bands = pl.pallas_call(
+    chunks = pl.pallas_call(
         functools.partial(late_kernel, late_starts, width),
         name="late",
-        out_shape=(
-            pltpu.HBM(chunk_shape, bf16),
-            *[pltpu.VMEM(values.shape, bf16) for values in constants],
-        ),
-        in_specs=[vmem] * 10 + [stay] * 3,
-        out_specs=(stay, vmem, vmem, vmem),
+        out_shape=pltpu.HBM(chunk_shape, bf16),
+        in_specs=[vmem] * 10,
+        out_specs=stay,
         scratch_shapes=scratch(late)
-        + [pltpu.VMEM(chunk_shape, bf16), pltpu.SemaphoreType.DMA((5,))],
+        + [pltpu.VMEM(chunk_shape, bf16), pltpu.SemaphoreType.DMA((2,))],
         cost_estimate=cost(late),
         compiler_params=params,
-    )(
-        far, near, x_late, z_parts, diagonal, early_sums, sides, own_tiles, temp, cure,
-        *[fixed(values) for values in constants],
-    )
+    )(far, near, x_late, z_parts, diagonal, early_sums, sides, own_tiles, temp, cure)
 
     faces = plan.reshape(2 * STEPS, 1) == jnp.arange(tool_levels.shape[0], dtype=jnp.int32)
     tools = jnp.sum(

time: 22.3 us -> 22.1 us (level)
  Pallas kernels: 5.58 us -> 5.23 us
    pallas_call x1, Pallas kernels: 1.93 us -> 1.56 us  [on_device(): pl.pallas_call(functools.partial(late_kernel, late_starts, width), name='...]
    unnamed x5 -> x11, local copies, waits for them, and re-layouts: 0.67 us -> 0.69 us
where the time goes in v17:
time: 22.1 us; the launch traced here: 21.9 us
  starting transfers between devices  11.1 us (50%)
  Pallas kernels  5.23 us (24%)
  waiting for transfers between devices  3.81 us (17%)
  local copies, waits for them, and re-layouts  0.87 us (4%)
  between operations  0.72 us (3%)
    all_to_all x1, starting transfers between devices, on_device(): lax.all_to_all(chunks, 'depth', split_axis=0, concat_axis=0, tiled=True,...  6.04 us
    ppermute x2, starting transfers between devices, moved(): return lax.ppermute(values, ('plane', 'depth'), index)  5.03 us
    all_to_all x1, waiting for transfers between devices, on_device(): lax.all_to_all(chunks, 'depth', split_axis=0, concat_axis=0, tiled=True,...  3.8 us
    pallas_call x1, Pallas kernels, on_device(): pl.pallas_call(functools.partial(late_kernel, late_starts, width), name='...  1.56 us
    pallas_call x1, Pallas kernels, on_device(): pl.pallas_call(functools.partial(cure_kernel, cells, rim_starts), name='c...  1.51 us
    pallas_call x1, Pallas kernels, on_device(): pl.pallas_call(pack_kernel, name='pack', out_shape=(pltpu.VMEM((slots, de...  1.13 us
    pallas_call x1, Pallas kernels, on_device(): pl.pallas_call(functools.partial(early_kernel, early_starts), name='early...  1.02 us
    unnamed x11, local copies, waits for them, and re-layouts  0.69 us
  transfers between devices with their start and end apart: 3, of which 1 were waited for; matrix products, arithmetic and copies ran while one was open for 2% of the time, Pallas kernels for 5%

profile of v17, /device:TPU:0, one launch (start us, length us, event | category | flops | bytes accessed | tf_op | source)
XLA Modules:
  0.0 21.9 jit_solution(14142049537558998789)
XLA Ops:
  0.6 1.1 %pack.1 = (bf16[208,128]{1,0:T(8,128)(2,1)S(1)}, bf16[208,128]{1,0:T(8,128)(2,1)S(1)}, bf16[4,96,256]{2,1,0:T(8,128)(2,1)S(1)}, bf16[320,96]{1,0:T(8,128)(2,1)S(...) custom-call(s32[8,96,128]{2,1,0:T(8,128)} %intensity.1, f32[6,128]{1,0:T(8,128)} %temp_hbm.1, ...), custom_call_target="tpu_custom_call" | custom-call | tf_op jit(solution)/shard_map/pack/pallas_call | solution.py:749
  1.8 0.7 %collective-permute-start = (bf16[208,128]{1,0:T(8,128)(2,1)S(1)}, bf16[208,128]{1,0:T(8,128)(2,1)S(1)}, u32[]{:S(2)}, u32[]{:S(2)}) collective-permute-start(bf16[208,128]{1,0:T(8,128)(2,1)S(1)} %get-tuple-element.15), channel_id=1, source_target_pairs={{4,8},{5,9},{6,10},{7,11},{12,16},{13,17},{14,18},{15,19},{20,24},... | collective-permute-start | bytes 159752 | tf_op jit(solution)/shard_map/ppermute | solution.py:771
  2.4 4.4 %collective-permute-start.1 = (bf16[208,128]{1,0:T(8,128)(2,1)S(1)}, bf16[208,128]{1,0:T(8,128)(2,1)S(1)}, u32[]{:S(2)}, u32[]{:S(2)}) collective-permute-start(bf16[208,128]{1,0:T(8,128)(2,1)S(1)} %get-tuple-element.16), channel_id=1, source_target_pairs={{0,4},{1,5},{2,6},{3,7},{8,12},{9,13},{10,14},{11,15},{16,20},{17,... | collective-permute-start | bytes 159752 | tf_op jit(solution)/shard_map/ppermute | solution.py:771
  6.8 1.0 %early.1 = (f32[4,32,128]{2,1,0:T(8,128)S(1)}, bf16[512,256]{1,0:T(8,128)(2,1)S(1)}, f32[96,1024]{1,0:T(8,128)S(1)}, f32[3,96,128]{2,1,0:T(8,128)S(1)}, bf16[128,48]{1,0:T(8,128)(2,1)S(1)}) custom-call(bf16[4,96,256]{2,1,0:T(8,128)(2,1)S(1)} %get-tuple-element.17.own, bf16[320,96]{1,0:T(8,128)(2,1)S(1)} %get-tuple-element.18.x_parts, ...), custom_call_target="tpu_custom_call" | custom-call | flops 251658240 | bytes 4000000 | tf_op jit(solution)/shard_map/early/pallas_call | solution.py:797
  7.8 0.0 collective-permute-done.far
  7.8 0.0 collective-permute-done.1.near
  7.9 0.0 copy-start.3
  7.9 0.0 copy-start.1
  7.9 1.6 %late.1 = bf16[4,144,128]{2,1,0:T(8,128)(2,1)} custom-call(bf16[208,128]{1,0:T(8,128)(2,1)S(1)} %collective-permute-done.far, bf16[208,128]{1,0:T(8,128)(2,1)S(1)} %collective-permute-done.1.near, bf16[128,48]{1,0:T(8,128)(2,1)S(1)} %get-tuple-element.20.x_late, bf16[384,128]{1,0:T(8,128)(2,1)S(1)} %get-tuple-element.19.z_parts, ...), custom_call_target="tpu_custom_call" | custom-call | flops 125829120 | bytes 4000000 | tf_op jit(solution)/shard_map/late/pallas_call | solution.py:816
  9.4 0.0 copy-start
  9.5 0.0 copy-start.2
  9.5 6.0 %all-to-all-start = ((bf16[4,144,128]{2,1,0:T(8,128)(2,1)}), bf16[4,144,128]{2,1,0:T(8,128)(2,1)S(1)}, u32[]{:S(2)}, u32[]{:S(2)}) async-start(bf16[4,144,128]{2,1,0:T(8,128)(2,1)} %late.1), calls=%async_computation | async-start | bytes 294912 | tf_op jit(solution)/shard_map/all_to_all | solution.py:833
  15.5 0.0 copy-done.3
  15.5 0.1 copy.18
  15.6 0.0 copy-start.4
  15.6 0.1 eq.15
  15.7 0.6 %copy-done.4 = f32[8]{0:T(128)S(1)} copy-done((f32[8]{0:T(128)S(1)}, f32[8]{0:T(128)}, u32[]{:S(2)}) %copy-start.4) | copy-done | bytes 56
  16.3 0.2 select_reduce_fusion
  16.4 0.1 copy.19.tools
  16.5 3.8 %all-to-all-done.chunks = bf16[4,144,128]{2,1,0:T(8,128)(2,1)S(1)} async-done(((bf16[4,144,128]{2,1,0:T(8,128)(2,1)}), bf16[4,144,128]{2,1,0:T(8,128)(2,1)S(1)}, u32[]{:S(2)}, u32[]{:S(2)}) %all-to-all-start) | async-done | bytes 147488 | tf_op jit(solution)/shard_map/all_to_all | solution.py:833
  20.3 0.0 copy-done.1
  20.3 0.0 copy-done
  20.3 0.0 copy-done.2
  20.4 1.5 %cure.1 = (f32[6,128]{1,0:T(8,128)}, f32[6,128]{1,0:T(8,128)}, f32[3,6,128]{2,1,0:T(8,128)}) custom-call(bf16[4,144,128]{2,1,0:T(8,128)(2,1)S(1)} %all-to-all-done.chunks, f32[6,128]{1,0:T(8,128)S(1)} %get-tuple-element.25.temp.temp_in, f32[6,128]{1,0:T(8,128)S(1)} %get-tuple-element.26.cure.cure_in, f32[6,1]{1,0:T(8,128)S(1)} %copy.19.tools, ...), custom_call_target="tpu_custom_call" | custom-call | tf_op jit(solution)/shard_map/cure/pallas_call | solution.py:842
Async XLA Ops:
  1.8 6.1 %collective-permute-start = (bf16[208,128]{1,0:T(8,128)(2,1)S(1)}, bf16[208,128]{1,0:T(8,128)(2,1)S(1)}, u32[]{:S(2)}, u32[]{:S(2)}) collective-permute-start(bf16[208,128]{1,0:T(8,128)(2,1)S(1)} %get-tuple-element.15), channel_id=1, source_target_pairs={{4,8},{5,9},{6,10},{7,11},{12,16},{13,17},{14,18},{15,19},{20,24},... | collective-permute-start | bytes 159752 | tf_op jit(solution)/shard_map/ppermute | solution.py:771
  2.4 5.4 %collective-permute-start.1 = (bf16[208,128]{1,0:T(8,128)(2,1)S(1)}, bf16[208,128]{1,0:T(8,128)(2,1)S(1)}, u32[]{:S(2)}, u32[]{:S(2)}) collective-permute-start(bf16[208,128]{1,0:T(8,128)(2,1)S(1)} %get-tuple-element.16), channel_id=1, source_target_pairs={{0,4},{1,5},{2,6},{3,7},{8,12},{9,13},{10,14},{11,15},{16,20},{17,... | collective-permute-start | bytes 159752 | tf_op jit(solution)/shard_map/ppermute | solution.py:771
  7.9 7.7 %copy-start.3 = (s32[3,2]{0,1:T(2,128)S(1)}, s32[3,2]{0,1:T(2,128)}, u32[]{:S(2)}) copy-start(s32[3,2]{0,1:T(2,128)} %param.15) | copy-start | bytes 76
  7.9 12.5 %copy-start.1 = (bf16[528,128]{1,0:T(8,128)(2,1)S(1)}, bf16[528,128]{1,0:T(8,128)(2,1)}, u32[]{:S(2)}) copy-start(bf16[528,128]{1,0:T(8,128)(2,1)} %constant.19.clone.steep) | copy-start | bytes 405508
  9.4 10.9 %copy-start = (bf16[384,256]{1,0:T(8,128)(2,1)S(1)}, bf16[384,256]{1,0:T(8,128)(2,1)}, u32[]{:S(2)}) copy-start(bf16[384,256]{1,0:T(8,128)(2,1)} %constant.18.clone.flat) | copy-start | bytes 589828
  9.5 10.9 %copy-start.2 = (bf16[384,128]{1,0:T(8,128)(2,1)S(1)}, bf16[384,128]{1,0:T(8,128)(2,1)}, u32[]{:S(2)}) copy-start(bf16[384,128]{1,0:T(8,128)(2,1)} %constant.20.clone.rim_bands) | copy-start | bytes 294916
  9.5 10.9 %all-to-all-start = ((bf16[4,144,128]{2,1,0:T(8,128)(2,1)}), bf16[4,144,128]{2,1,0:T(8,128)(2,1)S(1)}, u32[]{:S(2)}, u32[]{:S(2)}) async-start(bf16[4,144,128]{2,1,0:T(8,128)(2,1)} %late.1), calls=%async_computation | async-start | bytes 294912 | tf_op jit(solution)/shard_map/all_to_all | solution.py:833
  15.6 0.7 %copy-start.4 = (f32[8]{0:T(128)S(1)}, f32[8]{0:T(128)}, u32[]{:S(2)}) copy-start(f32[8]{0:T(128)} %param.14) | copy-start | bytes 100

commit v18 on v17

--- a/solution.py
+++ b/solution.py
@@ -263,21 +263,21 @@
     return lax.rem(lax.axis_index("plane"), 2) == 1
 
 
-def pack_kernel(
-    intensity, temp_hbm, cure_hbm, x_hbm, z_hbm, far, near, own, x_parts, z_parts, temp, cure,
-    grey, sems,
-):
+def pack_kernel(intensity, temp_hbm, cure_hbm, far, near, temp, cure, edges, sems):
     rows, width, depth = intensity.shape
     copies = [
-        pltpu.make_async_copy(intensity, grey, sems.at[0]),
-        pltpu.make_async_copy(temp_hbm, temp, sems.at[1]),
-        pltpu.make_async_copy(cure_hbm, cure, sems.at[2]),
-        pltpu.make_async_copy(x_hbm, x_parts, sems.at[3]),
-        pltpu.make_async_copy(z_hbm, z_parts, sems.at[4]),
+        pltpu.make_async_copy(
+            intensity.at[:, pl.ds(place, EDGE), :], edges.at[side], sems.at[side]
+        )
+        for side, place in enumerate((0, width - EDGE))
+    ]
+    copies += [
+        pltpu.make_async_copy(temp_hbm, temp, sems.at[2]),
+        pltpu.make_async_copy(cure_hbm, cure, sems.at[3]),
     ]
     for copy in copies:
         copy.start()
-    for copy in copies[:3]:
+    for copy in copies:
         copy.wait()
     odd = is_odd()
     sides = [
@@ -286,9 +286,9 @@
     ]
 
     def send(left, right):
-        for place, target, columns in ((0, left, sides[0]), (width - EDGE, right, sides[1])):
+        for side, (target, columns) in enumerate(((left, sides[0]), (right, sides[1]))):
             for pair in range(rows // 2):
-                two = [grey[2 * pair + i, place : place + EDGE, :] for i in range(2)]
+                two = [edges[side, 2 * pair + i] for i in range(2)]
                 two = jnp.concatenate(two, axis=0).astype(jnp.float32)
                 target[2 * EDGE * pair : 2 * EDGE * (pair + 1), :] = two.astype(jnp.bfloat16)
             for slot in range(temp.shape[1] // LANES):
@@ -302,12 +302,6 @@
     @pl.when(jnp.logical_not(odd))
     def _():
         send(far, near)
-
-    for row in range(rows):
-        half = (row % 2) * depth
-        own[row // 2, :, half : half + depth] = grey[row].astype(jnp.float32).astype(jnp.bfloat16)
-    for copy in copies[3:]:
-        copy.wait()
 
 
 def packed_rows(values, size, first):
@@ -444,13 +438,10 @@
 
 
 def early_kernel(
-    starts, own, x_parts, z_parts, late_hbm, sums, diagonal, sides, tiles, x_late, across,
-    filtered, grads, sem,
+    starts, grey, x_parts, z_parts, sums, diagonal, sides, tiles, across, filtered, grads
 ):
-    copy = pltpu.make_async_copy(late_hbm, x_late, sem.at[0])
-    copy.start()
-    pairs, width, double = own.shape
-    rows, depth = 2 * pairs, double // 2
+    rows, width, depth = grey.shape
+    double = 2 * depth
     empty = jnp.zeros((depth, depth), jnp.bfloat16)
     for kind in range(2):
         for half in range(2):
@@ -458,7 +449,8 @@
             band = z_parts[kind * depth : (kind + 1) * depth, :]
             diagonal[at, half * depth : (half + 1) * depth] = band
             diagonal[at, (1 - half) * depth : (2 - half) * depth] = empty
-    whole = jnp.concatenate([own[pair] for pair in range(pairs)], axis=1)
+    values = [grey[row].astype(jnp.float32) for row in range(rows)]
+    whole = jnp.concatenate([value.astype(jnp.bfloat16) for value in values], axis=1)
     result = product(x_parts[starts[0] : starts[2], :width], whole)
     across[...] = result[: starts[1]]
     sides[...] = result[starts[1] :]
@@ -466,13 +458,8 @@
     results = tensor_sums(across, sx, None, diagonal, z_parts, filtered, grads)
     for index, kind in enumerate(USED):
         sums[index] = results[kind]
-    values = [
-        own[row // 2, :, (row % 2) * depth : (row % 2 + 1) * depth].astype(jnp.float32)
-        for row in range(rows)
-    ]
     for index, tile in enumerate(rim_tiles(values)):
         tiles[index] = tile
-    copy.wait()
 
 
 def late_kernel(
@@ -736,35 +723,32 @@
     late = bands.shape[1] - EARLY
     middle = bands[:, :EARLY, EDGE : EDGE + width]
     sides = bands[:, EARLY:].reshape(2 * late, -1)
-    x_hbm, early_starts = stacked(
+    x_parts, early_starts = stacked(
         middle.reshape(2 * EARLY, -1), sides[:, EDGE : EDGE + width], coarse[:, :EARLY]
     )
-    z_hbm, _ = stacked(*depth_bands(depth), coarse_depth_bands(depth))
+    z_parts, _ = stacked(*depth_bands(depth), coarse_depth_bands(depth))
     halos = np.concatenate([sides[:, :EDGE], sides[:, EDGE + width :]], axis=1)
     x_late, late_starts = stacked(halos, coarse[:, EARLY:])
     rims = rim_bands(rows)
     flat, _ = stacked(np.concatenate([rims[0], rims[2]], axis=1))
     steep, rim_starts = stacked(rims[1], *rim_x_bands(count))
     cell_bands, _ = stacked(rim_cells(rows, depth, depths))
-    far, near, own, x_parts, z_parts, temp, cure = pl.pallas_call(
+    far, near, temp, cure = pl.pallas_call(
         pack_kernel,
         name="pack",
         out_shape=(
             pltpu.VMEM((slots, depth), bf16),
             pltpu.VMEM((slots, depth), bf16),
-            pltpu.VMEM((rows // 2, width, 2 * depth), bf16),
-            pltpu.VMEM(x_hbm.shape, bf16),
-            pltpu.VMEM(z_hbm.shape, bf16),
             pltpu.VMEM((count, lanes), jnp.float32),
             pltpu.VMEM((count, lanes), jnp.float32),
         ),
-        in_specs=[stay] * 5,
+        in_specs=[stay] * 3,
         scratch_shapes=[
-            pltpu.VMEM((rows, width, depth), jnp.int32),
-            pltpu.SemaphoreType.DMA((5,)),
+            pltpu.VMEM((2, rows, EDGE, depth), jnp.int32),
+            pltpu.SemaphoreType.DMA((4,)),
         ],
         compiler_params=params,
-    )(*[fixed(values) for values in (intensity, temp_start, cure_start, x_hbm, z_hbm)])
+    )(*[fixed(values) for values in (intensity, temp_start, cure_start)])
 
     def moved(values, pairs):
         index = [(p * depths + d, q * depths + e) for (p, d), (q, e) in pairs]
@@ -794,7 +778,7 @@
             transcendentals=0,
         )
 
-    early_sums, diagonal, sides, own_tiles, x_late = pl.pallas_call(
+    early_sums, diagonal, sides, own_tiles = pl.pallas_call(
         functools.partial(early_kernel, early_starts),
         name="early",
         out_shape=(
@@ -802,13 +786,11 @@
             pltpu.VMEM((4 * depth, 2 * depth), bf16),
             pltpu.VMEM((2 * late, rows * depth), jnp.float32),
             pltpu.VMEM((3, width, LANES), jnp.float32),
-            pltpu.VMEM(x_late.shape, bf16),
         ),
-        in_specs=[vmem] * 3 + [stay],
-        scratch_shapes=scratch(EARLY) + [pltpu.SemaphoreType.DMA((1,))],
+        scratch_shapes=scratch(EARLY),
         cost_estimate=cost(EARLY),
         compiler_params=params,
-    )(own, x_parts, z_parts, fixed(x_late))
+    )(intensity, x_parts, z_parts)
 
     products_x, voxels = own_columns(count)
     at_sums, half = chunk_rows(count, lanes)

time: 22.1 us -> 23.3 us (1.054)
  local copies, waits for them, and re-layouts: 0.87 us -> 2.66 us
  waiting for transfers between devices: 3.81 us -> 3.23 us
    unnamed x11 -> x19, local copies, waits for them, and re-layouts: 0.69 us -> 2.48 us
    all_to_all x1, waiting for transfers between devices: 3.8 us -> 3.22 us  [on_device(): lax.all_to_all(chunks, 'depth', split_axis=0, concat_axis=0, tiled=True,...]
  transfers between devices with their start and end apart: 3 -> 3, of which waited for: 1 -> 1; matrix products, arithmetic and copies ran while one was open for 2% -> 2% of each run, Pallas kernels for 5% -> 4%
where the time goes in v18:
time: 23.3 us; the launch traced here: 23 us
  starting transfers between devices  11.1 us (48%)
  Pallas kernels  5.14 us (22%)
  waiting for transfers between devices  3.23 us (14%)
  local copies, waits for them, and re-layouts  2.66 us (11%)
  between operations  0.74 us (3%)
    all_to_all x1, starting transfers between devices, on_device(): lax.all_to_all(chunks, 'depth', split_axis=0, concat_axis=0, tiled=True,...  6.04 us
    ppermute x2, starting transfers between devices, moved(): return lax.ppermute(values, ('plane', 'depth'), index)  5.03 us
    all_to_all x1, waiting for transfers between devices, on_device(): lax.all_to_all(chunks, 'depth', split_axis=0, concat_axis=0, tiled=True,...  3.22 us
    unnamed x19, local copies, waits for them, and re-layouts  2.48 us
    pallas_call x1, Pallas kernels, on_device(): pl.pallas_call(functools.partial(late_kernel, late_starts, width), name='...  1.56 us
    pallas_call x1, Pallas kernels, on_device(): pl.pallas_call(functools.partial(cure_kernel, cells, rim_starts), name='c...  1.52 us
    pallas_call x1, Pallas kernels, on_device(): pl.pallas_call(pack_kernel, name='pack', out_shape=(pltpu.VMEM((slots, de...  1.05 us
    pallas_call x1, Pallas kernels, on_device(): pl.pallas_call(functools.partial(early_kernel, early_starts), name='early...  1.01 us
  transfers between devices with their start and end apart: 3, of which 1 were waited for; matrix products, arithmetic and copies ran while one was open for 2% of the time, Pallas kernels for 4%

profile of v18, /device:TPU:0, one launch (start us, length us, event | category | flops | bytes accessed | tf_op | source)
XLA Modules:
  0.0 23.0 jit_solution(1135359426851952554)
XLA Ops:
  0.6 0.0 copy-start
  0.6 1.0 %pack.1 = (bf16[208,128]{1,0:T(8,128)(2,1)S(1)}, bf16[208,128]{1,0:T(8,128)(2,1)S(1)}, f32[6,128]{1,0:T(8,128)S(1)}, f32[6,128]{1,0:T(8,128)S(1)}) custom-call(s32[8,96,128]{2,1,0:T(8,128)} %grey.1, f32[6,128]{1,0:T(8,128)} %temp_hbm.1, f32[6,128]{1,0:T(8,128)} %cure_hbm.1), custom_call_target="tpu_custom_call" | custom-call | tf_op jit(solution)/shard_map/pack/pallas_call | solution.py:736
  1.7 0.7 %collective-permute-start = (bf16[208,128]{1,0:T(8,128)(2,1)S(1)}, bf16[208,128]{1,0:T(8,128)(2,1)S(1)}, u32[]{:S(2)}, u32[]{:S(2)}) collective-permute-start(bf16[208,128]{1,0:T(8,128)(2,1)S(1)} %get-tuple-element.11), channel_id=1, source_target_pairs={{4,8},{5,9},{6,10},{7,11},{12,16},{13,17},{14,18},{15,19},{20,24},... | collective-permute-start | bytes 159752 | tf_op jit(solution)/shard_map/ppermute | solution.py:755
  2.4 4.4 %collective-permute-start.1 = (bf16[208,128]{1,0:T(8,128)(2,1)S(1)}, bf16[208,128]{1,0:T(8,128)(2,1)S(1)}, u32[]{:S(2)}, u32[]{:S(2)}) collective-permute-start(bf16[208,128]{1,0:T(8,128)(2,1)S(1)} %get-tuple-element.12), channel_id=1, source_target_pairs={{0,4},{1,5},{2,6},{3,7},{8,12},{9,13},{10,14},{11,15},{16,20},{17,... | collective-permute-start | bytes 159752 | tf_op jit(solution)/shard_map/ppermute | solution.py:755
  6.7 0.0 copy-done
  6.7 0.9 %copy-done.4 = bf16[384,128]{1,0:T(8,128)(2,1)S(1)} copy-done((bf16[384,128]{1,0:T(8,128)(2,1)S(1)}, bf16[384,128]{1,0:T(8,128)(2,1)}, u32[]{:S(2)}) %copy-start.4) | copy-done | bytes 98328
  7.6 0.9 %copy-done.6 = bf16[320,96]{1,0:T(8,128)(2,1)S(1)} copy-done((bf16[320,96]{1,0:T(8,128)(2,1)S(1)}, bf16[320,96]{1,0:T(8,128)(2,1)}, u32[]{:S(2)}) %copy-start.6) | copy-done | bytes 61464
  8.5 1.0 %early.1 = (f32[4,32,128]{2,1,0:T(8,128)S(1)}, bf16[512,256]{1,0:T(8,128)(2,1)S(1)}, f32[96,1024]{1,0:T(8,128)S(1)}, f32[3,96,128]{2,1,0:T(8,128)S(1)}) custom-call(s32[8,96,128]{2,1,0:T(8,128)S(1)} %copy-done, bf16[320,96]{1,0:T(8,128)(2,1)S(1)} %copy-done.6, bf16[384,128]{1,0:T(8,128)(2,1)S(1)} %copy-done.4), custom_call_target="tpu_custom_call" | custom-call | flops 251658240 | bytes 4000000 | tf_op jit(solution)/shard_map/early/pallas_call | solution.py:781
  9.5 0.0 collective-permute-done.far
  9.5 0.0 collective-permute-done.1.near
  9.6 0.0 copy-start.7
  9.6 0.0 copy-start.2
  9.6 1.6 %late.1 = bf16[4,144,128]{2,1,0:T(8,128)(2,1)} custom-call(bf16[208,128]{1,0:T(8,128)(2,1)S(1)} %collective-permute-done.far, bf16[208,128]{1,0:T(8,128)(2,1)S(1)} %collective-permute-done.1.near, bf16[128,48]{1,0:T(8,128)(2,1)S(1)} %copy-done.5, bf16[384,128]{1,0:T(8,128)(2,1)S(1)} %copy-done.4, bf16[512,256]{1,0:T(8,128)(2,1)S(1)} %get-tuple-element.13.diagonal, ...), custom_call_target="tpu_custom_call" | custom-call | flops 125829120 | bytes 4000000 | tf_op jit(solution)/shard_map/late/pallas_call | solution.py:798
  11.2 0.0 copy-start.1
  11.2 0.0 copy-start.3
  11.2 6.0 %all-to-all-start = ((bf16[4,144,128]{2,1,0:T(8,128)(2,1)}), bf16[4,144,128]{2,1,0:T(8,128)(2,1)S(1)}, u32[]{:S(2)}, u32[]{:S(2)}) async-start(bf16[4,144,128]{2,1,0:T(8,128)(2,1)} %late.1), calls=%async_computation | async-start | bytes 294912 | tf_op jit(solution)/shard_map/all_to_all | solution.py:815
  17.2 0.1 copy.18
  17.3 0.1 eq.15
  17.4 0.6 %copy-done.8 = f32[8]{0:T(128)S(1)} copy-done((f32[8]{0:T(128)S(1)}, f32[8]{0:T(128)}, u32[]{:S(2)}) %copy-start.8) | copy-done | bytes 56
  18.0 0.2 select_reduce_fusion
  18.2 0.1 copy.19.tools
  18.3 3.2 %all-to-all-done.chunks = bf16[4,144,128]{2,1,0:T(8,128)(2,1)S(1)} async-done(((bf16[4,144,128]{2,1,0:T(8,128)(2,1)}), bf16[4,144,128]{2,1,0:T(8,128)(2,1)S(1)}, u32[]{:S(2)}, u32[]{:S(2)}) %all-to-all-start) | async-done | bytes 147488 | tf_op jit(solution)/shard_map/all_to_all | solution.py:815
  21.5 0.0 copy-done.2
  21.5 1.5 %cure.1 = (f32[6,128]{1,0:T(8,128)}, f32[6,128]{1,0:T(8,128)}, f32[3,6,128]{2,1,0:T(8,128)}) custom-call(bf16[4,144,128]{2,1,0:T(8,128)(2,1)S(1)} %all-to-all-done.chunks, f32[6,128]{1,0:T(8,128)S(1)} %get-tuple-element.17.temp.temp_in, f32[6,128]{1,0:T(8,128)S(1)} %get-tuple-element.18.cure.cure_in, f32[6,1]{1,0:T(8,128)S(1)} %copy.19.tools, ...), custom_call_target="tpu_custom_call" | custom-call | tf_op jit(solution)/shard_map/cure/pallas_call | solution.py:824
  (8 shorter events, 0.0 us)
Async XLA Ops:
  0.6 6.1 %copy-start = (s32[8,96,128]{2,1,0:T(8,128)S(1)}, s32[8,96,128]{2,1,0:T(8,128)}, u32[]{:S(2)}) copy-start(s32[8,96,128]{2,1,0:T(8,128)} %grey.1) | copy-start | bytes 1179652
  1.7 7.8 %collective-permute-start = (bf16[208,128]{1,0:T(8,128)(2,1)S(1)}, bf16[208,128]{1,0:T(8,128)(2,1)S(1)}, u32[]{:S(2)}, u32[]{:S(2)}) collective-permute-start(bf16[208,128]{1,0:T(8,128)(2,1)S(1)} %get-tuple-element.11), channel_id=1, source_target_pairs={{4,8},{5,9},{6,10},{7,11},{12,16},{13,17},{14,18},{15,19},{20,24},... | collective-permute-start | bytes 159752 | tf_op jit(solution)/shard_map/ppermute | solution.py:755
  2.4 7.2 %collective-permute-start.1 = (bf16[208,128]{1,0:T(8,128)(2,1)S(1)}, bf16[208,128]{1,0:T(8,128)(2,1)S(1)}, u32[]{:S(2)}, u32[]{:S(2)}) collective-permute-start(bf16[208,128]{1,0:T(8,128)(2,1)S(1)} %get-tuple-element.12), channel_id=1, source_target_pairs={{0,4},{1,5},{2,6},{3,7},{8,12},{9,13},{10,14},{11,15},{16,20},{17,... | collective-permute-start | bytes 159752 | tf_op jit(solution)/shard_map/ppermute | solution.py:755
  6.7 0.9 %copy-start.4 = (bf16[384,128]{1,0:T(8,128)(2,1)S(1)}, bf16[384,128]{1,0:T(8,128)(2,1)}, u32[]{:S(2)}) copy-start(bf16[384,128]{1,0:T(8,128)(2,1)} %constant.16.clone.z_parts) | copy-start | bytes 294916
  7.6 0.9 %copy-start.6 = (bf16[320,96]{1,0:T(8,128)(2,1)S(1)}, bf16[320,96]{1,0:T(8,128)(2,1)}, u32[]{:S(2)}) copy-start(bf16[320,96]{1,0:T(8,128)(2,1)} %constant.6.clone.x_parts) | copy-start | bytes 184324
  8.5 1.0 %copy-start.5 = (bf16[128,48]{1,0:T(8,128)(2,1)S(1)}, bf16[128,48]{1,0:T(8,128)(2,1)}, u32[]{:S(2)}) copy-start(bf16[128,48]{1,0:T(8,128)(2,1)} %constant.17.clone.x_late) | copy-start | bytes 36868
  9.6 7.7 %copy-start.7 = (s32[3,2]{0,1:T(2,128)S(1)}, s32[3,2]{0,1:T(2,128)}, u32[]{:S(2)}) copy-start(s32[3,2]{0,1:T(2,128)} %param.15) | copy-start | bytes 76
  9.6 11.9 %copy-start.2 = (bf16[528,128]{1,0:T(8,128)(2,1)S(1)}, bf16[528,128]{1,0:T(8,128)(2,1)}, u32[]{:S(2)}) copy-start(bf16[528,128]{1,0:T(8,128)(2,1)} %constant.19.clone.steep) | copy-start | bytes 405508
  11.2 10.3 %copy-start.1 = (bf16[384,256]{1,0:T(8,128)(2,1)S(1)}, bf16[384,256]{1,0:T(8,128)(2,1)}, u32[]{:S(2)}) copy-start(bf16[384,256]{1,0:T(8,128)(2,1)} %constant.18.clone.flat) | copy-start | bytes 589828
  11.2 10.3 %copy-start.3 = (bf16[384,128]{1,0:T(8,128)(2,1)S(1)}, bf16[384,128]{1,0:T(8,128)(2,1)}, u32[]{:S(2)}) copy-start(bf16[384,128]{1,0:T(8,128)(2,1)} %constant.20.clone.rim_bands) | copy-start | bytes 294916
  11.2 10.3 %all-to-all-start = ((bf16[4,144,128]{2,1,0:T(8,128)(2,1)}), bf16[4,144,128]{2,1,0:T(8,128)(2,1)S(1)}, u32[]{:S(2)}, u32[]{:S(2)}) async-start(bf16[4,144,128]{2,1,0:T(8,128)(2,1)} %late.1), calls=%async_computation | async-start | bytes 294912 | tf_op jit(solution)/shard_map/all_to_all | solution.py:815
  17.3 0.7 %copy-start.8 = (f32[8]{0:T(128)S(1)}, f32[8]{0:T(128)}, u32[]{:S(2)}) copy-start(f32[8]{0:T(128)} %param.14) | copy-start | bytes 100

commit v19 on v18

--- a/solution.py
+++ b/solution.py
@@ -34,6 +34,7 @@
 EARLY = 96
 GHOST = 3
 COLUMN_ROWS = 2 * GHOST - 1
+CODE_SCALE = 2.0**20
 RIM = 2 * R1
 BEFORE = -(-(R2 - R1) // COARSE)
 AFTER = BEFORE
@@ -244,6 +245,16 @@
     return parts[:half] + parts[half:]
 
 
+def coded(values):
+    values = values * CODE_SCALE
+    return (values * jnp.abs(values)) * (values * values)
+
+
+def decoded(values):
+    size = jnp.sqrt(jnp.sqrt(jnp.abs(values))) * (1.0 / CODE_SCALE)
+    return jnp.where(values < 0.0, -size, size)
+
+
 def column_rows(temp, cure, at_end):
     count = temp.shape[0]
     first, second = (count - GHOST, count - GHOST + 1) if at_end else (0, 0)
@@ -256,14 +267,17 @@
 def chunk_rows(count, lanes):
     products, voxels = own_columns(count)
     held = count + 2 * HALO + 1 + COLUMN_ROWS * (lanes // LANES)
-    return voxels + fold(voxels), -(-held // 8) * 8
+    return voxels + fold(voxels), -(-held // 16) * 16
 
 
 def is_odd():
     return lax.rem(lax.axis_index("plane"), 2) == 1
 
 
-def pack_kernel(intensity, temp_hbm, cure_hbm, far, near, temp, cure, edges, sems):
+def pack_kernel(
+    intensity, temp_hbm, cure_hbm, x_hbm, z_hbm, far, near, temp, cure, x_parts, z_parts, edges,
+    sems,
+):
     rows, width, depth = intensity.shape
     copies = [
         pltpu.make_async_copy(
@@ -274,6 +288,8 @@
     copies += [
         pltpu.make_async_copy(temp_hbm, temp, sems.at[2]),
         pltpu.make_async_copy(cure_hbm, cure, sems.at[3]),
+        pltpu.make_async_copy(x_hbm, x_parts, sems.at[4]),
+        pltpu.make_async_copy(z_hbm, z_parts, sems.at[5]),
     ]
     for copy in copies:
         copy.start()
@@ -542,14 +558,14 @@
         if target == out.shape[0] - 1:
             piece = jnp.where(layer == 0, right, piece)
         mine = slice(count * target, count * target + height)
-        pieces = [joint[mine], jnp.sum(rest[mine], axis=0, keepdims=True)]
+        pieces = [coded(joint[mine]), coded(jnp.sum(rest[mine], axis=0, keepdims=True))]
         for slot in range(lanes // LANES):
-            pieces.append(piece[0:COLUMN_ROWS, slot * LANES : (slot + 1) * LANES])
+            part = piece[:, slot * LANES : (slot + 1) * LANES]
+            pieces += [part[:GHOST] - reference_temp, part[GHOST:COLUMN_ROWS]]
         filled = sum(part.shape[0] for part in pieces)
         if filled < half:
             pieces.append(jnp.zeros((half - filled, LANES), jnp.float32))
-        sent = two_parts(jnp.concatenate(pieces, axis=0))
-        out[position, voxels + folded :, :] = sent.astype(jnp.bfloat16)
+        out[position, voxels + folded :, :] = jnp.concatenate(pieces, axis=0).astype(jnp.bfloat16)
     copies[1].start()
     for copy in copies:
         copy.wait()
@@ -618,9 +634,20 @@
 
     near = rim_sums(chunks, count, starts, flat, steep, rim_bands)
     sums = [near[0] + near[1] + near[2], near[1], near[2], near[5]]
-    blocks = [
-        joined(chunks[order.index(part), at_sums:, :].astype(jnp.float32)) for part in range(parts)
-    ]
+    blocks = [chunks[order.index(part), at_sums:, :].astype(jnp.float32) for part in range(parts)]
+    columns = [
+        jnp.concatenate(
+            [
+                block[at : at + COLUMN_ROWS]
+                for at in range(
+                    height + 1, height + 1 + COLUMN_ROWS * (lanes // LANES), COLUMN_ROWS
+                )
+            ],
+            axis=1,
+        )
+        for block in blocks
+    ]
+    blocks = [decoded(block[0:16]) for block in blocks]
     tails = [block[height : height + 1] for block in blocks]
     if parts % 8:
         tails.append(jnp.zeros((-parts % 8, LANES), jnp.float32))
@@ -662,16 +689,17 @@
     ]
     copies[0].start()
 
-    slots = range(height + 1, height + 1 + COLUMN_ROWS * (lanes // LANES), COLUMN_ROWS)
-    columns = [
-        jnp.concatenate([values[at : at + COLUMN_ROWS] for at in slots], axis=1) for values in blocks
-    ]
     before, after = columns[parts - 1], columns[0]
     for part in range(parts - 1):
         before = jnp.where(layer == part + 1, columns[part], before)
         after = jnp.where(layer == part, columns[part + 1], after)
     spare = jnp.full((16 - count - 2 * GHOST, lanes), 0.5, jnp.float32)
-    temp = jnp.concatenate([before[:GHOST], temp_in[...], after[:GHOST], 8.0 * spare], axis=0)
+    temp = jnp.concatenate([
+            before[:GHOST] + reference_temp,
+            temp_in[...],
+            after[:GHOST] + reference_temp,
+            8.0 * spare,
+        ], axis=0)
     cure = jnp.concatenate([spare[:1], before[GHOST:], cure_in[...], after[GHOST:], spare[:1], spare], axis=0)
     gap = GHOST - HALO
     xx, xz, zz = [pltpu.roll(part, gap, 0) for part in conduct]
@@ -723,17 +751,17 @@
     late = bands.shape[1] - EARLY
     middle = bands[:, :EARLY, EDGE : EDGE + width]
     sides = bands[:, EARLY:].reshape(2 * late, -1)
-    x_parts, early_starts = stacked(
+    x_hbm, early_starts = stacked(
         middle.reshape(2 * EARLY, -1), sides[:, EDGE : EDGE + width], coarse[:, :EARLY]
     )
-    z_parts, _ = stacked(*depth_bands(depth), coarse_depth_bands(depth))
+    z_hbm, _ = stacked(*depth_bands(depth), coarse_depth_bands(depth))
     halos = np.concatenate([sides[:, :EDGE], sides[:, EDGE + width :]], axis=1)
     x_late, late_starts = stacked(halos, coarse[:, EARLY:])
     rims = rim_bands(rows)
     flat, _ = stacked(np.concatenate([rims[0], rims[2]], axis=1))
     steep, rim_starts = stacked(rims[1], *rim_x_bands(count))
     cell_bands, _ = stacked(rim_cells(rows, depth, depths))
-    far, near, temp, cure = pl.pallas_call(
+    far, near, temp, cure, x_parts, z_parts = pl.pallas_call(
         pack_kernel,
         name="pack",
         out_shape=(
@@ -741,14 +769,16 @@
             pltpu.VMEM((slots, depth), bf16),
             pltpu.VMEM((count, lanes), jnp.float32),
             pltpu.VMEM((count, lanes), jnp.float32),
+            pltpu.VMEM(x_hbm.shape, bf16),
+            pltpu.VMEM(z_hbm.shape, bf16),
         ),
-        in_specs=[stay] * 3,
+        in_specs=[stay] * 5,
         scratch_shapes=[
             pltpu.VMEM((2, rows, EDGE, depth), jnp.int32),
-            pltpu.SemaphoreType.DMA((4,)),
+            pltpu.SemaphoreType.DMA((6,)),
         ],
         compiler_params=params,
-    )(*[fixed(values) for values in (intensity, temp_start, cure_start)])
+    )(*[fixed(values) for values in (intensity, temp_start, cure_start, x_hbm, z_hbm)])
 
     def moved(values, pairs):
         index = [(p * depths + d, q * depths + e) for (p, d), (q, e) in pairs]
@@ -794,7 +824,7 @@
 
     products_x, voxels = own_columns(count)
     at_sums, half = chunk_rows(count, lanes)
-    chunk_shape = (depths, at_sums + 2 * half, LANES)
+    chunk_shape = (depths, at_sums + half, LANES)
     chunks = pl.pallas_call(
         functools.partial(late_kernel, late_starts, width),
         name="late",

time: 23.3 us -> 22 us (0.944)
  local copies, waits for them, and re-layouts: 2.66 us -> 0.88 us
  waiting for transfers between devices: 3.23 us -> 3.63 us
    unnamed x19 -> x15, local copies, waits for them, and re-layouts: 2.48 us -> 0.7 us
    all_to_all x1, waiting for transfers between devices: 3.22 us -> 3.63 us  [on_device(): lax.all_to_all(chunks, 'depth', split_axis=0, concat_axis=0, tiled=True,...]
  transfers between devices with their start and end apart: 3 -> 3, of which waited for: 1 -> 1; matrix products, arithmetic and copies ran while one was open for 2% -> 2% of each run, Pallas kernels for 4% -> 5%
where the time goes in v19:
time: 22 us; the launch traced here: 21.7 us
  starting transfers between devices  11 us (50%)
  Pallas kernels  5.27 us (24%)
  waiting for transfers between devices  3.63 us (16%)
  local copies, waits for them, and re-layouts  0.88 us (4%)
  between operations  0.73 us (3%)
    all_to_all x1, starting transfers between devices, on_device(): lax.all_to_all(chunks, 'depth', split_axis=0, concat_axis=0, tiled=True,...  6.01 us
    ppermute x2, starting transfers between devices, moved(): return lax.ppermute(values, ('plane', 'depth'), index)  5.03 us
    all_to_all x1, waiting for transfers between devices, on_device(): lax.all_to_all(chunks, 'depth', split_axis=0, concat_axis=0, tiled=True,...  3.63 us
    pallas_call x1, Pallas kernels, on_device(): pl.pallas_call(functools.partial(late_kernel, late_starts, width), name='...  1.56 us
    pallas_call x1, Pallas kernels, on_device(): pl.pallas_call(functools.partial(cure_kernel, cells, rim_starts), name='c...  1.52 us
    pallas_call x1, Pallas kernels, on_device(): pl.pallas_call(pack_kernel, name='pack', out_shape=(pltpu.VMEM((slots, de...  1.18 us
    pallas_call x1, Pallas kernels, on_device(): pl.pallas_call(functools.partial(early_kernel, early_starts), name='early...  1.01 us
    unnamed x15, local copies, waits for them, and re-layouts  0.7 us
  transfers between devices with their start and end apart: 3, of which 1 were waited for; matrix products, arithmetic and copies ran while one was open for 2% of the time, Pallas kernels for 5%

profile of v19, /device:TPU:0, one launch (start us, length us, event | category | flops | bytes accessed | tf_op | source)
XLA Modules:
  0.0 21.7 jit_solution(1961231139183447957)
XLA Ops:
  0.6 0.0 copy-start
  0.6 1.2 %pack.1 = (bf16[208,128]{1,0:T(8,128)(2,1)S(1)}, bf16[208,128]{1,0:T(8,128)(2,1)S(1)}, f32[6,128]{1,0:T(8,128)S(1)}, f32[6,128]{1,0:T(8,128)S(1)}, bf16[320,96]{...) custom-call(s32[8,96,128]{2,1,0:T(8,128)} %grey.1, f32[6,128]{1,0:T(8,128)} %temp_hbm.1, f32[6,128]{1,0:T(8,128)} %cure_hbm.1, ...), custom_call_target="tpu_custom_call" | custom-call | tf_op jit(solution)/shard_map/pack/pallas_call | solution.py:764
  1.8 0.7 %collective-permute-start = (bf16[208,128]{1,0:T(8,128)(2,1)S(1)}, bf16[208,128]{1,0:T(8,128)(2,1)S(1)}, u32[]{:S(2)}, u32[]{:S(2)}) collective-permute-start(bf16[208,128]{1,0:T(8,128)(2,1)S(1)} %get-tuple-element.13), channel_id=1, source_target_pairs={{4,8},{5,9},{6,10},{7,11},{12,16},{13,17},{14,18},{15,19},{20,24},... | collective-permute-start | bytes 159752 | tf_op jit(solution)/shard_map/ppermute | solution.py:785
  2.5 4.4 %collective-permute-start.1 = (bf16[208,128]{1,0:T(8,128)(2,1)S(1)}, bf16[208,128]{1,0:T(8,128)(2,1)S(1)}, u32[]{:S(2)}, u32[]{:S(2)}) collective-permute-start(bf16[208,128]{1,0:T(8,128)(2,1)S(1)} %get-tuple-element.14), channel_id=1, source_target_pairs={{0,4},{1,5},{2,6},{3,7},{8,12},{9,13},{10,14},{11,15},{16,20},{17,... | collective-permute-start | bytes 159752 | tf_op jit(solution)/shard_map/ppermute | solution.py:785
  6.9 0.0 copy-done
  6.9 1.0 %early.1 = (f32[4,32,128]{2,1,0:T(8,128)S(1)}, bf16[512,256]{1,0:T(8,128)(2,1)S(1)}, f32[96,1024]{1,0:T(8,128)S(1)}, f32[3,96,128]{2,1,0:T(8,128)S(1)}) custom-call(s32[8,96,128]{2,1,0:T(8,128)S(1)} %copy-done, bf16[320,96]{1,0:T(8,128)(2,1)S(1)} %get-tuple-element.16.x_parts, bf16[384,128]{1,0:T(8,128)(2,1)S(1)} %get-tuple-element.15.z_parts), custom_call_target="tpu_custom_call" | custom-call | flops 251658240 | bytes 4000000 | tf_op jit(solution)/shard_map/early/pallas_call | solution.py:811
  7.9 0.0 collective-permute-done.far
  7.9 0.0 collective-permute-done.1.near
  7.9 0.0 copy-done.4
  7.9 0.0 copy-start.2
  7.9 0.0 copy-start.3
  7.9 1.6 %late.1 = bf16[4,128,128]{2,1,0:T(8,128)(2,1)} custom-call(bf16[208,128]{1,0:T(8,128)(2,1)S(1)} %collective-permute-done.far, bf16[208,128]{1,0:T(8,128)(2,1)S(1)} %collective-permute-done.1.near, bf16[128,48]{1,0:T(8,128)(2,1)S(1)} %copy-done.4, bf16[384,128]{1,0:T(8,128)(2,1)S(1)} %get-tuple-element.15.z_parts, ...), custom_call_target="tpu_custom_call" | custom-call | flops 125829120 | bytes 4000000 | tf_op jit(solution)/shard_map/late/pallas_call | solution.py:828
  9.5 0.0 copy-start.5
  9.5 0.0 copy-start.1
  9.5 6.0 %all-to-all-start = ((bf16[4,128,128]{2,1,0:T(8,128)(2,1)}), bf16[4,128,128]{2,1,0:T(8,128)(2,1)S(1)}, u32[]{:S(2)}, u32[]{:S(2)}) async-start(bf16[4,128,128]{2,1,0:T(8,128)(2,1)} %late.1), calls=%async_computation | async-start | bytes 262144 | tf_op jit(solution)/shard_map/all_to_all | solution.py:845
  15.6 0.0 copy-done.5
  15.6 0.1 copy.18
  15.6 0.1 eq.15
  15.7 0.6 %copy-done.6 = f32[8]{0:T(128)S(1)} copy-done((f32[8]{0:T(128)S(1)}, f32[8]{0:T(128)}, u32[]{:S(2)}) %copy-start.6) | copy-done | bytes 56
  16.3 0.2 select_reduce_fusion
  16.5 0.1 copy.19.tools
  16.6 3.6 %all-to-all-done.chunks = bf16[4,128,128]{2,1,0:T(8,128)(2,1)S(1)} async-done(((bf16[4,128,128]{2,1,0:T(8,128)(2,1)}), bf16[4,128,128]{2,1,0:T(8,128)(2,1)S(1)}, u32[]{:S(2)}, u32[]{:S(2)}) %all-to-all-start) | async-done | bytes 131104 | tf_op jit(solution)/shard_map/all_to_all | solution.py:845
  20.2 0.0 copy-done.3
  20.2 1.5 %cure.1 = (f32[6,128]{1,0:T(8,128)}, f32[6,128]{1,0:T(8,128)}, f32[3,6,128]{2,1,0:T(8,128)}) custom-call(bf16[4,128,128]{2,1,0:T(8,128)(2,1)S(1)} %all-to-all-done.chunks, f32[6,128]{1,0:T(8,128)S(1)} %get-tuple-element.21.temp.temp_in, f32[6,128]{1,0:T(8,128)S(1)} %get-tuple-element.22.cure.cure_in, f32[6,1]{1,0:T(8,128)S(1)} %copy.19.tools, ...), custom_call_target="tpu_custom_call" | custom-call | tf_op jit(solution)/shard_map/cure/pallas_call | solution.py:854
  (4 shorter events, 0.0 us)
Async XLA Ops:
  0.6 6.2 %copy-start = (s32[8,96,128]{2,1,0:T(8,128)S(1)}, s32[8,96,128]{2,1,0:T(8,128)}, u32[]{:S(2)}) copy-start(s32[8,96,128]{2,1,0:T(8,128)} %grey.1) | copy-start | bytes 1179652
  1.8 6.1 %collective-permute-start = (bf16[208,128]{1,0:T(8,128)(2,1)S(1)}, bf16[208,128]{1,0:T(8,128)(2,1)S(1)}, u32[]{:S(2)}, u32[]{:S(2)}) collective-permute-start(bf16[208,128]{1,0:T(8,128)(2,1)S(1)} %get-tuple-element.13), channel_id=1, source_target_pairs={{4,8},{5,9},{6,10},{7,11},{12,16},{13,17},{14,18},{15,19},{20,24},... | collective-permute-start | bytes 159752 | tf_op jit(solution)/shard_map/ppermute | solution.py:785
  2.5 5.4 %collective-permute-start.1 = (bf16[208,128]{1,0:T(8,128)(2,1)S(1)}, bf16[208,128]{1,0:T(8,128)(2,1)S(1)}, u32[]{:S(2)}, u32[]{:S(2)}) collective-permute-start(bf16[208,128]{1,0:T(8,128)(2,1)S(1)} %get-tuple-element.14), channel_id=1, source_target_pairs={{0,4},{1,5},{2,6},{3,7},{8,12},{9,13},{10,14},{11,15},{16,20},{17,... | collective-permute-start | bytes 159752 | tf_op jit(solution)/shard_map/ppermute | solution.py:785
  6.9 1.0 %copy-start.4 = (bf16[128,48]{1,0:T(8,128)(2,1)S(1)}, bf16[128,48]{1,0:T(8,128)(2,1)}, u32[]{:S(2)}) copy-start(bf16[128,48]{1,0:T(8,128)(2,1)} %constant.17.clone.x_late) | copy-start | bytes 36868
  7.9 12.3 %copy-start.2 = (bf16[528,128]{1,0:T(8,128)(2,1)S(1)}, bf16[528,128]{1,0:T(8,128)(2,1)}, u32[]{:S(2)}) copy-start(bf16[528,128]{1,0:T(8,128)(2,1)} %constant.19.clone.steep) | copy-start | bytes 405508
  7.9 12.3 %copy-start.3 = (bf16[384,128]{1,0:T(8,128)(2,1)S(1)}, bf16[384,128]{1,0:T(8,128)(2,1)}, u32[]{:S(2)}) copy-start(bf16[384,128]{1,0:T(8,128)(2,1)} %constant.20.clone.rim_bands) | copy-start | bytes 294916
  9.5 6.0 %copy-start.5 = (s32[3,2]{0,1:T(2,128)S(1)}, s32[3,2]{0,1:T(2,128)}, u32[]{:S(2)}) copy-start(s32[3,2]{0,1:T(2,128)} %param.15) | copy-start | bytes 76
  9.5 10.7 %copy-start.1 = (bf16[384,256]{1,0:T(8,128)(2,1)S(1)}, bf16[384,256]{1,0:T(8,128)(2,1)}, u32[]{:S(2)}) copy-start(bf16[384,256]{1,0:T(8,128)(2,1)} %constant.18.clone.flat) | copy-start | bytes 589828
  9.5 10.7 %all-to-all-start = ((bf16[4,128,128]{2,1,0:T(8,128)(2,1)}), bf16[4,128,128]{2,1,0:T(8,128)(2,1)S(1)}, u32[]{:S(2)}, u32[]{:S(2)}) async-start(bf16[4,128,128]{2,1,0:T(8,128)(2,1)} %late.1), calls=%async_computation | async-start | bytes 262144 | tf_op jit(solution)/shard_map/all_to_all | solution.py:845
  15.6 0.7 %copy-start.6 = (f32[8]{0:T(128)S(1)}, f32[8]{0:T(128)}, u32[]{:S(2)}) copy-start(f32[8]{0:T(128)} %param.14) | copy-start | bytes 100

commit v20 on v17

--- a/solution.py
+++ b/solution.py
@@ -157,7 +157,7 @@
 
 
 def meeting_order(blocks):
-    middle = blocks // 2
+    middle = (blocks - 1) // 2
     rest = [block for block in range(blocks) if block != middle]
     ends = [rest.pop(0 if turn % 2 == 0 else -1) for turn in range(blocks - 1)]
     return [middle, *ends]

time: 22.1 us -> 22.3 us (level)
  waiting for transfers between devices: 3.81 us -> 4.45 us
  starting transfers between devices: 11.1 us -> 10.6 us
    all_to_all x1, waiting for transfers between devices: 3.8 us -> 4.44 us  [on_device(): lax.all_to_all(chunks, 'depth', split_axis=0, concat_axis=0, tiled=True,...]
    all_to_all x1, starting transfers between devices: 6.04 us -> 5.6 us  [on_device(): lax.all_to_all(chunks, 'depth', split_axis=0, concat_axis=0, tiled=True,...]
where the time goes in v20:
time: 22.3 us; the launch traced here: 22.1 us
  starting transfers between devices  10.6 us (48%)
  Pallas kernels  5.22 us (23%)
  waiting for transfers between devices  4.45 us (20%)
  local copies, waits for them, and re-layouts  0.87 us (4%)
  between operations  0.72 us (3%)
    all_to_all x1, starting transfers between devices, on_device(): lax.all_to_all(chunks, 'depth', split_axis=0, concat_axis=0, tiled=True,...  5.6 us
    ppermute x2, starting transfers between devices, moved(): return lax.ppermute(values, ('plane', 'depth'), index)  5.03 us
    all_to_all x1, waiting for transfers between devices, on_device(): lax.all_to_all(chunks, 'depth', split_axis=0, concat_axis=0, tiled=True,...  4.44 us
    pallas_call x1, Pallas kernels, on_device(): pl.pallas_call(functools.partial(late_kernel, late_starts, width), name='...  1.56 us
    pallas_call x1, Pallas kernels, on_device(): pl.pallas_call(functools.partial(cure_kernel, cells, rim_starts), name='c...  1.51 us
    pallas_call x1, Pallas kernels, on_device(): pl.pallas_call(pack_kernel, name='pack', out_shape=(pltpu.VMEM((slots, de...  1.13 us
    pallas_call x1, Pallas kernels, on_device(): pl.pallas_call(functools.partial(early_kernel, early_starts), name='early...  1.02 us
    unnamed x11, local copies, waits for them, and re-layouts  0.69 us
  transfers between devices with their start and end apart: 3, of which 1 were waited for; matrix products, arithmetic and copies ran while one was open for 2% of the time, Pallas kernels for 5%

profile of v20, /device:TPU:0, one launch (start us, length us, event | category | flops | bytes accessed | tf_op | source)
XLA Modules:
  0.0 22.1 jit_solution(11203441380866969455)
XLA Ops:
  0.6 1.1 %pack.1 = (bf16[208,128]{1,0:T(8,128)(2,1)S(1)}, bf16[208,128]{1,0:T(8,128)(2,1)S(1)}, bf16[4,96,256]{2,1,0:T(8,128)(2,1)S(1)}, bf16[320,96]{1,0:T(8,128)(2,1)S(...) custom-call(s32[8,96,128]{2,1,0:T(8,128)} %intensity.1, f32[6,128]{1,0:T(8,128)} %temp_hbm.1, ...), custom_call_target="tpu_custom_call" | custom-call | tf_op jit(solution)/shard_map/pack/pallas_call | solution.py:749
  1.8 0.7 %collective-permute-start = (bf16[208,128]{1,0:T(8,128)(2,1)S(1)}, bf16[208,128]{1,0:T(8,128)(2,1)S(1)}, u32[]{:S(2)}, u32[]{:S(2)}) collective-permute-start(bf16[208,128]{1,0:T(8,128)(2,1)S(1)} %get-tuple-element.15), channel_id=1, source_target_pairs={{4,8},{5,9},{6,10},{7,11},{12,16},{13,17},{14,18},{15,19},{20,24},... | collective-permute-start | bytes 159752 | tf_op jit(solution)/shard_map/ppermute | solution.py:771
  2.4 4.4 %collective-permute-start.1 = (bf16[208,128]{1,0:T(8,128)(2,1)S(1)}, bf16[208,128]{1,0:T(8,128)(2,1)S(1)}, u32[]{:S(2)}, u32[]{:S(2)}) collective-permute-start(bf16[208,128]{1,0:T(8,128)(2,1)S(1)} %get-tuple-element.16), channel_id=1, source_target_pairs={{0,4},{1,5},{2,6},{3,7},{8,12},{9,13},{10,14},{11,15},{16,20},{17,... | collective-permute-start | bytes 159752 | tf_op jit(solution)/shard_map/ppermute | solution.py:771
  6.8 1.0 %early.1 = (f32[4,32,128]{2,1,0:T(8,128)S(1)}, bf16[512,256]{1,0:T(8,128)(2,1)S(1)}, f32[96,1024]{1,0:T(8,128)S(1)}, f32[3,96,128]{2,1,0:T(8,128)S(1)}, bf16[128,48]{1,0:T(8,128)(2,1)S(1)}) custom-call(bf16[4,96,256]{2,1,0:T(8,128)(2,1)S(1)} %get-tuple-element.17.own, bf16[320,96]{1,0:T(8,128)(2,1)S(1)} %get-tuple-element.18.x_parts, ...), custom_call_target="tpu_custom_call" | custom-call | flops 251658240 | bytes 4000000 | tf_op jit(solution)/shard_map/early/pallas_call | solution.py:797
  7.8 0.0 collective-permute-done.far
  7.8 0.0 collective-permute-done.1.near
  7.9 0.0 copy-start.3
  7.9 0.0 copy-start.1
  7.9 1.6 %late.1 = bf16[4,144,128]{2,1,0:T(8,128)(2,1)} custom-call(bf16[208,128]{1,0:T(8,128)(2,1)S(1)} %collective-permute-done.far, bf16[208,128]{1,0:T(8,128)(2,1)S(1)} %collective-permute-done.1.near, bf16[128,48]{1,0:T(8,128)(2,1)S(1)} %get-tuple-element.20.x_late, bf16[384,128]{1,0:T(8,128)(2,1)S(1)} %get-tuple-element.19.z_parts, ...), custom_call_target="tpu_custom_call" | custom-call | flops 125829120 | bytes 4000000 | tf_op jit(solution)/shard_map/late/pallas_call | solution.py:816
  9.4 0.0 copy-start
  9.5 0.0 copy-start.2
  9.5 5.6 %all-to-all-start = ((bf16[4,144,128]{2,1,0:T(8,128)(2,1)}), bf16[4,144,128]{2,1,0:T(8,128)(2,1)S(1)}, u32[]{:S(2)}, u32[]{:S(2)}) async-start(bf16[4,144,128]{2,1,0:T(8,128)(2,1)} %late.1), calls=%async_computation | async-start | bytes 294912 | tf_op jit(solution)/shard_map/all_to_all | solution.py:833
  15.1 0.0 copy-done.3
  15.1 0.1 copy.18
  15.2 0.0 copy-start.4
  15.2 0.1 eq.15
  15.3 0.6 %copy-done.4 = f32[8]{0:T(128)S(1)} copy-done((f32[8]{0:T(128)S(1)}, f32[8]{0:T(128)}, u32[]{:S(2)}) %copy-start.4) | copy-done | bytes 56
  15.8 0.2 select_reduce_fusion
  16.0 0.1 copy.19.tools
  16.1 4.4 %all-to-all-done.chunks = bf16[4,144,128]{2,1,0:T(8,128)(2,1)S(1)} async-done(((bf16[4,144,128]{2,1,0:T(8,128)(2,1)}), bf16[4,144,128]{2,1,0:T(8,128)(2,1)S(1)}, u32[]{:S(2)}, u32[]{:S(2)}) %all-to-all-start) | async-done | bytes 147488 | tf_op jit(solution)/shard_map/all_to_all | solution.py:833
  20.5 0.0 copy-done.1
  20.6 0.0 copy-done
  20.6 0.0 copy-done.2
  20.6 1.5 %cure.1 = (f32[6,128]{1,0:T(8,128)}, f32[6,128]{1,0:T(8,128)}, f32[3,6,128]{2,1,0:T(8,128)}) custom-call(bf16[4,144,128]{2,1,0:T(8,128)(2,1)S(1)} %all-to-all-done.chunks, f32[6,128]{1,0:T(8,128)S(1)} %get-tuple-element.25.temp.temp_in, f32[6,128]{1,0:T(8,128)S(1)} %get-tuple-element.26.cure.cure_in, f32[6,1]{1,0:T(8,128)S(1)} %copy.19.tools, ...), custom_call_target="tpu_custom_call" | custom-call | tf_op jit(solution)/shard_map/cure/pallas_call | solution.py:842
Async XLA Ops:
  1.8 6.1 %collective-permute-start = (bf16[208,128]{1,0:T(8,128)(2,1)S(1)}, bf16[208,128]{1,0:T(8,128)(2,1)S(1)}, u32[]{:S(2)}, u32[]{:S(2)}) collective-permute-start(bf16[208,128]{1,0:T(8,128)(2,1)S(1)} %get-tuple-element.15), channel_id=1, source_target_pairs={{4,8},{5,9},{6,10},{7,11},{12,16},{13,17},{14,18},{15,19},{20,24},... | collective-permute-start | bytes 159752 | tf_op jit(solution)/shard_map/ppermute | solution.py:771
  2.4 5.4 %collective-permute-start.1 = (bf16[208,128]{1,0:T(8,128)(2,1)S(1)}, bf16[208,128]{1,0:T(8,128)(2,1)S(1)}, u32[]{:S(2)}, u32[]{:S(2)}) collective-permute-start(bf16[208,128]{1,0:T(8,128)(2,1)S(1)} %get-tuple-element.16), channel_id=1, source_target_pairs={{0,4},{1,5},{2,6},{3,7},{8,12},{9,13},{10,14},{11,15},{16,20},{17,... | collective-permute-start | bytes 159752 | tf_op jit(solution)/shard_map/ppermute | solution.py:771
  7.9 7.2 %copy-start.3 = (s32[3,2]{0,1:T(2,128)S(1)}, s32[3,2]{0,1:T(2,128)}, u32[]{:S(2)}) copy-start(s32[3,2]{0,1:T(2,128)} %param.15) | copy-start | bytes 76
  7.9 12.7 %copy-start.1 = (bf16[528,128]{1,0:T(8,128)(2,1)S(1)}, bf16[528,128]{1,0:T(8,128)(2,1)}, u32[]{:S(2)}) copy-start(bf16[528,128]{1,0:T(8,128)(2,1)} %constant.19.clone.steep) | copy-start | bytes 405508
  9.4 11.1 %copy-start = (bf16[384,256]{1,0:T(8,128)(2,1)S(1)}, bf16[384,256]{1,0:T(8,128)(2,1)}, u32[]{:S(2)}) copy-start(bf16[384,256]{1,0:T(8,128)(2,1)} %constant.18.clone.flat) | copy-start | bytes 589828
  9.5 11.1 %copy-start.2 = (bf16[384,128]{1,0:T(8,128)(2,1)S(1)}, bf16[384,128]{1,0:T(8,128)(2,1)}, u32[]{:S(2)}) copy-start(bf16[384,128]{1,0:T(8,128)(2,1)} %constant.20.clone.rim_bands) | copy-start | bytes 294916
  9.5 11.1 %all-to-all-start = ((bf16[4,144,128]{2,1,0:T(8,128)(2,1)}), bf16[4,144,128]{2,1,0:T(8,128)(2,1)S(1)}, u32[]{:S(2)}, u32[]{:S(2)}) async-start(bf16[4,144,128]{2,1,0:T(8,128)(2,1)} %late.1), calls=%async_computation | async-start | bytes 294912 | tf_op jit(solution)/shard_map/all_to_all | solution.py:833
  15.2 0.7 %copy-start.4 = (f32[8]{0:T(128)S(1)}, f32[8]{0:T(128)}, u32[]{:S(2)}) copy-start(f32[8]{0:T(128)} %param.14) | copy-start | bytes 100

commit v21 on v17

--- a/solution.py
+++ b/solution.py
@@ -158,9 +158,7 @@
 
 def meeting_order(blocks):
     middle = blocks // 2
-    rest = [block for block in range(blocks) if block != middle]
-    ends = [rest.pop(0 if turn % 2 == 0 else -1) for turn in range(blocks - 1)]
-    return [middle, *ends]
+    return [*range(middle, blocks), *range(middle)]
 
 
 def own_columns(count):

time: 22.1 us -> 21.7 us (0.982)
  waiting for transfers between devices: 3.81 us -> 3.35 us
    all_to_all x1, waiting for transfers between devices: 3.8 us -> 3.35 us  [on_device(): lax.all_to_all(chunks, 'depth', split_axis=0, concat_axis=0, tiled=True,...]
where the time goes in v21:
time: 21.7 us; the launch traced here: 21.4 us
  starting transfers between devices  11.1 us (51%)
  Pallas kernels  5.22 us (24%)
  waiting for transfers between devices  3.35 us (15%)
  local copies, waits for them, and re-layouts  0.87 us (4%)
  between operations  0.72 us (3%)
    all_to_all x1, starting transfers between devices, on_device(): lax.all_to_all(chunks, 'depth', split_axis=0, concat_axis=0, tiled=True,...  6.04 us
    ppermute x2, starting transfers between devices, moved(): return lax.ppermute(values, ('plane', 'depth'), index)  5.03 us
    all_to_all x1, waiting for transfers between devices, on_device(): lax.all_to_all(chunks, 'depth', split_axis=0, concat_axis=0, tiled=True,...  3.35 us
    pallas_call x1, Pallas kernels, on_device(): pl.pallas_call(functools.partial(late_kernel, late_starts, width), name='...  1.56 us
    pallas_call x1, Pallas kernels, on_device(): pl.pallas_call(functools.partial(cure_kernel, cells, rim_starts), name='c...  1.51 us
    pallas_call x1, Pallas kernels, on_device(): pl.pallas_call(pack_kernel, name='pack', out_shape=(pltpu.VMEM((slots, de...  1.13 us
    pallas_call x1, Pallas kernels, on_device(): pl.pallas_call(functools.partial(early_kernel, early_starts), name='early...  1.02 us
    unnamed x11, local copies, waits for them, and re-layouts  0.69 us
  transfers between devices with their start and end apart: 3, of which 1 were waited for; matrix products, arithmetic and copies ran while one was open for 2% of the time, Pallas kernels for 5%

profile of v21, /device:TPU:0, one launch (start us, length us, event | category | flops | bytes accessed | tf_op | source)
XLA Modules:
  0.0 21.4 jit_solution(10053586215251136888)
XLA Ops:
  0.6 1.1 %pack.1 = (bf16[208,128]{1,0:T(8,128)(2,1)S(1)}, bf16[208,128]{1,0:T(8,128)(2,1)S(1)}, bf16[4,96,256]{2,1,0:T(8,128)(2,1)S(1)}, bf16[320,96]{1,0:T(8,128)(2,1)S(...) custom-call(s32[8,96,128]{2,1,0:T(8,128)} %intensity.1, f32[6,128]{1,0:T(8,128)} %temp_hbm.1, ...), custom_call_target="tpu_custom_call" | custom-call | tf_op jit(solution)/shard_map/pack/pallas_call | solution.py:747
  1.8 0.7 %collective-permute-start = (bf16[208,128]{1,0:T(8,128)(2,1)S(1)}, bf16[208,128]{1,0:T(8,128)(2,1)S(1)}, u32[]{:S(2)}, u32[]{:S(2)}) collective-permute-start(bf16[208,128]{1,0:T(8,128)(2,1)S(1)} %get-tuple-element.15), channel_id=1, source_target_pairs={{4,8},{5,9},{6,10},{7,11},{12,16},{13,17},{14,18},{15,19},{20,24},... | collective-permute-start | bytes 159752 | tf_op jit(solution)/shard_map/ppermute | solution.py:769
  2.4 4.4 %collective-permute-start.1 = (bf16[208,128]{1,0:T(8,128)(2,1)S(1)}, bf16[208,128]{1,0:T(8,128)(2,1)S(1)}, u32[]{:S(2)}, u32[]{:S(2)}) collective-permute-start(bf16[208,128]{1,0:T(8,128)(2,1)S(1)} %get-tuple-element.16), channel_id=1, source_target_pairs={{0,4},{1,5},{2,6},{3,7},{8,12},{9,13},{10,14},{11,15},{16,20},{17,... | collective-permute-start | bytes 159752 | tf_op jit(solution)/shard_map/ppermute | solution.py:769
  6.8 1.0 %early.1 = (f32[4,32,128]{2,1,0:T(8,128)S(1)}, bf16[512,256]{1,0:T(8,128)(2,1)S(1)}, f32[96,1024]{1,0:T(8,128)S(1)}, f32[3,96,128]{2,1,0:T(8,128)S(1)}, bf16[128,48]{1,0:T(8,128)(2,1)S(1)}) custom-call(bf16[4,96,256]{2,1,0:T(8,128)(2,1)S(1)} %get-tuple-element.17.own, bf16[320,96]{1,0:T(8,128)(2,1)S(1)} %get-tuple-element.18.x_parts, ...), custom_call_target="tpu_custom_call" | custom-call | flops 251658240 | bytes 4000000 | tf_op jit(solution)/shard_map/early/pallas_call | solution.py:795
  7.8 0.0 collective-permute-done.far
  7.8 0.0 collective-permute-done.1.near
  7.9 0.0 copy-start.3
  7.9 0.0 copy-start.1
  7.9 1.6 %late.1 = bf16[4,144,128]{2,1,0:T(8,128)(2,1)} custom-call(bf16[208,128]{1,0:T(8,128)(2,1)S(1)} %collective-permute-done.far, bf16[208,128]{1,0:T(8,128)(2,1)S(1)} %collective-permute-done.1.near, bf16[128,48]{1,0:T(8,128)(2,1)S(1)} %get-tuple-element.20.x_late, bf16[384,128]{1,0:T(8,128)(2,1)S(1)} %get-tuple-element.19.z_parts, ...), custom_call_target="tpu_custom_call" | custom-call | flops 125829120 | bytes 4000000 | tf_op jit(solution)/shard_map/late/pallas_call | solution.py:814
  9.4 0.0 copy-start
  9.5 0.0 copy-start.2
  9.5 6.0 %all-to-all-start = ((bf16[4,144,128]{2,1,0:T(8,128)(2,1)}), bf16[4,144,128]{2,1,0:T(8,128)(2,1)S(1)}, u32[]{:S(2)}, u32[]{:S(2)}) async-start(bf16[4,144,128]{2,1,0:T(8,128)(2,1)} %late.1), calls=%async_computation | async-start | bytes 294912 | tf_op jit(solution)/shard_map/all_to_all | solution.py:831
  15.5 0.0 copy-done.3
  15.5 0.1 copy.18
  15.6 0.0 copy-start.4
  15.6 0.1 eq.15
  15.7 0.6 %copy-done.4 = f32[8]{0:T(128)S(1)} copy-done((f32[8]{0:T(128)S(1)}, f32[8]{0:T(128)}, u32[]{:S(2)}) %copy-start.4) | copy-done | bytes 56
  16.3 0.2 select_reduce_fusion
  16.4 0.1 copy.19.tools
  16.5 3.3 %all-to-all-done.chunks = bf16[4,144,128]{2,1,0:T(8,128)(2,1)S(1)} async-done(((bf16[4,144,128]{2,1,0:T(8,128)(2,1)}), bf16[4,144,128]{2,1,0:T(8,128)(2,1)S(1)}, u32[]{:S(2)}, u32[]{:S(2)}) %all-to-all-start) | async-done | bytes 147488 | tf_op jit(solution)/shard_map/all_to_all | solution.py:831
  19.9 0.0 copy-done.1
  19.9 0.0 copy-done
  19.9 0.0 copy-done.2
  19.9 1.5 %cure.1 = (f32[6,128]{1,0:T(8,128)}, f32[6,128]{1,0:T(8,128)}, f32[3,6,128]{2,1,0:T(8,128)}) custom-call(bf16[4,144,128]{2,1,0:T(8,128)(2,1)S(1)} %all-to-all-done.chunks, f32[6,128]{1,0:T(8,128)S(1)} %get-tuple-element.25.temp.temp_in, f32[6,128]{1,0:T(8,128)S(1)} %get-tuple-element.26.cure.cure_in, f32[6,1]{1,0:T(8,128)S(1)} %copy.19.tools, ...), custom_call_target="tpu_custom_call" | custom-call | tf_op jit(solution)/shard_map/cure/pallas_call | solution.py:840
Async XLA Ops:
  1.8 6.1 %collective-permute-start = (bf16[208,128]{1,0:T(8,128)(2,1)S(1)}, bf16[208,128]{1,0:T(8,128)(2,1)S(1)}, u32[]{:S(2)}, u32[]{:S(2)}) collective-permute-start(bf16[208,128]{1,0:T(8,128)(2,1)S(1)} %get-tuple-element.15), channel_id=1, source_target_pairs={{4,8},{5,9},{6,10},{7,11},{12,16},{13,17},{14,18},{15,19},{20,24},... | collective-permute-start | bytes 159752 | tf_op jit(solution)/shard_map/ppermute | solution.py:769
  2.4 5.4 %collective-permute-start.1 = (bf16[208,128]{1,0:T(8,128)(2,1)S(1)}, bf16[208,128]{1,0:T(8,128)(2,1)S(1)}, u32[]{:S(2)}, u32[]{:S(2)}) collective-permute-start(bf16[208,128]{1,0:T(8,128)(2,1)S(1)} %get-tuple-element.16), channel_id=1, source_target_pairs={{0,4},{1,5},{2,6},{3,7},{8,12},{9,13},{10,14},{11,15},{16,20},{17,... | collective-permute-start | bytes 159752 | tf_op jit(solution)/shard_map/ppermute | solution.py:769
  7.9 7.7 %copy-start.3 = (s32[3,2]{0,1:T(2,128)S(1)}, s32[3,2]{0,1:T(2,128)}, u32[]{:S(2)}) copy-start(s32[3,2]{0,1:T(2,128)} %param.15) | copy-start | bytes 76
  7.9 12.0 %copy-start.1 = (bf16[528,128]{1,0:T(8,128)(2,1)S(1)}, bf16[528,128]{1,0:T(8,128)(2,1)}, u32[]{:S(2)}) copy-start(bf16[528,128]{1,0:T(8,128)(2,1)} %constant.19.clone.steep) | copy-start | bytes 405508
  9.4 10.4 %copy-start = (bf16[384,256]{1,0:T(8,128)(2,1)S(1)}, bf16[384,256]{1,0:T(8,128)(2,1)}, u32[]{:S(2)}) copy-start(bf16[384,256]{1,0:T(8,128)(2,1)} %constant.18.clone.flat) | copy-start | bytes 589828
  9.5 10.4 %copy-start.2 = (bf16[384,128]{1,0:T(8,128)(2,1)S(1)}, bf16[384,128]{1,0:T(8,128)(2,1)}, u32[]{:S(2)}) copy-start(bf16[384,128]{1,0:T(8,128)(2,1)} %constant.20.clone.rim_bands) | copy-start | bytes 294916
  9.5 10.4 %all-to-all-start = ((bf16[4,144,128]{2,1,0:T(8,128)(2,1)}), bf16[4,144,128]{2,1,0:T(8,128)(2,1)S(1)}, u32[]{:S(2)}, u32[]{:S(2)}) async-start(bf16[4,144,128]{2,1,0:T(8,128)(2,1)} %late.1), calls=%async_computation | async-start | bytes 294912 | tf_op jit(solution)/shard_map/all_to_all | solution.py:831
  15.6 0.7 %copy-start.4 = (f32[8]{0:T(128)S(1)}, f32[8]{0:T(128)}, u32[]{:S(2)}) copy-start(f32[8]{0:T(128)} %param.14) | copy-start | bytes 100

commit v22 on v21

--- a/solution.py
+++ b/solution.py
@@ -34,6 +34,7 @@
 EARLY = 96
 GHOST = 3
 COLUMN_ROWS = 2 * GHOST - 1
+CODE_SCALE = 2.0**20
 RIM = 2 * R1
 BEFORE = -(-(R2 - R1) // COARSE)
 AFTER = BEFORE
@@ -242,6 +243,16 @@
     return parts[:half] + parts[half:]
 
 
+def coded(values):
+    values = values * CODE_SCALE
+    return (values * jnp.abs(values)) * (values * values)
+
+
+def decoded(values):
+    size = jnp.sqrt(jnp.sqrt(jnp.abs(values))) * (1.0 / CODE_SCALE)
+    return jnp.where(values < 0.0, -size, size)
+
+
 def column_rows(temp, cure, at_end):
     count = temp.shape[0]
     first, second = (count - GHOST, count - GHOST + 1) if at_end else (0, 0)
@@ -254,7 +265,7 @@
 def chunk_rows(count, lanes):
     products, voxels = own_columns(count)
     held = count + 2 * HALO + 1 + COLUMN_ROWS * (lanes // LANES)
-    return voxels + fold(voxels), -(-held // 8) * 8
+    return voxels + fold(voxels), -(-held // 16) * 16
 
 
 def is_odd():
@@ -553,14 +564,14 @@
         if target == out.shape[0] - 1:
             piece = jnp.where(layer == 0, right, piece)
         mine = slice(count * target, count * target + height)
-        pieces = [joint[mine], jnp.sum(rest[mine], axis=0, keepdims=True)]
+        pieces = [coded(joint[mine]), coded(jnp.sum(rest[mine], axis=0, keepdims=True))]
         for slot in range(lanes // LANES):
-            pieces.append(piece[0:COLUMN_ROWS, slot * LANES : (slot + 1) * LANES])
+            part = piece[:, slot * LANES : (slot + 1) * LANES]
+            pieces += [part[:GHOST] - reference_temp, part[GHOST:COLUMN_ROWS]]
         filled = sum(part.shape[0] for part in pieces)
         if filled < half:
             pieces.append(jnp.zeros((half - filled, LANES), jnp.float32))
-        sent = two_parts(jnp.concatenate(pieces, axis=0))
-        out[position, voxels + folded :, :] = sent.astype(jnp.bfloat16)
+        out[position, voxels + folded :, :] = jnp.concatenate(pieces, axis=0).astype(jnp.bfloat16)
     copies[1].start()
     for copy in copies:
         copy.wait()
@@ -629,9 +640,20 @@
 
     near = rim_sums(chunks, count, starts, flat, steep, rim_bands)
     sums = [near[0] + near[1] + near[2], near[1], near[2], near[5]]
-    blocks = [
-        joined(chunks[order.index(part), at_sums:, :].astype(jnp.float32)) for part in range(parts)
+    blocks = [chunks[order.index(part), at_sums:, :].astype(jnp.float32) for part in range(parts)]
+    columns = [
+        jnp.concatenate(
+            [
+                block[at : at + COLUMN_ROWS]
+                for at in range(
+                    height + 1, height + 1 + COLUMN_ROWS * (lanes // LANES), COLUMN_ROWS
+                )
+            ],
+            axis=1,
+        )
+        for block in blocks
     ]
+    blocks = [decoded(block[0:16]) for block in blocks]
     tails = [block[height : height + 1] for block in blocks]
     if parts % 8:
         tails.append(jnp.zeros((-parts % 8, LANES), jnp.float32))
@@ -673,16 +695,17 @@
     ]
     copies[0].start()
 
-    slots = range(height + 1, height + 1 + COLUMN_ROWS * (lanes // LANES), COLUMN_ROWS)
-    columns = [
-        jnp.concatenate([values[at : at + COLUMN_ROWS] for at in slots], axis=1) for values in blocks
-    ]
     before, after = columns[parts - 1], columns[0]
     for part in range(parts - 1):
         before = jnp.where(layer == part + 1, columns[part], before)
         after = jnp.where(layer == part, columns[part + 1], after)
     spare = jnp.full((16 - count - 2 * GHOST, lanes), 0.5, jnp.float32)
-    temp = jnp.concatenate([before[:GHOST], temp_in[...], after[:GHOST], 8.0 * spare], axis=0)
+    temp = jnp.concatenate([
+            before[:GHOST] + reference_temp,
+            temp_in[...],
+            after[:GHOST] + reference_temp,
+            8.0 * spare,
+        ], axis=0)
     cure = jnp.concatenate([spare[:1], before[GHOST:], cure_in[...], after[GHOST:], spare[:1], spare], axis=0)
     gap = GHOST - HALO
     xx, xz, zz = [pltpu.roll(part, gap, 0) for part in conduct]
@@ -810,7 +833,7 @@
 
     products_x, voxels = own_columns(count)
     at_sums, half = chunk_rows(count, lanes)
-    chunk_shape = (depths, at_sums + 2 * half, LANES)
+    chunk_shape = (depths, at_sums + half, LANES)
     chunks = pl.pallas_call(
         functools.partial(late_kernel, late_starts, width),
         name="late",

time: 21.7 us -> 21.4 us (0.986)
  waiting for transfers between devices: 3.35 us -> 3.09 us
    all_to_all x1, waiting for transfers between devices: 3.35 us -> 3.08 us  [on_device(): lax.all_to_all(chunks, 'depth', split_axis=0, concat_axis=0, tiled=True,...]
where the time goes in v22:
time: 21.4 us; the launch traced here: 21.1 us
  starting transfers between devices  11.1 us (52%)
  Pallas kernels  5.24 us (24%)
  waiting for transfers between devices  3.09 us (14%)
  local copies, waits for them, and re-layouts  0.87 us (4%)
  between operations  0.72 us (3%)
    all_to_all x1, starting transfers between devices, on_device(): lax.all_to_all(chunks, 'depth', split_axis=0, concat_axis=0, tiled=True,...  6.03 us
    ppermute x2, starting transfers between devices, moved(): return lax.ppermute(values, ('plane', 'depth'), index)  5.03 us
    all_to_all x1, waiting for transfers between devices, on_device(): lax.all_to_all(chunks, 'depth', split_axis=0, concat_axis=0, tiled=True,...  3.08 us
    pallas_call x1, Pallas kernels, on_device(): pl.pallas_call(functools.partial(late_kernel, late_starts, width), name='...  1.57 us
    pallas_call x1, Pallas kernels, on_device(): pl.pallas_call(functools.partial(cure_kernel, cells, rim_starts), name='c...  1.52 us
    pallas_call x1, Pallas kernels, on_device(): pl.pallas_call(pack_kernel, name='pack', out_shape=(pltpu.VMEM((slots, de...  1.13 us
    pallas_call x1, Pallas kernels, on_device(): pl.pallas_call(functools.partial(early_kernel, early_starts), name='early...  1.02 us
    unnamed x11, local copies, waits for them, and re-layouts  0.69 us
  transfers between devices with their start and end apart: 3, of which 1 were waited for; matrix products, arithmetic and copies ran while one was open for 2% of the time, Pallas kernels for 5%

profile of v22, /device:TPU:0, one launch (start us, length us, event | category | flops | bytes accessed | tf_op | source)
XLA Modules:
  0.0 21.1 jit_solution(17075280023277832672)
XLA Ops:
  0.6 1.1 %pack.1 = (bf16[208,128]{1,0:T(8,128)(2,1)S(1)}, bf16[208,128]{1,0:T(8,128)(2,1)S(1)}, bf16[4,96,256]{2,1,0:T(8,128)(2,1)S(1)}, bf16[320,96]{1,0:T(8,128)(2,1)S(...) custom-call(s32[8,96,128]{2,1,0:T(8,128)} %intensity.1, f32[6,128]{1,0:T(8,128)} %temp_hbm.1, ...), custom_call_target="tpu_custom_call" | custom-call | tf_op jit(solution)/shard_map/pack/pallas_call | solution.py:770
  1.8 0.7 %collective-permute-start = (bf16[208,128]{1,0:T(8,128)(2,1)S(1)}, bf16[208,128]{1,0:T(8,128)(2,1)S(1)}, u32[]{:S(2)}, u32[]{:S(2)}) collective-permute-start(bf16[208,128]{1,0:T(8,128)(2,1)S(1)} %get-tuple-element.15), channel_id=1, source_target_pairs={{4,8},{5,9},{6,10},{7,11},{12,16},{13,17},{14,18},{15,19},{20,24},... | collective-permute-start | bytes 159752 | tf_op jit(solution)/shard_map/ppermute | solution.py:792
  2.4 4.4 %collective-permute-start.1 = (bf16[208,128]{1,0:T(8,128)(2,1)S(1)}, bf16[208,128]{1,0:T(8,128)(2,1)S(1)}, u32[]{:S(2)}, u32[]{:S(2)}) collective-permute-start(bf16[208,128]{1,0:T(8,128)(2,1)S(1)} %get-tuple-element.16), channel_id=1, source_target_pairs={{0,4},{1,5},{2,6},{3,7},{8,12},{9,13},{10,14},{11,15},{16,20},{17,... | collective-permute-start | bytes 159752 | tf_op jit(solution)/shard_map/ppermute | solution.py:792
  6.8 1.0 %early.1 = (f32[4,32,128]{2,1,0:T(8,128)S(1)}, bf16[512,256]{1,0:T(8,128)(2,1)S(1)}, f32[96,1024]{1,0:T(8,128)S(1)}, f32[3,96,128]{2,1,0:T(8,128)S(1)}, bf16[128,48]{1,0:T(8,128)(2,1)S(1)}) custom-call(bf16[4,96,256]{2,1,0:T(8,128)(2,1)S(1)} %get-tuple-element.17.own, bf16[320,96]{1,0:T(8,128)(2,1)S(1)} %get-tuple-element.18.x_parts, ...), custom_call_target="tpu_custom_call" | custom-call | flops 251658240 | bytes 4000000 | tf_op jit(solution)/shard_map/early/pallas_call | solution.py:818
  7.8 0.0 collective-permute-done.far
  7.8 0.0 collective-permute-done.1.near
  7.9 0.0 copy-start.1
  7.9 0.0 copy-start.2
  7.9 1.6 %late.1 = bf16[4,128,128]{2,1,0:T(8,128)(2,1)} custom-call(bf16[208,128]{1,0:T(8,128)(2,1)S(1)} %collective-permute-done.far, bf16[208,128]{1,0:T(8,128)(2,1)S(1)} %collective-permute-done.1.near, bf16[128,48]{1,0:T(8,128)(2,1)S(1)} %get-tuple-element.20.x_late, bf16[384,128]{1,0:T(8,128)(2,1)S(1)} %get-tuple-element.19.z_parts, ...), custom_call_target="tpu_custom_call" | custom-call | flops 125829120 | bytes 4000000 | tf_op jit(solution)/shard_map/late/pallas_call | solution.py:837
  9.5 0.0 copy-start.3
  9.5 0.0 copy-start
  9.5 6.0 %all-to-all-start = ((bf16[4,128,128]{2,1,0:T(8,128)(2,1)}), bf16[4,128,128]{2,1,0:T(8,128)(2,1)S(1)}, u32[]{:S(2)}, u32[]{:S(2)}) async-start(bf16[4,128,128]{2,1,0:T(8,128)(2,1)} %late.1), calls=%async_computation | async-start | bytes 262144 | tf_op jit(solution)/shard_map/all_to_all | solution.py:854
  15.5 0.0 copy-done.3
  15.5 0.1 copy.18
  15.6 0.0 copy-start.4
  15.6 0.1 eq.15
  15.7 0.6 %copy-done.4 = f32[8]{0:T(128)S(1)} copy-done((f32[8]{0:T(128)S(1)}, f32[8]{0:T(128)}, u32[]{:S(2)}) %copy-start.4) | copy-done | bytes 56
  16.3 0.2 select_reduce_fusion
  16.4 0.1 copy.19.tools
  16.5 3.1 %all-to-all-done.chunks = bf16[4,128,128]{2,1,0:T(8,128)(2,1)S(1)} async-done(((bf16[4,128,128]{2,1,0:T(8,128)(2,1)}), bf16[4,128,128]{2,1,0:T(8,128)(2,1)S(1)}, u32[]{:S(2)}, u32[]{:S(2)}) %all-to-all-start) | async-done | bytes 131104 | tf_op jit(solution)/shard_map/all_to_all | solution.py:854
  19.6 0.0 copy-done.1
  19.6 0.0 copy-done.2
  19.6 0.0 copy-done
  19.6 1.5 %cure.1 = (f32[6,128]{1,0:T(8,128)}, f32[6,128]{1,0:T(8,128)}, f32[3,6,128]{2,1,0:T(8,128)}) custom-call(bf16[4,128,128]{2,1,0:T(8,128)(2,1)S(1)} %all-to-all-done.chunks, f32[6,128]{1,0:T(8,128)S(1)} %get-tuple-element.25.temp.temp_in, f32[6,128]{1,0:T(8,128)S(1)} %get-tuple-element.26.cure.cure_in, f32[6,1]{1,0:T(8,128)S(1)} %copy.19.tools, ...), custom_call_target="tpu_custom_call" | custom-call | tf_op jit(solution)/shard_map/cure/pallas_call | solution.py:863
Async XLA Ops:
  1.8 6.1 %collective-permute-start = (bf16[208,128]{1,0:T(8,128)(2,1)S(1)}, bf16[208,128]{1,0:T(8,128)(2,1)S(1)}, u32[]{:S(2)}, u32[]{:S(2)}) collective-permute-start(bf16[208,128]{1,0:T(8,128)(2,1)S(1)} %get-tuple-element.15), channel_id=1, source_target_pairs={{4,8},{5,9},{6,10},{7,11},{12,16},{13,17},{14,18},{15,19},{20,24},... | collective-permute-start | bytes 159752 | tf_op jit(solution)/shard_map/ppermute | solution.py:792
  2.4 5.4 %collective-permute-start.1 = (bf16[208,128]{1,0:T(8,128)(2,1)S(1)}, bf16[208,128]{1,0:T(8,128)(2,1)S(1)}, u32[]{:S(2)}, u32[]{:S(2)}) collective-permute-start(bf16[208,128]{1,0:T(8,128)(2,1)S(1)} %get-tuple-element.16), channel_id=1, source_target_pairs={{0,4},{1,5},{2,6},{3,7},{8,12},{9,13},{10,14},{11,15},{16,20},{17,... | collective-permute-start | bytes 159752 | tf_op jit(solution)/shard_map/ppermute | solution.py:792
  7.9 11.8 %copy-start.1 = (bf16[528,128]{1,0:T(8,128)(2,1)S(1)}, bf16[528,128]{1,0:T(8,128)(2,1)}, u32[]{:S(2)}) copy-start(bf16[528,128]{1,0:T(8,128)(2,1)} %constant.19.clone.steep) | copy-start | bytes 405508
  7.9 11.8 %copy-start.2 = (bf16[384,128]{1,0:T(8,128)(2,1)S(1)}, bf16[384,128]{1,0:T(8,128)(2,1)}, u32[]{:S(2)}) copy-start(bf16[384,128]{1,0:T(8,128)(2,1)} %constant.20.clone.rim_bands) | copy-start | bytes 294916
  9.5 6.1 %copy-start.3 = (s32[3,2]{0,1:T(2,128)S(1)}, s32[3,2]{0,1:T(2,128)}, u32[]{:S(2)}) copy-start(s32[3,2]{0,1:T(2,128)} %param.15) | copy-start | bytes 76
  9.5 10.2 %copy-start = (bf16[384,256]{1,0:T(8,128)(2,1)S(1)}, bf16[384,256]{1,0:T(8,128)(2,1)}, u32[]{:S(2)}) copy-start(bf16[384,256]{1,0:T(8,128)(2,1)} %constant.18.clone.flat) | copy-start | bytes 589828
  9.5 10.1 %all-to-all-start = ((bf16[4,128,128]{2,1,0:T(8,128)(2,1)}), bf16[4,128,128]{2,1,0:T(8,128)(2,1)S(1)}, u32[]{:S(2)}, u32[]{:S(2)}) async-start(bf16[4,128,128]{2,1,0:T(8,128)(2,1)} %late.1), calls=%async_computation | async-start | bytes 262144 | tf_op jit(solution)/shard_map/all_to_all | solution.py:854
  15.6 0.7 %copy-start.4 = (f32[8]{0:T(128)S(1)}, f32[8]{0:T(128)}, u32[]{:S(2)}) copy-start(f32[8]{0:T(128)} %param.14) | copy-start | bytes 100

commit v23 on v22

--- a/solution.py
+++ b/solution.py
@@ -273,8 +273,8 @@
 
 
 def pack_kernel(
-    intensity, temp_hbm, cure_hbm, x_hbm, z_hbm, far, near, own, x_parts, z_parts, temp, cure,
-    grey, sems,
+    intensity, temp_hbm, cure_hbm, x_hbm, z_hbm, far, near, grey, x_parts, z_parts, temp, cure,
+    sems,
 ):
     rows, width, depth = intensity.shape
     copies = [
@@ -312,9 +312,6 @@
     def _():
         send(far, near)
 
-    for row in range(rows):
-        half = (row % 2) * depth
-        own[row // 2, :, half : half + depth] = grey[row].astype(jnp.float32).astype(jnp.bfloat16)
     for copy in copies[3:]:
         copy.wait()
 
@@ -453,13 +450,10 @@
 
 
 def early_kernel(
-    starts, own, x_parts, z_parts, late_hbm, sums, diagonal, sides, tiles, x_late, across,
-    filtered, grads, sem,
+    starts, grey, x_parts, z_parts, sums, diagonal, sides, tiles, across, filtered, grads
 ):
-    copy = pltpu.make_async_copy(late_hbm, x_late, sem.at[0])
-    copy.start()
-    pairs, width, double = own.shape
-    rows, depth = 2 * pairs, double // 2
+    rows, width, depth = grey.shape
+    double = 2 * depth
     empty = jnp.zeros((depth, depth), jnp.bfloat16)
     for kind in range(2):
         for half in range(2):
@@ -467,7 +461,8 @@
             band = z_parts[kind * depth : (kind + 1) * depth, :]
             diagonal[at, half * depth : (half + 1) * depth] = band
             diagonal[at, (1 - half) * depth : (2 - half) * depth] = empty
-    whole = jnp.concatenate([own[pair] for pair in range(pairs)], axis=1)
+    values = [grey[row].astype(jnp.float32) for row in range(rows)]
+    whole = jnp.concatenate([value.astype(jnp.bfloat16) for value in values], axis=1)
     result = product(x_parts[starts[0] : starts[2], :width], whole)
     across[...] = result[: starts[1]]
     sides[...] = result[starts[1] :]
@@ -475,13 +470,8 @@
     results = tensor_sums(across, sx, None, diagonal, z_parts, filtered, grads)
     for index, kind in enumerate(USED):
         sums[index] = results[kind]
-    values = [
-        own[row // 2, :, (row % 2) * depth : (row % 2 + 1) * depth].astype(jnp.float32)
-        for row in range(rows)
-    ]
     for index, tile in enumerate(rim_tiles(values)):
         tiles[index] = tile
-    copy.wait()
 
 
 def late_kernel(
@@ -589,7 +579,7 @@
         rims = chunks[order.index(part), 0 : voxels + folded, :].astype(jnp.float32)
         second = rims[voxels:]
         second = [second[: voxels - folded], pltpu.roll(second, HALF, 1)]
-        for tile in ([rims[:voxels]], second):
+        for tile in ([rims[:voxels]], second)[: 2 if part else 1]:
             tiles.append(jnp.concatenate(tile + spare, axis=0).astype(jnp.bfloat16))
     result = product(
         steep[starts[1] : starts[2], :tall], jnp.concatenate(tiles, axis=1)
@@ -599,7 +589,9 @@
         values = result[kind * rows_x : (kind + 1) * rows_x]
         tile = lambda index: values[:, index * LANES : (index + 1) * LANES]
         stack = [
-            jnp.concatenate([tile(2 * part), tile(2 * part + 2), tile(2 * part + 3)], axis=1)
+            jnp.concatenate(
+                [tile(max(2 * part - 1, 0)), tile(2 * part + 1), tile(2 * part + 2)], axis=1
+            )
             for part in range(parts - 1)
         ]
         kinds.append(jnp.concatenate(stack, axis=0))
@@ -767,13 +759,13 @@
     flat, _ = stacked(np.concatenate([rims[0], rims[2]], axis=1))
     steep, rim_starts = stacked(rims[1], *rim_x_bands(count))
     cell_bands, _ = stacked(rim_cells(rows, depth, depths))
-    far, near, own, x_parts, z_parts, temp, cure = pl.pallas_call(
+    far, near, grey, x_parts, z_parts, temp, cure = pl.pallas_call(
         pack_kernel,
         name="pack",
         out_shape=(
             pltpu.VMEM((slots, depth), bf16),
             pltpu.VMEM((slots, depth), bf16),
-            pltpu.VMEM((rows // 2, width, 2 * depth), bf16),
+            pltpu.VMEM((rows, width, depth), jnp.int32),
             pltpu.VMEM(x_hbm.shape, bf16),
             pltpu.VMEM(z_hbm.shape, bf16),
             pltpu.VMEM((count, lanes), jnp.float32),
@@ -781,7 +773,6 @@
         ),
         in_specs=[stay] * 5,
         scratch_shapes=[
-            pltpu.VMEM((rows, width, depth), jnp.int32),
             pltpu.SemaphoreType.DMA((5,)),
         ],
         compiler_params=params,
@@ -815,7 +806,7 @@
             transcendentals=0,
         )
 
-    early_sums, diagonal, sides, own_tiles, x_late = pl.pallas_call(
+    early_sums, diagonal, sides, own_tiles = pl.pallas_call(
         functools.partial(early_kernel, early_starts),
         name="early",
         out_shape=(
@@ -823,13 +814,11 @@
             pltpu.VMEM((4 * depth, 2 * depth), bf16),
             pltpu.VMEM((2 * late, rows * depth), jnp.float32),
             pltpu.VMEM((3, width, LANES), jnp.float32),
-            pltpu.VMEM(x_late.shape, bf16),
         ),
-        in_specs=[vmem] * 3 + [stay],
-        scratch_shapes=scratch(EARLY) + [pltpu.SemaphoreType.DMA((1,))],
+        scratch_shapes=scratch(EARLY),
         cost_estimate=cost(EARLY),
         compiler_params=params,
-    )(own, x_parts, z_parts, fixed(x_late))
+    )(grey, x_parts, z_parts)
 
     products_x, voxels = own_columns(count)
     at_sums, half = chunk_rows(count, lanes)

time: 21.4 us -> 21.4 us (level)
    unnamed x11 -> x13, local copies, waits for them, and re-layouts: 0.69 us -> 0.69 us
where the time goes in v23:
time: 21.4 us; the launch traced here: 21.1 us
  starting transfers between devices  11 us (51%)
  Pallas kernels  5.18 us (24%)
  waiting for transfers between devices  3.12 us (15%)
  local copies, waits for them, and re-layouts  0.87 us (4%)
  between operations  0.73 us (3%)
    all_to_all x1, starting transfers between devices, on_device(): lax.all_to_all(chunks, 'depth', split_axis=0, concat_axis=0, tiled=True,...  6.02 us
    ppermute x2, starting transfers between devices, moved(): return lax.ppermute(values, ('plane', 'depth'), index)  5.03 us
    all_to_all x1, waiting for transfers between devices, on_device(): lax.all_to_all(chunks, 'depth', split_axis=0, concat_axis=0, tiled=True,...  3.12 us
    pallas_call x1, Pallas kernels, on_device(): pl.pallas_call(functools.partial(late_kernel, late_starts, width), name='...  1.56 us
    pallas_call x1, Pallas kernels, on_device(): pl.pallas_call(functools.partial(cure_kernel, cells, rim_starts), name='c...  1.48 us
    pallas_call x1, Pallas kernels, on_device(): pl.pallas_call(pack_kernel, name='pack', out_shape=(pltpu.VMEM((slots, de...  1.13 us
    pallas_call x1, Pallas kernels, on_device(): pl.pallas_call(functools.partial(early_kernel, early_starts), name='early...  1.01 us
    unnamed x13, local copies, waits for them, and re-layouts  0.69 us
  transfers between devices with their start and end apart: 3, of which 1 were waited for; matrix products, arithmetic and copies ran while one was open for 2% of the time, Pallas kernels for 5%

profile of v23, /device:TPU:0, one launch (start us, length us, event | category | flops | bytes accessed | tf_op | source)
XLA Modules:
  0.0 21.1 jit_solution(17791636471477213051)
XLA Ops:
  0.6 1.1 %pack.1 = (bf16[208,128]{1,0:T(8,128)(2,1)S(1)}, bf16[208,128]{1,0:T(8,128)(2,1)S(1)}, s32[8,96,128]{2,1,0:T(8,128)S(1)}, bf16[320,96]{1,0:T(8,128)(2,1)S(1)}, b...) custom-call(s32[8,96,128]{2,1,0:T(8,128)} %intensity.1, f32[6,128]{1,0:T(8,128)} %temp_hbm.1, ...), custom_call_target="tpu_custom_call" | custom-call | tf_op jit(solution)/shard_map/pack/pallas_call | solution.py:762
  1.8 0.7 %collective-permute-start = (bf16[208,128]{1,0:T(8,128)(2,1)S(1)}, bf16[208,128]{1,0:T(8,128)(2,1)S(1)}, u32[]{:S(2)}, u32[]{:S(2)}) collective-permute-start(bf16[208,128]{1,0:T(8,128)(2,1)S(1)} %get-tuple-element.14), channel_id=1, source_target_pairs={{4,8},{5,9},{6,10},{7,11},{12,16},{13,17},{14,18},{15,19},{20,24},... | collective-permute-start | bytes 159752 | tf_op jit(solution)/shard_map/ppermute | solution.py:783
  2.4 4.4 %collective-permute-start.1 = (bf16[208,128]{1,0:T(8,128)(2,1)S(1)}, bf16[208,128]{1,0:T(8,128)(2,1)S(1)}, u32[]{:S(2)}, u32[]{:S(2)}) collective-permute-start(bf16[208,128]{1,0:T(8,128)(2,1)S(1)} %get-tuple-element.15), channel_id=1, source_target_pairs={{0,4},{1,5},{2,6},{3,7},{8,12},{9,13},{10,14},{11,15},{16,20},{17,... | collective-permute-start | bytes 159752 | tf_op jit(solution)/shard_map/ppermute | solution.py:783
  6.8 1.0 %early.1 = (f32[4,32,128]{2,1,0:T(8,128)S(1)}, bf16[512,256]{1,0:T(8,128)(2,1)S(1)}, f32[96,1024]{1,0:T(8,128)S(1)}, f32[3,96,128]{2,1,0:T(8,128)S(1)}) custom-call(s32[8,96,128]{2,1,0:T(8,128)S(1)} %get-tuple-element.17.grey, bf16[320,96]{1,0:T(8,128)(2,1)S(1)} %get-tuple-element.18.x_parts, bf16[384,128]{1,0:T(8,128)(2,1)S(1)} %get-tuple-element.16.z_parts), custom_call_target="tpu_custom_call" | custom-call | flops 251658240 | bytes 4000000 | tf_op jit(solution)/shard_map/early/pallas_call | solution.py:809
  7.8 0.0 collective-permute-done.far
  7.8 0.0 collective-permute-done.1.near
  7.8 0.0 copy-done.3
  7.9 0.0 copy-start.1
  7.9 0.0 copy-start.2
  7.9 1.6 %late.1 = bf16[4,128,128]{2,1,0:T(8,128)(2,1)} custom-call(bf16[208,128]{1,0:T(8,128)(2,1)S(1)} %collective-permute-done.far, bf16[208,128]{1,0:T(8,128)(2,1)S(1)} %collective-permute-done.1.near, bf16[128,48]{1,0:T(8,128)(2,1)S(1)} %copy-done.3, bf16[384,128]{1,0:T(8,128)(2,1)S(1)} %get-tuple-element.16.z_parts, ...), custom_call_target="tpu_custom_call" | custom-call | flops 125829120 | bytes 4000000 | tf_op jit(solution)/shard_map/late/pallas_call | solution.py:826
  9.4 0.0 copy-start.4
  9.5 0.0 copy-start
  9.5 6.0 %all-to-all-start = ((bf16[4,128,128]{2,1,0:T(8,128)(2,1)}), bf16[4,128,128]{2,1,0:T(8,128)(2,1)S(1)}, u32[]{:S(2)}, u32[]{:S(2)}) async-start(bf16[4,128,128]{2,1,0:T(8,128)(2,1)} %late.1), calls=%async_computation | async-start | bytes 262144 | tf_op jit(solution)/shard_map/all_to_all | solution.py:843
  15.5 0.0 copy-done.4
  15.5 0.1 copy.18
  15.6 0.1 eq.15
  15.7 0.6 %copy-done.5 = f32[8]{0:T(128)S(1)} copy-done((f32[8]{0:T(128)S(1)}, f32[8]{0:T(128)}, u32[]{:S(2)}) %copy-start.5) | copy-done | bytes 56
  16.2 0.2 select_reduce_fusion
  16.4 0.1 copy.19.tools
  16.5 3.1 %all-to-all-done.chunks = bf16[4,128,128]{2,1,0:T(8,128)(2,1)S(1)} async-done(((bf16[4,128,128]{2,1,0:T(8,128)(2,1)}), bf16[4,128,128]{2,1,0:T(8,128)(2,1)S(1)}, u32[]{:S(2)}, u32[]{:S(2)}) %all-to-all-start) | async-done | bytes 131104 | tf_op jit(solution)/shard_map/all_to_all | solution.py:843
  19.6 0.0 copy-done.1
  19.6 0.0 copy-done.2
  19.6 0.0 copy-done
  19.7 1.5 %cure.1 = (f32[6,128]{1,0:T(8,128)}, f32[6,128]{1,0:T(8,128)}, f32[3,6,128]{2,1,0:T(8,128)}) custom-call(bf16[4,128,128]{2,1,0:T(8,128)(2,1)S(1)} %all-to-all-done.chunks, f32[6,128]{1,0:T(8,128)S(1)} %get-tuple-element.23.temp.temp_in, f32[6,128]{1,0:T(8,128)S(1)} %get-tuple-element.24.cure.cure_in, f32[6,1]{1,0:T(8,128)S(1)} %copy.19.tools, ...), custom_call_target="tpu_custom_call" | custom-call | tf_op jit(solution)/shard_map/cure/pallas_call | solution.py:852
  (2 shorter events, 0.0 us)
Async XLA Ops:
  1.8 6.1 %collective-permute-start = (bf16[208,128]{1,0:T(8,128)(2,1)S(1)}, bf16[208,128]{1,0:T(8,128)(2,1)S(1)}, u32[]{:S(2)}, u32[]{:S(2)}) collective-permute-start(bf16[208,128]{1,0:T(8,128)(2,1)S(1)} %get-tuple-element.14), channel_id=1, source_target_pairs={{4,8},{5,9},{6,10},{7,11},{12,16},{13,17},{14,18},{15,19},{20,24},... | collective-permute-start | bytes 159752 | tf_op jit(solution)/shard_map/ppermute | solution.py:783
  2.4 5.4 %collective-permute-start.1 = (bf16[208,128]{1,0:T(8,128)(2,1)S(1)}, bf16[208,128]{1,0:T(8,128)(2,1)S(1)}, u32[]{:S(2)}, u32[]{:S(2)}) collective-permute-start(bf16[208,128]{1,0:T(8,128)(2,1)S(1)} %get-tuple-element.15), channel_id=1, source_target_pairs={{0,4},{1,5},{2,6},{3,7},{8,12},{9,13},{10,14},{11,15},{16,20},{17,... | collective-permute-start | bytes 159752 | tf_op jit(solution)/shard_map/ppermute | solution.py:783
  6.8 1.0 %copy-start.3 = (bf16[128,48]{1,0:T(8,128)(2,1)S(1)}, bf16[128,48]{1,0:T(8,128)(2,1)}, u32[]{:S(2)}) copy-start(bf16[128,48]{1,0:T(8,128)(2,1)} %constant.17.clone.x_late) | copy-start | bytes 36868
  7.9 11.8 %copy-start.1 = (bf16[528,128]{1,0:T(8,128)(2,1)S(1)}, bf16[528,128]{1,0:T(8,128)(2,1)}, u32[]{:S(2)}) copy-start(bf16[528,128]{1,0:T(8,128)(2,1)} %constant.19.clone.steep) | copy-start | bytes 405508
  7.9 11.8 %copy-start.2 = (bf16[384,128]{1,0:T(8,128)(2,1)S(1)}, bf16[384,128]{1,0:T(8,128)(2,1)}, u32[]{:S(2)}) copy-start(bf16[384,128]{1,0:T(8,128)(2,1)} %constant.20.clone.rim_bands) | copy-start | bytes 294916
  9.4 6.0 %copy-start.4 = (s32[3,2]{0,1:T(2,128)S(1)}, s32[3,2]{0,1:T(2,128)}, u32[]{:S(2)}) copy-start(s32[3,2]{0,1:T(2,128)} %param.15) | copy-start | bytes 76
  9.5 10.2 %copy-start = (bf16[384,256]{1,0:T(8,128)(2,1)S(1)}, bf16[384,256]{1,0:T(8,128)(2,1)}, u32[]{:S(2)}) copy-start(bf16[384,256]{1,0:T(8,128)(2,1)} %constant.18.clone.flat) | copy-start | bytes 589828
  9.5 10.2 %all-to-all-start = ((bf16[4,128,128]{2,1,0:T(8,128)(2,1)}), bf16[4,128,128]{2,1,0:T(8,128)(2,1)S(1)}, u32[]{:S(2)}, u32[]{:S(2)}) async-start(bf16[4,128,128]{2,1,0:T(8,128)(2,1)} %late.1), calls=%async_computation | async-start | bytes 262144 | tf_op jit(solution)/shard_map/all_to_all | solution.py:843
  15.6 0.7 %copy-start.5 = (f32[8]{0:T(128)S(1)}, f32[8]{0:T(128)}, u32[]{:S(2)}) copy-start(f32[8]{0:T(128)} %param.14) | copy-start | bytes 100

commit v24 on v23

--- a/solution.py
+++ b/solution.py
@@ -159,7 +159,7 @@
 
 def meeting_order(blocks):
     middle = blocks // 2
-    return [*range(middle, blocks), *range(middle)]
+    return [middle, *range(1, middle), *range(middle + 1, blocks), 0]
 
 
 def own_columns(count):

time: 21.4 us -> 21.8 us (1.019)
  waiting for transfers between devices: 3.12 us -> 3.52 us
    all_to_all x1, waiting for transfers between devices: 3.12 us -> 3.51 us  [on_device(): lax.all_to_all(chunks, 'depth', split_axis=0, concat_axis=0, tiled=True,...]
where the time goes in v24:
time: 21.8 us; the launch traced here: 21.5 us
  starting transfers between devices  11.1 us (51%)
  Pallas kernels  5.18 us (24%)
  waiting for transfers between devices  3.52 us (16%)
  local copies, waits for them, and re-layouts  0.87 us (4%)
  between operations  0.73 us (3%)
    all_to_all x1, starting transfers between devices, on_device(): lax.all_to_all(chunks, 'depth', split_axis=0, concat_axis=0, tiled=True,...  6.02 us
    ppermute x2, starting transfers between devices, moved(): return lax.ppermute(values, ('plane', 'depth'), index)  5.03 us
    all_to_all x1, waiting for transfers between devices, on_device(): lax.all_to_all(chunks, 'depth', split_axis=0, concat_axis=0, tiled=True,...  3.51 us
    pallas_call x1, Pallas kernels, on_device(): pl.pallas_call(functools.partial(late_kernel, late_starts, width), name='...  1.56 us
    pallas_call x1, Pallas kernels, on_device(): pl.pallas_call(functools.partial(cure_kernel, cells, rim_starts), name='c...  1.48 us
    pallas_call x1, Pallas kernels, on_device(): pl.pallas_call(pack_kernel, name='pack', out_shape=(pltpu.VMEM((slots, de...  1.13 us
    pallas_call x1, Pallas kernels, on_device(): pl.pallas_call(functools.partial(early_kernel, early_starts), name='early...  1.01 us
    unnamed x13, local copies, waits for them, and re-layouts  0.69 us
  transfers between devices with their start and end apart: 3, of which 1 were waited for; matrix products, arithmetic and copies ran while one was open for 2% of the time, Pallas kernels for 5%

profile of v24, /device:TPU:0, one launch (start us, length us, event | category | flops | bytes accessed | tf_op | source)
XLA Modules:
  0.0 21.5 jit_solution(14267974317168446307)
XLA Ops:
  0.6 1.1 %pack.1 = (bf16[208,128]{1,0:T(8,128)(2,1)S(1)}, bf16[208,128]{1,0:T(8,128)(2,1)S(1)}, s32[8,96,128]{2,1,0:T(8,128)S(1)}, bf16[320,96]{1,0:T(8,128)(2,1)S(1)}, b...) custom-call(s32[8,96,128]{2,1,0:T(8,128)} %intensity.1, f32[6,128]{1,0:T(8,128)} %temp_hbm.1, ...), custom_call_target="tpu_custom_call" | custom-call | tf_op jit(solution)/shard_map/pack/pallas_call | solution.py:762
  1.8 0.7 %collective-permute-start = (bf16[208,128]{1,0:T(8,128)(2,1)S(1)}, bf16[208,128]{1,0:T(8,128)(2,1)S(1)}, u32[]{:S(2)}, u32[]{:S(2)}) collective-permute-start(bf16[208,128]{1,0:T(8,128)(2,1)S(1)} %get-tuple-element.14), channel_id=1, source_target_pairs={{4,8},{5,9},{6,10},{7,11},{12,16},{13,17},{14,18},{15,19},{20,24},... | collective-permute-start | bytes 159752 | tf_op jit(solution)/shard_map/ppermute | solution.py:783
  2.4 4.4 %collective-permute-start.1 = (bf16[208,128]{1,0:T(8,128)(2,1)S(1)}, bf16[208,128]{1,0:T(8,128)(2,1)S(1)}, u32[]{:S(2)}, u32[]{:S(2)}) collective-permute-start(bf16[208,128]{1,0:T(8,128)(2,1)S(1)} %get-tuple-element.15), channel_id=1, source_target_pairs={{0,4},{1,5},{2,6},{3,7},{8,12},{9,13},{10,14},{11,15},{16,20},{17,... | collective-permute-start | bytes 159752 | tf_op jit(solution)/shard_map/ppermute | solution.py:783
  6.8 1.0 %early.1 = (f32[4,32,128]{2,1,0:T(8,128)S(1)}, bf16[512,256]{1,0:T(8,128)(2,1)S(1)}, f32[96,1024]{1,0:T(8,128)S(1)}, f32[3,96,128]{2,1,0:T(8,128)S(1)}) custom-call(s32[8,96,128]{2,1,0:T(8,128)S(1)} %get-tuple-element.17.grey, bf16[320,96]{1,0:T(8,128)(2,1)S(1)} %get-tuple-element.18.x_parts, bf16[384,128]{1,0:T(8,128)(2,1)S(1)} %get-tuple-element.16.z_parts), custom_call_target="tpu_custom_call" | custom-call | flops 251658240 | bytes 4000000 | tf_op jit(solution)/shard_map/early/pallas_call | solution.py:809
  7.8 0.0 collective-permute-done.far
  7.8 0.0 collective-permute-done.1.near
  7.8 0.0 copy-done.3
  7.9 0.0 copy-start.1
  7.9 0.0 copy-start.2
  7.9 1.6 %late.1 = bf16[4,128,128]{2,1,0:T(8,128)(2,1)} custom-call(bf16[208,128]{1,0:T(8,128)(2,1)S(1)} %collective-permute-done.far, bf16[208,128]{1,0:T(8,128)(2,1)S(1)} %collective-permute-done.1.near, bf16[128,48]{1,0:T(8,128)(2,1)S(1)} %copy-done.3, bf16[384,128]{1,0:T(8,128)(2,1)S(1)} %get-tuple-element.16.z_parts, ...), custom_call_target="tpu_custom_call" | custom-call | flops 125829120 | bytes 4000000 | tf_op jit(solution)/shard_map/late/pallas_call | solution.py:826
  9.4 0.0 copy-start.4
  9.5 0.0 copy-start
  9.5 6.0 %all-to-all-start = ((bf16[4,128,128]{2,1,0:T(8,128)(2,1)}), bf16[4,128,128]{2,1,0:T(8,128)(2,1)S(1)}, u32[]{:S(2)}, u32[]{:S(2)}) async-start(bf16[4,128,128]{2,1,0:T(8,128)(2,1)} %late.1), calls=%async_computation | async-start | bytes 262144 | tf_op jit(solution)/shard_map/all_to_all | solution.py:843
  15.5 0.0 copy-done.4
  15.5 0.1 copy.18
  15.6 0.1 eq.15
  15.7 0.6 %copy-done.5 = f32[8]{0:T(128)S(1)} copy-done((f32[8]{0:T(128)S(1)}, f32[8]{0:T(128)}, u32[]{:S(2)}) %copy-start.5) | copy-done | bytes 56
  16.2 0.2 select_reduce_fusion
  16.4 0.1 copy.19.tools
  16.5 3.5 %all-to-all-done.chunks = bf16[4,128,128]{2,1,0:T(8,128)(2,1)S(1)} async-done(((bf16[4,128,128]{2,1,0:T(8,128)(2,1)}), bf16[4,128,128]{2,1,0:T(8,128)(2,1)S(1)}, u32[]{:S(2)}, u32[]{:S(2)}) %all-to-all-start) | async-done | bytes 131104 | tf_op jit(solution)/shard_map/all_to_all | solution.py:843
  20.0 0.0 copy-done.1
  20.0 0.0 copy-done.2
  20.0 0.0 copy-done
  20.0 1.5 %cure.1 = (f32[6,128]{1,0:T(8,128)}, f32[6,128]{1,0:T(8,128)}, f32[3,6,128]{2,1,0:T(8,128)}) custom-call(bf16[4,128,128]{2,1,0:T(8,128)(2,1)S(1)} %all-to-all-done.chunks, f32[6,128]{1,0:T(8,128)S(1)} %get-tuple-element.23.temp.temp_in, f32[6,128]{1,0:T(8,128)S(1)} %get-tuple-element.24.cure.cure_in, f32[6,1]{1,0:T(8,128)S(1)} %copy.19.tools, ...), custom_call_target="tpu_custom_call" | custom-call | tf_op jit(solution)/shard_map/cure/pallas_call | solution.py:852
  (2 shorter events, 0.0 us)
Async XLA Ops:
  1.8 6.1 %collective-permute-start = (bf16[208,128]{1,0:T(8,128)(2,1)S(1)}, bf16[208,128]{1,0:T(8,128)(2,1)S(1)}, u32[]{:S(2)}, u32[]{:S(2)}) collective-permute-start(bf16[208,128]{1,0:T(8,128)(2,1)S(1)} %get-tuple-element.14), channel_id=1, source_target_pairs={{4,8},{5,9},{6,10},{7,11},{12,16},{13,17},{14,18},{15,19},{20,24},... | collective-permute-start | bytes 159752 | tf_op jit(solution)/shard_map/ppermute | solution.py:783
  2.4 5.4 %collective-permute-start.1 = (bf16[208,128]{1,0:T(8,128)(2,1)S(1)}, bf16[208,128]{1,0:T(8,128)(2,1)S(1)}, u32[]{:S(2)}, u32[]{:S(2)}) collective-permute-start(bf16[208,128]{1,0:T(8,128)(2,1)S(1)} %get-tuple-element.15), channel_id=1, source_target_pairs={{0,4},{1,5},{2,6},{3,7},{8,12},{9,13},{10,14},{11,15},{16,20},{17,... | collective-permute-start | bytes 159752 | tf_op jit(solution)/shard_map/ppermute | solution.py:783
  6.8 1.0 %copy-start.3 = (bf16[128,48]{1,0:T(8,128)(2,1)S(1)}, bf16[128,48]{1,0:T(8,128)(2,1)}, u32[]{:S(2)}) copy-start(bf16[128,48]{1,0:T(8,128)(2,1)} %constant.17.clone.x_late) | copy-start | bytes 36868
  7.9 12.2 %copy-start.1 = (bf16[528,128]{1,0:T(8,128)(2,1)S(1)}, bf16[528,128]{1,0:T(8,128)(2,1)}, u32[]{:S(2)}) copy-start(bf16[528,128]{1,0:T(8,128)(2,1)} %constant.19.clone.steep) | copy-start | bytes 405508
  7.9 12.2 %copy-start.2 = (bf16[384,128]{1,0:T(8,128)(2,1)S(1)}, bf16[384,128]{1,0:T(8,128)(2,1)}, u32[]{:S(2)}) copy-start(bf16[384,128]{1,0:T(8,128)(2,1)} %constant.20.clone.rim_bands) | copy-start | bytes 294916
  9.4 6.0 %copy-start.4 = (s32[3,2]{0,1:T(2,128)S(1)}, s32[3,2]{0,1:T(2,128)}, u32[]{:S(2)}) copy-start(s32[3,2]{0,1:T(2,128)} %param.15) | copy-start | bytes 76
  9.5 10.6 %copy-start = (bf16[384,256]{1,0:T(8,128)(2,1)S(1)}, bf16[384,256]{1,0:T(8,128)(2,1)}, u32[]{:S(2)}) copy-start(bf16[384,256]{1,0:T(8,128)(2,1)} %constant.18.clone.flat) | copy-start | bytes 589828
  9.5 10.6 %all-to-all-start = ((bf16[4,128,128]{2,1,0:T(8,128)(2,1)}), bf16[4,128,128]{2,1,0:T(8,128)(2,1)S(1)}, u32[]{:S(2)}, u32[]{:S(2)}) async-start(bf16[4,128,128]{2,1,0:T(8,128)(2,1)} %late.1), calls=%async_computation | async-start | bytes 262144 | tf_op jit(solution)/shard_map/all_to_all | solution.py:843
  15.6 0.7 %copy-start.5 = (f32[8]{0:T(128)S(1)}, f32[8]{0:T(128)}, u32[]{:S(2)}) copy-start(f32[8]{0:T(128)} %param.14) | copy-start | bytes 100

commit v25 on v23

--- a/solution.py
+++ b/solution.py
@@ -126,7 +126,7 @@
 
 
 def rim_bands(rows):
-    bands = np.zeros((3, 3 * LANES, LANES))
+    bands = np.zeros((3, 2 * LANES, LANES))
     for part in range(3):
         row_taps, depth_taps = grad_taps(ROW_KINDS[part]), grad_taps(DEPTH_KINDS[part])
         for source in range(rows):
@@ -135,7 +135,7 @@
                 for near in range(-RIM, RIM):
                     lane = source * RIM + near % RIM
                     if near >= 0:
-                        lane += rows * RIM + LANES
+                        lane += rows * RIM
                     for place in range(-R1, R1):
                         value = row_tap * tap(depth_taps, near - place)
                         bands[part, lane, target * 2 * R1 + R1 + place] = value
@@ -573,13 +573,18 @@
     folded = fold(voxels)
     tall = -(-voxels // 16) * 16
     spare = [jnp.zeros((tall - voxels, LANES), jnp.float32)] if tall > voxels else []
+    lane = lax.broadcasted_iota(jnp.int32, (voxels, LANES), 1)
+    order = meeting_order(parts)
+    rims = [
+        chunks[order.index(part), 0 : voxels + folded, :].astype(jnp.float32)
+        for part in range(parts)
+    ]
     tiles = []
-    order = meeting_order(parts)
-    for part in range(parts):
-        rims = chunks[order.index(part), 0 : voxels + folded, :].astype(jnp.float32)
-        second = rims[voxels:]
+    for below, above in zip(rims[:-1], rims[1:]):
+        first = jnp.where(lane < ROWS * RIM, below[:voxels], above[:voxels])
+        second = above[voxels:]
         second = [second[: voxels - folded], pltpu.roll(second, HALF, 1)]
-        for tile in ([rims[:voxels]], second)[: 2 if part else 1]:
+        for tile in ([first], second):
             tiles.append(jnp.concatenate(tile + spare, axis=0).astype(jnp.bfloat16))
     result = product(
         steep[starts[1] : starts[2], :tall], jnp.concatenate(tiles, axis=1)
@@ -587,12 +592,8 @@
     kinds = []
     for kind in range(2):
         values = result[kind * rows_x : (kind + 1) * rows_x]
-        tile = lambda index: values[:, index * LANES : (index + 1) * LANES]
         stack = [
-            jnp.concatenate(
-                [tile(max(2 * part - 1, 0)), tile(2 * part + 1), tile(2 * part + 2)], axis=1
-            )
-            for part in range(parts - 1)
+            values[:, 2 * part * LANES : 2 * (part + 1) * LANES] for part in range(parts - 1)
         ]
         kinds.append(jnp.concatenate(stack, axis=0))
     both = product(kinds[0], flat[...])

time: 21.4 us -> 21.4 us (level)
  no operation moved by 1% of the time
where the time goes in v25:
time: 21.4 us; the launch traced here: 21.1 us
  starting transfers between devices  11 us (51%)
  Pallas kernels  5.17 us (24%)
  waiting for transfers between devices  3.11 us (15%)
  local copies, waits for them, and re-layouts  0.87 us (4%)
  between operations  0.73 us (3%)
    all_to_all x1, starting transfers between devices, on_device(): lax.all_to_all(chunks, 'depth', split_axis=0, concat_axis=0, tiled=True,...  6.02 us
    ppermute x2, starting transfers between devices, moved(): return lax.ppermute(values, ('plane', 'depth'), index)  5.03 us
    all_to_all x1, waiting for transfers between devices, on_device(): lax.all_to_all(chunks, 'depth', split_axis=0, concat_axis=0, tiled=True,...  3.1 us
    pallas_call x1, Pallas kernels, on_device(): pl.pallas_call(functools.partial(late_kernel, late_starts, width), name='...  1.57 us
    pallas_call x1, Pallas kernels, on_device(): pl.pallas_call(functools.partial(cure_kernel, cells, rim_starts), name='c...  1.46 us
    pallas_call x1, Pallas kernels, on_device(): pl.pallas_call(pack_kernel, name='pack', out_shape=(pltpu.VMEM((slots, de...  1.13 us
    pallas_call x1, Pallas kernels, on_device(): pl.pallas_call(functools.partial(early_kernel, early_starts), name='early...  1.01 us
    unnamed x13, local copies, waits for them, and re-layouts  0.69 us
  transfers between devices with their start and end apart: 3, of which 1 were waited for; matrix products, arithmetic and copies ran while one was open for 2% of the time, Pallas kernels for 5%

profile of v25, /device:TPU:0, one launch (start us, length us, event | category | flops | bytes accessed | tf_op | source)
XLA Modules:
  0.0 21.1 jit_solution(9177106405487621043)
XLA Ops:
  0.6 1.1 %pack.1 = (bf16[208,128]{1,0:T(8,128)(2,1)S(1)}, bf16[208,128]{1,0:T(8,128)(2,1)S(1)}, s32[8,96,128]{2,1,0:T(8,128)S(1)}, bf16[320,96]{1,0:T(8,128)(2,1)S(1)}, b...) custom-call(s32[8,96,128]{2,1,0:T(8,128)} %intensity.1, f32[6,128]{1,0:T(8,128)} %temp_hbm.1, ...), custom_call_target="tpu_custom_call" | custom-call | tf_op jit(solution)/shard_map/pack/pallas_call | solution.py:763
  1.8 0.7 %collective-permute-start = (bf16[208,128]{1,0:T(8,128)(2,1)S(1)}, bf16[208,128]{1,0:T(8,128)(2,1)S(1)}, u32[]{:S(2)}, u32[]{:S(2)}) collective-permute-start(bf16[208,128]{1,0:T(8,128)(2,1)S(1)} %get-tuple-element.14), channel_id=1, source_target_pairs={{4,8},{5,9},{6,10},{7,11},{12,16},{13,17},{14,18},{15,19},{20,24},... | collective-permute-start | bytes 159752 | tf_op jit(solution)/shard_map/ppermute | solution.py:784
  2.4 4.4 %collective-permute-start.1 = (bf16[208,128]{1,0:T(8,128)(2,1)S(1)}, bf16[208,128]{1,0:T(8,128)(2,1)S(1)}, u32[]{:S(2)}, u32[]{:S(2)}) collective-permute-start(bf16[208,128]{1,0:T(8,128)(2,1)S(1)} %get-tuple-element.15), channel_id=1, source_target_pairs={{0,4},{1,5},{2,6},{3,7},{8,12},{9,13},{10,14},{11,15},{16,20},{17,... | collective-permute-start | bytes 159752 | tf_op jit(solution)/shard_map/ppermute | solution.py:784
  6.8 1.0 %early.1 = (f32[4,32,128]{2,1,0:T(8,128)S(1)}, bf16[512,256]{1,0:T(8,128)(2,1)S(1)}, f32[96,1024]{1,0:T(8,128)S(1)}, f32[3,96,128]{2,1,0:T(8,128)S(1)}) custom-call(s32[8,96,128]{2,1,0:T(8,128)S(1)} %get-tuple-element.17.grey, bf16[320,96]{1,0:T(8,128)(2,1)S(1)} %get-tuple-element.18.x_parts, bf16[384,128]{1,0:T(8,128)(2,1)S(1)} %get-tuple-element.16.z_parts), custom_call_target="tpu_custom_call" | custom-call | flops 251658240 | bytes 4000000 | tf_op jit(solution)/shard_map/early/pallas_call | solution.py:810
  7.8 0.0 collective-permute-done.far
  7.8 0.0 collective-permute-done.1.near
  7.8 0.0 copy-done.3
  7.9 0.0 copy-start.2
  7.9 1.6 %late.1 = bf16[4,128,128]{2,1,0:T(8,128)(2,1)} custom-call(bf16[208,128]{1,0:T(8,128)(2,1)S(1)} %collective-permute-done.far, bf16[208,128]{1,0:T(8,128)(2,1)S(1)} %collective-permute-done.1.near, bf16[128,48]{1,0:T(8,128)(2,1)S(1)} %copy-done.3, bf16[384,128]{1,0:T(8,128)(2,1)S(1)} %get-tuple-element.16.z_parts, ...), custom_call_target="tpu_custom_call" | custom-call | flops 125829120 | bytes 4000000 | tf_op jit(solution)/shard_map/late/pallas_call | solution.py:827
  9.4 0.0 copy-start.4
  9.5 0.0 copy-start
  9.5 0.0 copy-start.1
  9.5 6.0 %all-to-all-start = ((bf16[4,128,128]{2,1,0:T(8,128)(2,1)}), bf16[4,128,128]{2,1,0:T(8,128)(2,1)S(1)}, u32[]{:S(2)}, u32[]{:S(2)}) async-start(bf16[4,128,128]{2,1,0:T(8,128)(2,1)} %late.1), calls=%async_computation | async-start | bytes 262144 | tf_op jit(solution)/shard_map/all_to_all | solution.py:844
  15.5 0.0 copy-done.4
  15.5 0.1 copy.18
  15.6 0.1 eq.15
  15.7 0.6 %copy-done.5 = f32[8]{0:T(128)S(1)} copy-done((f32[8]{0:T(128)S(1)}, f32[8]{0:T(128)}, u32[]{:S(2)}) %copy-start.5) | copy-done | bytes 56
  16.3 0.2 select_reduce_fusion
  16.4 0.1 copy.19.tools
  16.5 3.1 %all-to-all-done.chunks = bf16[4,128,128]{2,1,0:T(8,128)(2,1)S(1)} async-done(((bf16[4,128,128]{2,1,0:T(8,128)(2,1)}), bf16[4,128,128]{2,1,0:T(8,128)(2,1)S(1)}, u32[]{:S(2)}, u32[]{:S(2)}) %all-to-all-start) | async-done | bytes 131104 | tf_op jit(solution)/shard_map/all_to_all | solution.py:844
  19.6 0.0 copy-done.2
  19.6 0.0 copy-done
  19.6 0.0 copy-done.1
  19.6 1.5 %cure.1 = (f32[6,128]{1,0:T(8,128)}, f32[6,128]{1,0:T(8,128)}, f32[3,6,128]{2,1,0:T(8,128)}) custom-call(bf16[4,128,128]{2,1,0:T(8,128)(2,1)S(1)} %all-to-all-done.chunks, f32[6,128]{1,0:T(8,128)S(1)} %get-tuple-element.23.temp.temp_in, f32[6,128]{1,0:T(8,128)S(1)} %get-tuple-element.24.cure.cure_in, f32[6,1]{1,0:T(8,128)S(1)} %copy.19.tools, ...), custom_call_target="tpu_custom_call" | custom-call | tf_op jit(solution)/shard_map/cure/pallas_call | solution.py:853
  (2 shorter events, 0.0 us)
Async XLA Ops:
  1.8 6.1 %collective-permute-start = (bf16[208,128]{1,0:T(8,128)(2,1)S(1)}, bf16[208,128]{1,0:T(8,128)(2,1)S(1)}, u32[]{:S(2)}, u32[]{:S(2)}) collective-permute-start(bf16[208,128]{1,0:T(8,128)(2,1)S(1)} %get-tuple-element.14), channel_id=1, source_target_pairs={{4,8},{5,9},{6,10},{7,11},{12,16},{13,17},{14,18},{15,19},{20,24},... | collective-permute-start | bytes 159752 | tf_op jit(solution)/shard_map/ppermute | solution.py:784
  2.4 5.4 %collective-permute-start.1 = (bf16[208,128]{1,0:T(8,128)(2,1)S(1)}, bf16[208,128]{1,0:T(8,128)(2,1)S(1)}, u32[]{:S(2)}, u32[]{:S(2)}) collective-permute-start(bf16[208,128]{1,0:T(8,128)(2,1)S(1)} %get-tuple-element.15), channel_id=1, source_target_pairs={{0,4},{1,5},{2,6},{3,7},{8,12},{9,13},{10,14},{11,15},{16,20},{17,... | collective-permute-start | bytes 159752 | tf_op jit(solution)/shard_map/ppermute | solution.py:784
  6.8 1.0 %copy-start.3 = (bf16[128,48]{1,0:T(8,128)(2,1)S(1)}, bf16[128,48]{1,0:T(8,128)(2,1)}, u32[]{:S(2)}) copy-start(bf16[128,48]{1,0:T(8,128)(2,1)} %constant.17.clone.x_late) | copy-start | bytes 36868
  7.9 11.8 %copy-start.2 = (bf16[384,128]{1,0:T(8,128)(2,1)S(1)}, bf16[384,128]{1,0:T(8,128)(2,1)}, u32[]{:S(2)}) copy-start(bf16[384,128]{1,0:T(8,128)(2,1)} %constant.20.clone.rim_bands) | copy-start | bytes 294916
  9.4 6.1 %copy-start.4 = (s32[3,2]{0,1:T(2,128)S(1)}, s32[3,2]{0,1:T(2,128)}, u32[]{:S(2)}) copy-start(s32[3,2]{0,1:T(2,128)} %param.15) | copy-start | bytes 76
  9.5 10.2 %copy-start = (bf16[256,256]{1,0:T(8,128)(2,1)S(1)}, bf16[256,256]{1,0:T(8,128)(2,1)}, u32[]{:S(2)}) copy-start(bf16[256,256]{1,0:T(8,128)(2,1)} %constant.18.clone.flat) | copy-start | bytes 393220
  9.5 10.2 %copy-start.1 = (bf16[400,128]{1,0:T(8,128)(2,1)S(1)}, bf16[400,128]{1,0:T(8,128)(2,1)}, u32[]{:S(2)}) copy-start(bf16[400,128]{1,0:T(8,128)(2,1)} %constant.19.clone.steep) | copy-start | bytes 307204
  9.5 10.2 %all-to-all-start = ((bf16[4,128,128]{2,1,0:T(8,128)(2,1)}), bf16[4,128,128]{2,1,0:T(8,128)(2,1)S(1)}, u32[]{:S(2)}, u32[]{:S(2)}) async-start(bf16[4,128,128]{2,1,0:T(8,128)(2,1)} %late.1), calls=%async_computation | async-start | bytes 262144 | tf_op jit(solution)/shard_map/all_to_all | solution.py:844
  15.6 0.7 %copy-start.5 = (f32[8]{0:T(128)S(1)}, f32[8]{0:T(128)}, u32[]{:S(2)}) copy-start(f32[8]{0:T(128)} %param.14) | copy-start | bytes 100

commit v26 on v25

--- a/solution.py
+++ b/solution.py
@@ -533,14 +533,13 @@
         across, sx, late_mask(late, width), diagonal, z_parts, filtered, grads
     )
     yy, xx, zz, xz = [early_sums[index] + results[kind] for index, kind in enumerate(USED)]
-    trace = yy + xx + zz
-    lane = lax.broadcasted_iota(jnp.int32, trace.shape, 1)
+    lane = lax.broadcasted_iota(jnp.int32, yy.shape, 1)
     columns, cells = sizes(width, depth)
     tail = 4 * cells - LANES
     joint = pltpu.roll(xz, 3 * cells, 1)
     rest = jnp.where(lane < tail, joint, 0.0)
     rest = pltpu.roll(rest, 0, 1, stride=tail, stride_axis=0)
-    for index, part in ((2, zz), (1, xx), (0, trace)):
+    for index, part in ((2, zz), (1, xx), (0, yy)):
         moved = part if index == 0 else pltpu.roll(part, index * cells, 1)
         joint = jnp.where(lane < (index + 1) * cells, moved, joint)
 
@@ -632,7 +631,7 @@
     order = meeting_order(parts)
 
     near = rim_sums(chunks, count, starts, flat, steep, rim_bands)
-    sums = [near[0] + near[1] + near[2], near[1], near[2], near[5]]
+    sums = [near[kind] for kind in USED]
     blocks = [chunks[order.index(part), at_sums:, :].astype(jnp.float32) for part in range(parts)]
     columns = [
         jnp.concatenate(
@@ -672,7 +671,7 @@
             shift = (first_cell - (index % 3) * cells) % lanes
             moved = chunk if shift == 0 else pltpu.roll(chunk, shift, 1)
             sums[index] = sums[index] + jnp.where(here, moved, 0.0)
-    trace = sums[0]
+    trace = sums[0] + sums[1] + sums[2]
     scale = (conduct_fiber - conduct_matrix) / (2.0 * trace + tensor_eps)
     conduct = [
         conduct_matrix + scale * (trace - sums[1]),

time: 21.4 us -> 21.4 us (level)
  no operation moved by 1% of the time
where the time goes in v26:
time: 21.4 us; the launch traced here: 21.1 us
  starting transfers between devices  11 us (51%)
  Pallas kernels  5.16 us (24%)
  waiting for transfers between devices  3.11 us (15%)
  local copies, waits for them, and re-layouts  0.87 us (4%)
  between operations  0.73 us (3%)
    all_to_all x1, starting transfers between devices, on_device(): lax.all_to_all(chunks, 'depth', split_axis=0, concat_axis=0, tiled=True,...  6.02 us
    ppermute x2, starting transfers between devices, moved(): return lax.ppermute(values, ('plane', 'depth'), index)  5.03 us
    all_to_all x1, waiting for transfers between devices, on_device(): lax.all_to_all(chunks, 'depth', split_axis=0, concat_axis=0, tiled=True,...  3.1 us
    pallas_call x1, Pallas kernels, on_device(): pl.pallas_call(functools.partial(late_kernel, late_starts, width), name='...  1.57 us
    pallas_call x1, Pallas kernels, on_device(): pl.pallas_call(functools.partial(cure_kernel, cells, rim_starts), name='c...  1.45 us
    pallas_call x1, Pallas kernels, on_device(): pl.pallas_call(pack_kernel, name='pack', out_shape=(pltpu.VMEM((slots, de...  1.13 us
    pallas_call x1, Pallas kernels, on_device(): pl.pallas_call(functools.partial(early_kernel, early_starts), name='early...  1.01 us
    unnamed x13, local copies, waits for them, and re-layouts  0.69 us
  transfers between devices with their start and end apart: 3, of which 1 were waited for; matrix products, arithmetic and copies ran while one was open for 2% of the time, Pallas kernels for 5%

profile of v26, /device:TPU:0, one launch (start us, length us, event | category | flops | bytes accessed | tf_op | source)
XLA Modules:
  0.0 21.1 jit_solution(9616281365725060623)
XLA Ops:
  0.6 1.1 %pack.1 = (bf16[208,128]{1,0:T(8,128)(2,1)S(1)}, bf16[208,128]{1,0:T(8,128)(2,1)S(1)}, s32[8,96,128]{2,1,0:T(8,128)S(1)}, bf16[320,96]{1,0:T(8,128)(2,1)S(1)}, b...) custom-call(s32[8,96,128]{2,1,0:T(8,128)} %intensity.1, f32[6,128]{1,0:T(8,128)} %temp_hbm.1, ...), custom_call_target="tpu_custom_call" | custom-call | tf_op jit(solution)/shard_map/pack/pallas_call | solution.py:762
  1.8 0.7 %collective-permute-start = (bf16[208,128]{1,0:T(8,128)(2,1)S(1)}, bf16[208,128]{1,0:T(8,128)(2,1)S(1)}, u32[]{:S(2)}, u32[]{:S(2)}) collective-permute-start(bf16[208,128]{1,0:T(8,128)(2,1)S(1)} %get-tuple-element.14), channel_id=1, source_target_pairs={{4,8},{5,9},{6,10},{7,11},{12,16},{13,17},{14,18},{15,19},{20,24},... | collective-permute-start | bytes 159752 | tf_op jit(solution)/shard_map/ppermute | solution.py:783
  2.4 4.4 %collective-permute-start.1 = (bf16[208,128]{1,0:T(8,128)(2,1)S(1)}, bf16[208,128]{1,0:T(8,128)(2,1)S(1)}, u32[]{:S(2)}, u32[]{:S(2)}) collective-permute-start(bf16[208,128]{1,0:T(8,128)(2,1)S(1)} %get-tuple-element.15), channel_id=1, source_target_pairs={{0,4},{1,5},{2,6},{3,7},{8,12},{9,13},{10,14},{11,15},{16,20},{17,... | collective-permute-start | bytes 159752 | tf_op jit(solution)/shard_map/ppermute | solution.py:783
  6.8 1.0 %early.1 = (f32[4,32,128]{2,1,0:T(8,128)S(1)}, bf16[512,256]{1,0:T(8,128)(2,1)S(1)}, f32[96,1024]{1,0:T(8,128)S(1)}, f32[3,96,128]{2,1,0:T(8,128)S(1)}) custom-call(s32[8,96,128]{2,1,0:T(8,128)S(1)} %get-tuple-element.17.grey, bf16[320,96]{1,0:T(8,128)(2,1)S(1)} %get-tuple-element.18.x_parts, bf16[384,128]{1,0:T(8,128)(2,1)S(1)} %get-tuple-element.16.z_parts), custom_call_target="tpu_custom_call" | custom-call | flops 251658240 | bytes 4000000 | tf_op jit(solution)/shard_map/early/pallas_call | solution.py:809
  7.8 0.0 collective-permute-done.far
  7.8 0.0 collective-permute-done.1.near
  7.8 0.0 copy-done.3
  7.9 0.0 copy-start.2
  7.9 1.6 %late.1 = bf16[4,128,128]{2,1,0:T(8,128)(2,1)} custom-call(bf16[208,128]{1,0:T(8,128)(2,1)S(1)} %collective-permute-done.far, bf16[208,128]{1,0:T(8,128)(2,1)S(1)} %collective-permute-done.1.near, bf16[128,48]{1,0:T(8,128)(2,1)S(1)} %copy-done.3, bf16[384,128]{1,0:T(8,128)(2,1)S(1)} %get-tuple-element.16.z_parts, ...), custom_call_target="tpu_custom_call" | custom-call | flops 125829120 | bytes 4000000 | tf_op jit(solution)/shard_map/late/pallas_call | solution.py:826
  9.4 0.0 copy-start.4
  9.5 0.0 copy-start
  9.5 0.0 copy-start.1
  9.5 6.0 %all-to-all-start = ((bf16[4,128,128]{2,1,0:T(8,128)(2,1)}), bf16[4,128,128]{2,1,0:T(8,128)(2,1)S(1)}, u32[]{:S(2)}, u32[]{:S(2)}) async-start(bf16[4,128,128]{2,1,0:T(8,128)(2,1)} %late.1), calls=%async_computation | async-start | bytes 262144 | tf_op jit(solution)/shard_map/all_to_all | solution.py:843
  15.5 0.0 copy-done.4
  15.5 0.1 copy.18
  15.6 0.1 eq.15
  15.7 0.6 %copy-done.5 = f32[8]{0:T(128)S(1)} copy-done((f32[8]{0:T(128)S(1)}, f32[8]{0:T(128)}, u32[]{:S(2)}) %copy-start.5) | copy-done | bytes 56
  16.3 0.2 select_reduce_fusion
  16.4 0.1 copy.19.tools
  16.5 3.1 %all-to-all-done.chunks = bf16[4,128,128]{2,1,0:T(8,128)(2,1)S(1)} async-done(((bf16[4,128,128]{2,1,0:T(8,128)(2,1)}), bf16[4,128,128]{2,1,0:T(8,128)(2,1)S(1)}, u32[]{:S(2)}, u32[]{:S(2)}) %all-to-all-start) | async-done | bytes 131104 | tf_op jit(solution)/shard_map/all_to_all | solution.py:843
  19.6 0.0 copy-done.2
  19.6 0.0 copy-done
  19.6 0.0 copy-done.1
  19.6 1.5 %cure.1 = (f32[6,128]{1,0:T(8,128)}, f32[6,128]{1,0:T(8,128)}, f32[3,6,128]{2,1,0:T(8,128)}) custom-call(bf16[4,128,128]{2,1,0:T(8,128)(2,1)S(1)} %all-to-all-done.chunks, f32[6,128]{1,0:T(8,128)S(1)} %get-tuple-element.23.temp.temp_in, f32[6,128]{1,0:T(8,128)S(1)} %get-tuple-element.24.cure.cure_in, f32[6,1]{1,0:T(8,128)S(1)} %copy.19.tools, ...), custom_call_target="tpu_custom_call" | custom-call | tf_op jit(solution)/shard_map/cure/pallas_call | solution.py:852
  (2 shorter events, 0.0 us)
Async XLA Ops:
  1.8 6.1 %collective-permute-start = (bf16[208,128]{1,0:T(8,128)(2,1)S(1)}, bf16[208,128]{1,0:T(8,128)(2,1)S(1)}, u32[]{:S(2)}, u32[]{:S(2)}) collective-permute-start(bf16[208,128]{1,0:T(8,128)(2,1)S(1)} %get-tuple-element.14), channel_id=1, source_target_pairs={{4,8},{5,9},{6,10},{7,11},{12,16},{13,17},{14,18},{15,19},{20,24},... | collective-permute-start | bytes 159752 | tf_op jit(solution)/shard_map/ppermute | solution.py:783
  2.4 5.4 %collective-permute-start.1 = (bf16[208,128]{1,0:T(8,128)(2,1)S(1)}, bf16[208,128]{1,0:T(8,128)(2,1)S(1)}, u32[]{:S(2)}, u32[]{:S(2)}) collective-permute-start(bf16[208,128]{1,0:T(8,128)(2,1)S(1)} %get-tuple-element.15), channel_id=1, source_target_pairs={{0,4},{1,5},{2,6},{3,7},{8,12},{9,13},{10,14},{11,15},{16,20},{17,... | collective-permute-start | bytes 159752 | tf_op jit(solution)/shard_map/ppermute | solution.py:783
  6.8 1.0 %copy-start.3 = (bf16[128,48]{1,0:T(8,128)(2,1)S(1)}, bf16[128,48]{1,0:T(8,128)(2,1)}, u32[]{:S(2)}) copy-start(bf16[128,48]{1,0:T(8,128)(2,1)} %constant.17.clone.x_late) | copy-start | bytes 36868
  7.9 11.8 %copy-start.2 = (bf16[384,128]{1,0:T(8,128)(2,1)S(1)}, bf16[384,128]{1,0:T(8,128)(2,1)}, u32[]{:S(2)}) copy-start(bf16[384,128]{1,0:T(8,128)(2,1)} %constant.20.clone.rim_bands) | copy-start | bytes 294916
  9.4 6.1 %copy-start.4 = (s32[3,2]{0,1:T(2,128)S(1)}, s32[3,2]{0,1:T(2,128)}, u32[]{:S(2)}) copy-start(s32[3,2]{0,1:T(2,128)} %param.15) | copy-start | bytes 76
  9.5 10.2 %copy-start = (bf16[256,256]{1,0:T(8,128)(2,1)S(1)}, bf16[256,256]{1,0:T(8,128)(2,1)}, u32[]{:S(2)}) copy-start(bf16[256,256]{1,0:T(8,128)(2,1)} %constant.18.clone.flat) | copy-start | bytes 393220
  9.5 10.2 %copy-start.1 = (bf16[400,128]{1,0:T(8,128)(2,1)S(1)}, bf16[400,128]{1,0:T(8,128)(2,1)}, u32[]{:S(2)}) copy-start(bf16[400,128]{1,0:T(8,128)(2,1)} %constant.19.clone.steep) | copy-start | bytes 307204
  9.5 10.2 %all-to-all-start = ((bf16[4,128,128]{2,1,0:T(8,128)(2,1)}), bf16[4,128,128]{2,1,0:T(8,128)(2,1)S(1)}, u32[]{:S(2)}, u32[]{:S(2)}) async-start(bf16[4,128,128]{2,1,0:T(8,128)(2,1)} %late.1), calls=%async_computation | async-start | bytes 262144 | tf_op jit(solution)/shard_map/all_to_all | solution.py:843
  15.6 0.7 %copy-start.5 = (f32[8]{0:T(128)S(1)}, f32[8]{0:T(128)}, u32[]{:S(2)}) copy-start(f32[8]{0:T(128)} %param.14) | copy-start | bytes 100

commit v27 on v26

--- a/solution.py
+++ b/solution.py
@@ -67,23 +67,13 @@
     return result
 
 
-def rounded(taps):
-    best = None
-    for factor in np.linspace(1.0, 2.0, 20001)[:-1]:
-        near = (taps * factor).astype(np.float32).astype(ml_dtypes.bfloat16).astype(np.float64)
-        error = np.abs(near / factor - taps).sum()
-        if best is None or error < best[0]:
-            best = (error, near, factor)
-    return best[1], best[2]
-
-
 def as_bfloat16(matrix):
     return matrix.astype(np.float32).astype(ml_dtypes.bfloat16)
 
 
-def halves(matrix):
-    high = as_bfloat16(matrix)
-    return high, as_bfloat16(matrix - high.astype(np.float64))
+def halves(matrix, axis):
+    high = as_bfloat16(matrix).astype(np.float64)
+    return np.concatenate([high, as_bfloat16(matrix - high).astype(np.float64)], axis=axis)
 
 
 def sizes(width, depth):
@@ -99,14 +89,8 @@
     return places + [None] * (-len(places) % 16)
 
 
-GRAD_TAPS = tuple(
-    rounded(taps(R1, sigma_grad)) for taps in (smooth_taps, slope_taps)
-)
-GRAD_FACTOR = GRAD_TAPS[0][1] ** 2 * GRAD_TAPS[1][1]
-
-
 def grad_taps(kind):
-    return GRAD_TAPS[kind][0]
+    return slope_taps(R1, sigma_grad) if kind else smooth_taps(R1, sigma_grad)
 
 
 def tap(taps, offset):
@@ -184,7 +168,7 @@
     for column in range(count + 2 * HALO):
         for voxel in range(column * COARSE, (column + 1) * COARSE):
             coarse[column, voxel : voxel + 2 * R2 + 1] += taps
-    return bands.reshape(2 * products, -1), coarse
+    return halves(bands.reshape(2 * products, -1), 1), coarse
 
 
 def depth_bands(depth):
@@ -197,7 +181,7 @@
 
 
 def product_weights(rows):
-    return row_weights(rows, R2, sigma_tensor) / (255.0 * GRAD_FACTOR) ** 2
+    return row_weights(rows, R2, sigma_tensor) / 255.0**2
 
 
 def coarse_depth_bands(depth):
@@ -414,8 +398,11 @@
                 filtered[at : at + 16, lanes] = result.astype(jnp.bfloat16)
 
     at = 2 * pairs * count
-    grads[:at] = product(filtered[:at, :], diagonal[0:double, :])
-    grads[at:] = product(filtered[at:, :], diagonal[double : 2 * double, :])
+    for kind, part in enumerate((slice(0, at), slice(at, filtered.shape[0]))):
+        twice = jnp.concatenate([filtered[part, :], filtered[part, :]], axis=1)
+        grads[part, :] = product(
+            twice, diagonal[2 * kind * double : 2 * (kind + 1) * double, :]
+        )
 
     weights = product_weights(rows)
     layer = lax.axis_index("depth")
@@ -438,7 +425,7 @@
         for index in range(6):
             groups[index].append((totals[index] * inside).astype(jnp.bfloat16))
     products = [[jnp.concatenate(group, axis=0)] for group in groups]
-    return all_sums(products, z_parts[double : double + depth, :], sx)
+    return all_sums(products, z_parts[2 * double : 2 * double + depth, :], sx)
 
 
 def rim_tiles(values):
@@ -455,15 +442,16 @@
     rows, width, depth = grey.shape
     double = 2 * depth
     empty = jnp.zeros((depth, depth), jnp.bfloat16)
-    for kind in range(2):
+    for part in range(4):
         for half in range(2):
-            at = pl.ds(kind * double + half * depth, depth)
-            band = z_parts[kind * depth : (kind + 1) * depth, :]
+            at = pl.ds(part * double + half * depth, depth)
+            band = z_parts[part * depth : (part + 1) * depth, :]
             diagonal[at, half * depth : (half + 1) * depth] = band
             diagonal[at, (1 - half) * depth : (2 - half) * depth] = empty
     values = [grey[row].astype(jnp.float32) for row in range(rows)]
     whole = jnp.concatenate([value.astype(jnp.bfloat16) for value in values], axis=1)
-    result = product(x_parts[starts[0] : starts[2], :width], whole)
+    twice = jnp.concatenate([whole, whole], axis=0)
+    result = product(x_parts[starts[0] : starts[2], : 2 * width], twice)
     across[...] = result[: starts[1]]
     sides[...] = result[starts[1] :]
     sx = x_parts[starts[2] : starts[3], :EARLY]
@@ -496,7 +484,8 @@
 
     late = across.shape[0] // 2
     halos = jnp.concatenate([value.astype(jnp.bfloat16) for value in values], axis=1)
-    across[...] = sides[...] + product(x_late[starts[0] : starts[1], : 2 * EDGE], halos)
+    halos = jnp.concatenate([halos, halos], axis=0)
+    across[...] = sides[...] + product(x_late[starts[0] : starts[1], : 4 * EDGE], halos)
 
     products_x, voxels = own_columns(count)
     folded, stride = fold(voxels), COARSE * count
@@ -585,8 +574,9 @@
         second = [second[: voxels - folded], pltpu.roll(second, HALF, 1)]
         for tile in ([first], second):
             tiles.append(jnp.concatenate(tile + spare, axis=0).astype(jnp.bfloat16))
+    wide = jnp.concatenate(tiles, axis=1)
     result = product(
-        steep[starts[1] : starts[2], :tall], jnp.concatenate(tiles, axis=1)
+        steep[starts[1] : starts[2], : 2 * tall], jnp.concatenate([wide, wide], axis=0)
     ).astype(jnp.bfloat16)
     kinds = []
     for kind in range(2):
@@ -594,9 +584,10 @@
         stack = [
             values[:, 2 * part * LANES : 2 * (part + 1) * LANES] for part in range(parts - 1)
         ]
-        kinds.append(jnp.concatenate(stack, axis=0))
+        stack = jnp.concatenate(stack, axis=0)
+        kinds.append(jnp.concatenate([stack, stack], axis=1))
     both = product(kinds[0], flat[...])
-    three = (both[:, :LANES], product(kinds[1], steep[starts[0] : starts[1], :]), both[:, LANES:])
+    three = (both[:, :LANES], product(kinds[1], steep[starts[0] : starts[1], :LANES]), both[:, LANES:])
 
     index = lax.axis_index("plane") * lax.axis_size("depth") + lax.axis_index("depth")
     total = lax.axis_size("plane") * lax.axis_size("depth") * count * COARSE
@@ -750,14 +741,18 @@
     middle = bands[:, :EARLY, EDGE : EDGE + width]
     sides = bands[:, EARLY:].reshape(2 * late, -1)
     x_hbm, early_starts = stacked(
-        middle.reshape(2 * EARLY, -1), sides[:, EDGE : EDGE + width], coarse[:, :EARLY]
+        halves(middle.reshape(2 * EARLY, -1), 1),
+        halves(sides[:, EDGE : EDGE + width], 1),
+        coarse[:, :EARLY],
     )
-    z_hbm, _ = stacked(*depth_bands(depth), coarse_depth_bands(depth))
+    z_hbm, _ = stacked(
+        *[halves(bands, 0) for bands in depth_bands(depth)], coarse_depth_bands(depth)
+    )
     halos = np.concatenate([sides[:, :EDGE], sides[:, EDGE + width :]], axis=1)
-    x_late, late_starts = stacked(halos, coarse[:, EARLY:])
+    x_late, late_starts = stacked(halves(halos, 1), coarse[:, EARLY:])
     rims = rim_bands(rows)
-    flat, _ = stacked(np.concatenate([rims[0], rims[2]], axis=1))
-    steep, rim_starts = stacked(rims[1], *rim_x_bands(count))
+    flat, _ = stacked(halves(np.concatenate([rims[0], rims[2]], axis=1), 0))
+    steep, rim_starts = stacked(halves(rims[1], 0), *rim_x_bands(count))
     cell_bands, _ = stacked(rim_cells(rows, depth, depths))
     far, near, grey, x_parts, z_parts, temp, cure = pl.pallas_call(
         pack_kernel,
@@ -811,7 +806,7 @@
         name="early",
         out_shape=(
             pltpu.VMEM((len(USED), high, LANES), jnp.float32),
-            pltpu.VMEM((4 * depth, 2 * depth), bf16),
+            pltpu.VMEM((8 * depth, 2 * depth), bf16),
             pltpu.VMEM((2 * late, rows * depth), jnp.float32),
             pltpu.VMEM((3, width, LANES), jnp.float32),
         ),

time: 21.4 us -> 21.7 us (1.014)
  Pallas kernels: 5.16 us -> 5.7 us
  waiting for transfers between devices: 3.11 us -> 2.85 us
    pallas_call x1, Pallas kernels: 1.01 us -> 1.29 us  [on_device(): pl.pallas_call(functools.partial(early_kernel, early_starts), name='early...]
    all_to_all x1, waiting for transfers between devices: 3.1 us -> 2.85 us  [on_device(): lax.all_to_all(chunks, 'depth', split_axis=0, concat_axis=0, tiled=True,...]
  transfers between devices with their start and end apart: 3 -> 3, of which waited for: 1 -> 1; matrix products, arithmetic and copies ran while one was open for 2% -> 2% of each run, Pallas kernels for 5% -> 6%
where the time goes in v27:
time: 21.7 us; the launch traced here: 21.4 us
  starting transfers between devices  11.1 us (51%)
  Pallas kernels  5.7 us (26%)
  waiting for transfers between devices  2.85 us (13%)
  local copies, waits for them, and re-layouts  0.87 us (4%)
  between operations  0.73 us (3%)
    all_to_all x1, starting transfers between devices, on_device(): lax.all_to_all(chunks, 'depth', split_axis=0, concat_axis=0, tiled=True,...  6.03 us
    ppermute x2, starting transfers between devices, moved(): return lax.ppermute(values, ('plane', 'depth'), index)  5.03 us
    all_to_all x1, waiting for transfers between devices, on_device(): lax.all_to_all(chunks, 'depth', split_axis=0, concat_axis=0, tiled=True,...  2.85 us
    pallas_call x1, Pallas kernels, on_device(): pl.pallas_call(functools.partial(late_kernel, late_starts, width), name='...  1.69 us
    pallas_call x1, Pallas kernels, on_device(): pl.pallas_call(functools.partial(cure_kernel, cells, rim_starts), name='c...  1.52 us
    pallas_call x1, Pallas kernels, on_device(): pl.pallas_call(functools.partial(early_kernel, early_starts), name='early...  1.29 us
    pallas_call x1, Pallas kernels, on_device(): pl.pallas_call(pack_kernel, name='pack', out_shape=(pltpu.VMEM((slots, de...  1.19 us
    unnamed x13, local copies, waits for them, and re-layouts  0.69 us
  transfers between devices with their start and end apart: 3, of which 1 were waited for; matrix products, arithmetic and copies ran while one was open for 2% of the time, Pallas kernels for 6%

profile of v27, /device:TPU:0, one launch (start us, length us, event | category | flops | bytes accessed | tf_op | source)
XLA Modules:
  0.0 21.4 jit_solution(14545570654098794166)
XLA Ops:
  0.6 1.2 %pack.1 = (bf16[208,128]{1,0:T(8,128)(2,1)S(1)}, bf16[208,128]{1,0:T(8,128)(2,1)S(1)}, s32[8,96,128]{2,1,0:T(8,128)S(1)}, bf16[320,192]{1,0:T(8,128)(2,1)S(1)}, ...) custom-call(s32[8,96,128]{2,1,0:T(8,128)} %intensity.1, f32[6,128]{1,0:T(8,128)} %temp_hbm.1, ...), custom_call_target="tpu_custom_call" | custom-call | tf_op jit(solution)/shard_map/pack/pallas_call | solution.py:757
  1.8 0.7 %collective-permute-start = (bf16[208,128]{1,0:T(8,128)(2,1)S(1)}, bf16[208,128]{1,0:T(8,128)(2,1)S(1)}, u32[]{:S(2)}, u32[]{:S(2)}) collective-permute-start(bf16[208,128]{1,0:T(8,128)(2,1)S(1)} %get-tuple-element.14), channel_id=1, source_target_pairs={{4,8},{5,9},{6,10},{7,11},{12,16},{13,17},{14,18},{15,19},{20,24},... | collective-permute-start | bytes 159752 | tf_op jit(solution)/shard_map/ppermute | solution.py:778
  2.5 4.4 %collective-permute-start.1 = (bf16[208,128]{1,0:T(8,128)(2,1)S(1)}, bf16[208,128]{1,0:T(8,128)(2,1)S(1)}, u32[]{:S(2)}, u32[]{:S(2)}) collective-permute-start(bf16[208,128]{1,0:T(8,128)(2,1)S(1)} %get-tuple-element.15), channel_id=1, source_target_pairs={{0,4},{1,5},{2,6},{3,7},{8,12},{9,13},{10,14},{11,15},{16,20},{17,... | collective-permute-start | bytes 159752 | tf_op jit(solution)/shard_map/ppermute | solution.py:778
  6.9 1.3 %early.1 = (f32[4,32,128]{2,1,0:T(8,128)S(1)}, bf16[1024,256]{1,0:T(8,128)(2,1)S(1)}, f32[96,1024]{1,0:T(8,128)S(1)}, f32[3,96,128]{2,1,0:T(8,128)S(1)}) custom-call(s32[8,96,128]{2,1,0:T(8,128)S(1)} %get-tuple-element.17.grey, bf16[320,192]{1,0:T(8,128)(2,1)S(1)} %get-tuple-element.18.x_parts, bf16[640,128]{1,0:T(8,128)(2,1)S(1)} %get-tuple-element.16.z_parts), custom_call_target="tpu_custom_call" | custom-call | flops 251658240 | bytes 4000000 | tf_op jit(solution)/shard_map/early/pallas_call | solution.py:804
  8.2 0.0 collective-permute-done.far
  8.2 0.0 collective-permute-done.1.near
  8.2 0.0 copy-done.3
  8.2 0.0 copy-start.4
  8.2 0.0 copy-start
  8.2 0.0 copy-start.2
  8.2 1.7 %late.1 = bf16[4,128,128]{2,1,0:T(8,128)(2,1)} custom-call(bf16[208,128]{1,0:T(8,128)(2,1)S(1)} %collective-permute-done.far, bf16[208,128]{1,0:T(8,128)(2,1)S(1)} %collective-permute-done.1.near, bf16[128,96]{1,0:T(8,128)(2,1)S(1)} %copy-done.3, bf16[640,128]{1,0:T(8,128)(2,1)S(1)} %get-tuple-element.16.z_parts, ...), custom_call_target="tpu_custom_call" | custom-call | flops 125829120 | bytes 4000000 | tf_op jit(solution)/shard_map/late/pallas_call | solution.py:821
  9.9 0.0 copy-start.1
  9.9 6.0 %all-to-all-start = ((bf16[4,128,128]{2,1,0:T(8,128)(2,1)}), bf16[4,128,128]{2,1,0:T(8,128)(2,1)S(1)}, u32[]{:S(2)}, u32[]{:S(2)}) async-start(bf16[4,128,128]{2,1,0:T(8,128)(2,1)} %late.1), calls=%async_computation | async-start | bytes 262144 | tf_op jit(solution)/shard_map/all_to_all | solution.py:838
  16.0 0.0 copy-done.4
  16.0 0.1 copy.18
  16.1 0.1 eq.15
  16.1 0.6 %copy-done.5 = f32[8]{0:T(128)S(1)} copy-done((f32[8]{0:T(128)S(1)}, f32[8]{0:T(128)}, u32[]{:S(2)}) %copy-start.5) | copy-done | bytes 56
  16.7 0.2 select_reduce_fusion
  16.9 0.1 copy.19.tools
  17.0 2.8 %all-to-all-done.chunks = bf16[4,128,128]{2,1,0:T(8,128)(2,1)S(1)} async-done(((bf16[4,128,128]{2,1,0:T(8,128)(2,1)}), bf16[4,128,128]{2,1,0:T(8,128)(2,1)S(1)}, u32[]{:S(2)}, u32[]{:S(2)}) %all-to-all-start) | async-done | bytes 131104 | tf_op jit(solution)/shard_map/all_to_all | solution.py:838
  19.8 0.0 copy-done
  19.9 0.0 copy-done.2
  19.9 0.0 copy-done.1
  19.9 1.5 %cure.1 = (f32[6,128]{1,0:T(8,128)}, f32[6,128]{1,0:T(8,128)}, f32[3,6,128]{2,1,0:T(8,128)}) custom-call(bf16[4,128,128]{2,1,0:T(8,128)(2,1)S(1)} %all-to-all-done.chunks, f32[6,128]{1,0:T(8,128)S(1)} %get-tuple-element.23.temp.temp_in, f32[6,128]{1,0:T(8,128)S(1)} %get-tuple-element.24.cure.cure_in, f32[6,1]{1,0:T(8,128)S(1)} %copy.19.tools, ...), custom_call_target="tpu_custom_call" | custom-call | tf_op jit(solution)/shard_map/cure/pallas_call | solution.py:847
  (2 shorter events, 0.0 us)
Async XLA Ops:
  1.8 6.3 %collective-permute-start = (bf16[208,128]{1,0:T(8,128)(2,1)S(1)}, bf16[208,128]{1,0:T(8,128)(2,1)S(1)}, u32[]{:S(2)}, u32[]{:S(2)}) collective-permute-start(bf16[208,128]{1,0:T(8,128)(2,1)S(1)} %get-tuple-element.14), channel_id=1, source_target_pairs={{4,8},{5,9},{6,10},{7,11},{12,16},{13,17},{14,18},{15,19},{20,24},... | collective-permute-start | bytes 159752 | tf_op jit(solution)/shard_map/ppermute | solution.py:778
  2.5 5.7 %collective-permute-start.1 = (bf16[208,128]{1,0:T(8,128)(2,1)S(1)}, bf16[208,128]{1,0:T(8,128)(2,1)S(1)}, u32[]{:S(2)}, u32[]{:S(2)}) collective-permute-start(bf16[208,128]{1,0:T(8,128)(2,1)S(1)} %get-tuple-element.15), channel_id=1, source_target_pairs={{0,4},{1,5},{2,6},{3,7},{8,12},{9,13},{10,14},{11,15},{16,20},{17,... | collective-permute-start | bytes 159752 | tf_op jit(solution)/shard_map/ppermute | solution.py:778
  6.9 1.3 %copy-start.3 = (bf16[128,96]{1,0:T(8,128)(2,1)S(1)}, bf16[128,96]{1,0:T(8,128)(2,1)}, u32[]{:S(2)}) copy-start(bf16[128,96]{1,0:T(8,128)(2,1)} %constant.17.clone.x_late) | copy-start | bytes 73732
  8.2 7.8 %copy-start.4 = (s32[3,2]{0,1:T(2,128)S(1)}, s32[3,2]{0,1:T(2,128)}, u32[]{:S(2)}) copy-start(s32[3,2]{0,1:T(2,128)} %param.15) | copy-start | bytes 76
  8.2 11.6 %copy-start = (bf16[656,160]{1,0:T(8,128)(2,1)S(1)}, bf16[656,160]{1,0:T(8,128)(2,1)}, u32[]{:S(2)}) copy-start(bf16[656,160]{1,0:T(8,128)(2,1)} %constant.19.clone.steep) | copy-start | bytes 629764
  8.2 11.6 %copy-start.2 = (bf16[384,128]{1,0:T(8,128)(2,1)S(1)}, bf16[384,128]{1,0:T(8,128)(2,1)}, u32[]{:S(2)}) copy-start(bf16[384,128]{1,0:T(8,128)(2,1)} %constant.20.clone.rim_bands) | copy-start | bytes 294916
  9.9 9.9 %copy-start.1 = (bf16[512,256]{1,0:T(8,128)(2,1)S(1)}, bf16[512,256]{1,0:T(8,128)(2,1)}, u32[]{:S(2)}) copy-start(bf16[512,256]{1,0:T(8,128)(2,1)} %constant.18.clone.flat) | copy-start | bytes 786436
  9.9 9.9 %all-to-all-start = ((bf16[4,128,128]{2,1,0:T(8,128)(2,1)}), bf16[4,128,128]{2,1,0:T(8,128)(2,1)S(1)}, u32[]{:S(2)}, u32[]{:S(2)}) async-start(bf16[4,128,128]{2,1,0:T(8,128)(2,1)} %late.1), calls=%async_computation | async-start | bytes 262144 | tf_op jit(solution)/shard_map/all_to_all | solution.py:838
  16.1 0.7 %copy-start.5 = (f32[8]{0:T(128)S(1)}, f32[8]{0:T(128)}, u32[]{:S(2)}) copy-start(f32[8]{0:T(128)} %param.14) | copy-start | bytes 100

commit v28 on v27

--- a/solution.py
+++ b/solution.py
@@ -395,13 +395,19 @@
             for row, result in enumerate(results):
                 at = (part * pairs + row // 2) * count + start
                 lanes = slice((row % 2) * depth, (row % 2 + 1) * depth)
-                filtered[at : at + 16, lanes] = result.astype(jnp.bfloat16)
+                high = result.astype(jnp.bfloat16)
+                filtered[0, at : at + 16, lanes] = high
+                low = result - high.astype(jnp.float32)
+                filtered[1, at : at + 16, lanes] = low.astype(jnp.bfloat16)
 
     at = 2 * pairs * count
-    for kind, part in enumerate((slice(0, at), slice(at, filtered.shape[0]))):
-        twice = jnp.concatenate([filtered[part, :], filtered[part, :]], axis=1)
+    for kind, part in enumerate((slice(0, at), slice(at, filtered.shape[1]))):
+        high, low = filtered[0, part, :], filtered[1, part, :]
+        high_bands = diagonal[2 * kind * double : (2 * kind + 1) * double, :]
+        low_bands = diagonal[(2 * kind + 1) * double : 2 * (kind + 1) * double, :]
         grads[part, :] = product(
-            twice, diagonal[2 * kind * double : 2 * (kind + 1) * double, :]
+            jnp.concatenate([high, low, high], axis=1),
+            jnp.concatenate([high_bands, high_bands, low_bands], axis=0),
         )
 
     weights = product_weights(rows)
@@ -790,7 +796,7 @@
     def scratch(count):
         return [
             pltpu.VMEM((2 * count, rows * depth), jnp.float32),
-            pltpu.VMEM((3 * rows // 2 * count, 2 * depth), bf16),
+            pltpu.VMEM((2, 3 * rows // 2 * count, 2 * depth), bf16),
             pltpu.VMEM((3 * rows // 2 * count, 2 * depth), jnp.float32),
         ]
 

time: 21.7 us -> 22 us (1.014)
  Pallas kernels: 5.7 us -> 6.12 us
    pallas_call x1, Pallas kernels: 1.29 us -> 1.52 us  [on_device(): pl.pallas_call(functools.partial(early_kernel, early_starts), name='early...]
  transfers between devices with their start and end apart: 3 -> 3, of which waited for: 1 -> 1; matrix products, arithmetic and copies ran while one was open for 2% -> 2% of each run, Pallas kernels for 6% -> 7%
where the time goes in v28:
time: 22 us; the launch traced here: 21.7 us
  starting transfers between devices  11 us (50%)
  Pallas kernels  6.12 us (28%)
  waiting for transfers between devices  2.79 us (13%)
  local copies, waits for them, and re-layouts  0.87 us (4%)
  between operations  0.73 us (3%)
    all_to_all x1, starting transfers between devices, on_device(): lax.all_to_all(chunks, 'depth', split_axis=0, concat_axis=0, tiled=True,...  6.02 us
    ppermute x2, starting transfers between devices, moved(): return lax.ppermute(values, ('plane', 'depth'), index)  5.03 us
    all_to_all x1, waiting for transfers between devices, on_device(): lax.all_to_all(chunks, 'depth', split_axis=0, concat_axis=0, tiled=True,...  2.79 us
    pallas_call x1, Pallas kernels, on_device(): pl.pallas_call(functools.partial(late_kernel, late_starts, width), name='...  1.88 us
    pallas_call x1, Pallas kernels, on_device(): pl.pallas_call(functools.partial(cure_kernel, cells, rim_starts), name='c...  1.53 us
    pallas_call x1, Pallas kernels, on_device(): pl.pallas_call(functools.partial(early_kernel, early_starts), name='early...  1.52 us
    pallas_call x1, Pallas kernels, on_device(): pl.pallas_call(pack_kernel, name='pack', out_shape=(pltpu.VMEM((slots, de...  1.19 us
    unnamed x13, local copies, waits for them, and re-layouts  0.69 us
  transfers between devices with their start and end apart: 3, of which 1 were waited for; matrix products, arithmetic and copies ran while one was open for 2% of the time, Pallas kernels for 7%

profile of v28, /device:TPU:0, one launch (start us, length us, event | category | flops | bytes accessed | tf_op | source)
XLA Modules:
  0.0 21.7 jit_solution(11839573223171400560)
XLA Ops:
  0.6 1.2 %pack.1 = (bf16[208,128]{1,0:T(8,128)(2,1)S(1)}, bf16[208,128]{1,0:T(8,128)(2,1)S(1)}, s32[8,96,128]{2,1,0:T(8,128)S(1)}, bf16[320,192]{1,0:T(8,128)(2,1)S(1)}, ...) custom-call(s32[8,96,128]{2,1,0:T(8,128)} %intensity.1, f32[6,128]{1,0:T(8,128)} %temp_hbm.1, ...), custom_call_target="tpu_custom_call" | custom-call | tf_op jit(solution)/shard_map/pack/pallas_call | solution.py:763
  1.8 0.7 %collective-permute-start = (bf16[208,128]{1,0:T(8,128)(2,1)S(1)}, bf16[208,128]{1,0:T(8,128)(2,1)S(1)}, u32[]{:S(2)}, u32[]{:S(2)}) collective-permute-start(bf16[208,128]{1,0:T(8,128)(2,1)S(1)} %get-tuple-element.14), channel_id=1, source_target_pairs={{4,8},{5,9},{6,10},{7,11},{12,16},{13,17},{14,18},{15,19},{20,24},... | collective-permute-start | bytes 159752 | tf_op jit(solution)/shard_map/ppermute | solution.py:784
  2.5 4.4 %collective-permute-start.1 = (bf16[208,128]{1,0:T(8,128)(2,1)S(1)}, bf16[208,128]{1,0:T(8,128)(2,1)S(1)}, u32[]{:S(2)}, u32[]{:S(2)}) collective-permute-start(bf16[208,128]{1,0:T(8,128)(2,1)S(1)} %get-tuple-element.15), channel_id=1, source_target_pairs={{0,4},{1,5},{2,6},{3,7},{8,12},{9,13},{10,14},{11,15},{16,20},{17,... | collective-permute-start | bytes 159752 | tf_op jit(solution)/shard_map/ppermute | solution.py:784
  6.9 1.5 %early.1 = (f32[4,32,128]{2,1,0:T(8,128)S(1)}, bf16[1024,256]{1,0:T(8,128)(2,1)S(1)}, f32[96,1024]{1,0:T(8,128)S(1)}, f32[3,96,128]{2,1,0:T(8,128)S(1)}) custom-call(s32[8,96,128]{2,1,0:T(8,128)S(1)} %get-tuple-element.17.grey, bf16[320,192]{1,0:T(8,128)(2,1)S(1)} %get-tuple-element.18.x_parts, bf16[640,128]{1,0:T(8,128)(2,1)S(1)} %get-tuple-element.16.z_parts), custom_call_target="tpu_custom_call" | custom-call | flops 251658240 | bytes 4000000 | tf_op jit(solution)/shard_map/early/pallas_call | solution.py:810
  8.4 0.0 collective-permute-done.far
  8.4 0.0 collective-permute-done.1.near
  8.4 0.0 copy-done.3
  8.4 0.0 copy-start.4
  8.4 0.0 copy-start
  8.5 0.0 copy-start.2
  8.5 1.9 %late.1 = bf16[4,128,128]{2,1,0:T(8,128)(2,1)} custom-call(bf16[208,128]{1,0:T(8,128)(2,1)S(1)} %collective-permute-done.far, bf16[208,128]{1,0:T(8,128)(2,1)S(1)} %collective-permute-done.1.near, bf16[128,96]{1,0:T(8,128)(2,1)S(1)} %copy-done.3, bf16[640,128]{1,0:T(8,128)(2,1)S(1)} %get-tuple-element.16.z_parts, ...), custom_call_target="tpu_custom_call" | custom-call | flops 125829120 | bytes 4000000 | tf_op jit(solution)/shard_map/late/pallas_call | solution.py:827
  10.4 0.0 copy-start.1
  10.4 6.0 %all-to-all-start = ((bf16[4,128,128]{2,1,0:T(8,128)(2,1)}), bf16[4,128,128]{2,1,0:T(8,128)(2,1)S(1)}, u32[]{:S(2)}, u32[]{:S(2)}) async-start(bf16[4,128,128]{2,1,0:T(8,128)(2,1)} %late.1), calls=%async_computation | async-start | bytes 262144 | tf_op jit(solution)/shard_map/all_to_all | solution.py:844
  16.4 0.0 copy-done.4
  16.4 0.1 copy.18
  16.5 0.1 eq.15
  16.6 0.6 %copy-done.5 = f32[8]{0:T(128)S(1)} copy-done((f32[8]{0:T(128)S(1)}, f32[8]{0:T(128)}, u32[]{:S(2)}) %copy-start.5) | copy-done | bytes 56
  17.1 0.2 select_reduce_fusion
  17.3 0.1 copy.19.tools
  17.4 2.8 %all-to-all-done.chunks = bf16[4,128,128]{2,1,0:T(8,128)(2,1)S(1)} async-done(((bf16[4,128,128]{2,1,0:T(8,128)(2,1)}), bf16[4,128,128]{2,1,0:T(8,128)(2,1)S(1)}, u32[]{:S(2)}, u32[]{:S(2)}) %all-to-all-start) | async-done | bytes 131104 | tf_op jit(solution)/shard_map/all_to_all | solution.py:844
  20.2 0.0 copy-done
  20.2 0.0 copy-done.2
  20.2 0.0 copy-done.1
  20.2 1.5 %cure.1 = (f32[6,128]{1,0:T(8,128)}, f32[6,128]{1,0:T(8,128)}, f32[3,6,128]{2,1,0:T(8,128)}) custom-call(bf16[4,128,128]{2,1,0:T(8,128)(2,1)S(1)} %all-to-all-done.chunks, f32[6,128]{1,0:T(8,128)S(1)} %get-tuple-element.23.temp.temp_in, f32[6,128]{1,0:T(8,128)S(1)} %get-tuple-element.24.cure.cure_in, f32[6,1]{1,0:T(8,128)S(1)} %copy.19.tools, ...), custom_call_target="tpu_custom_call" | custom-call | tf_op jit(solution)/shard_map/cure/pallas_call | solution.py:853
  (2 shorter events, 0.0 us)
Async XLA Ops:
  1.8 6.6 %collective-permute-start = (bf16[208,128]{1,0:T(8,128)(2,1)S(1)}, bf16[208,128]{1,0:T(8,128)(2,1)S(1)}, u32[]{:S(2)}, u32[]{:S(2)}) collective-permute-start(bf16[208,128]{1,0:T(8,128)(2,1)S(1)} %get-tuple-element.14), channel_id=1, source_target_pairs={{4,8},{5,9},{6,10},{7,11},{12,16},{13,17},{14,18},{15,19},{20,24},... | collective-permute-start | bytes 159752 | tf_op jit(solution)/shard_map/ppermute | solution.py:784
  2.5 5.9 %collective-permute-start.1 = (bf16[208,128]{1,0:T(8,128)(2,1)S(1)}, bf16[208,128]{1,0:T(8,128)(2,1)S(1)}, u32[]{:S(2)}, u32[]{:S(2)}) collective-permute-start(bf16[208,128]{1,0:T(8,128)(2,1)S(1)} %get-tuple-element.15), channel_id=1, source_target_pairs={{0,4},{1,5},{2,6},{3,7},{8,12},{9,13},{10,14},{11,15},{16,20},{17,... | collective-permute-start | bytes 159752 | tf_op jit(solution)/shard_map/ppermute | solution.py:784
  6.9 1.6 %copy-start.3 = (bf16[128,96]{1,0:T(8,128)(2,1)S(1)}, bf16[128,96]{1,0:T(8,128)(2,1)}, u32[]{:S(2)}) copy-start(bf16[128,96]{1,0:T(8,128)(2,1)} %constant.17.clone.x_late) | copy-start | bytes 73732
  8.4 8.0 %copy-start.4 = (s32[3,2]{0,1:T(2,128)S(1)}, s32[3,2]{0,1:T(2,128)}, u32[]{:S(2)}) copy-start(s32[3,2]{0,1:T(2,128)} %param.15) | copy-start | bytes 76
  8.4 11.8 %copy-start = (bf16[656,160]{1,0:T(8,128)(2,1)S(1)}, bf16[656,160]{1,0:T(8,128)(2,1)}, u32[]{:S(2)}) copy-start(bf16[656,160]{1,0:T(8,128)(2,1)} %constant.19.clone.steep) | copy-start | bytes 629764
  8.5 11.8 %copy-start.2 = (bf16[384,128]{1,0:T(8,128)(2,1)S(1)}, bf16[384,128]{1,0:T(8,128)(2,1)}, u32[]{:S(2)}) copy-start(bf16[384,128]{1,0:T(8,128)(2,1)} %constant.20.clone.rim_bands) | copy-start | bytes 294916
  10.4 9.9 %copy-start.1 = (bf16[512,256]{1,0:T(8,128)(2,1)S(1)}, bf16[512,256]{1,0:T(8,128)(2,1)}, u32[]{:S(2)}) copy-start(bf16[512,256]{1,0:T(8,128)(2,1)} %constant.18.clone.flat) | copy-start | bytes 786436
  10.4 9.8 %all-to-all-start = ((bf16[4,128,128]{2,1,0:T(8,128)(2,1)}), bf16[4,128,128]{2,1,0:T(8,128)(2,1)S(1)}, u32[]{:S(2)}, u32[]{:S(2)}) async-start(bf16[4,128,128]{2,1,0:T(8,128)(2,1)} %late.1), calls=%async_computation | async-start | bytes 262144 | tf_op jit(solution)/shard_map/all_to_all | solution.py:844
  16.5 0.7 %copy-start.5 = (f32[8]{0:T(128)S(1)}, f32[8]{0:T(128)}, u32[]{:S(2)}) copy-start(f32[8]{0:T(128)} %param.14) | copy-start | bytes 100

commit v29 on v28

--- a/solution.py
+++ b/solution.py
@@ -91,6 +91,19 @@
 
 def grad_taps(kind):
     return slope_taps(R1, sigma_grad) if kind else smooth_taps(R1, sigma_grad)
+
+
+def rounded(taps):
+    best = None
+    for factor in np.linspace(1.0, 2.0, 20001)[:-1]:
+        near = as_bfloat16(taps * factor).astype(np.float64)
+        error = np.abs(near / factor - taps).sum()
+        if best is None or error < best[0]:
+            best = (error, near, factor)
+    return best[1], best[2]
+
+
+DEPTH_TAPS = tuple(rounded(grad_taps(kind)) for kind in range(2))
 
 
 def tap(taps, offset):
@@ -176,7 +189,7 @@
     for kind in range(2):
         for place in range(depth):
             for near in range(max(place - R1, 0), min(place + R1 + 1, depth)):
-                bands[kind, near, place] = tap(grad_taps(kind), near - place)
+                bands[kind, near, place] = tap(DEPTH_TAPS[kind][0], near - place)
     return bands
 
 
@@ -326,7 +339,7 @@
     return jnp.dot(first, second, preferred_element_type=jnp.float32)
 
 
-def mirrored_filter(kind, values, even):
+def mirrored_filter(kind, values, even, factor):
     rows = len(values)
     use_sum = even == (kind == 0)
     sign = 1.0 if use_sum else -1.0
@@ -337,7 +350,7 @@
         for source, value in enumerate(half):
             near = tap(grad_taps(kind), source - row)
             far = tap(grad_taps(kind), rows - 1 - source - row)
-            weight = 0.5 * (near + sign * far)
+            weight = 0.5 * (near + sign * far) / factor
             total = weight * value if total is None else total + weight * value
         results.append(total)
     return results
@@ -390,8 +403,9 @@
         ]
         for part in range(3):
             values = kinds[X_KINDS[part]]
-            results = mirrored_filter(ROW_KINDS[part], values, True)
-            results += mirrored_filter(ROW_KINDS[part], values, False)
+            factor = float(DEPTH_TAPS[DEPTH_KINDS[part]][1])
+            results = mirrored_filter(ROW_KINDS[part], values, True, factor)
+            results += mirrored_filter(ROW_KINDS[part], values, False, factor)
             for row, result in enumerate(results):
                 at = (part * pairs + row // 2) * count + start
                 lanes = slice((row % 2) * depth, (row % 2 + 1) * depth)
@@ -403,11 +417,9 @@
     at = 2 * pairs * count
     for kind, part in enumerate((slice(0, at), slice(at, filtered.shape[1]))):
         high, low = filtered[0, part, :], filtered[1, part, :]
-        high_bands = diagonal[2 * kind * double : (2 * kind + 1) * double, :]
-        low_bands = diagonal[(2 * kind + 1) * double : 2 * (kind + 1) * double, :]
+        band = diagonal[kind * double : (kind + 1) * double, :]
         grads[part, :] = product(
-            jnp.concatenate([high, low, high], axis=1),
-            jnp.concatenate([high_bands, high_bands, low_bands], axis=0),
+            jnp.concatenate([high, low], axis=1), jnp.concatenate([band, band], axis=0)
         )
 
     weights = product_weights(rows)
@@ -431,7 +443,7 @@
         for index in range(6):
             groups[index].append((totals[index] * inside).astype(jnp.bfloat16))
     products = [[jnp.concatenate(group, axis=0)] for group in groups]
-    return all_sums(products, z_parts[2 * double : 2 * double + depth, :], sx)
+    return all_sums(products, z_parts[double : double + depth, :], sx)
 
 
 def rim_tiles(values):
@@ -448,7 +460,7 @@
     rows, width, depth = grey.shape
     double = 2 * depth
     empty = jnp.zeros((depth, depth), jnp.bfloat16)
-    for part in range(4):
+    for part in range(2):
         for half in range(2):
             at = pl.ds(part * double + half * depth, depth)
             band = z_parts[part * depth : (part + 1) * depth, :]
@@ -752,7 +764,7 @@
         coarse[:, :EARLY],
     )
     z_hbm, _ = stacked(
-        *[halves(bands, 0) for bands in depth_bands(depth)], coarse_depth_bands(depth)
+        *depth_bands(depth), coarse_depth_bands(depth)
     )
     halos = np.concatenate([sides[:, :EDGE], sides[:, EDGE + width :]], axis=1)
     x_late, late_starts = stacked(halves(halos, 1), coarse[:, EARLY:])
@@ -812,7 +824,7 @@
         name="early",
         out_shape=(
             pltpu.VMEM((len(USED), high, LANES), jnp.float32),
-            pltpu.VMEM((8 * depth, 2 * depth), bf16),
+            pltpu.VMEM((4 * depth, 2 * depth), bf16),
             pltpu.VMEM((2 * late, rows * depth), jnp.float32),
             pltpu.VMEM((3, width, LANES), jnp.float32),
         ),

time: 22 us -> 21.9 us (level)
  no operation moved by 1% of the time
where the time goes in v29:
time: 21.9 us; the launch traced here: 21.7 us
  starting transfers between devices  11 us (50%)
  Pallas kernels  6.01 us (27%)
  waiting for transfers between devices  2.81 us (13%)
  local copies, waits for them, and re-layouts  0.87 us (4%)
  between operations  0.73 us (3%)
    all_to_all x1, starting transfers between devices, on_device(): lax.all_to_all(chunks, 'depth', split_axis=0, concat_axis=0, tiled=True,...  6.02 us
    ppermute x2, starting transfers between devices, moved(): return lax.ppermute(values, ('plane', 'depth'), index)  5.03 us
    all_to_all x1, waiting for transfers between devices, on_device(): lax.all_to_all(chunks, 'depth', split_axis=0, concat_axis=0, tiled=True,...  2.81 us
    pallas_call x1, Pallas kernels, on_device(): pl.pallas_call(functools.partial(late_kernel, late_starts, width), name='...  1.82 us
    pallas_call x1, Pallas kernels, on_device(): pl.pallas_call(functools.partial(cure_kernel, cells, rim_starts), name='c...  1.53 us
    pallas_call x1, Pallas kernels, on_device(): pl.pallas_call(functools.partial(early_kernel, early_starts), name='early...  1.5 us
    pallas_call x1, Pallas kernels, on_device(): pl.pallas_call(pack_kernel, name='pack', out_shape=(pltpu.VMEM((slots, de...  1.17 us
    unnamed x13, local copies, waits for them, and re-layouts  0.69 us
  transfers between devices with their start and end apart: 3, of which 1 were waited for; matrix products, arithmetic and copies ran while one was open for 2% of the time, Pallas kernels for 7%

profile of v29, /device:TPU:0, one launch (start us, length us, event | category | flops | bytes accessed | tf_op | source)
XLA Modules:
  0.0 21.7 jit_solution(11806401369743967990)
XLA Ops:
  0.6 1.2 %pack.1 = (bf16[208,128]{1,0:T(8,128)(2,1)S(1)}, bf16[208,128]{1,0:T(8,128)(2,1)S(1)}, s32[8,96,128]{2,1,0:T(8,128)S(1)}, bf16[320,192]{1,0:T(8,128)(2,1)S(1)}, ...) custom-call(s32[8,96,128]{2,1,0:T(8,128)} %intensity.1, f32[6,128]{1,0:T(8,128)} %temp_hbm.1, ...), custom_call_target="tpu_custom_call" | custom-call | tf_op jit(solution)/shard_map/pack/pallas_call | solution.py:775
  1.8 0.7 %collective-permute-start = (bf16[208,128]{1,0:T(8,128)(2,1)S(1)}, bf16[208,128]{1,0:T(8,128)(2,1)S(1)}, u32[]{:S(2)}, u32[]{:S(2)}) collective-permute-start(bf16[208,128]{1,0:T(8,128)(2,1)S(1)} %get-tuple-element.14), channel_id=1, source_target_pairs={{4,8},{5,9},{6,10},{7,11},{12,16},{13,17},{14,18},{15,19},{20,24},... | collective-permute-start | bytes 159752 | tf_op jit(solution)/shard_map/ppermute | solution.py:796
  2.5 4.4 %collective-permute-start.1 = (bf16[208,128]{1,0:T(8,128)(2,1)S(1)}, bf16[208,128]{1,0:T(8,128)(2,1)S(1)}, u32[]{:S(2)}, u32[]{:S(2)}) collective-permute-start(bf16[208,128]{1,0:T(8,128)(2,1)S(1)} %get-tuple-element.15), channel_id=1, source_target_pairs={{0,4},{1,5},{2,6},{3,7},{8,12},{9,13},{10,14},{11,15},{16,20},{17,... | collective-permute-start | bytes 159752 | tf_op jit(solution)/shard_map/ppermute | solution.py:796
  6.8 1.5 %early.1 = (f32[4,32,128]{2,1,0:T(8,128)S(1)}, bf16[512,256]{1,0:T(8,128)(2,1)S(1)}, f32[96,1024]{1,0:T(8,128)S(1)}, f32[3,96,128]{2,1,0:T(8,128)S(1)}) custom-call(s32[8,96,128]{2,1,0:T(8,128)S(1)} %get-tuple-element.17.grey, bf16[320,192]{1,0:T(8,128)(2,1)S(1)} %get-tuple-element.18.x_parts, bf16[384,128]{1,0:T(8,128)(2,1)S(1)} %get-tuple-element.16.z_parts), custom_call_target="tpu_custom_call" | custom-call | flops 251658240 | bytes 4000000 | tf_op jit(solution)/shard_map/early/pallas_call | solution.py:822
  8.4 0.0 collective-permute-done.far
  8.4 0.0 collective-permute-done.1.near
  8.4 0.0 copy-done.3
  8.4 0.0 copy-start.4
  8.4 0.0 copy-start
  8.4 0.0 copy-start.2
  8.4 1.8 %late.1 = bf16[4,128,128]{2,1,0:T(8,128)(2,1)} custom-call(bf16[208,128]{1,0:T(8,128)(2,1)S(1)} %collective-permute-done.far, bf16[208,128]{1,0:T(8,128)(2,1)S(1)} %collective-permute-done.1.near, bf16[128,96]{1,0:T(8,128)(2,1)S(1)} %copy-done.3, bf16[384,128]{1,0:T(8,128)(2,1)S(1)} %get-tuple-element.16.z_parts, ...), custom_call_target="tpu_custom_call" | custom-call | flops 125829120 | bytes 4000000 | tf_op jit(solution)/shard_map/late/pallas_call | solution.py:839
  10.2 0.0 copy-start.1
  10.3 6.0 %all-to-all-start = ((bf16[4,128,128]{2,1,0:T(8,128)(2,1)}), bf16[4,128,128]{2,1,0:T(8,128)(2,1)S(1)}, u32[]{:S(2)}, u32[]{:S(2)}) async-start(bf16[4,128,128]{2,1,0:T(8,128)(2,1)} %late.1), calls=%async_computation | async-start | bytes 262144 | tf_op jit(solution)/shard_map/all_to_all | solution.py:856
  16.3 0.0 copy-done.4
  16.3 0.1 copy.18
  16.4 0.1 eq.15
  16.5 0.6 %copy-done.5 = f32[8]{0:T(128)S(1)} copy-done((f32[8]{0:T(128)S(1)}, f32[8]{0:T(128)}, u32[]{:S(2)}) %copy-start.5) | copy-done | bytes 56
  17.0 0.2 select_reduce_fusion
  17.2 0.1 copy.19.tools
  17.3 2.8 %all-to-all-done.chunks = bf16[4,128,128]{2,1,0:T(8,128)(2,1)S(1)} async-done(((bf16[4,128,128]{2,1,0:T(8,128)(2,1)}), bf16[4,128,128]{2,1,0:T(8,128)(2,1)S(1)}, u32[]{:S(2)}, u32[]{:S(2)}) %all-to-all-start) | async-done | bytes 131104 | tf_op jit(solution)/shard_map/all_to_all | solution.py:856
  20.1 0.0 copy-done
  20.1 0.0 copy-done.2
  20.1 0.0 copy-done.1
  20.1 1.5 %cure.1 = (f32[6,128]{1,0:T(8,128)}, f32[6,128]{1,0:T(8,128)}, f32[3,6,128]{2,1,0:T(8,128)}) custom-call(bf16[4,128,128]{2,1,0:T(8,128)(2,1)S(1)} %all-to-all-done.chunks, f32[6,128]{1,0:T(8,128)S(1)} %get-tuple-element.23.temp.temp_in, f32[6,128]{1,0:T(8,128)S(1)} %get-tuple-element.24.cure.cure_in, f32[6,1]{1,0:T(8,128)S(1)} %copy.19.tools, ...), custom_call_target="tpu_custom_call" | custom-call | tf_op jit(solution)/shard_map/cure/pallas_call | solution.py:865
  (2 shorter events, 0.0 us)
Async XLA Ops:
  1.8 6.5 %collective-permute-start = (bf16[208,128]{1,0:T(8,128)(2,1)S(1)}, bf16[208,128]{1,0:T(8,128)(2,1)S(1)}, u32[]{:S(2)}, u32[]{:S(2)}) collective-permute-start(bf16[208,128]{1,0:T(8,128)(2,1)S(1)} %get-tuple-element.14), channel_id=1, source_target_pairs={{4,8},{5,9},{6,10},{7,11},{12,16},{13,17},{14,18},{15,19},{20,24},... | collective-permute-start | bytes 159752 | tf_op jit(solution)/shard_map/ppermute | solution.py:796
  2.5 5.9 %collective-permute-start.1 = (bf16[208,128]{1,0:T(8,128)(2,1)S(1)}, bf16[208,128]{1,0:T(8,128)(2,1)S(1)}, u32[]{:S(2)}, u32[]{:S(2)}) collective-permute-start(bf16[208,128]{1,0:T(8,128)(2,1)S(1)} %get-tuple-element.15), channel_id=1, source_target_pairs={{0,4},{1,5},{2,6},{3,7},{8,12},{9,13},{10,14},{11,15},{16,20},{17,... | collective-permute-start | bytes 159752 | tf_op jit(solution)/shard_map/ppermute | solution.py:796
  6.8 1.5 %copy-start.3 = (bf16[128,96]{1,0:T(8,128)(2,1)S(1)}, bf16[128,96]{1,0:T(8,128)(2,1)}, u32[]{:S(2)}) copy-start(bf16[128,96]{1,0:T(8,128)(2,1)} %constant.17.clone.x_late) | copy-start | bytes 73732
  8.4 7.9 %copy-start.4 = (s32[3,2]{0,1:T(2,128)S(1)}, s32[3,2]{0,1:T(2,128)}, u32[]{:S(2)}) copy-start(s32[3,2]{0,1:T(2,128)} %param.15) | copy-start | bytes 76
  8.4 11.7 %copy-start = (bf16[656,160]{1,0:T(8,128)(2,1)S(1)}, bf16[656,160]{1,0:T(8,128)(2,1)}, u32[]{:S(2)}) copy-start(bf16[656,160]{1,0:T(8,128)(2,1)} %constant.19.clone.steep) | copy-start | bytes 629764
  8.4 11.7 %copy-start.2 = (bf16[384,128]{1,0:T(8,128)(2,1)S(1)}, bf16[384,128]{1,0:T(8,128)(2,1)}, u32[]{:S(2)}) copy-start(bf16[384,128]{1,0:T(8,128)(2,1)} %constant.20.clone.rim_bands) | copy-start | bytes 294916
  10.2 9.9 %copy-start.1 = (bf16[512,256]{1,0:T(8,128)(2,1)S(1)}, bf16[512,256]{1,0:T(8,128)(2,1)}, u32[]{:S(2)}) copy-start(bf16[512,256]{1,0:T(8,128)(2,1)} %constant.18.clone.flat) | copy-start | bytes 786436
  10.3 9.9 %all-to-all-start = ((bf16[4,128,128]{2,1,0:T(8,128)(2,1)}), bf16[4,128,128]{2,1,0:T(8,128)(2,1)S(1)}, u32[]{:S(2)}, u32[]{:S(2)}) async-start(bf16[4,128,128]{2,1,0:T(8,128)(2,1)} %late.1), calls=%async_computation | async-start | bytes 262144 | tf_op jit(solution)/shard_map/all_to_all | solution.py:856
  16.4 0.7 %copy-start.5 = (f32[8]{0:T(128)S(1)}, f32[8]{0:T(128)}, u32[]{:S(2)}) copy-start(f32[8]{0:T(128)} %param.14) | copy-start | bytes 100
